TPU v7x, 128 devices: a whole 4x4x4 slice. The times are simulated.
128 devices in a mesh: freq: 4 (over x), tile: 32 (over y, z, core).
Axes of the slice: x: 4, y: 4, z: 4, core: 2. Of those that a mesh axis runs over, the one named last changes fastest.
Arguments:
- voltages: bfloat16 [4096, 98688], P(('freq', 'tile')), may hold values from -16 to 16, as said below
- channel_ids: int32 [12], replicated, may hold values from 1 to 63
- start_basis: float32 [2, 8, 4096], replicated, may hold values from -0.0625 to 0.0625
Outputs:
- cleaned: float32 [2, 12, 768, 4096], P(None, 'freq', 'tile')
Inputs may be any that keep to these rules, and one draw needn't show every extreme that they name: `voltages`: real samples of each input over the whole window.
All inputs are finite; a program needn't handle non-finite values.
Results may differ from a plain program's by a relative error of at most 0.0048.
Values may be sent and summed in bfloat16 or wider, within the bound.
No kernel may reach another device: no remote copies, remote signals or barrier semaphores. Data moves between devices by JAX's collectives and lax.ppermute only.
A program may use at most 128 MiB of HBM per device.

v0:
```python
import math

import jax
import jax.numpy as jnp
from jax import lax
from jax.sharding import PartitionSpec as P

TAPS = 4
P_SIZE = 128
ITERS = 3


loading = 0.5
highest = lax.Precision.HIGHEST


def make_table(channel_ids, taps_count, points):
    length = taps_count * points
    offsets = jnp.arange(length, dtype=jnp.float32)
    shifted = (offsets + 0.5 - length / 2.0) / points
    window = jnp.sinc(shifted) * (0.5 - 0.5 * jnp.cos(2.0 * math.pi * (offsets + 0.5) / length))
    window = window / jnp.sqrt(jnp.sum(window * window))
    window = window.reshape(taps_count, points)
    phases = channel_ids[:, None] * jnp.arange(points, dtype=jnp.int32)[None, :] % points
    angles = 2.0 * math.pi / points * phases.astype(jnp.float32)
    rotors = jnp.stack([jnp.cos(angles), -jnp.sin(angles)])
    return (window[:, None, None, :] * rotors[None]).astype(jnp.bfloat16)


def contract(form, left, right):
    return jnp.einsum(form, left, right, precision=highest)


def image_of(values, basis):
    real_v, imag_v = (values[0], values[1])
    real_q, imag_q = (basis[0], basis[1])
    weight_re = contract("csi,cki->csk", real_v, real_q) + contract("csi,cki->csk", imag_v, imag_q)
    weight_im = contract("csi,cki->csk", real_v, imag_q) - contract("csi,cki->csk", imag_v, real_q)
    image_re = contract("csi,csk->cki", real_v, weight_re) - contract(
        "csi,csk->cki", imag_v, weight_im
    )
    image_im = contract("csi,csk->cki", real_v, weight_im) + contract(
        "csi,csk->cki", imag_v, weight_re
    )
    return jnp.stack([image_re, image_im])


def gram_parts(image):
    real_z, imag_z = (image[0], image[1])
    gram_re = contract("cki,cji->ckj", real_z, real_z) + contract("cki,cji->ckj", imag_z, imag_z)
    gram_im = contract("cki,cji->ckj", real_z, imag_z) - contract("cki,cji->ckj", imag_z, real_z)
    return (gram_re, gram_im)


def lower_factor(gram_re, gram_im):
    basis_width = gram_re.shape[-1]
    lower_re = {}
    lower_im = {}
    pivots = []
    for column in range(basis_width):
        pivot_square = gram_re[:, column, column]
        for earlier in range(column):
            pivot_square = (
                pivot_square - lower_re[column, earlier] ** 2 - lower_im[column, earlier] ** 2
            )
        pivot_value = jnp.sqrt(pivot_square)
        pivots.append(pivot_value)
        for row_at in range(column + 1, basis_width):
            value_re = gram_re[:, row_at, column]
            value_im = gram_im[:, row_at, column]
            for earlier in range(column):
                left_re, left_im = (lower_re[row_at, earlier], lower_im[row_at, earlier])
                right_re, right_im = (lower_re[column, earlier], lower_im[column, earlier])
                value_re = value_re - (left_re * right_re + left_im * right_im)
                value_im = value_im - (left_im * right_re - left_re * right_im)
            lower_re[row_at, column] = value_re / pivot_value
            lower_im[row_at, column] = value_im / pivot_value
    return (lower_re, lower_im, pivots)


def apply_factor(image, lower_re, lower_im, pivots):
    basis_width = image.shape[2]
    result_re = []
    result_im = []
    for column in range(basis_width):
        value_re = image[0, :, column, :]
        value_im = image[1, :, column, :]
        for earlier in range(column):
            left_re, left_im = (result_re[earlier], result_im[earlier])
            right_re = lower_re[column, earlier][:, None]
            right_im = lower_im[column, earlier][:, None]
            value_re = value_re - (left_re * right_re + left_im * right_im)
            value_im = value_im - (left_im * right_re - left_re * right_im)
        divisor = pivots[column][:, None]
        result_re.append(value_re / divisor)
        result_im.append(value_im / divisor)
    return jnp.stack([jnp.stack(result_re, axis=1), jnp.stack(result_im, axis=1)])


def remove_subspace(values, basis):
    real_v, imag_v = (values[0], values[1])
    real_q, imag_q = (basis[0], basis[1])
    coord_re = contract("cki,csi->cks", real_q, real_v) + contract("cki,csi->cks", imag_q, imag_v)
    coord_im = contract("cki,csi->cks", real_q, imag_v) - contract("cki,csi->cks", imag_q, real_v)
    fitted_re = contract("cki,cks->csi", real_q, coord_re) - contract(
        "cki,cks->csi", imag_q, coord_im
    )
    fitted_im = contract("cki,cks->csi", real_q, coord_im) + contract(
        "cki,cks->csi", imag_q, coord_re
    )
    return values - jnp.stack([fitted_re, fitted_im])


def body(voltages, channel_ids, start_basis):
    inputs_local, samples_count = voltages.shape
    freq_count = lax.axis_size("freq")
    tile_count = lax.axis_size("tile")
    group_count = freq_count * tile_count
    chan_local = channel_ids.shape[0] // freq_count
    spectra_all = samples_count // P_SIZE - TAPS + 1
    spectra_local = spectra_all // tile_count
    block_width = spectra_local * inputs_local
    coeffs = make_table(channel_ids, TAPS, P_SIZE).reshape(TAPS, 2, freq_count, chan_local, P_SIZE)
    frames = voltages.reshape(inputs_local, spectra_all + TAPS - 1, P_SIZE)
    summed = jnp.zeros((2, freq_count, tile_count, chan_local, block_width), jnp.float32)
    for offset in range(TAPS):
        window_frames = frames[:, offset : offset + spectra_all, :].reshape(
            inputs_local, tile_count, spectra_local, P_SIZE
        )
        term = jnp.einsum(
            "rfcp,itsp->rftcsi", coeffs[offset], window_frames, preferred_element_type=jnp.float32
        )
        summed = summed + term.reshape(2, freq_count, tile_count, chan_local, block_width)
    local_spectra = summed.astype(jnp.bfloat16)
    parcel = local_spectra.reshape(2, group_count, chan_local, 1, block_width)
    arrived = lax.all_to_all(parcel, ("freq", "tile"), split_axis=1, concat_axis=3, tiled=True)
    inputs_all = inputs_local * group_count
    ordered = arrived.reshape(2, chan_local, group_count, spectra_local, inputs_local).astype(
        jnp.float32
    )
    values = jnp.transpose(ordered, (0, 1, 3, 2, 4)).reshape(
        2, chan_local, spectra_local, inputs_all
    )
    basis_width = start_basis.shape[1]
    basis = jnp.broadcast_to(start_basis[:, None], (2, chan_local, basis_width, inputs_all))
    share_rows = inputs_all // tile_count
    share_start = lax.axis_index("tile") * share_rows
    for step_at in range(ITERS):
        partial_image = image_of(values, basis)
        share = lax.psum_scatter(partial_image, "tile", scatter_dimension=3, tiled=True)
        basis_share = lax.dynamic_slice_in_dim(basis, share_start, share_rows, 3)
        image = share / spectra_all + loading * basis_share
        gram_re, gram_im = gram_parts(image)
        gram_re, gram_im = lax.psum((gram_re, gram_im), "tile")
        lower_re, lower_im, pivots = lower_factor(gram_re, gram_im)
        new_share = apply_factor(image, lower_re, lower_im, pivots)
        basis = lax.all_gather(new_share, "tile", axis=3, tiled=True)
    return remove_subspace(values, basis)


def solution(mesh):
    in_specs = (P(("freq", "tile"), None), P(), P())
    out_specs = P(None, "freq", "tile", None)
    return jax.shard_map(body, mesh=mesh, in_specs=in_specs, out_specs=out_specs, check_vma=False)
```

profile of v0, /device:TPU:1, one launch (start us, length us, event | category | flops | bytes accessed | tf_op | source)
XLA Modules:
  0.0 883.9 jit_solution(13837673244160623513)
XLA Ops:
  7.2 0.9 fusion.46
  9.0 7.3 reshape.53938
  16.3 19.9 %fusion.237 = (bf16[32,768,128]{2,1,0:T(8,128)(2,1)}, bf16[32,768,128]{2,1,0:T(8,128)(2,1)S(1)}, bf16[32,768,128]{2,1,0:T(8,128)(2,1)}, bf16[32,768,128]{2,1,0:T(8,128)(2,1)}) fusion(bf16[32,771,128]{2,1,0:T(8,128)(2,1)} %reshape.53938), kind=kLoop, calls=%fused_computation.950 | loop fusion | bytes 50331648 | tf_op jit(solution)/shard_map/slice | solution.py:127
  36.2 14.7 %fusion.2 = f32[2,4,3,32,32,24]{4,1,5,3,2,0:T(4,128)} fusion(bf16[32,32,24,128,1,1]{3,2,1,0,5,4:T(8,128)(2,1)} %bitcast.624, bf16[2,4,3,128,1,1]{3,0,2,1,5,4:T(2,128)(2,1)S(1)} %bitcast.637), kind=kOutput, calls=%fused_computation.3 | convolution fusion | flops 150994944 | bytes 8656896 | tf_op jit(solution)/shard_map/rfcp,itsp->rftcsi/dot_general | solution.py:130
  50.8 14.7 %fusion.4 = f32[2,4,3,32,32,24]{4,1,5,3,2,0:T(4,128)} fusion(bf16[32,32,24,128,1,1]{3,2,1,0,5,4:T(8,128)(2,1)} %bitcast.623, bf16[2,4,3,128,1,1]{3,0,2,1,5,4:T(2,128)(2,1)S(1)} %bitcast.636), kind=kOutput, calls=%fused_computation.5 | convolution fusion | flops 150994944 | bytes 8656896 | tf_op jit(solution)/shard_map/rfcp,itsp->rftcsi/dot_general | solution.py:130
  65.5 12.4 %fusion = f32[2,4,3,32,32,24]{4,1,5,3,2,0:T(4,128)} fusion(bf16[32,32,24,128,1,1]{3,2,1,0,5,4:T(8,128)(2,1)S(1)} %bitcast.622, bf16[2,4,3,128,1,1]{3,0,2,1,5,4:T(2,128)(2,1)S(1)} %bitcast.635), kind=kOutput, calls=%fused_computation.1 | convolution fusion | flops 150994944 | bytes 8656896 | tf_op jit(solution)/shard_map/rfcp,itsp->rftcsi/dot_general | solution.py:130
  77.9 27.5 %fusion.8 = bf16[2,4,32,3,24,32]{2,1,4,5,3,0:T(4,128)(2,1)} fusion(f32[2,4,3,32,32,24]{4,1,5,3,2,0:T(4,128)} %fusion, f32[2,4,3,32,32,24]{4,1,5,3,2,0:T(4,128)} %fusion.2, f32[2,4,3,32,32,24]{4,1,5,3,2,0:T(4,128)} %fusion.4, bf16[32,32,24,128,1,1]{3,2,1,0,5,4:T(8,128)(2,1)} %bitcast.625, bf16[2,4,3,128,1,1]{3,0,2,1,5,4:T(2,128)(2,1)S(1)} %bitcast.638), kind=kOutput, calls=%fused_computation.9 | convolution fusion | flops 153354240 | bytes 14555136 | tf_op jit(solution)/shard_map/rfcp,itsp->rftcsi/dot_general | solution.py:130
  105.4 11.1 %copy.71 = bf16[2,4,32,3,24,32]{5,4,0,3,2,1:T(8,128)(2,1)} copy(bf16[2,4,32,3,24,32]{2,1,4,5,3,0:T(4,128)(2,1)} %fusion.8) | data formatting | bytes 2359296 | tf_op jit(solution)/shard_map/convert_element_type | solution.py:134
  116.4 7.7 reshape.53956
  124.2 11.5 %all-to-all-start = ((bf16[2,128,3,1,768]{4,0,3,2,1:T(2,128)(2,1)}), bf16[2,128,3,1,768]{4,0,3,2,1:T(2,128)(2,1)S(1)}, u32[]{:S(2)}, u32[]{:S(2)}) async-start(bf16[2,128,3,1,768]{4,0,3,2,1:T(2,128)(2,1)} %reshape.53956), calls=%async_computation | async-start | bytes 2359296 | tf_op jit(solution)/shard_map/all_to_all | solution.py:136
  135.7 0.7 slice_bitcast_fusion.23
  136.4 19.9 %all-to-all-done = bf16[2,128,3,1,768]{4,0,3,2,1:T(2,128)(2,1)S(1)} async-done(((bf16[2,128,3,1,768]{4,0,3,2,1:T(2,128)(2,1)}), bf16[2,128,3,1,768]{4,0,3,2,1:T(2,128)(2,1)S(1)}, u32[]{:S(2)}, u32[]{:S(2)}) %all-to-all-start) | async-done | bytes 1179680 | tf_op jit(solution)/shard_map/all_to_all | solution.py:136
  156.5 0.9 copy.43
  157.7 1.9 copy.45
  159.5 3.8 squeeze.780
  163.3 1.9 copy.46
  165.2 3.8 squeeze.781
  173.1 0.9 pad_maximum_fusion
  174.9 69.5 %reduce-scatter.4.cloned.1.call-done = f32[2,3,8,128]{3,2,1,0:T(8,128)} async-done(((f32[2,3,8,4096]{3,2,1,0:T(8,128)}), f32[2,3,8,128]{3,2,1,0:T(8,128)}) %reduce-scatter.4.cloned.1.call-update) | async-done | bytes 24592 | tf_op jit(solution)/shard_map/reduce_scatter | solution.py:150
  244.3 0.7 multiply_add_fusion.2
  245.7 120.9 %all-reduce.2 = (f32[3,8,8]{2,1,0:T(8,128)S(1)}, f32[3,8,8]{2,1,0:T(8,128)S(1)}) all-reduce(f32[3,8,8]{2,1,0:T(8,128)S(1)} %convolution_add_fusion.9, f32[3,8,8]{2,1,0:T(8,128)S(1)} %convolution_subtract_fusion.9), channel_id=1, replica_groups=mesh['freq'=4,'tile'=32] {'tile'}, use_global_device_ids=true, to_apply=%region_2.3 | all-reduce | flops 384 | bytes 3072 | tf_op jit(solution)/shard_map/psum | solution.py:154
  368.8 27.3 %all_gather.9 = f32[2,3,8,4096]{3,2,1,0:T(8,128)S(1)} all-gather(f32[2,3,8,128]{3,2,1,0:T(8,128)S(1)} %pad_maximum_fusion.3), channel_id=1, replica_groups=mesh['freq'=4,'tile'=32] {'tile'}, dimensions={3}, use_global_device_ids=true | all-gather | bytes 811008 | tf_op jit(solution)/shard_map/all_gather | solution.py:157
  400.3 0.9 pad_maximum_fusion.1
  401.3 74.0 %reduce-scatter.6.cloned.1.call-done = f32[2,3,8,128]{3,2,1,0:T(8,128)} async-done(((f32[2,3,8,4096]{3,2,1,0:T(8,128)}), f32[2,3,8,128]{3,2,1,0:T(8,128)}) %reduce-scatter.6.cloned.1.call-update) | async-done | bytes 24592 | tf_op jit(solution)/shard_map/reduce_scatter | solution.py:150
  475.3 0.7 multiply_add_fusion.1
  476.7 121.0 %all-reduce.1 = (f32[3,8,8]{2,1,0:T(8,128)S(1)}, f32[3,8,8]{2,1,0:T(8,128)S(1)}) all-reduce(f32[3,8,8]{2,1,0:T(8,128)S(1)} %convolution_add_fusion.7, f32[3,8,8]{2,1,0:T(8,128)S(1)} %convolution_subtract_fusion.7), channel_id=1, replica_groups=mesh['freq'=4,'tile'=32] {'tile'}, use_global_device_ids=true, to_apply=%region_5.6 | all-reduce | flops 384 | bytes 3072 | tf_op jit(solution)/shard_map/psum | solution.py:154
  600.0 27.3 %all_gather.10 = f32[2,3,8,4096]{3,2,1,0:T(8,128)S(1)} all-gather(f32[2,3,8,128]{3,2,1,0:T(8,128)S(1)} %pad_maximum_fusion.4), channel_id=1, replica_groups=mesh['freq'=4,'tile'=32] {'tile'}, dimensions={3}, use_global_device_ids=true | all-gather | bytes 811008 | tf_op jit(solution)/shard_map/all_gather | solution.py:157
  631.4 0.9 pad_maximum_fusion.2
  632.4 4.4 copy.44
  636.8 6.9 reshape.53947
  643.7 62.7 %reduce-scatter.8.cloned.1.call-done = f32[2,3,8,128]{3,2,1,0:T(8,128)} async-done(((f32[2,3,8,4096]{3,2,1,0:T(8,128)}), f32[2,3,8,128]{3,2,1,0:T(8,128)}) %reduce-scatter.8.cloned.1.call-update) | async-done | bytes 24592 | tf_op jit(solution)/shard_map/reduce_scatter | solution.py:150
  706.4 0.8 multiply_add_fusion
  707.5 0.8 convolution_subtract_fusion.5
  708.3 0.8 convolution_add_fusion.5
  709.0 120.9 %all-reduce = (f32[3,8,8]{2,1,0:T(8,128)S(1)}, f32[3,8,8]{2,1,0:T(8,128)}) all-reduce(f32[3,8,8]{2,1,0:T(8,128)} %convolution_add_fusion.5, f32[3,8,8]{2,1,0:T(8,128)} %convolution_subtract_fusion.5), channel_id=1, replica_groups=mesh['freq'=4,'tile'=32] {'tile'}, use_global_device_ids=true, to_apply=%region_8.9 | all-reduce | flops 384 | bytes 3072 | tf_op jit(solution)/shard_map/psum | solution.py:154
  830.5 1.7 slice_reduce_fusion.3
  832.2 1.2 slice_reduce_fusion.42
  834.3 2.0 subtract_divide_fusion.1
  836.5 0.8 stack.76
  837.2 1.5 subtract_divide_fusion
  838.8 1.3 stack.156
  840.1 0.7 pad_maximum_fusion.5
  840.8 27.3 %all_gather.11 = f32[2,3,8,4096]{3,2,1,0:T(8,128)S(1)} all-gather(f32[2,3,8,128]{3,2,1,0:T(8,128)S(1)} %pad_maximum_fusion.5), channel_id=1, replica_groups=mesh['freq'=4,'tile'=32] {'tile'}, dimensions={3}, use_global_device_ids=true | all-gather | bytes 811008 | tf_op jit(solution)/shard_map/all_gather | solution.py:157
  870.0 1.1 fusion.25
  871.7 1.1 fusion.23
  872.8 1.1 fusion.10
  874.0 1.1 fusion.9
  875.1 1.7 maximum_subtract_fusion
  (167 shorter events, 23.7 us)
Async XLA Ops:
  116.4 19.3 %copy-start.4 = (f32[2,8,4096]{2,1,0:T(8,128)S(1)}, f32[2,8,4096]{2,1,0:T(8,128)}, u32[]{:S(2)}) copy-start(f32[2,8,4096]{2,1,0:T(8,128)} %param.5) | copy-start | bytes 786436
  124.2 32.2 %all-to-all-start = ((bf16[2,128,3,1,768]{4,0,3,2,1:T(2,128)(2,1)}), bf16[2,128,3,1,768]{4,0,3,2,1:T(2,128)(2,1)S(1)}, u32[]{:S(2)}, u32[]{:S(2)}) async-start(bf16[2,128,3,1,768]{4,0,3,2,1:T(2,128)(2,1)} %reshape.53956), calls=%async_computation | async-start | bytes 2359296 | tf_op jit(solution)/shard_map/all_to_all | solution.py:136
  135.7 108.7 %reduce-scatter.4.cloned.1.call-start = ((), (), s32[]{:S(2)}) async-start(), calls=%async_computation.4 | async-start | bytes 811008 | tf_op jit(solution)/shard_map/reduce_scatter | solution.py:150
  157.6 11.4 %copy-start.1 = (f32[8,4096]{1,0:T(8,128)S(1)}, f32[8,4096]{1,0:T(8,128)}, u32[]{:S(2)}) copy-start(f32[8,4096]{1,0:T(8,128)} %get-tuple-element.521) | copy-start | bytes 393220
  157.6 12.0 %copy-start.2 = (f32[8,4096]{1,0:T(8,128)S(1)}, f32[8,4096]{1,0:T(8,128)}, u32[]{:S(2)}) copy-start(f32[8,4096]{1,0:T(8,128)} %get-tuple-element.522) | copy-start | bytes 393220
  174.1 301.2 %reduce-scatter.6.cloned.1.call-start = ((), (), s32[]{:S(2)}) async-start(), calls=%async_computation.5 | async-start | bytes 811008 | tf_op jit(solution)/shard_map/reduce_scatter | solution.py:150
  401.2 305.2 %reduce-scatter.8.cloned.1.call-start = ((), (), s32[]{:S(2)}) async-start(), calls=%async_computation.6 | async-start | bytes 811008 | tf_op jit(solution)/shard_map/reduce_scatter | solution.py:150
  627.3 2.3 copy-start
  707.2 1.1 copy-start.3
  833.4 2.9 copy-start.8
  833.5 2.9 copy-start.9
  833.5 2.9 copy-start.10
  833.5 2.9 copy-start.17
  833.5 2.8 copy-start.18
  833.6 2.8 copy-start.11
  833.6 2.8 copy-start.12
  833.7 2.7 copy-start.13
  833.8 2.7 copy-start.14
  833.8 2.6 copy-start.15
  833.9 2.5 copy-start.5
  833.9 2.5 copy-start.7
  834.1 2.4 copy-start.6
  834.2 2.3 copy-start.16
  834.3 2.2 copy-start.19
Sparse Core Ops, SparseCore 0:
  174.2 70.0 reduce-scatter.3
  401.4 73.9 reduce-scatter.5
  632.5 73.8 reduce-scatter.7
where the time goes:
time: 889 us; the launch traced here: 884 us
  blocking collectives  445 us (50%)
  waiting for transfers between devices  226 us (25%)
  matrix products  91.4 us (10%)
  local copies, waits for them, and re-layouts  78.2 us (9%)
  other arithmetic  16.2 us (2%)
  between operations  15.5 us (2%)
  starting transfers between devices  11.6 us (1%)
    psum x3, blocking collectives, body(): gram_re, gram_im = lax.psum((gram_re, gram_im), 'tile')  363 us
    reduce_scatter x3, waiting for transfers between devices, body(): lax.psum_scatter(partial_image, 'tile', scatter_dimension=3, tiled=True)  206 us
    all_gather x3, blocking collectives, body(): basis = lax.all_gather(new_share, 'tile', axis=3, tiled=True)  81.9 us
    dot_general x4, matrix products, body(): jnp.einsum('rfcp,itsp->rftcsi', coeffs[offset], window_frames, preferred_...  69.2 us
    dot_general x44, matrix products, contract(): return jnp.einsum(form, left, right, precision=highest)  22.3 us
    all_to_all x1, waiting for transfers between devices, body(): lax.all_to_all(parcel, ('freq', 'tile'), split_axis=1, concat_axis=3, til...  19.9 us
    slice x1, local copies, waits for them, and re-layouts, body(): frames[:, offset:offset + spectra_all, :]  19.9 us
    convert_element_type x2, local copies, waits for them, and re-layouts, body(): local_spectra = summed.astype(jnp.bfloat16)  18.8 us
  transfers between devices with their start and end apart: 4, of which 4 were waited for; matrix products, arithmetic and copies ran while one was open for 1% of the time, Pallas kernels for 0%

commit v1 on v0

v1 whole, which is shorter than its diff:
```python
import functools
import math

import jax
import jax.numpy as jnp
from jax import lax
from jax.experimental import pallas as pl
from jax.experimental.pallas import tpu as pltpu
from jax.sharding import Mesh, PartitionSpec as P

TAPS = 4
P_SIZE = 128
INPUTS = 4096
KDIM = 8
CHANNELS = 12
SPECTRA = 768
LOADING = 0.5

NX, NY, NZ, NC = 4, 4, 4, 2
LOCAL = INPUTS // (NX * NY * NZ * NC)
GROUP = CHANNELS // NX
HELD = LOCAL * NX * NZ
PHASES = 6
ROWS = SPECTRA // PHASES
SPAN = (PHASES + TAPS - 1) * P_SIZE
SHARE = SPECTRA // (NY * NZ * NC)
RC = 2 * CHANNELS

F32, BF16 = jnp.float32, jnp.bfloat16
VMEM_LIMIT = 56 * 1024 * 1024
params = pltpu.CompilerParams(vmem_limit_bytes=VMEM_LIMIT)
in_vmem = pl.BlockSpec(memory_space=pltpu.VMEM)


def dot_nn(a, b):
    return lax.dot_general(a, b, (((1,), (0,)), ((), ())), preferred_element_type=F32)


def dot_nt(a, b):
    return lax.dot_general(a, b, (((1,), (1,)), ((), ())), preferred_element_type=F32)


def dot_tn(a, b, precision=None):
    return lax.dot_general(
        a, b, (((0,), (0,)), ((), ())), preferred_element_type=F32, precision=precision
    )


def split3(x):
    hi = x.astype(BF16)
    rest = x - hi.astype(F32)
    mid = rest.astype(BF16)
    lo = (rest - mid.astype(F32)).astype(BF16)
    return jnp.concatenate([hi, mid, lo], axis=0)


def sum3(x):
    n = x.shape[0] // 3
    return x[:n] + (x[n : 2 * n] + x[2 * n :])


def make_table(channel_ids):
    length = TAPS * P_SIZE
    offsets = jnp.arange(length, dtype=F32)
    shifted = (offsets + 0.5 - length / 2.0) / P_SIZE
    window = jnp.sinc(shifted) * (0.5 - 0.5 * jnp.cos(2.0 * math.pi * (offsets + 0.5) / length))
    window = window / jnp.sqrt(jnp.sum(window * window))
    window = window.reshape(TAPS, P_SIZE)
    phases = channel_ids[:, None] * jnp.arange(P_SIZE, dtype=jnp.int32)[None, :] % P_SIZE
    angles = 2.0 * math.pi / P_SIZE * phases.astype(F32)
    rotors = jnp.stack([jnp.cos(angles), -jnp.sin(angles)])
    return (window[:, None, None, :] * rotors[None]).astype(BF16)


def banded_table(channel_ids):
    columns = jnp.transpose(make_table(channel_ids), (0, 3, 1, 2)).reshape(TAPS * P_SIZE, RC)
    parts = [
        jnp.pad(columns, ((q * P_SIZE, (PHASES - 1 - q) * P_SIZE), (0, 0))) for q in range(PHASES)
    ]
    parts.append(jnp.zeros((SPAN, 256 - PHASES * RC), BF16))
    return jnp.concatenate(parts, axis=1)


STEP_ROWS = 8


def channelize_kernel(x_ref, c_ref, o_ref, wide, tall):
    def filter_rows(at, carry):
        rows = []
        for k in range(STEP_ROWS):
            start = pl.multiple_of((at * STEP_ROWS + k) * (PHASES * P_SIZE), 128)
            rows.append(x_ref[:, pl.ds(start, SPAN)])
        got = dot_nn(jnp.concatenate(rows, axis=0), c_ref[...])
        wide[pl.ds(at * STEP_ROWS, STEP_ROWS)] = got.reshape(STEP_ROWS, LOCAL, 256)
        return carry

    lax.fori_loop(0, ROWS // STEP_ROWS, filter_rows, 0)

    for n in range(LOCAL):
        turned = jnp.concatenate(
            [wide[:, n, 0:128].T, wide[:, n, 128:256].T[0 : PHASES * RC - 128]], axis=0
        )
        for q in range(PHASES):
            tall[:, n, q * 128 : (q + 1) * 128] = turned[q * RC : (q + 1) * RC]

    for x in range(NX):
        for z in range(NZ):
            for r in range(2):
                if z < GROUP:
                    o_ref[x * NZ + z, r] = tall[r * CHANNELS + x * GROUP + z].astype(BF16)
                else:
                    o_ref[x * NZ + z, r] = jnp.zeros((LOCAL, SPECTRA), BF16)


def channelize(x, table):
    return pl.pallas_call(
        channelize_kernel,
        out_shape=jax.ShapeDtypeStruct((NX * NZ, 2, LOCAL, SPECTRA), BF16),
        in_specs=[in_vmem] * 2,
        out_specs=in_vmem,
        scratch_shapes=[
            pltpu.VMEM((ROWS, LOCAL, 256), F32),
            pltpu.VMEM((RC, LOCAL, SPECTRA), F32),
        ],
        compiler_params=params,
    )(x, table)


def halves(v_ref):
    return v_ref[:, 0].reshape(HELD, SPECTRA), v_ref[:, 1].reshape(HELD, SPECTRA)


def turn_kernel(v_ref, o_ref):
    row = lax.broadcasted_iota(jnp.int32, (SPECTRA, SPECTRA), 0)
    col = lax.broadcasted_iota(jnp.int32, (SPECTRA, SPECTRA), 1)
    pick = jnp.where(row == (col % ROWS) * PHASES + col // ROWS, 1.0, 0.0).astype(BF16)
    real_v, imag_v = halves(v_ref)
    real_t, imag_t = dot_nt(pick, real_v), dot_nt(pick, imag_v)
    for t in range(NY * NZ * NC):
        rows = slice(t * SHARE, (t + 1) * SHARE)
        o_ref[t] = jnp.concatenate([real_t[rows], imag_t[rows]], axis=0).astype(BF16)


def turn(v):
    return pl.pallas_call(
        turn_kernel,
        out_shape=jax.ShapeDtypeStruct((NY * NZ * NC, 2 * SHARE, HELD), BF16),
        in_specs=[in_vmem],
        out_specs=in_vmem,
        compiler_params=params,
    )(v)


def project(v_halves, pieces):
    a, b = sum3(dot_nn(pieces, v_halves[0])), sum3(dot_nn(pieces, v_halves[1]))
    return a[0:KDIM] + b[KDIM:], a[KDIM:] - b[0:KDIM]


def expand(v_halves, pieces):
    a, b = sum3(dot_nt(pieces, v_halves[0])), sum3(dot_nt(pieces, v_halves[1]))
    return a[0:KDIM] - b[KDIM:], a[KDIM:] + b[0:KDIM]


def gram_from(products):
    p0, p1, p2 = products[0:16], products[16:32], products[32:48]
    m = (p0 + (p1 + p2)) + pltpu.roll(p0 + p1, 112, 1) + pltpu.roll(p0, 96, 1)
    up, down = m[0:KDIM], m[KDIM:]
    return up + pltpu.roll(down, 120, 1), down - pltpu.roll(up, 120, 1)


def eliminate(gram, others):
    row_id = lax.broadcasted_iota(jnp.int32, (KDIM, 1), 0)
    gram_re, gram_im = gram
    pairs = [(gram_re, gram_im)] + list(others)
    for j in range(KDIM):
        gram_re, gram_im = pairs[0]
        scale = 1.0 / jnp.sqrt(gram_re[j : j + 1, j : j + 1])
        below = jnp.where(row_id > j, scale, 0.0)
        m_re, m_im = gram_re[:, j : j + 1] * below, gram_im[:, j : j + 1] * below
        done = []
        for re, im in pairs:
            top_re, top_im = re[j : j + 1] * scale, im[j : j + 1] * scale
            new_re = re - (m_re * top_re - m_im * top_im)
            new_im = im - (m_re * top_im + m_im * top_re)
            here = row_id == j
            done.append((jnp.where(here, top_re, new_re), jnp.where(here, top_im, new_im)))
        pairs = done
    return pairs


def first_kernel(v_ref, q_ref, s_ref):
    u_re, u_im = project(halves(v_ref), split3(q_ref[...]))
    s_ref[...] = jnp.concatenate([u_re, u_im], axis=0)


def step_kernel(step, v_ref, z_ref, s0, s1, s2, s3, *outs):
    s = (s0[...] + s2[...]) + (s1[...] + s3[...])
    w = (s[0:KDIM, 0:SPECTRA], s[KDIM:, 0:SPECTRA])
    q = (z_ref[0:KDIM], z_ref[KDIM:])
    if step > 0:
        gram = (s[0:KDIM, SPECTRA:], s[KDIM:, SPECTRA:])
        _, w, q = eliminate(gram, [w, q])
    v = halves(v_ref)
    i_re, i_im = expand(v, split3(jnp.concatenate(w, axis=0)))
    z_re = i_re * (1.0 / SPECTRA) + LOADING * q[0]
    z_im = i_im * (1.0 / SPECTRA) + LOADING * q[1]
    z = jnp.concatenate([z_re, z_im], axis=0)
    if step == 2:
        (many_ref,) = outs
        for d in range(NY * NZ):
            many_ref[d] = z
        return
    new_z, new_s = outs
    new_z[...] = z
    pieces = split3(z)
    u_re, u_im = project(v, pieces)
    padded = jnp.concatenate([pieces, jnp.zeros((80, HELD), BF16)], axis=0)
    g_re, g_im = gram_from(dot_nt(pieces, padded))
    new_s[0:KDIM, 0:SPECTRA] = u_re
    new_s[KDIM:, 0:SPECTRA] = u_im
    new_s[0:KDIM, SPECTRA:] = g_re
    new_s[KDIM:, SPECTRA:] = g_im


def first(v, q):
    return pl.pallas_call(
        first_kernel,
        out_shape=jax.ShapeDtypeStruct((2 * KDIM, SPECTRA), F32),
        in_specs=[in_vmem] * 2,
        out_specs=in_vmem,
        compiler_params=params,
    )(v, q)


def step(at, v, z, sums):
    if at == 2:
        shapes = [jax.ShapeDtypeStruct((NY * NZ, 2 * KDIM, HELD), F32)]
    else:
        shapes = [
            jax.ShapeDtypeStruct((2 * KDIM, HELD), F32),
            jax.ShapeDtypeStruct((2 * KDIM, SPECTRA + 128), F32),
        ]
    return pl.pallas_call(
        functools.partial(step_kernel, at),
        out_shape=shapes,
        in_specs=[in_vmem] * 6,
        out_specs=[in_vmem] * len(shapes),
        compiler_params=params,
    )(v, z, *sums)


def final_kernel(v_ref, own_ref, far_ref, core_ref, o_ref, flat, basis):
    row = lax.broadcasted_iota(jnp.int32, (256, 256), 0)
    col = lax.broadcasted_iota(jnp.int32, (256, 256), 1)
    source = ((col // 32) % 2) * 128 + (col // 64) * 32 + col % 32
    place = jnp.where(row == source, 1.0, 0.0).astype(BF16)
    lane = lax.broadcasted_iota(jnp.int32, (2 * KDIM, 128), 1) // 32
    is_zero = core_ref[0] == 0
    for x in range(NX):
        lanes = slice(x * 128, (x + 1) * 128)
        rows = []
        for y in range(NY):
            for z in range(GROUP):
                at = (y * NZ + z) * NC
                rows.append(
                    jnp.concatenate([v_ref[at, :, lanes], v_ref[at + 1, :, lanes]], axis=1)
                )
        got = dot_nn(jnp.concatenate(rows, axis=0), place)
        flat[x] = got.reshape(NY, GROUP, 2 * SHARE, 256)
        for y in range(NY):
            for z in range(GROUP):
                own, far = own_ref[y * NZ + z, :, lanes], far_ref[y * NZ + z, :, lanes]
                a, b = jnp.where(is_zero, own, far), jnp.where(is_zero, far, own)
                left = jnp.where(
                    lane < 2,
                    jnp.where(lane == 0, a, pltpu.roll(b, 32, 1)),
                    jnp.where(lane == 2, pltpu.roll(a, 32, 1), pltpu.roll(b, 64, 1)),
                )
                right = jnp.where(
                    lane < 2,
                    jnp.where(lane == 0, pltpu.roll(a, 64, 1), pltpu.roll(b, 96, 1)),
                    jnp.where(lane == 2, pltpu.roll(a, 96, 1), b),
                )
                at = (x * NY + y) * 256
                basis[z, :, at : at + 128] = left
                basis[z, :, at + 128 : at + 256] = right

    lane = lax.broadcasted_iota(jnp.int32, (KDIM, 128), 1)
    unit = lane == lax.broadcasted_iota(jnp.int32, (KDIM, 128), 0) + KDIM
    unit_lanes = (lane >= KDIM) & (lane < 2 * KDIM)
    u_lanes = (lane >= 48) & (lane < 72)
    wide = NY * 256
    for z in range(GROUP):
        products = jnp.zeros((48, 128), F32)
        for x in range(NX):
            pieces = split3(basis[z, :, x * wide : (x + 1) * wide])
            block = jnp.concatenate([flat[x, y, z] for y in range(NY)], axis=1).astype(BF16)
            right = jnp.concatenate([pieces, block, jnp.zeros((32, wide), BF16)], axis=0)
            products = products + dot_nt(pieces, right)
        g_re, g_im = gram_from(products)
        up_down = sum3(products)
        up, down = up_down[0:KDIM], up_down[KDIM:]
        u_re = up + pltpu.roll(down, 104, 1)
        u_im = down - pltpu.roll(up, 104, 1)
        x_re = jnp.where(u_lanes, u_re, jnp.where(unit_lanes, jnp.where(unit, 1.0, 0.0), g_re))
        x_im = jnp.where(u_lanes, u_im, jnp.where(unit_lanes, 0.0, g_im))
        used = lane < 72
        x_re, x_im = jnp.where(used, x_re, 0.0), jnp.where(used, x_im, 0.0)
        ((x_re, x_im),) = eliminate((x_re, x_im), [])
        both = jnp.concatenate([x_re, x_im], axis=0)
        cross = jnp.concatenate([x_im, -x_re], axis=0)
        t_re = dot_tn(both, both, lax.Precision.HIGHEST)[KDIM : 2 * KDIM]
        t_im = dot_tn(cross, both, lax.Precision.HIGHEST)[KDIM : 2 * KDIM]

        def sides(a, b):
            near, away = pltpu.roll(a, 80, 1), pltpu.roll(b, 104, 1)
            return jnp.where(lane < SHARE, near, jnp.where(lane < 2 * SHARE, away, 0.0))

        t = split3(jnp.concatenate([sides(t_re, t_im), sides(-t_im, t_re)], axis=0))
        hi, mid, lo = t[0:16], t[16:32], t[32:48]
        left = jnp.concatenate([hi, hi, hi, mid, mid, lo], axis=0)
        for x in range(NX):
            pieces = split3(basis[z, :, x * wide : (x + 1) * wide])
            right = jnp.concatenate([pieces, pieces[0:32], pieces[0:16]], axis=0)
            fitted = dot_tn(left, right)[0 : 2 * SHARE]
            for y in range(NY):
                rest = flat[x, y, z] - fitted[:, y * 256 : (y + 1) * 256]
                at = x * wide + y * 256
                o_ref[0, z, :, at : at + 256] = rest[0:SHARE]
                o_ref[1, z, :, at : at + 256] = rest[SHARE:]


def finish(v, own, far, core):
    return pl.pallas_call(
        final_kernel,
        out_shape=jax.ShapeDtypeStruct((2, GROUP, SHARE, INPUTS), F32),
        in_specs=[in_vmem] * 3 + [pl.BlockSpec(memory_space=pltpu.SMEM)],
        out_specs=in_vmem,
        scratch_shapes=[
            pltpu.VMEM((NX, NY, GROUP, 2 * SHARE, 256), F32),
            pltpu.VMEM((GROUP, 2 * KDIM, INPUTS), F32),
        ],
        compiler_params=params,
    )(v, own, far, core)


def turned_by(count, distance):
    return [(i, (i + distance) % count) for i in range(count)]


def sums_over(s):
    s = s + lax.ppermute(s, "core", turned_by(NC, 1))
    return [s] + [lax.ppermute(s, "y", turned_by(NY, d)) for d in range(1, NY)]


def body(voltages, channel_ids, start_basis):
    y, core = lax.axis_index("y"), lax.axis_index("core")
    parcels = channelize(voltages, banded_table(channel_ids))
    v = lax.all_to_all(parcels, ("x", "z"), 0, 0, tiled=True)
    split = start_basis.reshape(2 * KDIM, NX, NY, NZ, NC, LOCAL)
    split = lax.dynamic_index_in_dim(split, y, 2, keepdims=False)
    z = lax.dynamic_index_in_dim(split, core, 3, keepdims=False).reshape(2 * KDIM, HELD)
    s = first(v, z)
    sums = sums_over(s)
    blocks = lax.all_to_all(turn(v), ("y", "z", "core"), 0, 0, tiled=True)
    z, s = step(0, v, z, sums)
    z, s = step(1, v, z, sums_over(s))
    (many,) = step(2, v, z, sums_over(s))
    own = lax.all_to_all(many, ("y", "z"), 0, 0, tiled=True)
    far = lax.ppermute(own, "core", turned_by(NC, 1))
    return finish(blocks, own, far, core.reshape(1).astype(jnp.int32))


def solution(mesh):
    fine = Mesh(mesh.devices.reshape(NX, NY, NZ, NC), ("x", "y", "z", "core"))
    in_specs = (P(("x", "y", "z", "core"), None), P(), P())
    out_specs = P(None, "x", ("y", "z", "core"), None)
    return jax.shard_map(body, mesh=fine, in_specs=in_specs, out_specs=out_specs, check_vma=False)
```

time: 889 us -> 151 us (0.17)
  blocking collectives: 445 us -> 0 us
  waiting for transfers between devices: 226 us -> 62.7 us
  matrix products: 91.4 us -> 0 us
  local copies, waits for them, and re-layouts: 78.2 us -> 8.51 us
  Pallas kernels: 0 us -> 39.3 us
  starting transfers between devices: 11.6 us -> 34.6 us
  between operations: 15.5 us -> 0.88 us
  other arithmetic: 16.2 us -> 4.16 us
    psum x3 -> x0, blocking collectives: 363 us -> none  [body(): gram_re, gram_im = lax.psum((gram_re, gram_im), 'tile')]
    reduce_scatter x3 -> x0, waiting for transfers between devices: 206 us -> none  [body(): lax.psum_scatter(partial_image, 'tile', scatter_dimension=3, tiled=True)]
    dot_general x48 -> x0, matrix products: 91.4 us -> none  [the longest x4 69.2 us: body(): jnp.einsum('rfcp,itsp->rftcsi', coeffs[offset], window_frames, preferred_...]
    all_gather x3 -> x0, blocking collectives: 81.9 us -> none  [body(): basis = lax.all_gather(new_share, 'tile', axis=3, tiled=True)]
    pallas_call x0 -> x7, Pallas kernels: none -> 39.3 us  [the longest x1 12.5 us: channelize(): pl.pallas_call(channelize_kernel, out_shape=jax.ShapeDtypeStruct((NX * NZ...]
    slice x17 -> x0, local copies, waits for them, and re-layouts: 29.1 us -> none  [the longest x1 19.9 us: body(): frames[:, offset:offset + spectra_all, :]]
    all_to_all x1 -> x3, waiting for transfers between devices: 19.9 us -> 44.4 us  [the longest x1 20.8 us: body(): blocks = lax.all_to_all(turn(v), ('y', 'z', 'core'), 0, 0, tiled=True)]
    convert_element_type x2 -> x0, local copies, waits for them, and re-layouts: 18.8 us -> none  [body(): local_spectra = summed.astype(jnp.bfloat16)]
  transfers between devices with their start and end apart: 4 -> 16, of which waited for: 4 -> 16; matrix products, arithmetic and copies ran while one was open for 1% -> 1% of each run, Pallas kernels for 0% -> 3%
where the time goes in v1:
time: 151 us; the launch traced here: 150 us
  waiting for transfers between devices  62.7 us (42%)
  Pallas kernels  39.3 us (26%)
  starting transfers between devices  34.6 us (23%)
  local copies, waits for them, and re-layouts  8.51 us (6%)
  other arithmetic  4.16 us (3%)
    all_to_all x1, waiting for transfers between devices, body(): blocks = lax.all_to_all(turn(v), ('y', 'z', 'core'), 0, 0, tiled=True)  20.8 us
    all_to_all x1, waiting for transfers between devices, body(): v = lax.all_to_all(parcels, ('x', 'z'), 0, 0, tiled=True)  18.8 us
    ppermute x9, waiting for transfers between devices, sums_over(): return [s] + [lax.ppermute(s, 'y', turned_by(NY, d)) for d in range(1, NY)]  13.5 us
    pallas_call x1, Pallas kernels, channelize(): pl.pallas_call(channelize_kernel, out_shape=jax.ShapeDtypeStruct((NX * NZ...  12.5 us
    pallas_call x3, Pallas kernels, step(): pl.pallas_call(functools.partial(step_kernel, at), out_shape=shapes, in_s...  10.5 us
    pallas_call x1, Pallas kernels, finish(): pl.pallas_call(final_kernel, out_shape=jax.ShapeDtypeStruct((2, GROUP, SH...  9.89 us
    all_to_all x1, starting transfers between devices, body(): v = lax.all_to_all(parcels, ('x', 'z'), 0, 0, tiled=True)  8.56 us
    ppermute x9, starting transfers between devices, sums_over(): return [s] + [lax.ppermute(s, 'y', turned_by(NY, d)) for d in range(1, NY)]  8.07 us
  transfers between devices with their start and end apart: 16, of which 16 were waited for; matrix products, arithmetic and copies ran while one was open for 1% of the time, Pallas kernels for 3%

profile of v1, /device:TPU:1, one launch (start us, length us, event | category | flops | bytes accessed | tf_op | source)
XLA Modules:
  0.0 150.2 jit_solution(656026326440860803)
XLA Ops:
  0.0 0.7 fusion.40
  1.4 0.8 fusion.6
  2.9 2.0 %concatenate.3.c_ref = bf16[1152,256]{1,0:T(8,128)(2,1)} concatenate(bf16[1152,24]{1,0:T(8,128)(2,1)S(1)} %get-tuple-element.18, bf16[1152,24]{1,0:T(8,128)(2,1)S(1)} %get-tuple-element.17, bf16[1152,24]{1,0:T(8,128)(2,1)S(1)} %get-tuple-element.16, bf16[1152,24]{1,0:T(8,128)(2,1)S(1)} %get-tuple-element.15, bf16[1152,24]{1,0:T(8,128)(2,1)S(1)} %get-tuple-element.14, ...), dimensions={1} | concatenate | bytes 1179648 | tf_op jit(solution)/shard_map/concatenate | solution.py:81
  4.8 12.5 %shard_map.37 = bf16[16,2,32,768]{3,2,1,0:T(8,128)(2,1)} custom-call(bf16[32,98688]{1,0:T(8,128)(2,1)} %x_ref.1, bf16[1152,256]{1,0:T(8,128)(2,1)} %concatenate.3.c_ref), custom_call_target="tpu_custom_call" | custom-call | tf_op jit(solution)/shard_map/pallas_call | solution.py:116
  17.4 8.6 %all-to-all-start = ((bf16[16,2,32,768]{3,2,1,0:T(8,128)(2,1)}), bf16[16,2,32,768]{3,2,1,0:T(8,128)(2,1)S(1)}, u32[]{:S(2)}, u32[]{:S(2)}) async-start(bf16[16,2,32,768]{3,2,1,0:T(8,128)(2,1)} %shard_map.37), calls=%async_computation | async-start | bytes 3145728 | tf_op jit(solution)/shard_map/all_to_all | solution.py:359
  25.9 0.9 reshape.173
  27.0 0.7 reshape.174.q_ref.z_ref
  27.8 18.8 %all-to-all-done.v_ref = bf16[16,2,32,768]{3,2,1,0:T(8,128)(2,1)S(1)} async-done(((bf16[16,2,32,768]{3,2,1,0:T(8,128)(2,1)}), bf16[16,2,32,768]{3,2,1,0:T(8,128)(2,1)S(1)}, u32[]{:S(2)}, u32[]{:S(2)}) %all-to-all-start) | async-done | bytes 1572896 | tf_op jit(solution)/shard_map/all_to_all | solution.py:359
  46.6 1.1 copy-done
  47.7 2.4 %shard_map.39 = f32[16,768]{1,0:T(8,128)} custom-call(bf16[16,2,32,768]{3,2,1,0:T(8,128)(2,1)} %copy-done, f32[16,512]{1,0:T(8,128)} %reshape.174.q_ref.z_ref), custom_call_target="tpu_custom_call" | custom-call | tf_op jit(solution)/shard_map/pallas_call | solution.py:226
  50.1 4.1 %collective-permute-start = (f32[16,768]{1,0:T(8,128)}, f32[16,768]{1,0:T(8,128)S(1)}, u32[]{:S(2)}, u32[]{:S(2)}) collective-permute-start(f32[16,768]{1,0:T(8,128)} %shard_map.39), channel_id=1, source_target_pairs={{0,1},{1,0},{2,3},{3,2},{4,5},{5,4},{6,7},{7,6},{8,9},{9,8},{10,11... | collective-permute-start | bytes 147464 | tf_op jit(solution)/shard_map/ppermute | solution.py:352
  54.2 1.1 collective-permute-done
  55.3 0.8 add.199.s0
  56.1 2.8 %collective-permute-start.3 = (f32[16,768]{1,0:T(8,128)S(1)}, f32[16,768]{1,0:T(8,128)S(1)}, u32[]{:S(2)}, u32[]{:S(2)}) collective-permute-start(f32[16,768]{1,0:T(8,128)S(1)} %add.199.s0), channel_id=1, source_target_pairs={{0,24},{8,0},{16,8},{24,16},{1,25},{9,1},{17,9},{25,17},{2,26},{10... | collective-permute-start | bytes 147464 | tf_op jit(solution)/shard_map/ppermute | solution.py:353
  59.2 0.7 collective-permute-start.1
  60.1 3.3 %collective-permute-done.2.s2 = f32[16,768]{1,0:T(8,128)S(1)} collective-permute-done((f32[16,768]{1,0:T(8,128)S(1)}, f32[16,768]{1,0:T(8,128)S(1)}, u32[]{:S(2)}, u32[]{:S(2)}) %collective-permute-start.2) | collective-permute-done | bytes 49184 | tf_op jit(solution)/shard_map/ppermute | solution.py:353
  63.4 0.5 collective-permute-done.1.s1
  64.0 0.6 copy-done.16
  64.6 3.2 %shard_map.40 = (f32[16,512]{1,0:T(8,128)}, f32[16,896]{1,0:T(8,128)}) custom-call(bf16[16,2,32,768]{3,2,1,0:T(8,128)(2,1)} %copy-done, f32[16,512]{1,0:T(8,128)} %reshape.174.q_ref.z_ref, f32[16,768]{1,0:T(8,128)} %copy-done.7, f32[16,768]{1,0:T(8,128)} %copy-done.16, f32[16,768]{1,0:T(8,128)} %copy-done.15, f32[16,768]{1,0:T(8,128)} %copy-done.14), custom_call_target="tpu_custom_call" | custom-call | tf_op jit(solution)/shard_map/pallas_call | solution.py:243
  67.8 1.7 %collective-permute-start.4 = (f32[16,896]{1,0:T(8,128)}, f32[16,896]{1,0:T(8,128)S(1)}, u32[]{:S(2)}, u32[]{:S(2)}) collective-permute-start(f32[16,896]{1,0:T(8,128)} %get-tuple-element.10), channel_id=1, source_target_pairs={{0,1},{1,0},{2,3},{3,2},{4,5},{5,4},{6,7},{7,6},{8,9},{9,8},{10,11... | collective-permute-start | bytes 172040 | tf_op jit(solution)/shard_map/ppermute | solution.py:352
  69.5 1.1 collective-permute-done.4
  70.6 0.8 add.200.s0
  71.4 0.5 collective-permute-start.7
  72.0 0.8 collective-permute-start.6
  72.7 0.8 collective-permute-start.5
  73.5 1.0 collective-permute-done.7.s3
  74.5 2.0 %collective-permute-done.6.s2 = f32[16,896]{1,0:T(8,128)S(1)} collective-permute-done((f32[16,896]{1,0:T(8,128)S(1)}, f32[16,896]{1,0:T(8,128)S(1)}, u32[]{:S(2)}, u32[]{:S(2)}) %collective-permute-start.6) | collective-permute-done | bytes 57376 | tf_op jit(solution)/shard_map/ppermute | solution.py:353
  76.5 1.6 %collective-permute-done.5.s1 = f32[16,896]{1,0:T(8,128)S(1)} collective-permute-done((f32[16,896]{1,0:T(8,128)S(1)}, f32[16,896]{1,0:T(8,128)S(1)}, u32[]{:S(2)}, u32[]{:S(2)}) %collective-permute-start.5) | collective-permute-done | bytes 57376 | tf_op jit(solution)/shard_map/ppermute | solution.py:353
  78.1 0.6 copy-done.12
  78.7 3.8 %shard_map.41 = (f32[16,512]{1,0:T(8,128)}, f32[16,896]{1,0:T(8,128)}) custom-call(bf16[16,2,32,768]{3,2,1,0:T(8,128)(2,1)} %copy-done, f32[16,512]{1,0:T(8,128)} %get-tuple-element.9.z_ref, f32[16,896]{1,0:T(8,128)} %copy-done.5, f32[16,896]{1,0:T(8,128)} %copy-done.12, f32[16,896]{1,0:T(8,128)} %copy-done.10, f32[16,896]{1,0:T(8,128)} %copy-done.8), custom_call_target="tpu_custom_call" | custom-call | tf_op jit(solution)/shard_map/pallas_call | solution.py:243
  82.5 0.9 collective-permute-start.8
  83.5 1.1 collective-permute-done.8
  84.6 0.8 add.201.s0
  85.4 1.5 %collective-permute-start.11 = (f32[16,896]{1,0:T(8,128)S(1)}, f32[16,896]{1,0:T(8,128)S(1)}, u32[]{:S(2)}, u32[]{:S(2)}) collective-permute-start(f32[16,896]{1,0:T(8,128)S(1)} %add.201.s0), channel_id=1, source_target_pairs={{0,24},{8,0},{16,8},{24,16},{1,25},{9,1},{17,9},{25,17},{2,26},{10... | collective-permute-start | bytes 172040 | tf_op jit(solution)/shard_map/ppermute | solution.py:353
  86.9 0.6 collective-permute-start.10
  87.6 0.9 collective-permute-done.11.s3
  88.5 3.0 %collective-permute-done.10.s2 = f32[16,896]{1,0:T(8,128)S(1)} collective-permute-done((f32[16,896]{1,0:T(8,128)S(1)}, f32[16,896]{1,0:T(8,128)S(1)}, u32[]{:S(2)}, u32[]{:S(2)}) %collective-permute-start.10) | collective-permute-done | bytes 57376 | tf_op jit(solution)/shard_map/ppermute | solution.py:353
  91.5 1.1 collective-permute-done.9.s1
  92.6 0.6 copy-done.13
  93.2 3.5 %shard_map.42 = f32[16,16,512]{2,1,0:T(8,128)} custom-call(bf16[16,2,32,768]{3,2,1,0:T(8,128)(2,1)} %copy-done, f32[16,512]{1,0:T(8,128)} %get-tuple-element.11.z_ref, f32[16,896]{1,0:T(8,128)} %copy-done.6, f32[16,896]{1,0:T(8,128)} %copy-done.13, f32[16,896]{1,0:T(8,128)} %copy-done.11, f32[16,896]{1,0:T(8,128)} %copy-done.9), custom_call_target="tpu_custom_call" | custom-call | tf_op jit(solution)/shard_map/pallas_call | solution.py:243
  96.7 3.8 %all-to-all-start.2 = ((f32[16,16,512]{2,1,0:T(8,128)}), f32[16,16,512]{2,1,0:T(8,128)S(1)}, u32[]{:S(2)}, u32[]{:S(2)}) async-start(f32[16,16,512]{2,1,0:T(8,128)} %shard_map.42), calls=%async_computation.2 | async-start | bytes 1048576 | tf_op jit(solution)/shard_map/all_to_all | solution.py:369
  100.5 4.0 %shard_map.38 = bf16[32,48,512]{2,1,0:T(8,128)(2,1)} custom-call(bf16[16,2,32,768]{3,2,1,0:T(8,128)(2,1)} %copy-done), custom_call_target="tpu_custom_call" | custom-call | tf_op jit(solution)/shard_map/pallas_call | solution.py:145
  104.5 4.8 %all-to-all-done.2.own_ref = f32[16,16,512]{2,1,0:T(8,128)S(1)} async-done(((f32[16,16,512]{2,1,0:T(8,128)}), f32[16,16,512]{2,1,0:T(8,128)S(1)}, u32[]{:S(2)}, u32[]{:S(2)}) %all-to-all-start.2) | async-done | bytes 524320 | tf_op jit(solution)/shard_map/all_to_all | solution.py:369
  109.3 7.0 %all-to-all-start.1 = ((bf16[32,48,512]{2,1,0:T(8,128)(2,1)}), bf16[32,48,512]{2,1,0:T(8,128)(2,1)S(1)}, u32[]{:S(2)}, u32[]{:S(2)}) async-start(bf16[32,48,512]{2,1,0:T(8,128)(2,1)} %shard_map.38), calls=%async_computation.1 | async-start | bytes 3145728 | tf_op jit(solution)/shard_map/all_to_all | solution.py:365
  116.8 1.6 %collective-permute-done.12.far_ref = f32[16,16,512]{2,1,0:T(8,128)S(1)} collective-permute-done((f32[16,16,512]{2,1,0:T(8,128)S(1)}, f32[16,16,512]{2,1,0:T(8,128)S(1)}, u32[]{:S(2)}, u32[]{:S(2)}) %collective-permute-start.12) | collective-permute-done | bytes 524320 | tf_op jit(solution)/shard_map/ppermute | solution.py:370
  118.3 20.8 %all-to-all-done.1.v_ref = bf16[32,48,512]{2,1,0:T(8,128)(2,1)S(1)} async-done(((bf16[32,48,512]{2,1,0:T(8,128)(2,1)}), bf16[32,48,512]{2,1,0:T(8,128)(2,1)S(1)}, u32[]{:S(2)}, u32[]{:S(2)}) %all-to-all-start.1) | async-done | bytes 1572896 | tf_op jit(solution)/shard_map/all_to_all | solution.py:365
  139.1 1.2 copy-done.1
  140.3 9.9 %shard_map.43 = f32[2,3,24,4096]{3,2,1,0:T(8,128)} custom-call(bf16[32,48,512]{2,1,0:T(8,128)(2,1)} %copy-done.1, f32[16,16,512]{2,1,0:T(8,128)} %copy-done.2, f32[16,16,512]{2,1,0:T(8,128)} %copy-done.3, s32[1]{0:T(128)} %bitcast.3.core_ref), custom_call_target="tpu_custom_call" | custom-call | tf_op jit(solution)/shard_map/pallas_call | solution.py:334
  (44 shorter events, 1.9 us)
Async XLA Ops:
  17.4 8.6 %copy-start.4 = (f32[2,8,4096]{2,1,0:T(8,128)S(1)}, f32[2,8,4096]{2,1,0:T(8,128)}, u32[]{:S(2)}) copy-start(f32[2,8,4096]{2,1,0:T(8,128)} %param.5) | copy-start | bytes 786436
  17.4 29.2 %all-to-all-start = ((bf16[16,2,32,768]{3,2,1,0:T(8,128)(2,1)}), bf16[16,2,32,768]{3,2,1,0:T(8,128)(2,1)S(1)}, u32[]{:S(2)}, u32[]{:S(2)}) async-start(bf16[16,2,32,768]{3,2,1,0:T(8,128)(2,1)} %shard_map.37), calls=%async_computation | async-start | bytes 3145728 | tf_op jit(solution)/shard_map/all_to_all | solution.py:359
  46.5 1.1 copy-start
  50.1 5.2 %collective-permute-start = (f32[16,768]{1,0:T(8,128)}, f32[16,768]{1,0:T(8,128)S(1)}, u32[]{:S(2)}, u32[]{:S(2)}) collective-permute-start(f32[16,768]{1,0:T(8,128)} %shard_map.39), channel_id=1, source_target_pairs={{0,1},{1,0},{2,3},{3,2},{4,5},{5,4},{6,7},{7,6},{8,9},{9,8},{10,11... | collective-permute-start | bytes 147464 | tf_op jit(solution)/shard_map/ppermute | solution.py:352
  56.1 7.8 %copy-start.7 = (f32[16,768]{1,0:T(8,128)}, f32[16,768]{1,0:T(8,128)S(1)}, u32[]{:S(2)}) copy-start(f32[16,768]{1,0:T(8,128)S(1)} %add.199.s0) | copy-start | bytes 147460
  56.1 4.0 %collective-permute-start.3 = (f32[16,768]{1,0:T(8,128)S(1)}, f32[16,768]{1,0:T(8,128)S(1)}, u32[]{:S(2)}, u32[]{:S(2)}) collective-permute-start(f32[16,768]{1,0:T(8,128)S(1)} %add.199.s0), channel_id=1, source_target_pairs={{0,24},{8,0},{16,8},{24,16},{1,25},{9,1},{17,9},{25,17},{2,26},{10... | collective-permute-start | bytes 147464 | tf_op jit(solution)/shard_map/ppermute | solution.py:353
  58.9 4.5 %collective-permute-start.2 = (f32[16,768]{1,0:T(8,128)S(1)}, f32[16,768]{1,0:T(8,128)S(1)}, u32[]{:S(2)}, u32[]{:S(2)}) collective-permute-start(f32[16,768]{1,0:T(8,128)S(1)} %add.199.s0), channel_id=1, source_target_pairs={{0,16},{8,24},{16,0},{24,8},{1,17},{9,25},{17,1},{25,9},{2,18},{10... | collective-permute-start | bytes 147464 | tf_op jit(solution)/shard_map/ppermute | solution.py:353
  59.2 4.6 %collective-permute-start.1 = (f32[16,768]{1,0:T(8,128)S(1)}, f32[16,768]{1,0:T(8,128)S(1)}, u32[]{:S(2)}, u32[]{:S(2)}) collective-permute-start(f32[16,768]{1,0:T(8,128)S(1)} %add.199.s0), channel_id=1, source_target_pairs={{0,8},{8,16},{16,24},{24,0},{1,9},{9,17},{17,25},{25,1},{2,10},{10... | collective-permute-start | bytes 147464 | tf_op jit(solution)/shard_map/ppermute | solution.py:353
  60.1 3.8 %copy-start.14 = (f32[16,768]{1,0:T(8,128)}, f32[16,768]{1,0:T(8,128)S(1)}, u32[]{:S(2)}) copy-start(f32[16,768]{1,0:T(8,128)S(1)} %collective-permute-done.3.s3) | copy-start | bytes 147460
  63.4 0.6 copy-start.15
  64.0 0.6 copy-start.16
  67.8 2.8 %collective-permute-start.4 = (f32[16,896]{1,0:T(8,128)}, f32[16,896]{1,0:T(8,128)S(1)}, u32[]{:S(2)}, u32[]{:S(2)}) collective-permute-start(f32[16,896]{1,0:T(8,128)} %get-tuple-element.10), channel_id=1, source_target_pairs={{0,1},{1,0},{2,3},{3,2},{4,5},{5,4},{6,7},{7,6},{8,9},{9,8},{10,11... | collective-permute-start | bytes 172040 | tf_op jit(solution)/shard_map/ppermute | solution.py:352
  71.4 6.7 %copy-start.5 = (f32[16,896]{1,0:T(8,128)}, f32[16,896]{1,0:T(8,128)S(1)}, u32[]{:S(2)}) copy-start(f32[16,896]{1,0:T(8,128)S(1)} %add.200.s0) | copy-start | bytes 172036
  71.4 3.1 %collective-permute-start.7 = (f32[16,896]{1,0:T(8,128)S(1)}, f32[16,896]{1,0:T(8,128)S(1)}, u32[]{:S(2)}, u32[]{:S(2)}) collective-permute-start(f32[16,896]{1,0:T(8,128)S(1)} %add.200.s0), channel_id=1, source_target_pairs={{0,24},{8,0},{16,8},{24,16},{1,25},{9,1},{17,9},{25,17},{2,26},{10... | collective-permute-start | bytes 172040 | tf_op jit(solution)/shard_map/ppermute | solution.py:353
  72.0 4.5 %collective-permute-start.6 = (f32[16,896]{1,0:T(8,128)S(1)}, f32[16,896]{1,0:T(8,128)S(1)}, u32[]{:S(2)}, u32[]{:S(2)}) collective-permute-start(f32[16,896]{1,0:T(8,128)S(1)} %add.200.s0), channel_id=1, source_target_pairs={{0,16},{8,24},{16,0},{24,8},{1,17},{9,25},{17,1},{25,9},{2,18},{10... | collective-permute-start | bytes 172040 | tf_op jit(solution)/shard_map/ppermute | solution.py:353
  72.7 5.3 %collective-permute-start.5 = (f32[16,896]{1,0:T(8,128)S(1)}, f32[16,896]{1,0:T(8,128)S(1)}, u32[]{:S(2)}, u32[]{:S(2)}) collective-permute-start(f32[16,896]{1,0:T(8,128)S(1)} %add.200.s0), channel_id=1, source_target_pairs={{0,8},{8,16},{16,24},{24,0},{1,9},{9,17},{17,25},{25,1},{2,10},{10... | collective-permute-start | bytes 172040 | tf_op jit(solution)/shard_map/ppermute | solution.py:353
  74.5 3.6 %copy-start.8 = (f32[16,896]{1,0:T(8,128)}, f32[16,896]{1,0:T(8,128)S(1)}, u32[]{:S(2)}) copy-start(f32[16,896]{1,0:T(8,128)S(1)} %collective-permute-done.7.s3) | copy-start | bytes 172036
  76.5 1.6 %copy-start.10 = (f32[16,896]{1,0:T(8,128)}, f32[16,896]{1,0:T(8,128)S(1)}, u32[]{:S(2)}) copy-start(f32[16,896]{1,0:T(8,128)S(1)} %collective-permute-done.6.s2) | copy-start | bytes 172036
  78.1 0.6 copy-start.12
  82.5 2.0 %collective-permute-start.8 = (f32[16,896]{1,0:T(8,128)}, f32[16,896]{1,0:T(8,128)S(1)}, u32[]{:S(2)}, u32[]{:S(2)}) collective-permute-start(f32[16,896]{1,0:T(8,128)} %get-tuple-element.12), channel_id=1, source_target_pairs={{0,1},{1,0},{2,3},{3,2},{4,5},{5,4},{6,7},{7,6},{8,9},{9,8},{10,11... | collective-permute-start | bytes 172040 | tf_op jit(solution)/shard_map/ppermute | solution.py:352
  85.4 7.2 %copy-start.6 = (f32[16,896]{1,0:T(8,128)}, f32[16,896]{1,0:T(8,128)S(1)}, u32[]{:S(2)}) copy-start(f32[16,896]{1,0:T(8,128)S(1)} %add.201.s0) | copy-start | bytes 172036
  85.4 3.1 %collective-permute-start.11 = (f32[16,896]{1,0:T(8,128)S(1)}, f32[16,896]{1,0:T(8,128)S(1)}, u32[]{:S(2)}, u32[]{:S(2)}) collective-permute-start(f32[16,896]{1,0:T(8,128)S(1)} %add.201.s0), channel_id=1, source_target_pairs={{0,24},{8,0},{16,8},{24,16},{1,25},{9,1},{17,9},{25,17},{2,26},{10... | collective-permute-start | bytes 172040 | tf_op jit(solution)/shard_map/ppermute | solution.py:353
  86.9 4.6 %collective-permute-start.10 = (f32[16,896]{1,0:T(8,128)S(1)}, f32[16,896]{1,0:T(8,128)S(1)}, u32[]{:S(2)}, u32[]{:S(2)}) collective-permute-start(f32[16,896]{1,0:T(8,128)S(1)} %add.201.s0), channel_id=1, source_target_pairs={{0,16},{8,24},{16,0},{24,8},{1,17},{9,25},{17,1},{25,9},{2,18},{10... | collective-permute-start | bytes 172040 | tf_op jit(solution)/shard_map/ppermute | solution.py:353
  87.5 5.0 %collective-permute-start.9 = (f32[16,896]{1,0:T(8,128)S(1)}, f32[16,896]{1,0:T(8,128)S(1)}, u32[]{:S(2)}, u32[]{:S(2)}) collective-permute-start(f32[16,896]{1,0:T(8,128)S(1)} %add.201.s0), channel_id=1, source_target_pairs={{0,8},{8,16},{16,24},{24,0},{1,9},{9,17},{17,25},{25,1},{2,10},{10... | collective-permute-start | bytes 172040 | tf_op jit(solution)/shard_map/ppermute | solution.py:353
  88.5 4.1 %copy-start.9 = (f32[16,896]{1,0:T(8,128)}, f32[16,896]{1,0:T(8,128)S(1)}, u32[]{:S(2)}) copy-start(f32[16,896]{1,0:T(8,128)S(1)} %collective-permute-done.11.s3) | copy-start | bytes 172036
  91.5 1.1 copy-start.11
  92.5 0.6 copy-start.13
  96.7 12.6 %all-to-all-start.2 = ((f32[16,16,512]{2,1,0:T(8,128)}), f32[16,16,512]{2,1,0:T(8,128)S(1)}, u32[]{:S(2)}, u32[]{:S(2)}) async-start(f32[16,16,512]{2,1,0:T(8,128)} %shard_map.42), calls=%async_computation.2 | async-start | bytes 1048576 | tf_op jit(solution)/shard_map/all_to_all | solution.py:369
  109.3 7.1 %copy-start.2 = (f32[16,16,512]{2,1,0:T(8,128)}, f32[16,16,512]{2,1,0:T(8,128)S(1)}, u32[]{:S(2)}) copy-start(f32[16,16,512]{2,1,0:T(8,128)S(1)} %all-to-all-done.2.own_ref) | copy-start | bytes 1572868
  109.3 29.8 %all-to-all-start.1 = ((bf16[32,48,512]{2,1,0:T(8,128)(2,1)}), bf16[32,48,512]{2,1,0:T(8,128)(2,1)S(1)}, u32[]{:S(2)}, u32[]{:S(2)}) async-start(bf16[32,48,512]{2,1,0:T(8,128)(2,1)} %shard_map.38), calls=%async_computation.1 | async-start | bytes 3145728 | tf_op jit(solution)/shard_map/all_to_all | solution.py:365
  116.3 2.0 %collective-permute-start.12 = (f32[16,16,512]{2,1,0:T(8,128)S(1)}, f32[16,16,512]{2,1,0:T(8,128)S(1)}, u32[]{:S(2)}, u32[]{:S(2)}) collective-permute-start(f32[16,16,512]{2,1,0:T(8,128)S(1)} %all-to-all-done.2.own_ref), channel_id=1, source_target_pairs={{0,1},{1,0},{2,3},{3,2},{4,5},{5,4},{6,7},{7,6},{8,9},{9,8},{10,11... | collective-permute-start | bytes 1572872 | tf_op jit(solution)/shard_map/ppermute | solution.py:370
  118.3 20.8 %copy-start.3 = (f32[16,16,512]{2,1,0:T(8,128)}, f32[16,16,512]{2,1,0:T(8,128)S(1)}, u32[]{:S(2)}) copy-start(f32[16,16,512]{2,1,0:T(8,128)S(1)} %collective-permute-done.12.far_ref) | copy-start | bytes 1572868
  139.1 1.2 copy-start.1

commit v2 on v1

--- a/solution.py
+++ b/solution.py
@@ -27,8 +27,16 @@
 RC = 2 * CHANNELS
 
 F32, BF16 = jnp.float32, jnp.bfloat16
-VMEM_LIMIT = 56 * 1024 * 1024
-params = pltpu.CompilerParams(vmem_limit_bytes=VMEM_LIMIT)
+
+
+def params(mib):
+    return pltpu.CompilerParams(vmem_limit_bytes=mib * 1024 * 1024)
+
+
+def cost(microseconds):
+    return pl.CostEstimate(flops=0, bytes_accessed=int(microseconds * 3e6), transcendentals=0)
+
+
 in_vmem = pl.BlockSpec(memory_space=pltpu.VMEM)
 
 
@@ -122,7 +130,8 @@
             pltpu.VMEM((ROWS, LOCAL, 256), F32),
             pltpu.VMEM((RC, LOCAL, SPECTRA), F32),
         ],
-        compiler_params=params,
+        compiler_params=params(28),
+        cost_estimate=cost(8),
     )(x, table)
 
 
@@ -147,7 +156,8 @@
         out_shape=jax.ShapeDtypeStruct((NY * NZ * NC, 2 * SHARE, HELD), BF16),
         in_specs=[in_vmem],
         out_specs=in_vmem,
-        compiler_params=params,
+        compiler_params=params(14),
+        cost_estimate=cost(4),
     )(v)
 
 
@@ -228,7 +238,8 @@
         out_shape=jax.ShapeDtypeStruct((2 * KDIM, SPECTRA), F32),
         in_specs=[in_vmem] * 2,
         out_specs=in_vmem,
-        compiler_params=params,
+        compiler_params=params(12),
+        cost_estimate=cost(2),
     )(v, q)
 
 
@@ -245,7 +256,8 @@
         out_shape=shapes,
         in_specs=[in_vmem] * 6,
         out_specs=[in_vmem] * len(shapes),
-        compiler_params=params,
+        compiler_params=params(12),
+        cost_estimate=cost(3),
     )(v, z, *sums)
 
 
@@ -340,7 +352,8 @@
             pltpu.VMEM((NX, NY, GROUP, 2 * SHARE, 256), F32),
             pltpu.VMEM((GROUP, 2 * KDIM, INPUTS), F32),
         ],
-        compiler_params=params,
+        compiler_params=params(24),
+        cost_estimate=cost(6),
     )(v, own, far, core)
 
 
@@ -349,8 +362,11 @@
 
 
 def sums_over(s):
-    s = s + lax.ppermute(s, "core", turned_by(NC, 1))
     return [s] + [lax.ppermute(s, "y", turned_by(NY, d)) for d in range(1, NY)]
+
+
+def core_sum(s):
+    return s + lax.ppermute(s, "core", turned_by(NC, 1))
 
 
 def body(voltages, channel_ids, start_basis):
@@ -360,12 +376,14 @@
     split = start_basis.reshape(2 * KDIM, NX, NY, NZ, NC, LOCAL)
     split = lax.dynamic_index_in_dim(split, y, 2, keepdims=False)
     z = lax.dynamic_index_in_dim(split, core, 3, keepdims=False).reshape(2 * KDIM, HELD)
-    s = first(v, z)
+    s = core_sum(first(v, z))
     sums = sums_over(s)
-    blocks = lax.all_to_all(turn(v), ("y", "z", "core"), 0, 0, tiled=True)
+    turned = turn(lax.optimization_barrier((v, s))[0])
+    blocks = lax.all_to_all(turned, ("y", "z", "core"), 0, 0, tiled=True)
     z, s = step(0, v, z, sums)
-    z, s = step(1, v, z, sums_over(s))
-    (many,) = step(2, v, z, sums_over(s))
+    z, s = step(1, v, z, sums_over(core_sum(s)))
+    (many,) = step(2, v, z, sums_over(core_sum(s)))
+    many, blocks = lax.optimization_barrier((many, blocks))
     own = lax.all_to_all(many, ("y", "z"), 0, 0, tiled=True)
     far = lax.ppermute(own, "core", turned_by(NC, 1))
     return finish(blocks, own, far, core.reshape(1).astype(jnp.int32))

time: 151 us -> 131 us (0.87)
  Pallas kernels: 39.3 us -> 23.6 us
  blocking collectives: 0 us -> 14 us
  waiting for transfers between devices: 62.7 us -> 51.5 us
  starting transfers between devices: 34.6 us -> 31.4 us
  other arithmetic: 4.16 us -> 1.72 us
    all_to_all x2 -> x1, waiting for transfers between devices: 25.6 us -> 0.01 us  [body(): blocks = lax.all_to_all(turned, ('y', 'z', 'core'), 0, 0, tiled=True)]
    ppermute x9, waiting for transfers between devices: 13.5 us -> 27.9 us  [sums_over(): return [s] + [lax.ppermute(s, 'y', turned_by(NY, d)) for d in range(1, NY)]]
    all_to_all x0 -> x1, blocking collectives: none -> 14 us  [body(): own = lax.all_to_all(many, ('y', 'z'), 0, 0, tiled=True)]
    pallas_call x3, Pallas kernels: 10.5 us -> 4.02 us  [step(): pl.pallas_call(functools.partial(step_kernel, at), out_shape=shapes, in_s...]
    all_to_all x2 -> x1, starting transfers between devices: 10.8 us -> 4.98 us  [body(): blocks = lax.all_to_all(turned, ('y', 'z', 'core'), 0, 0, tiled=True)]
    pallas_call x1, Pallas kernels: 12.5 us -> 9.65 us  [channelize(): pl.pallas_call(channelize_kernel, out_shape=jax.ShapeDtypeStruct((NX * NZ...]
    ppermute x1, starting transfers between devices: 0.43 us -> 3.23 us  [body(): far = lax.ppermute(own, 'core', turned_by(NC, 1))]
    pallas_call x1, Pallas kernels: 4.01 us -> 1.41 us  [turn(): pl.pallas_call(turn_kernel, out_shape=jax.ShapeDtypeStruct((NY * NZ * NC,...]
  transfers between devices with their start and end apart: 16 -> 15, of which waited for: 16 -> 14; matrix products, arithmetic and copies ran while one was open for 1% -> 1% of each run, Pallas kernels for 3% -> 3%
where the time goes in v2:
time: 131 us; the launch traced here: 130 us
  waiting for transfers between devices  51.5 us (39%)
  starting transfers between devices  31.4 us (24%)
  Pallas kernels  23.6 us (18%)
  blocking collectives  14 us (11%)
  local copies, waits for them, and re-layouts  7.27 us (6%)
  other arithmetic  1.72 us (1%)
    ppermute x9, waiting for transfers between devices, sums_over(): return [s] + [lax.ppermute(s, 'y', turned_by(NY, d)) for d in range(1, NY)]  27.9 us
    all_to_all x1, waiting for transfers between devices, body(): v = lax.all_to_all(parcels, ('x', 'z'), 0, 0, tiled=True)  19.4 us
    all_to_all x1, blocking collectives, body(): own = lax.all_to_all(many, ('y', 'z'), 0, 0, tiled=True)  14 us
    pallas_call x1, Pallas kernels, channelize(): pl.pallas_call(channelize_kernel, out_shape=jax.ShapeDtypeStruct((NX * NZ...  9.65 us
    all_to_all x1, starting transfers between devices, body(): v = lax.all_to_all(parcels, ('x', 'z'), 0, 0, tiled=True)  8.56 us
    pallas_call x1, Pallas kernels, finish(): pl.pallas_call(final_kernel, out_shape=jax.ShapeDtypeStruct((2, GROUP, SH...  8.21 us
    ppermute x9, starting transfers between devices, sums_over(): return [s] + [lax.ppermute(s, 'y', turned_by(NY, d)) for d in range(1, NY)]  7.94 us
    ppermute x3, starting transfers between devices, core_sum(): return s + lax.ppermute(s, 'core', turned_by(NC, 1))  6.66 us
  transfers between devices with their start and end apart: 15, of which 14 were waited for; matrix products, arithmetic and copies ran while one was open for 1% of the time, Pallas kernels for 3%

profile of v2, /device:TPU:1, one launch (start us, length us, event | category | flops | bytes accessed | tf_op | source)
XLA Modules:
  0.0 130.4 jit_solution(17736238148713958632)
XLA Ops:
  0.0 0.7 fusion.40
  1.4 0.8 fusion.6
  2.3 0.1 copy.5
  2.4 0.1 multiply_convert_fusion
  2.6 0.2 fusion.41
  2.9 1.0 concatenate.3.c_ref
  3.8 2.8 %copy-done = bf16[32,98688]{1,0:T(8,128)(2,1)S(1)} copy-done((bf16[32,98688]{1,0:T(8,128)(2,1)S(1)}, bf16[32,98688]{1,0:T(8,128)(2,1)}, u32[]{:S(2)}) %copy-start) | copy-done | bytes 6316056
  6.6 9.6 %shard_map.37 = bf16[16,2,32,768]{3,2,1,0:T(8,128)(2,1)} custom-call(bf16[32,98688]{1,0:T(8,128)(2,1)S(1)} %copy-done, bf16[1152,256]{1,0:T(8,128)(2,1)S(1)} %concatenate.3.c_ref), custom_call_target="tpu_custom_call" | custom-call | bytes 24000000 | tf_op jit(solution)/shard_map/pallas_call | solution.py:124
  16.3 8.6 %all-to-all-start = ((bf16[16,2,32,768]{3,2,1,0:T(8,128)(2,1)}), bf16[16,2,32,768]{3,2,1,0:T(8,128)(2,1)S(1)}, u32[]{:S(2)}, u32[]{:S(2)}) async-start(bf16[16,2,32,768]{3,2,1,0:T(8,128)(2,1)} %shard_map.37), calls=%async_computation | async-start | bytes 3145728 | tf_op jit(solution)/shard_map/all_to_all | solution.py:375
  24.9 0.9 reshape.173
  25.8 0.1 constant_dynamic-slice_fusion
  25.9 0.1 reshape.174.q_ref.z_ref
  26.1 19.4 %all-to-all-done.v_ref = bf16[16,2,32,768]{3,2,1,0:T(8,128)(2,1)S(1)} async-done(((bf16[16,2,32,768]{3,2,1,0:T(8,128)(2,1)}), bf16[16,2,32,768]{3,2,1,0:T(8,128)(2,1)S(1)}, u32[]{:S(2)}, u32[]{:S(2)}) %all-to-all-start) | async-done | bytes 1572896 | tf_op jit(solution)/shard_map/all_to_all | solution.py:375
  45.5 0.3 shard_map.38
  45.8 4.2 %collective-permute-start = (f32[16,768]{1,0:T(8,128)S(1)}, f32[16,768]{1,0:T(8,128)S(1)}, u32[]{:S(2)}, u32[]{:S(2)}) collective-permute-start(f32[16,768]{1,0:T(8,128)S(1)} %shard_map.38), channel_id=1, source_target_pairs={{0,1},{1,0},{2,3},{3,2},{4,5},{5,4},{6,7},{7,6},{8,9},{9,8},{10,11... | collective-permute-start | bytes 147464 | tf_op jit(solution)/shard_map/ppermute | solution.py:369
  49.9 0.9 collective-permute-done
  50.8 1.4 %shard_map.42 = bf16[32,48,512]{2,1,0:T(8,128)(2,1)S(1)} custom-call(bf16[16,2,32,768]{3,2,1,0:T(8,128)(2,1)S(1)} %all-to-all-done.v_ref), custom_call_target="tpu_custom_call" | custom-call | bytes 12000000 | tf_op jit(solution)/shard_map/pallas_call | solution.py:154
  52.3 1.1 copy-done.1
  53.4 5.0 %all-to-all-start.1 = ((bf16[32,48,512]{2,1,0:T(8,128)(2,1)}), bf16[32,48,512]{2,1,0:T(8,128)(2,1)S(1)}, u32[]{:S(2)}, u32[]{:S(2)}) async-start(bf16[32,48,512]{2,1,0:T(8,128)(2,1)} %copy-done.1), calls=%async_computation.1 | async-start | bytes 3145728 | tf_op jit(solution)/shard_map/all_to_all | solution.py:382
  58.4 2.7 %collective-permute-start.3 = (f32[16,768]{1,0:T(8,128)S(1)}, f32[16,768]{1,0:T(8,128)S(1)}, u32[]{:S(2)}, u32[]{:S(2)}) collective-permute-start(f32[16,768]{1,0:T(8,128)S(1)} %add.199.s0), channel_id=1, source_target_pairs={{0,24},{8,0},{16,8},{24,16},{1,25},{9,1},{17,9},{25,17},{2,26},{10... | collective-permute-start | bytes 147464 | tf_op jit(solution)/shard_map/ppermute | solution.py:365
  61.1 0.5 collective-permute-start.2
  61.6 0.6 collective-permute-start.1
  62.2 16.5 %collective-permute-done.3.s3 = f32[16,768]{1,0:T(8,128)S(1)} collective-permute-done((f32[16,768]{1,0:T(8,128)S(1)}, f32[16,768]{1,0:T(8,128)S(1)}, u32[]{:S(2)}, u32[]{:S(2)}) %collective-permute-start.3) | collective-permute-done | bytes 49184 | tf_op jit(solution)/shard_map/ppermute | solution.py:365
  78.7 1.5 %collective-permute-done.2.s2 = f32[16,768]{1,0:T(8,128)S(1)} collective-permute-done((f32[16,768]{1,0:T(8,128)S(1)}, f32[16,768]{1,0:T(8,128)S(1)}, u32[]{:S(2)}, u32[]{:S(2)}) %collective-permute-start.2) | collective-permute-done | bytes 49184 | tf_op jit(solution)/shard_map/ppermute | solution.py:365
  80.2 0.4 collective-permute-done.1.s1
  80.6 1.1 shard_map.39
  81.6 1.2 collective-permute-start.4
  82.8 0.9 collective-permute-done.4
  83.7 1.3 collective-permute-start.7
  85.0 1.2 collective-permute-start.6
  86.2 0.5 collective-permute-done.7.s3
  86.7 2.8 %collective-permute-done.6.s2 = f32[16,896]{1,0:T(8,128)S(1)} collective-permute-done((f32[16,896]{1,0:T(8,128)S(1)}, f32[16,896]{1,0:T(8,128)S(1)}, u32[]{:S(2)}, u32[]{:S(2)}) %collective-permute-start.6) | collective-permute-done | bytes 57376 | tf_op jit(solution)/shard_map/ppermute | solution.py:365
  89.5 1.7 %collective-permute-done.5.s1 = f32[16,896]{1,0:T(8,128)S(1)} collective-permute-done((f32[16,896]{1,0:T(8,128)S(1)}, f32[16,896]{1,0:T(8,128)S(1)}, u32[]{:S(2)}, u32[]{:S(2)}) %collective-permute-start.5) | collective-permute-done | bytes 57376 | tf_op jit(solution)/shard_map/ppermute | solution.py:365
  91.2 1.7 %shard_map.40 = (f32[16,512]{1,0:T(8,128)S(1)}, f32[16,896]{1,0:T(8,128)S(1)}) custom-call(bf16[16,2,32,768]{3,2,1,0:T(8,128)(2,1)S(1)} %all-to-all-done.v_ref, f32[16,512]{1,0:T(8,128)S(1)} %get-tuple-element.12.z_ref, f32[16,896]{1,0:T(8,128)S(1)} %add.200.s0, f32[16,896]{1,0:T(8,128)S(1)} %collective-permute-done.5.s1, ...), custom_call_target="tpu_custom_call" | custom-call | bytes 9000000 | tf_op jit(solution)/shard_map/pallas_call | solution.py:254
  92.9 1.3 %collective-permute-start.8 = (f32[16,896]{1,0:T(8,128)S(1)}, f32[16,896]{1,0:T(8,128)S(1)}, u32[]{:S(2)}, u32[]{:S(2)}) collective-permute-start(f32[16,896]{1,0:T(8,128)S(1)} %get-tuple-element.15), channel_id=1, source_target_pairs={{0,1},{1,0},{2,3},{3,2},{4,5},{5,4},{6,7},{7,6},{8,9},{9,8},{10,11... | collective-permute-start | bytes 172040 | tf_op jit(solution)/shard_map/ppermute | solution.py:369
  94.3 0.9 collective-permute-done.8
  95.2 0.2 collective-permute-start.11
  95.3 0.8 collective-permute-start.10
  96.2 0.6 collective-permute-start.9
  96.8 1.4 %collective-permute-done.11.s3 = f32[16,896]{1,0:T(8,128)S(1)} collective-permute-done((f32[16,896]{1,0:T(8,128)S(1)}, f32[16,896]{1,0:T(8,128)S(1)}, u32[]{:S(2)}, u32[]{:S(2)}) %collective-permute-start.11) | collective-permute-done | bytes 57376 | tf_op jit(solution)/shard_map/ppermute | solution.py:365
  98.2 1.8 %collective-permute-done.10.s2 = f32[16,896]{1,0:T(8,128)S(1)} collective-permute-done((f32[16,896]{1,0:T(8,128)S(1)}, f32[16,896]{1,0:T(8,128)S(1)}, u32[]{:S(2)}, u32[]{:S(2)}) %collective-permute-start.10) | collective-permute-done | bytes 57376 | tf_op jit(solution)/shard_map/ppermute | solution.py:365
  100.0 1.3 %collective-permute-done.9.s1 = f32[16,896]{1,0:T(8,128)S(1)} collective-permute-done((f32[16,896]{1,0:T(8,128)S(1)}, f32[16,896]{1,0:T(8,128)S(1)}, u32[]{:S(2)}, u32[]{:S(2)}) %collective-permute-start.9) | collective-permute-done | bytes 57376 | tf_op jit(solution)/shard_map/ppermute | solution.py:365
  101.3 1.3 shard_map.41
  102.6 0.8 copy-done.2
  103.4 14.0 %all_to_all.15.own_ref = f32[16,16,512]{2,1,0:T(8,128)S(1)} all-to-all(f32[16,16,512]{2,1,0:T(8,128)} %copy-done.2), channel_id=1, replica_groups=mesh['x'=4,'y'=4,'z'=4,'core'=2] {'y','z'}, dimensions={0} | all-to-all | bytes 1048576 | tf_op jit(solution)/shard_map/all_to_all | solution.py:387
  117.4 3.2 %collective-permute-start.12 = (f32[16,16,512]{2,1,0:T(8,128)S(1)}, f32[16,16,512]{2,1,0:T(8,128)S(1)}, u32[]{:S(2)}, u32[]{:S(2)}) collective-permute-start(f32[16,16,512]{2,1,0:T(8,128)S(1)} %all_to_all.15.own_ref), channel_id=1, source_target_pairs={{0,1},{1,0},{2,3},{3,2},{4,5},{5,4},{6,7},{7,6},{8,9},{9,8},{10,11... | collective-permute-start | bytes 1572872 | tf_op jit(solution)/shard_map/ppermute | solution.py:388
  120.7 1.5 %collective-permute-done.12.far_ref = f32[16,16,512]{2,1,0:T(8,128)S(1)} collective-permute-done((f32[16,16,512]{2,1,0:T(8,128)S(1)}, f32[16,16,512]{2,1,0:T(8,128)S(1)}, u32[]{:S(2)}, u32[]{:S(2)}) %collective-permute-start.12) | collective-permute-done | bytes 524320 | tf_op jit(solution)/shard_map/ppermute | solution.py:388
  122.2 8.2 %shard_map.43 = f32[2,3,24,4096]{3,2,1,0:T(8,128)} custom-call(bf16[32,48,512]{2,1,0:T(8,128)(2,1)S(1)} %all-to-all-done.1.v_ref, f32[16,16,512]{2,1,0:T(8,128)S(1)} %all_to_all.15.own_ref, f32[16,16,512]{2,1,0:T(8,128)S(1)} %collective-permute-done.12.far_ref, s32[1]{0:T(128)} %bitcast.3.core_ref), custom_call_target="tpu_custom_call" | custom-call | bytes 18000000 | tf_op jit(solution)/shard_map/pallas_call | solution.py:346
  (17 shorter events, 0.2 us)
Async XLA Ops:
  3.8 2.8 %copy-start = (bf16[32,98688]{1,0:T(8,128)(2,1)S(1)}, bf16[32,98688]{1,0:T(8,128)(2,1)}, u32[]{:S(2)}) copy-start(bf16[32,98688]{1,0:T(8,128)(2,1)} %x_ref.1) | copy-start | bytes 18948100
  16.3 8.6 %copy-start.3 = (f32[2,8,4096]{2,1,0:T(8,128)S(1)}, f32[2,8,4096]{2,1,0:T(8,128)}, u32[]{:S(2)}) copy-start(f32[2,8,4096]{2,1,0:T(8,128)} %param.5) | copy-start | bytes 786436
  16.3 29.2 %all-to-all-start = ((bf16[16,2,32,768]{3,2,1,0:T(8,128)(2,1)}), bf16[16,2,32,768]{3,2,1,0:T(8,128)(2,1)S(1)}, u32[]{:S(2)}, u32[]{:S(2)}) async-start(bf16[16,2,32,768]{3,2,1,0:T(8,128)(2,1)} %shard_map.37), calls=%async_computation | async-start | bytes 3145728 | tf_op jit(solution)/shard_map/all_to_all | solution.py:375
  45.8 5.0 %collective-permute-start = (f32[16,768]{1,0:T(8,128)S(1)}, f32[16,768]{1,0:T(8,128)S(1)}, u32[]{:S(2)}, u32[]{:S(2)}) collective-permute-start(f32[16,768]{1,0:T(8,128)S(1)} %shard_map.38), channel_id=1, source_target_pairs={{0,1},{1,0},{2,3},{3,2},{4,5},{5,4},{6,7},{7,6},{8,9},{9,8},{10,11... | collective-permute-start | bytes 147464 | tf_op jit(solution)/shard_map/ppermute | solution.py:369
  52.2 1.1 copy-start.1
  53.4 50.0 %all-to-all-start.1 = ((bf16[32,48,512]{2,1,0:T(8,128)(2,1)}), bf16[32,48,512]{2,1,0:T(8,128)(2,1)S(1)}, u32[]{:S(2)}, u32[]{:S(2)}) async-start(bf16[32,48,512]{2,1,0:T(8,128)(2,1)} %copy-done.1), calls=%async_computation.1 | async-start | bytes 3145728 | tf_op jit(solution)/shard_map/all_to_all | solution.py:382
  58.4 20.3 %collective-permute-start.3 = (f32[16,768]{1,0:T(8,128)S(1)}, f32[16,768]{1,0:T(8,128)S(1)}, u32[]{:S(2)}, u32[]{:S(2)}) collective-permute-start(f32[16,768]{1,0:T(8,128)S(1)} %add.199.s0), channel_id=1, source_target_pairs={{0,24},{8,0},{16,8},{24,16},{1,25},{9,1},{17,9},{25,17},{2,26},{10... | collective-permute-start | bytes 147464 | tf_op jit(solution)/shard_map/ppermute | solution.py:365
  61.1 19.1 %collective-permute-start.2 = (f32[16,768]{1,0:T(8,128)S(1)}, f32[16,768]{1,0:T(8,128)S(1)}, u32[]{:S(2)}, u32[]{:S(2)}) collective-permute-start(f32[16,768]{1,0:T(8,128)S(1)} %add.199.s0), channel_id=1, source_target_pairs={{0,16},{8,24},{16,0},{24,8},{1,17},{9,25},{17,1},{25,9},{2,18},{10... | collective-permute-start | bytes 147464 | tf_op jit(solution)/shard_map/ppermute | solution.py:365
  61.6 18.9 %collective-permute-start.1 = (f32[16,768]{1,0:T(8,128)S(1)}, f32[16,768]{1,0:T(8,128)S(1)}, u32[]{:S(2)}, u32[]{:S(2)}) collective-permute-start(f32[16,768]{1,0:T(8,128)S(1)} %add.199.s0), channel_id=1, source_target_pairs={{0,8},{8,16},{16,24},{24,0},{1,9},{9,17},{17,25},{25,1},{2,10},{10... | collective-permute-start | bytes 147464 | tf_op jit(solution)/shard_map/ppermute | solution.py:365
  81.6 2.1 %collective-permute-start.4 = (f32[16,896]{1,0:T(8,128)S(1)}, f32[16,896]{1,0:T(8,128)S(1)}, u32[]{:S(2)}, u32[]{:S(2)}) collective-permute-start(f32[16,896]{1,0:T(8,128)S(1)} %get-tuple-element.13), channel_id=1, source_target_pairs={{0,1},{1,0},{2,3},{3,2},{4,5},{5,4},{6,7},{7,6},{8,9},{9,8},{10,11... | collective-permute-start | bytes 172040 | tf_op jit(solution)/shard_map/ppermute | solution.py:369
  83.7 3.1 %collective-permute-start.7 = (f32[16,896]{1,0:T(8,128)S(1)}, f32[16,896]{1,0:T(8,128)S(1)}, u32[]{:S(2)}, u32[]{:S(2)}) collective-permute-start(f32[16,896]{1,0:T(8,128)S(1)} %add.200.s0), channel_id=1, source_target_pairs={{0,24},{8,0},{16,8},{24,16},{1,25},{9,1},{17,9},{25,17},{2,26},{10... | collective-permute-start | bytes 172040 | tf_op jit(solution)/shard_map/ppermute | solution.py:365
  85.0 4.5 %collective-permute-start.6 = (f32[16,896]{1,0:T(8,128)S(1)}, f32[16,896]{1,0:T(8,128)S(1)}, u32[]{:S(2)}, u32[]{:S(2)}) collective-permute-start(f32[16,896]{1,0:T(8,128)S(1)} %add.200.s0), channel_id=1, source_target_pairs={{0,16},{8,24},{16,0},{24,8},{1,17},{9,25},{17,1},{25,9},{2,18},{10... | collective-permute-start | bytes 172040 | tf_op jit(solution)/shard_map/ppermute | solution.py:365
  86.2 5.0 %collective-permute-start.5 = (f32[16,896]{1,0:T(8,128)S(1)}, f32[16,896]{1,0:T(8,128)S(1)}, u32[]{:S(2)}, u32[]{:S(2)}) collective-permute-start(f32[16,896]{1,0:T(8,128)S(1)} %add.200.s0), channel_id=1, source_target_pairs={{0,8},{8,16},{16,24},{24,0},{1,9},{9,17},{17,25},{25,1},{2,10},{10... | collective-permute-start | bytes 172040 | tf_op jit(solution)/shard_map/ppermute | solution.py:365
  92.9 2.2 %collective-permute-start.8 = (f32[16,896]{1,0:T(8,128)S(1)}, f32[16,896]{1,0:T(8,128)S(1)}, u32[]{:S(2)}, u32[]{:S(2)}) collective-permute-start(f32[16,896]{1,0:T(8,128)S(1)} %get-tuple-element.15), channel_id=1, source_target_pairs={{0,1},{1,0},{2,3},{3,2},{4,5},{5,4},{6,7},{7,6},{8,9},{9,8},{10,11... | collective-permute-start | bytes 172040 | tf_op jit(solution)/shard_map/ppermute | solution.py:369
  95.2 3.1 %collective-permute-start.11 = (f32[16,896]{1,0:T(8,128)S(1)}, f32[16,896]{1,0:T(8,128)S(1)}, u32[]{:S(2)}, u32[]{:S(2)}) collective-permute-start(f32[16,896]{1,0:T(8,128)S(1)} %add.201.s0), channel_id=1, source_target_pairs={{0,24},{8,0},{16,8},{24,16},{1,25},{9,1},{17,9},{25,17},{2,26},{10... | collective-permute-start | bytes 172040 | tf_op jit(solution)/shard_map/ppermute | solution.py:365
  95.3 4.6 %collective-permute-start.10 = (f32[16,896]{1,0:T(8,128)S(1)}, f32[16,896]{1,0:T(8,128)S(1)}, u32[]{:S(2)}, u32[]{:S(2)}) collective-permute-start(f32[16,896]{1,0:T(8,128)S(1)} %add.201.s0), channel_id=1, source_target_pairs={{0,16},{8,24},{16,0},{24,8},{1,17},{9,25},{17,1},{25,9},{2,18},{10... | collective-permute-start | bytes 172040 | tf_op jit(solution)/shard_map/ppermute | solution.py:365
  96.2 5.1 %collective-permute-start.9 = (f32[16,896]{1,0:T(8,128)S(1)}, f32[16,896]{1,0:T(8,128)S(1)}, u32[]{:S(2)}, u32[]{:S(2)}) collective-permute-start(f32[16,896]{1,0:T(8,128)S(1)} %add.201.s0), channel_id=1, source_target_pairs={{0,8},{8,16},{16,24},{24,0},{1,9},{9,17},{17,25},{25,1},{2,10},{10... | collective-permute-start | bytes 172040 | tf_op jit(solution)/shard_map/ppermute | solution.py:365
  102.6 0.8 copy-start.2
  117.4 4.8 %collective-permute-start.12 = (f32[16,16,512]{2,1,0:T(8,128)S(1)}, f32[16,16,512]{2,1,0:T(8,128)S(1)}, u32[]{:S(2)}, u32[]{:S(2)}) collective-permute-start(f32[16,16,512]{2,1,0:T(8,128)S(1)} %all_to_all.15.own_ref), channel_id=1, source_target_pairs={{0,1},{1,0},{2,3},{3,2},{4,5},{5,4},{6,7},{7,6},{8,9},{9,8},{10,11... | collective-permute-start | bytes 1572872 | tf_op jit(solution)/shard_map/ppermute | solution.py:388

commit v3 on v2

--- a/solution.py
+++ b/solution.py
@@ -67,49 +67,74 @@
     return x[:n] + (x[n : 2 * n] + x[2 * n :])
 
 
-def make_table(channel_ids):
+STEP_ROWS = 8
+CHUNKS = 4
+
+
+def fill_table(ids_ref, turned):
     length = TAPS * P_SIZE
-    offsets = jnp.arange(length, dtype=F32)
-    shifted = (offsets + 0.5 - length / 2.0) / P_SIZE
-    window = jnp.sinc(shifted) * (0.5 - 0.5 * jnp.cos(2.0 * math.pi * (offsets + 0.5) / length))
+    shape = (TAPS, P_SIZE)
+    at = (
+        lax.broadcasted_iota(jnp.int32, shape, 0) * P_SIZE
+        + lax.broadcasted_iota(jnp.int32, shape, 1)
+    ).astype(F32)
+    angle = math.pi * ((at + 0.5 - length / 2.0) / P_SIZE)
+    window = jnp.sin(angle) / angle * (0.5 - 0.5 * jnp.cos(2.0 * math.pi * (at + 0.5) / length))
     window = window / jnp.sqrt(jnp.sum(window * window))
-    window = window.reshape(TAPS, P_SIZE)
-    phases = channel_ids[:, None] * jnp.arange(P_SIZE, dtype=jnp.int32)[None, :] % P_SIZE
-    angles = 2.0 * math.pi / P_SIZE * phases.astype(F32)
-    rotors = jnp.stack([jnp.cos(angles), -jnp.sin(angles)])
-    return (window[:, None, None, :] * rotors[None]).astype(BF16)
-
-
-def banded_table(channel_ids):
-    columns = jnp.transpose(make_table(channel_ids), (0, 3, 1, 2)).reshape(TAPS * P_SIZE, RC)
-    parts = [
-        jnp.pad(columns, ((q * P_SIZE, (PHASES - 1 - q) * P_SIZE), (0, 0))) for q in range(PHASES)
-    ]
-    parts.append(jnp.zeros((SPAN, 256 - PHASES * RC), BF16))
-    return jnp.concatenate(parts, axis=1)
-
-
-STEP_ROWS = 8
-
-
-def channelize_kernel(x_ref, c_ref, o_ref, wide, tall):
+    row = lax.broadcasted_iota(jnp.int32, (RC, P_SIZE), 0)
+    point = lax.broadcasted_iota(jnp.int32, (RC, P_SIZE), 1)
+    channel = jnp.where(row >= CHANNELS, row - CHANNELS, row)
+    ids = jnp.zeros((RC, P_SIZE), jnp.int32)
+    for c in range(CHANNELS):
+        ids = jnp.where(channel == c, ids_ref[c], ids)
+    angles = 2.0 * math.pi / P_SIZE * ((ids * point) % P_SIZE).astype(F32)
+    rotors = jnp.where(row < CHANNELS, jnp.cos(angles), -jnp.sin(angles))
+    turned[...] = jnp.zeros((256, SPAN), F32)
+    for m in range(TAPS):
+        taps = window[m : m + 1] * rotors
+        for q in range(PHASES):
+            turned[q * RC : (q + 1) * RC, (q + m) * P_SIZE : (q + m + 1) * P_SIZE] = taps
+
+
+def channelize_kernel(ids_ref, x_hbm, o_ref, x_ref, turned, table, wide, tall, sems):
+    step = ROWS // CHUNKS * PHASES * P_SIZE
+    halo = (TAPS - 1) * P_SIZE
+    copies = []
+    for k in range(CHUNKS):
+        low = k * step + (halo if k else 0)
+        lanes = pl.ds(low, (k + 1) * step + halo - low)
+        copies.append(
+            pltpu.make_async_copy(x_hbm.at[:, lanes], x_ref.at[:, lanes], sems.at[k])
+        )
+        copies[-1].start()
+    fill_table(ids_ref, turned)
+    for k in range(SPAN // P_SIZE):
+        lanes = slice(k * P_SIZE, (k + 1) * P_SIZE)
+        table[lanes] = turned[:, lanes].T.astype(BF16)
+
     def filter_rows(at, carry):
         rows = []
         for k in range(STEP_ROWS):
             start = pl.multiple_of((at * STEP_ROWS + k) * (PHASES * P_SIZE), 128)
             rows.append(x_ref[:, pl.ds(start, SPAN)])
-        got = dot_nn(jnp.concatenate(rows, axis=0), c_ref[...])
-        wide[pl.ds(at * STEP_ROWS, STEP_ROWS)] = got.reshape(STEP_ROWS, LOCAL, 256)
+        got = dot_nn(jnp.concatenate(rows, axis=0), table[...])
+        got = got.reshape(NC, STEP_ROWS // NC, LOCAL, 256)
+        y, z = at // NZ, at % NZ
+        for core in range(NC):
+            wide[pl.ds((y * NC + core) * 16 + z * 4, STEP_ROWS // NC)] = got[core]
         return carry
 
-    lax.fori_loop(0, ROWS // STEP_ROWS, filter_rows, 0)
+    for k in range(CHUNKS):
+        copies[k].wait()
+        each = ROWS // STEP_ROWS // CHUNKS
+        lax.fori_loop(k * each, (k + 1) * each, filter_rows, 0)
 
     for n in range(LOCAL):
-        turned = jnp.concatenate(
+        turned_n = jnp.concatenate(
             [wide[:, n, 0:128].T, wide[:, n, 128:256].T[0 : PHASES * RC - 128]], axis=0
         )
         for q in range(PHASES):
-            tall[:, n, q * 128 : (q + 1) * 128] = turned[q * RC : (q + 1) * RC]
+            tall[:, n, q * 128 : (q + 1) * 128] = turned_n[q * RC : (q + 1) * RC]
 
     for x in range(NX):
         for z in range(NZ):
@@ -120,45 +145,96 @@
                     o_ref[x * NZ + z, r] = jnp.zeros((LOCAL, SPECTRA), BF16)
 
 
-def channelize(x, table):
+def channelize(ids, x):
     return pl.pallas_call(
         channelize_kernel,
         out_shape=jax.ShapeDtypeStruct((NX * NZ, 2, LOCAL, SPECTRA), BF16),
-        in_specs=[in_vmem] * 2,
+        in_specs=[pl.BlockSpec(memory_space=pltpu.SMEM), pl.BlockSpec(memory_space=pltpu.HBM)],
         out_specs=in_vmem,
         scratch_shapes=[
+            pltpu.VMEM(x.shape, BF16),
+            pltpu.VMEM((256, SPAN), F32),
+            pltpu.VMEM((SPAN, 256), BF16),
             pltpu.VMEM((ROWS, LOCAL, 256), F32),
             pltpu.VMEM((RC, LOCAL, SPECTRA), F32),
+            pltpu.SemaphoreType.DMA((CHUNKS,)),
         ],
-        compiler_params=params(28),
+        compiler_params=params(32),
         cost_estimate=cost(8),
-    )(x, table)
+    )(ids, x)
+
+
+PAD = 128
+TURN_ROWS = GROUP * 2 * SHARE
+
+
+def spread_kernel(y_ref, v_ref, *outs):
+    row = lax.broadcasted_iota(jnp.int32, (SPECTRA, NC * PAD), 0)
+    col = lax.broadcasted_iota(jnp.int32, (SPECTRA, NC * PAD), 1)
+    inside = col % PAD
+    wanted = (inside // 16) * ROWS + (col // PAD) * 16 + inside % 16
+    for d in range(NY):
+        y = (y_ref[0] + d) % NY
+        hit = (row == wanted + y * (NC * 16)) & (inside < PHASES * 16)
+        pick = jnp.where(hit, 1.0, 0.0).astype(BF16)
+        for c in range(CHANNELS):
+            at = c // GROUP * NZ + c % GROUP
+            got = dot_nn(v_ref[at].reshape(2 * LOCAL, SPECTRA), pick)
+            got = got.astype(BF16).reshape(2, LOCAL, NC * PAD)
+            for core in range(NC):
+                lanes = slice(core * PAD, (core + 1) * PAD)
+                for r in range(2):
+                    outs[d][core, c * 2 + r] = got[r, :, lanes]
+
+
+def spread(y, v):
+    return pl.pallas_call(
+        spread_kernel,
+        out_shape=[jax.ShapeDtypeStruct((NC, RC, LOCAL, PAD), BF16)] * NY,
+        in_specs=[pl.BlockSpec(memory_space=pltpu.SMEM), in_vmem],
+        out_specs=[in_vmem] * NY,
+        compiler_params=params(16),
+        cost_estimate=cost(4),
+    )(y, v)
+
+
+def turn_kernel(at_ref, *refs):
+    parts, o_ref = refs[:-1], refs[-1]
+    core = at_ref[1]
+    row = lax.broadcasted_iota(jnp.int32, (NZ * SHARE, PAD), 0)
+    col = lax.broadcasted_iota(jnp.int32, (NZ * SHARE, PAD), 1)
+    z, s = row // SHARE, row % SHARE
+    pick = (col == (s % PHASES) * 16 + z * 4 + s // PHASES)
+    pick = jnp.where(pick, 1.0, 0.0).astype(BF16)
+    for other in range(NC):
+        side = core if other == 0 else 1 - core
+        for x in range(NX):
+            blocks = []
+            for rc in range(2 * GROUP):
+                stack = jnp.concatenate(
+                    [parts[d][side, x * 2 * GROUP + rc] for d in range(NY)], axis=0
+                )
+                blocks.append(dot_nt(pick, stack))
+            for z_to in range(NZ):
+                rows = slice(z_to * SHARE, (z_to + 1) * SHARE)
+                o_ref[x * NZ + z_to, other] = jnp.concatenate(
+                    [g[rows] for g in blocks], axis=0
+                ).astype(BF16)
+
+
+def turn(at, parts):
+    return pl.pallas_call(
+        turn_kernel,
+        out_shape=jax.ShapeDtypeStruct((NX * NZ, NC, TURN_ROWS, NY * LOCAL), BF16),
+        in_specs=[pl.BlockSpec(memory_space=pltpu.SMEM)] + [in_vmem] * NY,
+        out_specs=in_vmem,
+        compiler_params=params(16),
+        cost_estimate=cost(3),
+    )(at, *parts)
 
 
 def halves(v_ref):
     return v_ref[:, 0].reshape(HELD, SPECTRA), v_ref[:, 1].reshape(HELD, SPECTRA)
-
-
-def turn_kernel(v_ref, o_ref):
-    row = lax.broadcasted_iota(jnp.int32, (SPECTRA, SPECTRA), 0)
-    col = lax.broadcasted_iota(jnp.int32, (SPECTRA, SPECTRA), 1)
-    pick = jnp.where(row == (col % ROWS) * PHASES + col // ROWS, 1.0, 0.0).astype(BF16)
-    real_v, imag_v = halves(v_ref)
-    real_t, imag_t = dot_nt(pick, real_v), dot_nt(pick, imag_v)
-    for t in range(NY * NZ * NC):
-        rows = slice(t * SHARE, (t + 1) * SHARE)
-        o_ref[t] = jnp.concatenate([real_t[rows], imag_t[rows]], axis=0).astype(BF16)
-
-
-def turn(v):
-    return pl.pallas_call(
-        turn_kernel,
-        out_shape=jax.ShapeDtypeStruct((NY * NZ * NC, 2 * SHARE, HELD), BF16),
-        in_specs=[in_vmem],
-        out_specs=in_vmem,
-        compiler_params=params(14),
-        cost_estimate=cost(4),
-    )(v)
 
 
 def project(v_halves, pieces):
@@ -261,24 +337,28 @@
     )(v, z, *sums)
 
 
-def final_kernel(v_ref, own_ref, far_ref, core_ref, o_ref, flat, basis):
-    row = lax.broadcasted_iota(jnp.int32, (256, 256), 0)
-    col = lax.broadcasted_iota(jnp.int32, (256, 256), 1)
-    source = ((col // 32) % 2) * 128 + (col // 64) * 32 + col % 32
-    place = jnp.where(row == source, 1.0, 0.0).astype(BF16)
+def placing(y, core):
+    side = NY * NZ * NC * LOCAL
+    row = lax.broadcasted_iota(jnp.int32, (side, side), 0)
+    col = lax.broadcasted_iota(jnp.int32, (side, side), 1)
+    to_y, to_z, to_core, i = col // 256, (col // 64) % 4, (col // 32) % 2, col % 32
+    source = to_z * 256 + ((to_core + core) % 2) * 128 + ((y - to_y) % 4) * 32 + i
+    return jnp.where(row == source, 1.0, 0.0).astype(BF16)
+
+
+def final_kernel(mine_ref, theirs_ref, own_ref, far_ref, core_ref, place_ref, o_ref, flat, basis):
     lane = lax.broadcasted_iota(jnp.int32, (2 * KDIM, 128), 1) // 32
-    is_zero = core_ref[0] == 0
+    is_zero = core_ref[1] == 0
+    rows = []
+    for x in range(NX):
+        parts = []
+        for z in range(NZ):
+            parts += [mine_ref[x * NZ + z], theirs_ref[x * NZ + z]]
+        rows.append(jnp.concatenate(parts, axis=1))
+    got = dot_nn(jnp.concatenate(rows, axis=0), place_ref[...])
+    flat[...] = got.reshape(NX, GROUP, 2 * SHARE, NY * 256)
     for x in range(NX):
         lanes = slice(x * 128, (x + 1) * 128)
-        rows = []
-        for y in range(NY):
-            for z in range(GROUP):
-                at = (y * NZ + z) * NC
-                rows.append(
-                    jnp.concatenate([v_ref[at, :, lanes], v_ref[at + 1, :, lanes]], axis=1)
-                )
-        got = dot_nn(jnp.concatenate(rows, axis=0), place)
-        flat[x] = got.reshape(NY, GROUP, 2 * SHARE, 256)
         for y in range(NY):
             for z in range(GROUP):
                 own, far = own_ref[y * NZ + z, :, lanes], far_ref[y * NZ + z, :, lanes]
@@ -306,7 +386,7 @@
         products = jnp.zeros((48, 128), F32)
         for x in range(NX):
             pieces = split3(basis[z, :, x * wide : (x + 1) * wide])
-            block = jnp.concatenate([flat[x, y, z] for y in range(NY)], axis=1).astype(BF16)
+            block = flat[x, z].astype(BF16)
             right = jnp.concatenate([pieces, block, jnp.zeros((32, wide), BF16)], axis=0)
             products = products + dot_nt(pieces, right)
         g_re, g_im = gram_from(products)
@@ -335,26 +415,24 @@
             pieces = split3(basis[z, :, x * wide : (x + 1) * wide])
             right = jnp.concatenate([pieces, pieces[0:32], pieces[0:16]], axis=0)
             fitted = dot_tn(left, right)[0 : 2 * SHARE]
-            for y in range(NY):
-                rest = flat[x, y, z] - fitted[:, y * 256 : (y + 1) * 256]
-                at = x * wide + y * 256
-                o_ref[0, z, :, at : at + 256] = rest[0:SHARE]
-                o_ref[1, z, :, at : at + 256] = rest[SHARE:]
-
-
-def finish(v, own, far, core):
+            rest = flat[x, z] - fitted
+            o_ref[0, z, :, x * wide : (x + 1) * wide] = rest[0:SHARE]
+            o_ref[1, z, :, x * wide : (x + 1) * wide] = rest[SHARE:]
+
+
+def finish(mine, theirs, own, far, at, place):
     return pl.pallas_call(
         final_kernel,
         out_shape=jax.ShapeDtypeStruct((2, GROUP, SHARE, INPUTS), F32),
-        in_specs=[in_vmem] * 3 + [pl.BlockSpec(memory_space=pltpu.SMEM)],
+        in_specs=[in_vmem] * 4 + [pl.BlockSpec(memory_space=pltpu.SMEM), in_vmem],
         out_specs=in_vmem,
         scratch_shapes=[
-            pltpu.VMEM((NX, NY, GROUP, 2 * SHARE, 256), F32),
+            pltpu.VMEM((NX, GROUP, 2 * SHARE, NY * 256), F32),
             pltpu.VMEM((GROUP, 2 * KDIM, INPUTS), F32),
         ],
         compiler_params=params(24),
         cost_estimate=cost(6),
-    )(v, own, far, core)
+    )(mine, theirs, own, far, at, place)
 
 
 def turned_by(count, distance):
@@ -371,22 +449,28 @@
 
 def body(voltages, channel_ids, start_basis):
     y, core = lax.axis_index("y"), lax.axis_index("core")
-    parcels = channelize(voltages, banded_table(channel_ids))
+    at = jnp.stack([y, core]).astype(jnp.int32)
+    parcels = channelize(channel_ids, voltages)
     v = lax.all_to_all(parcels, ("x", "z"), 0, 0, tiled=True)
+    parts = spread(at, parcels)
+    parts = [parts[0]] + [lax.ppermute(parts[d], "y", turned_by(NY, d)) for d in range(1, NY)]
+    turned = turn(at, parts)
     split = start_basis.reshape(2 * KDIM, NX, NY, NZ, NC, LOCAL)
     split = lax.dynamic_index_in_dim(split, y, 2, keepdims=False)
     z = lax.dynamic_index_in_dim(split, core, 3, keepdims=False).reshape(2 * KDIM, HELD)
     s = core_sum(first(v, z))
     sums = sums_over(s)
-    turned = turn(lax.optimization_barrier((v, s))[0])
-    blocks = lax.all_to_all(turned, ("y", "z", "core"), 0, 0, tiled=True)
+    turned = lax.optimization_barrier((turned, s))[0]
+    blocks = lax.all_to_all(turned, ("x", "z"), 0, 0, tiled=True)
+    place = placing(y, core)
     z, s = step(0, v, z, sums)
     z, s = step(1, v, z, sums_over(core_sum(s)))
     (many,) = step(2, v, z, sums_over(core_sum(s)))
     many, blocks = lax.optimization_barrier((many, blocks))
+    mine, theirs = blocks[:, 0], lax.ppermute(blocks[:, 1], "core", turned_by(NC, 1))
     own = lax.all_to_all(many, ("y", "z"), 0, 0, tiled=True)
     far = lax.ppermute(own, "core", turned_by(NC, 1))
-    return finish(blocks, own, far, core.reshape(1).astype(jnp.int32))
+    return finish(mine, theirs, own, far, at, place)
 
 
 def solution(mesh):

time: 131 us -> 120 us (0.916)
  waiting for transfers between devices: 51.5 us -> 31.5 us
  starting transfers between devices: 31.4 us -> 46.9 us
  blocking collectives: 14 us -> 0 us
  Pallas kernels: 23.6 us -> 34.2 us
    ppermute x9, waiting for transfers between devices: 27.9 us -> 13.4 us  [sums_over(): return [s] + [lax.ppermute(s, 'y', turned_by(NY, d)) for d in range(1, NY)]]
    all_to_all x1 -> x0, blocking collectives: 14 us -> none  [body(): own = lax.all_to_all(many, ('y', 'z'), 0, 0, tiled=True)]
    all_to_all x1, waiting for transfers between devices: 19.4 us -> 6.89 us  [body(): v = lax.all_to_all(parcels, ('x', 'z'), 0, 0, tiled=True)]
    all_to_all x1 -> x2, waiting for transfers between devices: 0.01 us -> 7.22 us  [the longest x1 7.21 us: body(): own = lax.all_to_all(many, ('y', 'z'), 0, 0, tiled=True)]
    all_to_all x1 -> x2, starting transfers between devices: 4.98 us -> 11.9 us  [the longest x1 6.52 us: body(): blocks = lax.all_to_all(turned, ('x', 'z'), 0, 0, tiled=True)]
    pallas_call x1 -> x2, Pallas kernels: 1.41 us -> 8.29 us  [the longest x1 5.54 us: spread(): pl.pallas_call(spread_kernel, out_shape=[jax.ShapeDtypeStruct((NC, RC, LO...]
    ppermute x0 -> x4, starting transfers between devices: none -> 6.77 us  [the longest x3 4.98 us: body(): lax.ppermute(parts[d], 'y', turned_by(NY, d))]
    ppermute x3, starting transfers between devices: 6.66 us -> 8.23 us  [core_sum(): return s + lax.ppermute(s, 'core', turned_by(NC, 1))]
  transfers between devices with their start and end apart: 15 -> 20, of which waited for: 14 -> 15; matrix products, arithmetic and copies ran while one was open for 1% -> 3% of each run, Pallas kernels for 3% -> 11%
where the time goes in v3:
time: 120 us
  starting transfers between devices  46.9 us (39%)
  Pallas kernels  34.2 us (29%)
  waiting for transfers between devices  31.5 us (26%)
  local copies, waits for them, and re-layouts  6.65 us (6%)
    ppermute x9, waiting for transfers between devices, sums_over(): return [s] + [lax.ppermute(s, 'y', turned_by(NY, d)) for d in range(1, NY)]  13.4 us
    pallas_call x1, Pallas kernels, channelize(): pl.pallas_call(channelize_kernel, out_shape=jax.ShapeDtypeStruct((NX * NZ...  11.1 us
    pallas_call x1, Pallas kernels, finish(): pl.pallas_call(final_kernel, out_shape=jax.ShapeDtypeStruct((2, GROUP, SH...  9.65 us
    all_to_all x1, starting transfers between devices, body(): v = lax.all_to_all(parcels, ('x', 'z'), 0, 0, tiled=True)  8.57 us
    ppermute x3, starting transfers between devices, core_sum(): return s + lax.ppermute(s, 'core', turned_by(NC, 1))  8.23 us
    ppermute x9, starting transfers between devices, sums_over(): return [s] + [lax.ppermute(s, 'y', turned_by(NY, d)) for d in range(1, NY)]  8.08 us
    all_to_all x1, waiting for transfers between devices, body(): own = lax.all_to_all(many, ('y', 'z'), 0, 0, tiled=True)  7.21 us
    all_to_all x1, waiting for transfers between devices, body(): v = lax.all_to_all(parcels, ('x', 'z'), 0, 0, tiled=True)  6.89 us
  transfers between devices with their start and end apart: 20, of which 15 were waited for; matrix products, arithmetic and copies ran while one was open for 3% of the time, Pallas kernels for 11%

profile of v3, /device:TPU:1, one launch (start us, length us, event | category | flops | bytes accessed | tf_op | source)
XLA Modules:
  0.0 120.0 jit_solution(18138647475692882384)
XLA Ops:
  0.0 2.8 %copy-done = bf16[32,98688]{1,0:T(8,128)(2,1)S(1)} copy-done((bf16[32,98688]{1,0:T(8,128)(2,1)S(1)}, bf16[32,98688]{1,0:T(8,128)(2,1)}, u32[]{:S(2)}) %copy-start) | copy-done | bytes 6316056
  2.8 0.7 copy-done.1
  3.4 11.1 %shard_map.37.v_ref = bf16[16,2,32,768]{3,2,1,0:T(8,128)(2,1)} custom-call(s32[12]{0:T(128)S(1)} %copy-done.1, bf16[32,98688]{1,0:T(8,128)(2,1)S(1)} %copy-done), custom_call_target="tpu_custom_call" | custom-call | bytes 24000000 | tf_op jit(solution)/shard_map/pallas_call | solution.py:149
  14.6 8.6 %all-to-all-start = ((bf16[16,2,32,768]{3,2,1,0:T(8,128)(2,1)}), bf16[16,2,32,768]{3,2,1,0:T(8,128)(2,1)S(1)}, u32[]{:S(2)}, u32[]{:S(2)}) async-start(bf16[16,2,32,768]{3,2,1,0:T(8,128)(2,1)} %shard_map.37.v_ref), calls=%async_computation | async-start | bytes 3145728 | tf_op jit(solution)/shard_map/all_to_all | solution.py:454
  23.2 0.1 pad_add_fusion.y_ref.at_ref.core_ref
  23.2 5.5 %shard_map.42 = (bf16[2,24,32,128]{3,2,1,0:T(8,128)(2,1)S(1)}, bf16[2,24,32,128]{3,2,1,0:T(8,128)(2,1)}, bf16[2,24,32,128]{3,2,1,0:T(8,128)(2,1)}, bf16[2,24,32,128]{3,2,1,0:T(8,128)(2,1)}) custom-call(s32[2]{0:T(128)S(1)} %pad_add_fusion.y_ref.at_ref.core_ref, bf16[16,2,32,768]{3,2,1,0:T(8,128)(2,1)} %shard_map.37.v_ref), custom_call_target="tpu_custom_call" | custom-call | bytes 12000000 | tf_op jit(solution)/shard_map/pallas_call | solution.py:191
  28.8 1.3 %collective-permute-start.12 = (bf16[2,24,32,128]{3,2,1,0:T(8,128)(2,1)}, bf16[2,24,32,128]{3,2,1,0:T(8,128)(2,1)S(1)}, u32[]{:S(2)}, u32[]{:S(2)}) collective-permute-start(bf16[2,24,32,128]{3,2,1,0:T(8,128)(2,1)} %get-tuple-element.21), channel_id=1, source_target_pairs={{0,8},{8,16},{16,24},{24,0},{1,9},{9,17},{17,25},{25,1},{2,10},{10... | collective-permute-start | bytes 1179656 | tf_op jit(solution)/shard_map/ppermute | solution.py:456
  30.1 2.6 %collective-permute-start.13 = (bf16[2,24,32,128]{3,2,1,0:T(8,128)(2,1)}, bf16[2,24,32,128]{3,2,1,0:T(8,128)(2,1)S(1)}, u32[]{:S(2)}, u32[]{:S(2)}) collective-permute-start(bf16[2,24,32,128]{3,2,1,0:T(8,128)(2,1)} %get-tuple-element.22), channel_id=1, source_target_pairs={{0,16},{8,24},{16,0},{24,8},{1,17},{9,25},{17,1},{25,9},{2,18},{10... | collective-permute-start | bytes 1179656 | tf_op jit(solution)/shard_map/ppermute | solution.py:456
  32.7 1.1 collective-permute-start.14
  33.8 1.9 %reshape.9 = f32[16,4,4,4,2,32]{5,4,3,2,1,0:T(2,128)} reshape(f32[2,8,4096]{2,1,0:T(8,128)S(1)} %copy-done.2) | data formatting | bytes 524288 | tf_op jit(solution)/shard_map/reshape | solution.py:458
  35.7 1.1 constant_dynamic-slice_fusion
  36.8 0.1 reshape.10.q_ref.z_ref
  36.9 6.9 %all-to-all-done.v_ref = bf16[16,2,32,768]{3,2,1,0:T(8,128)(2,1)S(1)} async-done(((bf16[16,2,32,768]{3,2,1,0:T(8,128)(2,1)}), bf16[16,2,32,768]{3,2,1,0:T(8,128)(2,1)S(1)}, u32[]{:S(2)}, u32[]{:S(2)}) %all-to-all-start) | async-done | bytes 1572896 | tf_op jit(solution)/shard_map/all_to_all | solution.py:454
  43.8 0.3 shard_map.38
  44.1 4.2 %collective-permute-start = (f32[16,768]{1,0:T(8,128)S(1)}, f32[16,768]{1,0:T(8,128)S(1)}, u32[]{:S(2)}, u32[]{:S(2)}) collective-permute-start(f32[16,768]{1,0:T(8,128)S(1)} %shard_map.38), channel_id=1, source_target_pairs={{0,1},{1,0},{2,3},{3,2},{4,5},{5,4},{6,7},{7,6},{8,9},{9,8},{10,11... | collective-permute-start | bytes 147464 | tf_op jit(solution)/shard_map/ppermute | solution.py:447
  48.3 1.3 %collective-permute-done.13.refs_2_ = bf16[2,24,32,128]{3,2,1,0:T(8,128)(2,1)S(1)} collective-permute-done((bf16[2,24,32,128]{3,2,1,0:T(8,128)(2,1)}, bf16[2,24,32,128]{3,2,1,0:T(8,128)(2,1)S(1)}, u32[]{:S(2)}, u32[]{:S(2)}) %collective-permute-start.13) | collective-permute-done | bytes 393248 | tf_op jit(solution)/shard_map/ppermute | solution.py:456
  49.5 2.7 %shard_map.43 = bf16[16,2,144,128]{3,2,1,0:T(8,128)(2,1)} custom-call(s32[2]{0:T(128)S(1)} %pad_add_fusion.y_ref.at_ref.core_ref, bf16[2,24,32,128]{3,2,1,0:T(8,128)(2,1)S(1)} %get-tuple-element.20.refs_0_, bf16[2,24,32,128]{3,2,1,0:T(8,128)(2,1)S(1)} %collective-permute-done.12.refs_1_, bf16[2,24,32,128]{3,2,1,0:T(8,128)(2,1)S(1)} %collective-permute-done.13.refs_2_, ...), custom_call_target="tpu_custom_call" | custom-call | bytes 9000000 | tf_op jit(solution)/shard_map/pallas_call | solution.py:226
  52.3 6.5 %all-to-all-start.1 = ((bf16[16,2,144,128]{3,2,1,0:T(8,128)(2,1)}), bf16[16,2,144,128]{3,2,1,0:T(8,128)(2,1)S(1)}, u32[]{:S(2)}, u32[]{:S(2)}) async-start(bf16[16,2,144,128]{3,2,1,0:T(8,128)(2,1)} %shard_map.43), calls=%async_computation.1 | async-start | bytes 2359296 | tf_op jit(solution)/shard_map/all_to_all | solution.py:464
  58.8 3.4 %collective-permute-start.3 = (f32[16,768]{1,0:T(8,128)S(1)}, f32[16,768]{1,0:T(8,128)S(1)}, u32[]{:S(2)}, u32[]{:S(2)}) collective-permute-start(f32[16,768]{1,0:T(8,128)S(1)} %add.69.s0), channel_id=1, source_target_pairs={{0,24},{8,0},{16,8},{24,16},{1,25},{9,1},{17,9},{25,17},{2,26},{10... | collective-permute-start | bytes 147464 | tf_op jit(solution)/shard_map/ppermute | solution.py:443
  62.2 0.7 collective-permute-start.1
  62.9 0.5 collective-permute-done.3.s3
  63.4 3.6 %collective-permute-done.2.s2 = f32[16,768]{1,0:T(8,128)S(1)} collective-permute-done((f32[16,768]{1,0:T(8,128)S(1)}, f32[16,768]{1,0:T(8,128)S(1)}, u32[]{:S(2)}, u32[]{:S(2)}) %collective-permute-start.2) | collective-permute-done | bytes 49184 | tf_op jit(solution)/shard_map/ppermute | solution.py:443
  66.9 0.2 collective-permute-done.1.s1
  67.2 1.1 shard_map.39
  68.3 2.7 %collective-permute-start.4 = (f32[16,896]{1,0:T(8,128)S(1)}, f32[16,896]{1,0:T(8,128)S(1)}, u32[]{:S(2)}, u32[]{:S(2)}) collective-permute-start(f32[16,896]{1,0:T(8,128)S(1)} %get-tuple-element.17), channel_id=1, source_target_pairs={{0,1},{1,0},{2,3},{3,2},{4,5},{5,4},{6,7},{7,6},{8,9},{9,8},{10,11... | collective-permute-start | bytes 172040 | tf_op jit(solution)/shard_map/ppermute | solution.py:447
  70.9 0.9 collective-permute-done.4
  71.9 1.1 collective-permute-start.6
  72.9 0.7 collective-permute-start.5
  73.6 1.6 %collective-permute-done.7.s3 = f32[16,896]{1,0:T(8,128)S(1)} collective-permute-done((f32[16,896]{1,0:T(8,128)S(1)}, f32[16,896]{1,0:T(8,128)S(1)}, u32[]{:S(2)}, u32[]{:S(2)}) %collective-permute-start.7) | collective-permute-done | bytes 57376 | tf_op jit(solution)/shard_map/ppermute | solution.py:443
  75.2 1.6 %collective-permute-done.6.s2 = f32[16,896]{1,0:T(8,128)S(1)} collective-permute-done((f32[16,896]{1,0:T(8,128)S(1)}, f32[16,896]{1,0:T(8,128)S(1)}, u32[]{:S(2)}, u32[]{:S(2)}) %collective-permute-start.6) | collective-permute-done | bytes 57376 | tf_op jit(solution)/shard_map/ppermute | solution.py:443
  76.8 1.1 collective-permute-done.5.s1
  77.9 1.7 %shard_map.40 = (f32[16,512]{1,0:T(8,128)S(1)}, f32[16,896]{1,0:T(8,128)S(1)}) custom-call(bf16[16,2,32,768]{3,2,1,0:T(8,128)(2,1)S(1)} %all-to-all-done.v_ref, f32[16,512]{1,0:T(8,128)S(1)} %get-tuple-element.16.z_ref, f32[16,896]{1,0:T(8,128)S(1)} %add.70.s0, f32[16,896]{1,0:T(8,128)S(1)} %collective-permute-done.5.s1, ...), custom_call_target="tpu_custom_call" | custom-call | bytes 9000000 | tf_op jit(solution)/shard_map/pallas_call | solution.py:330
  79.6 1.4 %collective-permute-start.8 = (f32[16,896]{1,0:T(8,128)S(1)}, f32[16,896]{1,0:T(8,128)S(1)}, u32[]{:S(2)}, u32[]{:S(2)}) collective-permute-start(f32[16,896]{1,0:T(8,128)S(1)} %get-tuple-element.19), channel_id=1, source_target_pairs={{0,1},{1,0},{2,3},{3,2},{4,5},{5,4},{6,7},{7,6},{8,9},{9,8},{10,11... | collective-permute-start | bytes 172040 | tf_op jit(solution)/shard_map/ppermute | solution.py:447
  81.0 0.9 collective-permute-done.8
  81.9 1.6 %collective-permute-start.11 = (f32[16,896]{1,0:T(8,128)S(1)}, f32[16,896]{1,0:T(8,128)S(1)}, u32[]{:S(2)}, u32[]{:S(2)}) collective-permute-start(f32[16,896]{1,0:T(8,128)S(1)} %add.71.s0), channel_id=1, source_target_pairs={{0,24},{8,0},{16,8},{24,16},{1,25},{9,1},{17,9},{25,17},{2,26},{10... | collective-permute-start | bytes 172040 | tf_op jit(solution)/shard_map/ppermute | solution.py:443
  83.5 0.6 collective-permute-start.10
  84.2 0.8 collective-permute-done.11.s3
  84.9 3.1 %collective-permute-done.10.s2 = f32[16,896]{1,0:T(8,128)S(1)} collective-permute-done((f32[16,896]{1,0:T(8,128)S(1)}, f32[16,896]{1,0:T(8,128)S(1)}, u32[]{:S(2)}, u32[]{:S(2)}) %collective-permute-start.10) | collective-permute-done | bytes 57376 | tf_op jit(solution)/shard_map/ppermute | solution.py:443
  88.0 1.0 collective-permute-done.9.s1
  89.0 2.0 %shard_map.41 = f32[16,16,512]{2,1,0:T(8,128)} custom-call(bf16[16,2,32,768]{3,2,1,0:T(8,128)(2,1)S(1)} %all-to-all-done.v_ref, f32[16,512]{1,0:T(8,128)S(1)} %get-tuple-element.18.z_ref, f32[16,896]{1,0:T(8,128)S(1)} %add.71.s0, f32[16,896]{1,0:T(8,128)S(1)} %collective-permute-done.9.s1, f32[16,896]{1,0:T(8,128)S(1)} %collective-permute-done.10.s2, ...), custom_call_target="tpu_custom_call" | custom-call | bytes 9000000 | tf_op jit(solution)/shard_map/pallas_call | solution.py:330
  91.0 5.4 %all-to-all-start.2 = ((f32[16,16,512]{2,1,0:T(8,128)}), f32[16,16,512]{2,1,0:T(8,128)S(1)}, u32[]{:S(2)}, u32[]{:S(2)}) async-start(f32[16,16,512]{2,1,0:T(8,128)} %shard_map.41), calls=%async_computation.2 | async-start | bytes 1048576 | tf_op jit(solution)/shard_map/all_to_all | solution.py:471
  96.4 0.1 slice_bitcast_fusion
  96.5 1.8 %collective-permute-start.15 = (bf16[16,144,128]{2,1,0:T(8,128)(2,1)S(1)}, bf16[16,144,128]{2,1,0:T(8,128)(2,1)S(1)}, u32[]{:S(2)}, u32[]{:S(2)}) collective-permute-start(bf16[16,144,128]{2,1,0:T(8,128)(2,1)S(1)} %get-tuple-element.27), channel_id=1, source_target_pairs={{0,1},{1,0},{2,3},{3,2},{4,5},{5,4},{6,7},{7,6},{8,9},{9,8},{10,11... | collective-permute-start | bytes 1769480 | tf_op jit(solution)/shard_map/ppermute | solution.py:470
  98.3 7.2 %all-to-all-done.2.own_ref = f32[16,16,512]{2,1,0:T(8,128)S(1)} async-done(((f32[16,16,512]{2,1,0:T(8,128)}), f32[16,16,512]{2,1,0:T(8,128)S(1)}, u32[]{:S(2)}, u32[]{:S(2)}) %all-to-all-start.2) | async-done | bytes 524320 | tf_op jit(solution)/shard_map/all_to_all | solution.py:471
  105.5 3.3 %collective-permute-start.16 = (f32[16,16,512]{2,1,0:T(8,128)S(1)}, f32[16,16,512]{2,1,0:T(8,128)S(1)}, u32[]{:S(2)}, u32[]{:S(2)}) collective-permute-start(f32[16,16,512]{2,1,0:T(8,128)S(1)} %all-to-all-done.2.own_ref), channel_id=1, source_target_pairs={{0,1},{1,0},{2,3},{3,2},{4,5},{5,4},{6,7},{7,6},{8,9},{9,8},{10,11... | collective-permute-start | bytes 1572872 | tf_op jit(solution)/shard_map/ppermute | solution.py:472
  108.8 0.6 select_convert_fusion.place_ref
  109.5 0.9 collective-permute-done.16.far_ref
  110.4 9.6 %shard_map.44 = f32[2,3,24,4096]{3,2,1,0:T(8,128)} custom-call(bf16[16,144,128]{2,1,0:T(8,128)(2,1)S(1)} %get-tuple-element.28.mine_ref, bf16[16,144,128]{2,1,0:T(8,128)(2,1)S(1)} %collective-permute-done.15.theirs_ref, f32[16,16,512]{2,1,0:T(8,128)S(1)} %all-to-all-done.2.own_ref, f32[16,16,512]{2,1,0:T(8,128)S(1)} %collective-permute-done.16.far_ref, ...), custom_call_target="tpu_custom_call" | custom-call | bytes 18000000 | tf_op jit(solution)/shard_map/pallas_call | solution.py:424
  (21 shorter events, 0.2 us)
Async XLA Ops:
  0.0 2.8 %copy-start = (bf16[32,98688]{1,0:T(8,128)(2,1)S(1)}, bf16[32,98688]{1,0:T(8,128)(2,1)}, u32[]{:S(2)}) copy-start(bf16[32,98688]{1,0:T(8,128)(2,1)} %x_hbm.1) | copy-start | bytes 18948100
  2.8 0.7 copy-start.1
  14.6 19.2 %copy-start.2 = (f32[2,8,4096]{2,1,0:T(8,128)S(1)}, f32[2,8,4096]{2,1,0:T(8,128)}, u32[]{:S(2)}) copy-start(f32[2,8,4096]{2,1,0:T(8,128)} %param.5) | copy-start | bytes 786436
  14.6 29.2 %all-to-all-start = ((bf16[16,2,32,768]{3,2,1,0:T(8,128)(2,1)}), bf16[16,2,32,768]{3,2,1,0:T(8,128)(2,1)S(1)}, u32[]{:S(2)}, u32[]{:S(2)}) async-start(bf16[16,2,32,768]{3,2,1,0:T(8,128)(2,1)} %shard_map.37.v_ref), calls=%async_computation | async-start | bytes 3145728 | tf_op jit(solution)/shard_map/all_to_all | solution.py:454
  28.8 19.5 %collective-permute-start.12 = (bf16[2,24,32,128]{3,2,1,0:T(8,128)(2,1)}, bf16[2,24,32,128]{3,2,1,0:T(8,128)(2,1)S(1)}, u32[]{:S(2)}, u32[]{:S(2)}) collective-permute-start(bf16[2,24,32,128]{3,2,1,0:T(8,128)(2,1)} %get-tuple-element.21), channel_id=1, source_target_pairs={{0,8},{8,16},{16,24},{24,0},{1,9},{9,17},{17,25},{25,1},{2,10},{10... | collective-permute-start | bytes 1179656 | tf_op jit(solution)/shard_map/ppermute | solution.py:456
  30.1 19.5 %collective-permute-start.13 = (bf16[2,24,32,128]{3,2,1,0:T(8,128)(2,1)}, bf16[2,24,32,128]{3,2,1,0:T(8,128)(2,1)S(1)}, u32[]{:S(2)}, u32[]{:S(2)}) collective-permute-start(bf16[2,24,32,128]{3,2,1,0:T(8,128)(2,1)} %get-tuple-element.22), channel_id=1, source_target_pairs={{0,16},{8,24},{16,0},{24,8},{1,17},{9,25},{17,1},{25,9},{2,18},{10... | collective-permute-start | bytes 1179656 | tf_op jit(solution)/shard_map/ppermute | solution.py:456
  32.7 16.8 %collective-permute-start.14 = (bf16[2,24,32,128]{3,2,1,0:T(8,128)(2,1)}, bf16[2,24,32,128]{3,2,1,0:T(8,128)(2,1)S(1)}, u32[]{:S(2)}, u32[]{:S(2)}) collective-permute-start(bf16[2,24,32,128]{3,2,1,0:T(8,128)(2,1)} %get-tuple-element.23), channel_id=1, source_target_pairs={{0,24},{8,0},{16,8},{24,16},{1,25},{9,1},{17,9},{25,17},{2,26},{10... | collective-permute-start | bytes 1179656 | tf_op jit(solution)/shard_map/ppermute | solution.py:456
  44.1 8.2 %collective-permute-start = (f32[16,768]{1,0:T(8,128)S(1)}, f32[16,768]{1,0:T(8,128)S(1)}, u32[]{:S(2)}, u32[]{:S(2)}) collective-permute-start(f32[16,768]{1,0:T(8,128)S(1)} %shard_map.38), channel_id=1, source_target_pairs={{0,1},{1,0},{2,3},{3,2},{4,5},{5,4},{6,7},{7,6},{8,9},{9,8},{10,11... | collective-permute-start | bytes 147464 | tf_op jit(solution)/shard_map/ppermute | solution.py:447
  52.3 38.7 %all-to-all-start.1 = ((bf16[16,2,144,128]{3,2,1,0:T(8,128)(2,1)}), bf16[16,2,144,128]{3,2,1,0:T(8,128)(2,1)S(1)}, u32[]{:S(2)}, u32[]{:S(2)}) async-start(bf16[16,2,144,128]{3,2,1,0:T(8,128)(2,1)} %shard_map.43), calls=%async_computation.1 | async-start | bytes 2359296 | tf_op jit(solution)/shard_map/all_to_all | solution.py:464
  58.8 4.6 %collective-permute-start.3 = (f32[16,768]{1,0:T(8,128)S(1)}, f32[16,768]{1,0:T(8,128)S(1)}, u32[]{:S(2)}, u32[]{:S(2)}) collective-permute-start(f32[16,768]{1,0:T(8,128)S(1)} %add.69.s0), channel_id=1, source_target_pairs={{0,24},{8,0},{16,8},{24,16},{1,25},{9,1},{17,9},{25,17},{2,26},{10... | collective-permute-start | bytes 147464 | tf_op jit(solution)/shard_map/ppermute | solution.py:443
  62.2 4.7 %collective-permute-start.2 = (f32[16,768]{1,0:T(8,128)S(1)}, f32[16,768]{1,0:T(8,128)S(1)}, u32[]{:S(2)}, u32[]{:S(2)}) collective-permute-start(f32[16,768]{1,0:T(8,128)S(1)} %add.69.s0), channel_id=1, source_target_pairs={{0,16},{8,24},{16,0},{24,8},{1,17},{9,25},{17,1},{25,9},{2,18},{10... | collective-permute-start | bytes 147464 | tf_op jit(solution)/shard_map/ppermute | solution.py:443
  62.2 5.0 %collective-permute-start.1 = (f32[16,768]{1,0:T(8,128)S(1)}, f32[16,768]{1,0:T(8,128)S(1)}, u32[]{:S(2)}, u32[]{:S(2)}) collective-permute-start(f32[16,768]{1,0:T(8,128)S(1)} %add.69.s0), channel_id=1, source_target_pairs={{0,8},{8,16},{16,24},{24,0},{1,9},{9,17},{17,25},{25,1},{2,10},{10... | collective-permute-start | bytes 147464 | tf_op jit(solution)/shard_map/ppermute | solution.py:443
  68.3 3.6 %collective-permute-start.4 = (f32[16,896]{1,0:T(8,128)S(1)}, f32[16,896]{1,0:T(8,128)S(1)}, u32[]{:S(2)}, u32[]{:S(2)}) collective-permute-start(f32[16,896]{1,0:T(8,128)S(1)} %get-tuple-element.17), channel_id=1, source_target_pairs={{0,1},{1,0},{2,3},{3,2},{4,5},{5,4},{6,7},{7,6},{8,9},{9,8},{10,11... | collective-permute-start | bytes 172040 | tf_op jit(solution)/shard_map/ppermute | solution.py:447
  71.8 3.3 %collective-permute-start.7 = (f32[16,896]{1,0:T(8,128)S(1)}, f32[16,896]{1,0:T(8,128)S(1)}, u32[]{:S(2)}, u32[]{:S(2)}) collective-permute-start(f32[16,896]{1,0:T(8,128)S(1)} %add.70.s0), channel_id=1, source_target_pairs={{0,24},{8,0},{16,8},{24,16},{1,25},{9,1},{17,9},{25,17},{2,26},{10... | collective-permute-start | bytes 172040 | tf_op jit(solution)/shard_map/ppermute | solution.py:443
  71.9 4.9 %collective-permute-start.6 = (f32[16,896]{1,0:T(8,128)S(1)}, f32[16,896]{1,0:T(8,128)S(1)}, u32[]{:S(2)}, u32[]{:S(2)}) collective-permute-start(f32[16,896]{1,0:T(8,128)S(1)} %add.70.s0), channel_id=1, source_target_pairs={{0,16},{8,24},{16,0},{24,8},{1,17},{9,25},{17,1},{25,9},{2,18},{10... | collective-permute-start | bytes 172040 | tf_op jit(solution)/shard_map/ppermute | solution.py:443
  72.9 5.0 %collective-permute-start.5 = (f32[16,896]{1,0:T(8,128)S(1)}, f32[16,896]{1,0:T(8,128)S(1)}, u32[]{:S(2)}, u32[]{:S(2)}) collective-permute-start(f32[16,896]{1,0:T(8,128)S(1)} %add.70.s0), channel_id=1, source_target_pairs={{0,8},{8,16},{16,24},{24,0},{1,9},{9,17},{17,25},{25,1},{2,10},{10... | collective-permute-start | bytes 172040 | tf_op jit(solution)/shard_map/ppermute | solution.py:443
  79.6 2.3 %collective-permute-start.8 = (f32[16,896]{1,0:T(8,128)S(1)}, f32[16,896]{1,0:T(8,128)S(1)}, u32[]{:S(2)}, u32[]{:S(2)}) collective-permute-start(f32[16,896]{1,0:T(8,128)S(1)} %get-tuple-element.19), channel_id=1, source_target_pairs={{0,1},{1,0},{2,3},{3,2},{4,5},{5,4},{6,7},{7,6},{8,9},{9,8},{10,11... | collective-permute-start | bytes 172040 | tf_op jit(solution)/shard_map/ppermute | solution.py:447
  81.9 3.1 %collective-permute-start.11 = (f32[16,896]{1,0:T(8,128)S(1)}, f32[16,896]{1,0:T(8,128)S(1)}, u32[]{:S(2)}, u32[]{:S(2)}) collective-permute-start(f32[16,896]{1,0:T(8,128)S(1)} %add.71.s0), channel_id=1, source_target_pairs={{0,24},{8,0},{16,8},{24,16},{1,25},{9,1},{17,9},{25,17},{2,26},{10... | collective-permute-start | bytes 172040 | tf_op jit(solution)/shard_map/ppermute | solution.py:443
  83.5 4.6 %collective-permute-start.10 = (f32[16,896]{1,0:T(8,128)S(1)}, f32[16,896]{1,0:T(8,128)S(1)}, u32[]{:S(2)}, u32[]{:S(2)}) collective-permute-start(f32[16,896]{1,0:T(8,128)S(1)} %add.71.s0), channel_id=1, source_target_pairs={{0,16},{8,24},{16,0},{24,8},{1,17},{9,25},{17,1},{25,9},{2,18},{10... | collective-permute-start | bytes 172040 | tf_op jit(solution)/shard_map/ppermute | solution.py:443
  84.1 4.9 %collective-permute-start.9 = (f32[16,896]{1,0:T(8,128)S(1)}, f32[16,896]{1,0:T(8,128)S(1)}, u32[]{:S(2)}, u32[]{:S(2)}) collective-permute-start(f32[16,896]{1,0:T(8,128)S(1)} %add.71.s0), channel_id=1, source_target_pairs={{0,8},{8,16},{16,24},{24,0},{1,9},{9,17},{17,25},{25,1},{2,10},{10... | collective-permute-start | bytes 172040 | tf_op jit(solution)/shard_map/ppermute | solution.py:443
  91.0 14.5 %all-to-all-start.2 = ((f32[16,16,512]{2,1,0:T(8,128)}), f32[16,16,512]{2,1,0:T(8,128)S(1)}, u32[]{:S(2)}, u32[]{:S(2)}) async-start(f32[16,16,512]{2,1,0:T(8,128)} %shard_map.41), calls=%async_computation.2 | async-start | bytes 1048576 | tf_op jit(solution)/shard_map/all_to_all | solution.py:471
  96.5 13.0 %collective-permute-start.15 = (bf16[16,144,128]{2,1,0:T(8,128)(2,1)S(1)}, bf16[16,144,128]{2,1,0:T(8,128)(2,1)S(1)}, u32[]{:S(2)}, u32[]{:S(2)}) collective-permute-start(bf16[16,144,128]{2,1,0:T(8,128)(2,1)S(1)} %get-tuple-element.27), channel_id=1, source_target_pairs={{0,1},{1,0},{2,3},{3,2},{4,5},{5,4},{6,7},{7,6},{8,9},{9,8},{10,11... | collective-permute-start | bytes 1769480 | tf_op jit(solution)/shard_map/ppermute | solution.py:470
  105.5 4.9 %collective-permute-start.16 = (f32[16,16,512]{2,1,0:T(8,128)S(1)}, f32[16,16,512]{2,1,0:T(8,128)S(1)}, u32[]{:S(2)}, u32[]{:S(2)}) collective-permute-start(f32[16,16,512]{2,1,0:T(8,128)S(1)} %all-to-all-done.2.own_ref), channel_id=1, source_target_pairs={{0,1},{1,0},{2,3},{3,2},{4,5},{5,4},{6,7},{7,6},{8,9},{9,8},{10,11... | collective-permute-start | bytes 1572872 | tf_op jit(solution)/shard_map/ppermute | solution.py:472

commit v4 on v3

--- a/solution.py
+++ b/solution.py
@@ -159,7 +159,7 @@
             pltpu.VMEM((RC, LOCAL, SPECTRA), F32),
             pltpu.SemaphoreType.DMA((CHUNKS,)),
         ],
-        compiler_params=params(32),
+        compiler_params=params(58),
         cost_estimate=cost(8),
     )(ids, x)
 
@@ -170,21 +170,18 @@
 
 def spread_kernel(y_ref, v_ref, *outs):
     row = lax.broadcasted_iota(jnp.int32, (SPECTRA, NC * PAD), 0)
-    col = lax.broadcasted_iota(jnp.int32, (SPECTRA, NC * PAD), 1)
+    col = lax.broadcasted_iota(jnp.int32, (1, NC * PAD), 1)
     inside = col % PAD
     wanted = (inside // 16) * ROWS + (col // PAD) * 16 + inside % 16
+    wanted = jnp.where(inside < PHASES * 16, wanted, -SPECTRA)
+    rows = [v_ref[c // GROUP * NZ + c % GROUP].reshape(2 * LOCAL, SPECTRA) for c in range(CHANNELS)]
+    rows = jnp.concatenate(rows, axis=0)
     for d in range(NY):
         y = (y_ref[0] + d) % NY
-        hit = (row == wanted + y * (NC * 16)) & (inside < PHASES * 16)
-        pick = jnp.where(hit, 1.0, 0.0).astype(BF16)
-        for c in range(CHANNELS):
-            at = c // GROUP * NZ + c % GROUP
-            got = dot_nn(v_ref[at].reshape(2 * LOCAL, SPECTRA), pick)
-            got = got.astype(BF16).reshape(2, LOCAL, NC * PAD)
-            for core in range(NC):
-                lanes = slice(core * PAD, (core + 1) * PAD)
-                for r in range(2):
-                    outs[d][core, c * 2 + r] = got[r, :, lanes]
+        pick = jnp.where(row == wanted + y * (NC * 16), 1.0, 0.0).astype(BF16)
+        got = dot_nn(rows, pick).astype(BF16).reshape(RC, LOCAL, NC * PAD)
+        for core in range(NC):
+            outs[d][core] = got[:, :, core * PAD : (core + 1) * PAD]
 
 
 def spread(y, v):
@@ -210,11 +207,13 @@
         side = core if other == 0 else 1 - core
         for x in range(NX):
             blocks = []
-            for rc in range(2 * GROUP):
+            for rc in range(0, 2 * GROUP, 2):
+                at = x * 2 * GROUP + rc
                 stack = jnp.concatenate(
-                    [parts[d][side, x * 2 * GROUP + rc] for d in range(NY)], axis=0
+                    [parts[d][side, at + k] for k in range(2) for d in range(NY)], axis=0
                 )
-                blocks.append(dot_nt(pick, stack))
+                got = dot_nt(pick, stack)
+                blocks += [got[:, 0 : NY * LOCAL], got[:, NY * LOCAL :]]
             for z_to in range(NZ):
                 rows = slice(z_to * SHARE, (z_to + 1) * SHARE)
                 o_ref[x * NZ + z_to, other] = jnp.concatenate(
@@ -346,9 +345,7 @@
     return jnp.where(row == source, 1.0, 0.0).astype(BF16)
 
 
-def final_kernel(mine_ref, theirs_ref, own_ref, far_ref, core_ref, place_ref, o_ref, flat, basis):
-    lane = lax.broadcasted_iota(jnp.int32, (2 * KDIM, 128), 1) // 32
-    is_zero = core_ref[1] == 0
+def arrange_kernel(mine_ref, theirs_ref, place_ref, flat):
     rows = []
     for x in range(NX):
         parts = []
@@ -357,82 +354,94 @@
         rows.append(jnp.concatenate(parts, axis=1))
     got = dot_nn(jnp.concatenate(rows, axis=0), place_ref[...])
     flat[...] = got.reshape(NX, GROUP, 2 * SHARE, NY * 256)
+
+
+def arrange(mine, theirs, place):
+    return pl.pallas_call(
+        arrange_kernel,
+        out_shape=jax.ShapeDtypeStruct((NX, GROUP, 2 * SHARE, NY * 256), F32),
+        in_specs=[in_vmem] * 3,
+        out_specs=in_vmem,
+        compiler_params=params(16),
+        cost_estimate=cost(4),
+    )(mine, theirs, place)
+
+
+def final_kernel(flat, own_ref, far_ref, core_ref, o_ref, basis):
+    z = pl.program_id(0)
+    lane = lax.broadcasted_iota(jnp.int32, (2 * KDIM, 128), 1) // 32
+    is_zero = core_ref[1] == 0
     for x in range(NX):
         lanes = slice(x * 128, (x + 1) * 128)
         for y in range(NY):
-            for z in range(GROUP):
-                own, far = own_ref[y * NZ + z, :, lanes], far_ref[y * NZ + z, :, lanes]
-                a, b = jnp.where(is_zero, own, far), jnp.where(is_zero, far, own)
-                left = jnp.where(
-                    lane < 2,
-                    jnp.where(lane == 0, a, pltpu.roll(b, 32, 1)),
-                    jnp.where(lane == 2, pltpu.roll(a, 32, 1), pltpu.roll(b, 64, 1)),
-                )
-                right = jnp.where(
-                    lane < 2,
-                    jnp.where(lane == 0, pltpu.roll(a, 64, 1), pltpu.roll(b, 96, 1)),
-                    jnp.where(lane == 2, pltpu.roll(a, 96, 1), b),
-                )
-                at = (x * NY + y) * 256
-                basis[z, :, at : at + 128] = left
-                basis[z, :, at + 128 : at + 256] = right
+            own, far = own_ref[y * NZ + z, :, lanes], far_ref[y * NZ + z, :, lanes]
+            a, b = jnp.where(is_zero, own, far), jnp.where(is_zero, far, own)
+            left = jnp.where(
+                lane < 2,
+                jnp.where(lane == 0, a, pltpu.roll(b, 32, 1)),
+                jnp.where(lane == 2, pltpu.roll(a, 32, 1), pltpu.roll(b, 64, 1)),
+            )
+            right = jnp.where(
+                lane < 2,
+                jnp.where(lane == 0, pltpu.roll(a, 64, 1), pltpu.roll(b, 96, 1)),
+                jnp.where(lane == 2, pltpu.roll(a, 96, 1), b),
+            )
+            at = (x * NY + y) * 256
+            for k, part in enumerate((left, right)):
+                basis[:, at + k * 128 : at + (k + 1) * 128] = split3(part)
 
     lane = lax.broadcasted_iota(jnp.int32, (KDIM, 128), 1)
     unit = lane == lax.broadcasted_iota(jnp.int32, (KDIM, 128), 0) + KDIM
     unit_lanes = (lane >= KDIM) & (lane < 2 * KDIM)
     u_lanes = (lane >= 48) & (lane < 72)
     wide = NY * 256
-    for z in range(GROUP):
-        products = jnp.zeros((48, 128), F32)
-        for x in range(NX):
-            pieces = split3(basis[z, :, x * wide : (x + 1) * wide])
-            block = flat[x, z].astype(BF16)
-            right = jnp.concatenate([pieces, block, jnp.zeros((32, wide), BF16)], axis=0)
-            products = products + dot_nt(pieces, right)
-        g_re, g_im = gram_from(products)
-        up_down = sum3(products)
-        up, down = up_down[0:KDIM], up_down[KDIM:]
-        u_re = up + pltpu.roll(down, 104, 1)
-        u_im = down - pltpu.roll(up, 104, 1)
-        x_re = jnp.where(u_lanes, u_re, jnp.where(unit_lanes, jnp.where(unit, 1.0, 0.0), g_re))
-        x_im = jnp.where(u_lanes, u_im, jnp.where(unit_lanes, 0.0, g_im))
-        used = lane < 72
-        x_re, x_im = jnp.where(used, x_re, 0.0), jnp.where(used, x_im, 0.0)
-        ((x_re, x_im),) = eliminate((x_re, x_im), [])
-        both = jnp.concatenate([x_re, x_im], axis=0)
-        cross = jnp.concatenate([x_im, -x_re], axis=0)
-        t_re = dot_tn(both, both, lax.Precision.HIGHEST)[KDIM : 2 * KDIM]
-        t_im = dot_tn(cross, both, lax.Precision.HIGHEST)[KDIM : 2 * KDIM]
-
-        def sides(a, b):
-            near, away = pltpu.roll(a, 80, 1), pltpu.roll(b, 104, 1)
-            return jnp.where(lane < SHARE, near, jnp.where(lane < 2 * SHARE, away, 0.0))
-
-        t = split3(jnp.concatenate([sides(t_re, t_im), sides(-t_im, t_re)], axis=0))
-        hi, mid, lo = t[0:16], t[16:32], t[32:48]
-        left = jnp.concatenate([hi, hi, hi, mid, mid, lo], axis=0)
-        for x in range(NX):
-            pieces = split3(basis[z, :, x * wide : (x + 1) * wide])
-            right = jnp.concatenate([pieces, pieces[0:32], pieces[0:16]], axis=0)
-            fitted = dot_tn(left, right)[0 : 2 * SHARE]
-            rest = flat[x, z] - fitted
-            o_ref[0, z, :, x * wide : (x + 1) * wide] = rest[0:SHARE]
-            o_ref[1, z, :, x * wide : (x + 1) * wide] = rest[SHARE:]
-
-
-def finish(mine, theirs, own, far, at, place):
+    products = jnp.zeros((48, 128), F32)
+    for x in range(NX):
+        pieces = basis[:, x * wide : (x + 1) * wide]
+        block = flat[x, z].astype(BF16)
+        right = jnp.concatenate([pieces, block, jnp.zeros((32, wide), BF16)], axis=0)
+        products = products + dot_nt(pieces, right)
+    g_re, g_im = gram_from(products)
+    up_down = sum3(products)
+    up, down = up_down[0:KDIM], up_down[KDIM:]
+    u_re = up + pltpu.roll(down, 104, 1)
+    u_im = down - pltpu.roll(up, 104, 1)
+    x_re = jnp.where(u_lanes, u_re, jnp.where(unit_lanes, jnp.where(unit, 1.0, 0.0), g_re))
+    x_im = jnp.where(u_lanes, u_im, jnp.where(unit_lanes, 0.0, g_im))
+    used = lane < 72
+    x_re, x_im = jnp.where(used, x_re, 0.0), jnp.where(used, x_im, 0.0)
+    ((x_re, x_im),) = eliminate((x_re, x_im), [])
+    both = jnp.concatenate([x_re, x_im], axis=0)
+    cross = jnp.concatenate([x_im, -x_re], axis=0)
+    t_re = dot_tn(both, both, lax.Precision.HIGHEST)[KDIM : 2 * KDIM]
+    t_im = dot_tn(cross, both, lax.Precision.HIGHEST)[KDIM : 2 * KDIM]
+
+    def sides(a, b):
+        near, away = pltpu.roll(a, 80, 1), pltpu.roll(b, 104, 1)
+        return jnp.where(lane < SHARE, near, jnp.where(lane < 2 * SHARE, away, 0.0))
+
+    t = split3(jnp.concatenate([sides(t_re, t_im), sides(-t_im, t_re)], axis=0))
+    hi, mid, lo = t[0:16], t[16:32], t[32:48]
+    left = jnp.concatenate([hi, hi, hi, mid, mid, lo], axis=0)
+    for x in range(NX):
+        pieces = basis[:, x * wide : (x + 1) * wide]
+        right = jnp.concatenate([pieces, pieces[0:32], pieces[0:16]], axis=0)
+        rest = flat[x, z] - dot_tn(left, right)[0 : 2 * SHARE]
+        o_ref[0, 0, :, x * wide : (x + 1) * wide] = rest[0:SHARE]
+        o_ref[1, 0, :, x * wide : (x + 1) * wide] = rest[SHARE:]
+
+
+def finish(flat, own, far, at):
     return pl.pallas_call(
         final_kernel,
+        grid=(GROUP,),
         out_shape=jax.ShapeDtypeStruct((2, GROUP, SHARE, INPUTS), F32),
-        in_specs=[in_vmem] * 4 + [pl.BlockSpec(memory_space=pltpu.SMEM), in_vmem],
-        out_specs=in_vmem,
-        scratch_shapes=[
-            pltpu.VMEM((NX, GROUP, 2 * SHARE, NY * 256), F32),
-            pltpu.VMEM((GROUP, 2 * KDIM, INPUTS), F32),
-        ],
-        compiler_params=params(24),
+        in_specs=[in_vmem] * 3 + [pl.BlockSpec(memory_space=pltpu.SMEM)],
+        out_specs=pl.BlockSpec((2, 1, SHARE, INPUTS), lambda z: (0, z, 0, 0)),
+        scratch_shapes=[pltpu.VMEM((6 * KDIM, INPUTS), BF16)],
+        compiler_params=params(16),
         cost_estimate=cost(6),
-    )(mine, theirs, own, far, at, place)
+    )(flat, own, far, at)
 
 
 def turned_by(count, distance):
@@ -465,12 +474,15 @@
     place = placing(y, core)
     z, s = step(0, v, z, sums)
     z, s = step(1, v, z, sums_over(core_sum(s)))
-    (many,) = step(2, v, z, sums_over(core_sum(s)))
-    many, blocks = lax.optimization_barrier((many, blocks))
+    s, blocks = lax.optimization_barrier((core_sum(s), blocks))
+    sums = sums_over(s)
     mine, theirs = blocks[:, 0], lax.ppermute(blocks[:, 1], "core", turned_by(NC, 1))
+    flat = arrange(mine, theirs, place)
+    z, flat = lax.optimization_barrier((z, flat))
+    (many,) = step(2, v, z, sums)
     own = lax.all_to_all(many, ("y", "z"), 0, 0, tiled=True)
     far = lax.ppermute(own, "core", turned_by(NC, 1))
-    return finish(mine, theirs, own, far, at, place)
+    return finish(flat, own, far, at)
 
 
 def solution(mesh):

time: 120 us -> 116 us (0.967)
  blocking collectives: 0 us -> 16.1 us
  waiting for transfers between devices: 31.5 us -> 19.8 us
  starting transfers between devices: 46.9 us -> 41.7 us
  Pallas kernels: 34.2 us -> 31.5 us
  local copies, waits for them, and re-layouts: 6.65 us -> 5.38 us
    all_to_all x0 -> x1, blocking collectives: none -> 16.1 us  [body(): own = lax.all_to_all(many, ('y', 'z'), 0, 0, tiled=True)]
    all_to_all x1 -> x0, waiting for transfers between devices: 7.21 us -> none  [body(): own = lax.all_to_all(many, ('y', 'z'), 0, 0, tiled=True)]
    ppermute x9, waiting for transfers between devices: 13.4 us -> 6.86 us  [sums_over(): return [s] + [lax.ppermute(s, 'y', turned_by(NY, d)) for d in range(1, NY)]]
    all_to_all x1 -> x0, starting transfers between devices: 5.36 us -> none  [body(): own = lax.all_to_all(many, ('y', 'z'), 0, 0, tiled=True)]
    ppermute x9, starting transfers between devices: 8.08 us -> 11.7 us  [sums_over(): return [s] + [lax.ppermute(s, 'y', turned_by(NY, d)) for d in range(1, NY)]]
    unnamed x6 -> x2, local copies, waits for them, and re-layouts: 3.45 us -> 0.01 us
    pallas_call x1, Pallas kernels: 5.54 us -> 2.82 us  [spread(): pl.pallas_call(spread_kernel, out_shape=[jax.ShapeDtypeStruct((NC, RC, LO...]
    all_to_all x1, waiting for transfers between devices: 6.89 us -> 8.67 us  [body(): v = lax.all_to_all(parcels, ('x', 'z'), 0, 0, tiled=True)]
  transfers between devices with their start and end apart: 20 -> 19, of which waited for: 15 -> 11; matrix products, arithmetic and copies ran while one was open for 3% -> 5% of each run, Pallas kernels for 11% -> 8%
where the time goes in v4:
time: 116 us; the launch traced here: 115 us
  starting transfers between devices  41.7 us (36%)
  Pallas kernels  31.5 us (27%)
  waiting for transfers between devices  19.8 us (17%)
  blocking collectives  16.1 us (14%)
  local copies, waits for them, and re-layouts  5.38 us (5%)
    all_to_all x1, blocking collectives, body(): own = lax.all_to_all(many, ('y', 'z'), 0, 0, tiled=True)  16.1 us
    pallas_call x1, Pallas kernels, channelize(): pl.pallas_call(channelize_kernel, out_shape=jax.ShapeDtypeStruct((NX * NZ...  11.8 us
    ppermute x9, starting transfers between devices, sums_over(): return [s] + [lax.ppermute(s, 'y', turned_by(NY, d)) for d in range(1, NY)]  11.7 us
    pallas_call x1, Pallas kernels, finish(): pl.pallas_call(final_kernel, grid=(GROUP,), out_shape=jax.ShapeDtypeStruc...  8.95 us
    all_to_all x1, waiting for transfers between devices, body(): v = lax.all_to_all(parcels, ('x', 'z'), 0, 0, tiled=True)  8.67 us
    all_to_all x1, starting transfers between devices, body(): v = lax.all_to_all(parcels, ('x', 'z'), 0, 0, tiled=True)  8.57 us
    ppermute x3, starting transfers between devices, core_sum(): return s + lax.ppermute(s, 'core', turned_by(NC, 1))  7.88 us
    ppermute x9, waiting for transfers between devices, sums_over(): return [s] + [lax.ppermute(s, 'y', turned_by(NY, d)) for d in range(1, NY)]  6.86 us
  transfers between devices with their start and end apart: 19, of which 11 were waited for; matrix products, arithmetic and copies ran while one was open for 5% of the time, Pallas kernels for 8%

profile of v4, /device:TPU:1, one launch (start us, length us, event | category | flops | bytes accessed | tf_op | source)
XLA Modules:
  0.0 115.3 jit_solution(15877457396198586340)
XLA Ops:
  0.0 11.8 %shard_map.37.v_ref = bf16[16,2,32,768]{3,2,1,0:T(8,128)(2,1)} custom-call(s32[12]{0:T(128)} %ids_ref.1, bf16[32,98688]{1,0:T(8,128)(2,1)} %x_hbm.1), custom_call_target="tpu_custom_call" | custom-call | bytes 24000000 | tf_op jit(solution)/shard_map/pallas_call | solution.py:149
  11.8 0.0 copy-start
  11.8 8.6 %all-to-all-start = ((bf16[16,2,32,768]{3,2,1,0:T(8,128)(2,1)}), bf16[16,2,32,768]{3,2,1,0:T(8,128)(2,1)S(1)}, u32[]{:S(2)}, u32[]{:S(2)}) async-start(bf16[16,2,32,768]{3,2,1,0:T(8,128)(2,1)} %shard_map.37.v_ref), calls=%async_computation | async-start | bytes 3145728 | tf_op jit(solution)/shard_map/all_to_all | solution.py:463
  20.4 0.1 pad_add_fusion.y_ref.at_ref.core_ref
  20.4 2.8 %shard_map.41 = (bf16[2,24,32,128]{3,2,1,0:T(8,128)(2,1)S(1)}, bf16[2,24,32,128]{3,2,1,0:T(8,128)(2,1)}, bf16[2,24,32,128]{3,2,1,0:T(8,128)(2,1)}, bf16[2,24,32,128]{3,2,1,0:T(8,128)(2,1)}) custom-call(s32[2]{0:T(128)S(1)} %pad_add_fusion.y_ref.at_ref.core_ref, bf16[16,2,32,768]{3,2,1,0:T(8,128)(2,1)S(1)} %copy-done), custom_call_target="tpu_custom_call" | custom-call | bytes 12000000 | tf_op jit(solution)/shard_map/pallas_call | solution.py:188
  23.3 1.3 %collective-permute-start.9 = (bf16[2,24,32,128]{3,2,1,0:T(8,128)(2,1)}, bf16[2,24,32,128]{3,2,1,0:T(8,128)(2,1)S(1)}, u32[]{:S(2)}, u32[]{:S(2)}) collective-permute-start(bf16[2,24,32,128]{3,2,1,0:T(8,128)(2,1)} %get-tuple-element.23), channel_id=1, source_target_pairs={{0,8},{8,16},{16,24},{24,0},{1,9},{9,17},{17,25},{25,1},{2,10},{10... | collective-permute-start | bytes 1179656 | tf_op jit(solution)/shard_map/ppermute | solution.py:465
  24.6 2.6 %collective-permute-start.10 = (bf16[2,24,32,128]{3,2,1,0:T(8,128)(2,1)}, bf16[2,24,32,128]{3,2,1,0:T(8,128)(2,1)S(1)}, u32[]{:S(2)}, u32[]{:S(2)}) collective-permute-start(bf16[2,24,32,128]{3,2,1,0:T(8,128)(2,1)} %get-tuple-element.24), channel_id=1, source_target_pairs={{0,16},{8,24},{16,0},{24,8},{1,17},{9,25},{17,1},{25,9},{2,18},{10... | collective-permute-start | bytes 1179656 | tf_op jit(solution)/shard_map/ppermute | solution.py:465
  27.2 1.1 collective-permute-start.11
  28.3 2.8 %reshape.9 = f32[16,4,4,4,2,32]{5,4,3,2,1,0:T(2,128)} reshape(f32[2,8,4096]{2,1,0:T(8,128)} %param.5) | data formatting | bytes 524288 | tf_op jit(solution)/shard_map/reshape | solution.py:467
  31.1 1.1 constant_dynamic-slice_fusion
  32.2 0.1 reshape.10.q_ref.z_ref
  32.3 8.7 %all-to-all-done.v_ref = bf16[16,2,32,768]{3,2,1,0:T(8,128)(2,1)S(1)} async-done(((bf16[16,2,32,768]{3,2,1,0:T(8,128)(2,1)}), bf16[16,2,32,768]{3,2,1,0:T(8,128)(2,1)S(1)}, u32[]{:S(2)}, u32[]{:S(2)}) %all-to-all-start) | async-done | bytes 1572896 | tf_op jit(solution)/shard_map/all_to_all | solution.py:463
  41.0 0.3 shard_map.38
  41.3 4.2 %collective-permute-start = (f32[16,768]{1,0:T(8,128)S(1)}, f32[16,768]{1,0:T(8,128)S(1)}, u32[]{:S(2)}, u32[]{:S(2)}) collective-permute-start(f32[16,768]{1,0:T(8,128)S(1)} %shard_map.38), channel_id=1, source_target_pairs={{0,1},{1,0},{2,3},{3,2},{4,5},{5,4},{6,7},{7,6},{8,9},{9,8},{10,11... | collective-permute-start | bytes 147464 | tf_op jit(solution)/shard_map/ppermute | solution.py:456
  45.5 0.0 collective-permute-done.10.refs_2_
  45.5 0.0 collective-permute-done.11.refs_3_
  45.5 2.2 %shard_map.42 = bf16[16,2,144,128]{3,2,1,0:T(8,128)(2,1)} custom-call(s32[2]{0:T(128)S(1)} %pad_add_fusion.y_ref.at_ref.core_ref, bf16[2,24,32,128]{3,2,1,0:T(8,128)(2,1)S(1)} %get-tuple-element.22.refs_0_, bf16[2,24,32,128]{3,2,1,0:T(8,128)(2,1)S(1)} %collective-permute-done.9.refs_1_, bf16[2,24,32,128]{3,2,1,0:T(8,128)(2,1)S(1)} %collective-permute-done.10.refs_2_, ...), custom_call_target="tpu_custom_call" | custom-call | bytes 9000000 | tf_op jit(solution)/shard_map/pallas_call | solution.py:225
  47.7 5.1 %all-to-all-start.1 = ((bf16[16,2,144,128]{3,2,1,0:T(8,128)(2,1)}), bf16[16,2,144,128]{3,2,1,0:T(8,128)(2,1)}, u32[]{:S(2)}, u32[]{:S(2)}) async-start(bf16[16,2,144,128]{3,2,1,0:T(8,128)(2,1)} %shard_map.42), calls=%async_computation.1 | async-start | bytes 2359296 | tf_op jit(solution)/shard_map/all_to_all | solution.py:473
  52.8 1.6 %collective-permute-start.1 = (f32[16,768]{1,0:T(8,128)S(1)}, f32[16,768]{1,0:T(8,128)S(1)}, u32[]{:S(2)}, u32[]{:S(2)}) collective-permute-start(f32[16,768]{1,0:T(8,128)S(1)} %add.69.s0), channel_id=1, source_target_pairs={{0,8},{8,16},{16,24},{24,0},{1,9},{9,17},{17,25},{25,1},{2,10},{10... | collective-permute-start | bytes 147464 | tf_op jit(solution)/shard_map/ppermute | solution.py:452
  54.4 3.0 %collective-permute-start.2 = (f32[16,768]{1,0:T(8,128)S(1)}, f32[16,768]{1,0:T(8,128)S(1)}, u32[]{:S(2)}, u32[]{:S(2)}) collective-permute-start(f32[16,768]{1,0:T(8,128)S(1)} %add.69.s0), channel_id=1, source_target_pairs={{0,16},{8,24},{16,0},{24,8},{1,17},{9,25},{17,1},{25,9},{2,18},{10... | collective-permute-start | bytes 147464 | tf_op jit(solution)/shard_map/ppermute | solution.py:452
  57.4 0.3 collective-permute-done.1.s1
  57.7 1.7 %collective-permute-done.2.s2 = f32[16,768]{1,0:T(8,128)S(1)} collective-permute-done((f32[16,768]{1,0:T(8,128)S(1)}, f32[16,768]{1,0:T(8,128)S(1)}, u32[]{:S(2)}, u32[]{:S(2)}) %collective-permute-start.2) | collective-permute-done | bytes 49184 | tf_op jit(solution)/shard_map/ppermute | solution.py:452
  59.4 1.5 %collective-permute-done.3.s3 = f32[16,768]{1,0:T(8,128)S(1)} collective-permute-done((f32[16,768]{1,0:T(8,128)S(1)}, f32[16,768]{1,0:T(8,128)S(1)}, u32[]{:S(2)}, u32[]{:S(2)}) %collective-permute-start.3) | collective-permute-done | bytes 49184 | tf_op jit(solution)/shard_map/ppermute | solution.py:452
  60.9 1.1 shard_map.39
  62.0 1.9 %collective-permute-start.4 = (f32[16,896]{1,0:T(8,128)S(1)}, f32[16,896]{1,0:T(8,128)S(1)}, u32[]{:S(2)}, u32[]{:S(2)}) collective-permute-start(f32[16,896]{1,0:T(8,128)S(1)} %get-tuple-element.19), channel_id=1, source_target_pairs={{0,1},{1,0},{2,3},{3,2},{4,5},{5,4},{6,7},{7,6},{8,9},{9,8},{10,11... | collective-permute-start | bytes 172040 | tf_op jit(solution)/shard_map/ppermute | solution.py:456
  63.9 0.9 collective-permute-done.4
  64.8 0.8 collective-permute-start.5
  65.6 3.0 %collective-permute-start.6 = (f32[16,896]{1,0:T(8,128)S(1)}, f32[16,896]{1,0:T(8,128)S(1)}, u32[]{:S(2)}, u32[]{:S(2)}) collective-permute-start(f32[16,896]{1,0:T(8,128)S(1)} %add.70.s0), channel_id=1, source_target_pairs={{0,16},{8,24},{16,0},{24,8},{1,17},{9,25},{17,1},{25,9},{2,18},{10... | collective-permute-start | bytes 172040 | tf_op jit(solution)/shard_map/ppermute | solution.py:452
  68.6 0.0 collective-permute-start.7
  68.6 0.8 collective-permute-done.5.s1
  69.5 2.1 %collective-permute-done.6.s2 = f32[16,896]{1,0:T(8,128)S(1)} collective-permute-done((f32[16,896]{1,0:T(8,128)S(1)}, f32[16,896]{1,0:T(8,128)S(1)}, u32[]{:S(2)}, u32[]{:S(2)}) %collective-permute-start.6) | collective-permute-done | bytes 57376 | tf_op jit(solution)/shard_map/ppermute | solution.py:452
  71.6 0.4 collective-permute-done.7.s3
  72.0 1.7 %shard_map.40 = (f32[16,512]{1,0:T(8,128)S(1)}, f32[16,896]{1,0:T(8,128)S(1)}) custom-call(bf16[16,2,32,768]{3,2,1,0:T(8,128)(2,1)S(1)} %all-to-all-done.v_ref, f32[16,512]{1,0:T(8,128)S(1)} %get-tuple-element.18.z_ref, f32[16,896]{1,0:T(8,128)S(1)} %add.70.s0, f32[16,896]{1,0:T(8,128)S(1)} %collective-permute-done.5.s1, ...), custom_call_target="tpu_custom_call" | custom-call | bytes 9000000 | tf_op jit(solution)/shard_map/pallas_call | solution.py:329
  73.7 1.8 %collective-permute-start.8 = (f32[16,896]{1,0:T(8,128)S(1)}, f32[16,896]{1,0:T(8,128)S(1)}, u32[]{:S(2)}, u32[]{:S(2)}) collective-permute-start(f32[16,896]{1,0:T(8,128)S(1)} %get-tuple-element.21), channel_id=1, source_target_pairs={{0,1},{1,0},{2,3},{3,2},{4,5},{5,4},{6,7},{7,6},{8,9},{9,8},{10,11... | collective-permute-start | bytes 172040 | tf_op jit(solution)/shard_map/ppermute | solution.py:456
  75.5 0.9 collective-permute-done.8
  76.4 0.1 collective-permute-start.13
  76.4 2.2 %collective-permute-start.14 = (f32[16,896]{1,0:T(8,128)S(1)}, f32[16,896]{1,0:T(8,128)S(1)}, u32[]{:S(2)}, u32[]{:S(2)}) collective-permute-start(f32[16,896]{1,0:T(8,128)S(1)} %add.71.s0), channel_id=1, source_target_pairs={{0,16},{8,24},{16,0},{24,8},{1,17},{9,25},{17,1},{25,9},{2,18},{10... | collective-permute-start | bytes 172040 | tf_op jit(solution)/shard_map/ppermute | solution.py:452
  78.6 1.1 collective-permute-start.15
  79.7 1.3 %slice_bitcast_fusion = (bf16[16,144,128]{2,1,0:T(8,128)(2,1)S(1)}, bf16[16,144,128]{2,1,0:T(8,128)(2,1)S(1)}) fusion(bf16[16,2,144,128]{3,2,1,0:T(8,128)(2,1)} %all-to-all-done.1), kind=kLoop, calls=%fused_computation.29 | loop fusion | bytes 2359296 | tf_op jit(solution)/shard_map/squeeze | solution.py:479
  81.1 1.3 %collective-permute-start.12 = (bf16[16,144,128]{2,1,0:T(8,128)(2,1)S(1)}, bf16[16,144,128]{2,1,0:T(8,128)(2,1)S(1)}, u32[]{:S(2)}, u32[]{:S(2)}) collective-permute-start(bf16[16,144,128]{2,1,0:T(8,128)(2,1)S(1)} %get-tuple-element.31), channel_id=1, source_target_pairs={{0,1},{1,0},{2,3},{3,2},{4,5},{5,4},{6,7},{7,6},{8,9},{9,8},{10,11... | collective-permute-start | bytes 1769480 | tf_op jit(solution)/shard_map/ppermute | solution.py:479
  82.3 0.6 select_convert_fusion.place_ref
  83.0 1.0 collective-permute-done.12.theirs_ref
  84.0 1.4 %shard_map.43.flat = f32[4,3,48,1024]{3,2,1,0:T(8,128)S(1)} custom-call(bf16[16,144,128]{2,1,0:T(8,128)(2,1)S(1)} %get-tuple-element.32.mine_ref, bf16[16,144,128]{2,1,0:T(8,128)(2,1)S(1)} %collective-permute-done.12.theirs_ref, bf16[1024,1024]{1,0:T(8,128)(2,1)S(1)} %select_convert_fusion.place_ref), custom_call_target="tpu_custom_call" | custom-call | bytes 12000000 | tf_op jit(solution)/shard_map/pallas_call | solution.py:360
  85.4 1.3 %shard_map.44 = f32[16,16,512]{2,1,0:T(8,128)S(1)} custom-call(bf16[16,2,32,768]{3,2,1,0:T(8,128)(2,1)S(1)} %all-to-all-done.v_ref, f32[16,512]{1,0:T(8,128)S(1)} %get-tuple-element.29.z_ref, f32[16,896]{1,0:T(8,128)S(1)} %add.71.s0, f32[16,896]{1,0:T(8,128)S(1)} %collective-permute-done.13.s1, f32[16,896]{1,0:T(8,128)S(1)} %collective-permute-done.14.s2, ...), custom_call_target="tpu_custom_call" | custom-call | bytes 9000000 | tf_op jit(solution)/shard_map/pallas_call | solution.py:329
  86.7 16.1 %all_to_all.15.own_ref = f32[16,16,512]{2,1,0:T(8,128)S(1)} all-to-all(f32[16,16,512]{2,1,0:T(8,128)S(1)} %shard_map.44), channel_id=1, replica_groups=mesh['x'=4,'y'=4,'z'=4,'core'=2] {'y','z'}, dimensions={0} | all-to-all | bytes 1048576 | tf_op jit(solution)/shard_map/all_to_all | solution.py:483
  102.7 2.1 %collective-permute-start.16 = (f32[16,16,512]{2,1,0:T(8,128)S(1)}, f32[16,16,512]{2,1,0:T(8,128)S(1)}, u32[]{:S(2)}, u32[]{:S(2)}) collective-permute-start(f32[16,16,512]{2,1,0:T(8,128)S(1)} %all_to_all.15.own_ref), channel_id=1, source_target_pairs={{0,1},{1,0},{2,3},{3,2},{4,5},{5,4},{6,7},{7,6},{8,9},{9,8},{10,11... | collective-permute-start | bytes 1572872 | tf_op jit(solution)/shard_map/ppermute | solution.py:484
  104.8 1.5 %collective-permute-done.16.far_ref = f32[16,16,512]{2,1,0:T(8,128)S(1)} collective-permute-done((f32[16,16,512]{2,1,0:T(8,128)S(1)}, f32[16,16,512]{2,1,0:T(8,128)S(1)}, u32[]{:S(2)}, u32[]{:S(2)}) %collective-permute-start.16) | collective-permute-done | bytes 524320 | tf_op jit(solution)/shard_map/ppermute | solution.py:484
  106.4 9.0 %shard_map.45 = f32[2,3,24,4096]{3,2,1,0:T(8,128)} custom-call(f32[4,3,48,1024]{3,2,1,0:T(8,128)S(1)} %shard_map.43.flat, f32[16,16,512]{2,1,0:T(8,128)S(1)} %all_to_all.15.own_ref, f32[16,16,512]{2,1,0:T(8,128)S(1)} %collective-permute-done.16.far_ref, s32[2]{0:T(128)S(1)} %pad_add_fusion.y_ref.at_ref.core_ref), custom_call_target="tpu_custom_call" | custom-call | bytes 18000000 | tf_op jit(solution)/shard_map/pallas_call | solution.py:435
  (17 shorter events, 0.1 us)
Async XLA Ops:
  11.8 8.7 %copy-start = (bf16[16,2,32,768]{3,2,1,0:T(8,128)(2,1)S(1)}, bf16[16,2,32,768]{3,2,1,0:T(8,128)(2,1)}, u32[]{:S(2)}) copy-start(bf16[16,2,32,768]{3,2,1,0:T(8,128)(2,1)} %shard_map.37.v_ref) | copy-start | bytes 4718596
  11.8 29.2 %all-to-all-start = ((bf16[16,2,32,768]{3,2,1,0:T(8,128)(2,1)}), bf16[16,2,32,768]{3,2,1,0:T(8,128)(2,1)S(1)}, u32[]{:S(2)}, u32[]{:S(2)}) async-start(bf16[16,2,32,768]{3,2,1,0:T(8,128)(2,1)} %shard_map.37.v_ref), calls=%async_computation | async-start | bytes 3145728 | tf_op jit(solution)/shard_map/all_to_all | solution.py:463
  23.3 22.2 %collective-permute-start.9 = (bf16[2,24,32,128]{3,2,1,0:T(8,128)(2,1)}, bf16[2,24,32,128]{3,2,1,0:T(8,128)(2,1)S(1)}, u32[]{:S(2)}, u32[]{:S(2)}) collective-permute-start(bf16[2,24,32,128]{3,2,1,0:T(8,128)(2,1)} %get-tuple-element.23), channel_id=1, source_target_pairs={{0,8},{8,16},{16,24},{24,0},{1,9},{9,17},{17,25},{25,1},{2,10},{10... | collective-permute-start | bytes 1179656 | tf_op jit(solution)/shard_map/ppermute | solution.py:465
  24.6 20.9 %collective-permute-start.10 = (bf16[2,24,32,128]{3,2,1,0:T(8,128)(2,1)}, bf16[2,24,32,128]{3,2,1,0:T(8,128)(2,1)S(1)}, u32[]{:S(2)}, u32[]{:S(2)}) collective-permute-start(bf16[2,24,32,128]{3,2,1,0:T(8,128)(2,1)} %get-tuple-element.24), channel_id=1, source_target_pairs={{0,16},{8,24},{16,0},{24,8},{1,17},{9,25},{17,1},{25,9},{2,18},{10... | collective-permute-start | bytes 1179656 | tf_op jit(solution)/shard_map/ppermute | solution.py:465
  27.2 18.3 %collective-permute-start.11 = (bf16[2,24,32,128]{3,2,1,0:T(8,128)(2,1)}, bf16[2,24,32,128]{3,2,1,0:T(8,128)(2,1)S(1)}, u32[]{:S(2)}, u32[]{:S(2)}) collective-permute-start(bf16[2,24,32,128]{3,2,1,0:T(8,128)(2,1)} %get-tuple-element.25), channel_id=1, source_target_pairs={{0,24},{8,0},{16,8},{24,16},{1,25},{9,1},{17,9},{25,17},{2,26},{10... | collective-permute-start | bytes 1179656 | tf_op jit(solution)/shard_map/ppermute | solution.py:465
  41.3 6.4 %collective-permute-start = (f32[16,768]{1,0:T(8,128)S(1)}, f32[16,768]{1,0:T(8,128)S(1)}, u32[]{:S(2)}, u32[]{:S(2)}) collective-permute-start(f32[16,768]{1,0:T(8,128)S(1)} %shard_map.38), channel_id=1, source_target_pairs={{0,1},{1,0},{2,3},{3,2},{4,5},{5,4},{6,7},{7,6},{8,9},{9,8},{10,11... | collective-permute-start | bytes 147464 | tf_op jit(solution)/shard_map/ppermute | solution.py:456
  47.7 28.7 %all-to-all-start.1 = ((bf16[16,2,144,128]{3,2,1,0:T(8,128)(2,1)}), bf16[16,2,144,128]{3,2,1,0:T(8,128)(2,1)}, u32[]{:S(2)}, u32[]{:S(2)}) async-start(bf16[16,2,144,128]{3,2,1,0:T(8,128)(2,1)} %shard_map.42), calls=%async_computation.1 | async-start | bytes 2359296 | tf_op jit(solution)/shard_map/all_to_all | solution.py:473
  52.8 4.9 %collective-permute-start.1 = (f32[16,768]{1,0:T(8,128)S(1)}, f32[16,768]{1,0:T(8,128)S(1)}, u32[]{:S(2)}, u32[]{:S(2)}) collective-permute-start(f32[16,768]{1,0:T(8,128)S(1)} %add.69.s0), channel_id=1, source_target_pairs={{0,8},{8,16},{16,24},{24,0},{1,9},{9,17},{17,25},{25,1},{2,10},{10... | collective-permute-start | bytes 147464 | tf_op jit(solution)/shard_map/ppermute | solution.py:452
  54.4 5.0 %collective-permute-start.2 = (f32[16,768]{1,0:T(8,128)S(1)}, f32[16,768]{1,0:T(8,128)S(1)}, u32[]{:S(2)}, u32[]{:S(2)}) collective-permute-start(f32[16,768]{1,0:T(8,128)S(1)} %add.69.s0), channel_id=1, source_target_pairs={{0,16},{8,24},{16,0},{24,8},{1,17},{9,25},{17,1},{25,9},{2,18},{10... | collective-permute-start | bytes 147464 | tf_op jit(solution)/shard_map/ppermute | solution.py:452
  57.4 3.5 %collective-permute-start.3 = (f32[16,768]{1,0:T(8,128)S(1)}, f32[16,768]{1,0:T(8,128)S(1)}, u32[]{:S(2)}, u32[]{:S(2)}) collective-permute-start(f32[16,768]{1,0:T(8,128)S(1)} %add.69.s0), channel_id=1, source_target_pairs={{0,24},{8,0},{16,8},{24,16},{1,25},{9,1},{17,9},{25,17},{2,26},{10... | collective-permute-start | bytes 147464 | tf_op jit(solution)/shard_map/ppermute | solution.py:452
  62.0 2.8 %collective-permute-start.4 = (f32[16,896]{1,0:T(8,128)S(1)}, f32[16,896]{1,0:T(8,128)S(1)}, u32[]{:S(2)}, u32[]{:S(2)}) collective-permute-start(f32[16,896]{1,0:T(8,128)S(1)} %get-tuple-element.19), channel_id=1, source_target_pairs={{0,1},{1,0},{2,3},{3,2},{4,5},{5,4},{6,7},{7,6},{8,9},{9,8},{10,11... | collective-permute-start | bytes 172040 | tf_op jit(solution)/shard_map/ppermute | solution.py:456
  64.8 4.7 %collective-permute-start.5 = (f32[16,896]{1,0:T(8,128)S(1)}, f32[16,896]{1,0:T(8,128)S(1)}, u32[]{:S(2)}, u32[]{:S(2)}) collective-permute-start(f32[16,896]{1,0:T(8,128)S(1)} %add.70.s0), channel_id=1, source_target_pairs={{0,8},{8,16},{16,24},{24,0},{1,9},{9,17},{17,25},{25,1},{2,10},{10... | collective-permute-start | bytes 172040 | tf_op jit(solution)/shard_map/ppermute | solution.py:452
  65.6 6.0 %collective-permute-start.6 = (f32[16,896]{1,0:T(8,128)S(1)}, f32[16,896]{1,0:T(8,128)S(1)}, u32[]{:S(2)}, u32[]{:S(2)}) collective-permute-start(f32[16,896]{1,0:T(8,128)S(1)} %add.70.s0), channel_id=1, source_target_pairs={{0,16},{8,24},{16,0},{24,8},{1,17},{9,25},{17,1},{25,9},{2,18},{10... | collective-permute-start | bytes 172040 | tf_op jit(solution)/shard_map/ppermute | solution.py:452
  68.6 3.3 %collective-permute-start.7 = (f32[16,896]{1,0:T(8,128)S(1)}, f32[16,896]{1,0:T(8,128)S(1)}, u32[]{:S(2)}, u32[]{:S(2)}) collective-permute-start(f32[16,896]{1,0:T(8,128)S(1)} %add.70.s0), channel_id=1, source_target_pairs={{0,24},{8,0},{16,8},{24,16},{1,25},{9,1},{17,9},{25,17},{2,26},{10... | collective-permute-start | bytes 172040 | tf_op jit(solution)/shard_map/ppermute | solution.py:452
  73.7 2.7 %collective-permute-start.8 = (f32[16,896]{1,0:T(8,128)S(1)}, f32[16,896]{1,0:T(8,128)S(1)}, u32[]{:S(2)}, u32[]{:S(2)}) collective-permute-start(f32[16,896]{1,0:T(8,128)S(1)} %get-tuple-element.21), channel_id=1, source_target_pairs={{0,1},{1,0},{2,3},{3,2},{4,5},{5,4},{6,7},{7,6},{8,9},{9,8},{10,11... | collective-permute-start | bytes 172040 | tf_op jit(solution)/shard_map/ppermute | solution.py:456
  76.4 9.0 %collective-permute-start.13 = (f32[16,896]{1,0:T(8,128)S(1)}, f32[16,896]{1,0:T(8,128)S(1)}, u32[]{:S(2)}, u32[]{:S(2)}) collective-permute-start(f32[16,896]{1,0:T(8,128)S(1)} %add.71.s0), channel_id=1, source_target_pairs={{0,8},{8,16},{16,24},{24,0},{1,9},{9,17},{17,25},{25,1},{2,10},{10... | collective-permute-start | bytes 172040 | tf_op jit(solution)/shard_map/ppermute | solution.py:452
  76.4 8.9 %collective-permute-start.14 = (f32[16,896]{1,0:T(8,128)S(1)}, f32[16,896]{1,0:T(8,128)S(1)}, u32[]{:S(2)}, u32[]{:S(2)}) collective-permute-start(f32[16,896]{1,0:T(8,128)S(1)} %add.71.s0), channel_id=1, source_target_pairs={{0,16},{8,24},{16,0},{24,8},{1,17},{9,25},{17,1},{25,9},{2,18},{10... | collective-permute-start | bytes 172040 | tf_op jit(solution)/shard_map/ppermute | solution.py:452
  78.6 6.7 %collective-permute-start.15 = (f32[16,896]{1,0:T(8,128)S(1)}, f32[16,896]{1,0:T(8,128)S(1)}, u32[]{:S(2)}, u32[]{:S(2)}) collective-permute-start(f32[16,896]{1,0:T(8,128)S(1)} %add.71.s0), channel_id=1, source_target_pairs={{0,24},{8,0},{16,8},{24,16},{1,25},{9,1},{17,9},{25,17},{2,26},{10... | collective-permute-start | bytes 172040 | tf_op jit(solution)/shard_map/ppermute | solution.py:452
  81.1 2.9 %collective-permute-start.12 = (bf16[16,144,128]{2,1,0:T(8,128)(2,1)S(1)}, bf16[16,144,128]{2,1,0:T(8,128)(2,1)S(1)}, u32[]{:S(2)}, u32[]{:S(2)}) collective-permute-start(bf16[16,144,128]{2,1,0:T(8,128)(2,1)S(1)} %get-tuple-element.31), channel_id=1, source_target_pairs={{0,1},{1,0},{2,3},{3,2},{4,5},{5,4},{6,7},{7,6},{8,9},{9,8},{10,11... | collective-permute-start | bytes 1769480 | tf_op jit(solution)/shard_map/ppermute | solution.py:479
  102.7 3.6 %collective-permute-start.16 = (f32[16,16,512]{2,1,0:T(8,128)S(1)}, f32[16,16,512]{2,1,0:T(8,128)S(1)}, u32[]{:S(2)}, u32[]{:S(2)}) collective-permute-start(f32[16,16,512]{2,1,0:T(8,128)S(1)} %all_to_all.15.own_ref), channel_id=1, source_target_pairs={{0,1},{1,0},{2,3},{3,2},{4,5},{5,4},{6,7},{7,6},{8,9},{9,8},{10,11... | collective-permute-start | bytes 1572872 | tf_op jit(solution)/shard_map/ppermute | solution.py:484

commit v5 on v4

--- a/solution.py
+++ b/solution.py
@@ -34,7 +34,7 @@
 
 
 def cost(microseconds):
-    return pl.CostEstimate(flops=0, bytes_accessed=int(microseconds * 3e6), transcendentals=0)
+    return pl.CostEstimate(flops=int(microseconds * 9e8), bytes_accessed=int(microseconds * 3e6), transcendentals=0)
 
 
 in_vmem = pl.BlockSpec(memory_space=pltpu.VMEM)
@@ -67,7 +67,7 @@
     return x[:n] + (x[n : 2 * n] + x[2 * n :])
 
 
-STEP_ROWS = 8
+STEP_ROWS = 16
 CHUNKS = 4
 
 
@@ -118,10 +118,11 @@
             start = pl.multiple_of((at * STEP_ROWS + k) * (PHASES * P_SIZE), 128)
             rows.append(x_ref[:, pl.ds(start, SPAN)])
         got = dot_nn(jnp.concatenate(rows, axis=0), table[...])
-        got = got.reshape(NC, STEP_ROWS // NC, LOCAL, 256)
-        y, z = at // NZ, at % NZ
-        for core in range(NC):
-            wide[pl.ds((y * NC + core) * 16 + z * 4, STEP_ROWS // NC)] = got[core]
+        got = got.reshape(STEP_ROWS // 4, 4, LOCAL, 256)
+        for k in range(STEP_ROWS // 4):
+            owner = at * (STEP_ROWS // 4) + k
+            y, z, core = owner // (NZ * NC), owner // NC % NZ, owner % NC
+            wide[pl.ds((y * NC + core) * 16 + z * 4, 4)] = got[k]
         return carry
 
     for k in range(CHUNKS):
@@ -254,17 +255,16 @@
 
 
 def eliminate(gram, others):
-    row_id = lax.broadcasted_iota(jnp.int32, (KDIM, 1), 0)
-    gram_re, gram_im = gram
-    pairs = [(gram_re, gram_im)] + list(others)
+    row_id = lax.broadcasted_iota(jnp.int32, gram[0].shape[:-1] + (1,), gram[0].ndim - 2)
+    pairs = [gram] + list(others)
     for j in range(KDIM):
         gram_re, gram_im = pairs[0]
-        scale = 1.0 / jnp.sqrt(gram_re[j : j + 1, j : j + 1])
+        scale = 1.0 / jnp.sqrt(gram_re[..., j : j + 1, j : j + 1])
         below = jnp.where(row_id > j, scale, 0.0)
-        m_re, m_im = gram_re[:, j : j + 1] * below, gram_im[:, j : j + 1] * below
+        m_re, m_im = gram_re[..., j : j + 1] * below, gram_im[..., j : j + 1] * below
         done = []
         for re, im in pairs:
-            top_re, top_im = re[j : j + 1] * scale, im[j : j + 1] * scale
+            top_re, top_im = re[..., j : j + 1, :] * scale, im[..., j : j + 1, :] * scale
             new_re = re - (m_re * top_re - m_im * top_im)
             new_im = im - (m_re * top_im + m_im * top_re)
             here = row_id == j
@@ -332,7 +332,7 @@
         in_specs=[in_vmem] * 6,
         out_specs=[in_vmem] * len(shapes),
         compiler_params=params(12),
-        cost_estimate=cost(3),
+        cost_estimate=cost(5),
     )(v, z, *sums)
 
 
@@ -367,78 +367,98 @@
     )(mine, theirs, place)
 
 
-def final_kernel(flat, own_ref, far_ref, core_ref, o_ref, basis):
-    z = pl.program_id(0)
+def final_kernel(flat, own_ref, far_ref, core_ref, o_hbm, basis, result, sems):
     lane = lax.broadcasted_iota(jnp.int32, (2 * KDIM, 128), 1) // 32
     is_zero = core_ref[1] == 0
-    for x in range(NX):
-        lanes = slice(x * 128, (x + 1) * 128)
-        for y in range(NY):
-            own, far = own_ref[y * NZ + z, :, lanes], far_ref[y * NZ + z, :, lanes]
-            a, b = jnp.where(is_zero, own, far), jnp.where(is_zero, far, own)
-            left = jnp.where(
-                lane < 2,
-                jnp.where(lane == 0, a, pltpu.roll(b, 32, 1)),
-                jnp.where(lane == 2, pltpu.roll(a, 32, 1), pltpu.roll(b, 64, 1)),
-            )
-            right = jnp.where(
-                lane < 2,
-                jnp.where(lane == 0, pltpu.roll(a, 64, 1), pltpu.roll(b, 96, 1)),
-                jnp.where(lane == 2, pltpu.roll(a, 96, 1), b),
-            )
-            at = (x * NY + y) * 256
-            for k, part in enumerate((left, right)):
-                basis[:, at + k * 128 : at + (k + 1) * 128] = split3(part)
+    wide = NY * 256
+    solved = []
+    for z in range(GROUP):
+        products = jnp.zeros((48, 128), F32)
+        for x in range(NX):
+            lanes = slice(x * 128, (x + 1) * 128)
+            for y in range(NY):
+                own, far = own_ref[y * NZ + z, :, lanes], far_ref[y * NZ + z, :, lanes]
+                a, b = jnp.where(is_zero, own, far), jnp.where(is_zero, far, own)
+                left = jnp.where(
+                    lane < 2,
+                    jnp.where(lane == 0, a, pltpu.roll(b, 32, 1)),
+                    jnp.where(lane == 2, pltpu.roll(a, 32, 1), pltpu.roll(b, 64, 1)),
+                )
+                right = jnp.where(
+                    lane < 2,
+                    jnp.where(lane == 0, pltpu.roll(a, 64, 1), pltpu.roll(b, 96, 1)),
+                    jnp.where(lane == 2, pltpu.roll(a, 96, 1), b),
+                )
+                at = (x * NY + y) * 256
+                for k, part in enumerate((left, right)):
+                    basis[z, :, at + k * 128 : at + (k + 1) * 128] = split3(part)
+            pieces = basis[z, :, x * wide : (x + 1) * wide]
+            block = flat[x, z].astype(BF16)
+            right = jnp.concatenate([pieces, block, jnp.zeros((32, wide), BF16)], axis=0)
+            products = products + dot_nt(pieces, right)
+        g_re, g_im = gram_from(products)
+        up_down = sum3(products)
+        up, down = up_down[0:KDIM], up_down[KDIM:]
+        u_re = up + pltpu.roll(down, 104, 1)
+        u_im = down - pltpu.roll(up, 104, 1)
+        solved.append((g_re, g_im, u_re, u_im))
 
     lane = lax.broadcasted_iota(jnp.int32, (KDIM, 128), 1)
     unit = lane == lax.broadcasted_iota(jnp.int32, (KDIM, 128), 0) + KDIM
     unit_lanes = (lane >= KDIM) & (lane < 2 * KDIM)
     u_lanes = (lane >= 48) & (lane < 72)
-    wide = NY * 256
-    products = jnp.zeros((48, 128), F32)
-    for x in range(NX):
-        pieces = basis[:, x * wide : (x + 1) * wide]
-        block = flat[x, z].astype(BF16)
-        right = jnp.concatenate([pieces, block, jnp.zeros((32, wide), BF16)], axis=0)
-        products = products + dot_nt(pieces, right)
-    g_re, g_im = gram_from(products)
-    up_down = sum3(products)
-    up, down = up_down[0:KDIM], up_down[KDIM:]
-    u_re = up + pltpu.roll(down, 104, 1)
-    u_im = down - pltpu.roll(up, 104, 1)
-    x_re = jnp.where(u_lanes, u_re, jnp.where(unit_lanes, jnp.where(unit, 1.0, 0.0), g_re))
-    x_im = jnp.where(u_lanes, u_im, jnp.where(unit_lanes, 0.0, g_im))
     used = lane < 72
-    x_re, x_im = jnp.where(used, x_re, 0.0), jnp.where(used, x_im, 0.0)
-    ((x_re, x_im),) = eliminate((x_re, x_im), [])
-    both = jnp.concatenate([x_re, x_im], axis=0)
-    cross = jnp.concatenate([x_im, -x_re], axis=0)
-    t_re = dot_tn(both, both, lax.Precision.HIGHEST)[KDIM : 2 * KDIM]
-    t_im = dot_tn(cross, both, lax.Precision.HIGHEST)[KDIM : 2 * KDIM]
+    all_re, all_im = [], []
+    for g_re, g_im, u_re, u_im in solved:
+        x_re = jnp.where(u_lanes, u_re, jnp.where(unit_lanes, jnp.where(unit, 1.0, 0.0), g_re))
+        x_im = jnp.where(u_lanes, u_im, jnp.where(unit_lanes, 0.0, g_im))
+        all_re.append(jnp.where(used, x_re, 0.0))
+        all_im.append(jnp.where(used, x_im, 0.0))
+    ((all_re, all_im),) = eliminate((jnp.stack(all_re), jnp.stack(all_im)), [])
 
     def sides(a, b):
         near, away = pltpu.roll(a, 80, 1), pltpu.roll(b, 104, 1)
         return jnp.where(lane < SHARE, near, jnp.where(lane < 2 * SHARE, away, 0.0))
 
-    t = split3(jnp.concatenate([sides(t_re, t_im), sides(-t_im, t_re)], axis=0))
-    hi, mid, lo = t[0:16], t[16:32], t[32:48]
-    left = jnp.concatenate([hi, hi, hi, mid, mid, lo], axis=0)
-    for x in range(NX):
-        pieces = basis[:, x * wide : (x + 1) * wide]
-        right = jnp.concatenate([pieces, pieces[0:32], pieces[0:16]], axis=0)
-        rest = flat[x, z] - dot_tn(left, right)[0 : 2 * SHARE]
-        o_ref[0, 0, :, x * wide : (x + 1) * wide] = rest[0:SHARE]
-        o_ref[1, 0, :, x * wide : (x + 1) * wide] = rest[SHARE:]
+    lefts = []
+    for z in range(GROUP):
+        x_re, x_im = all_re[z], all_im[z]
+        both = jnp.concatenate([x_re, x_im], axis=0)
+        cross = jnp.concatenate([x_im, -x_re], axis=0)
+        t_re = dot_tn(both, both, lax.Precision.HIGHEST)[KDIM : 2 * KDIM]
+        t_im = dot_tn(cross, both, lax.Precision.HIGHEST)[KDIM : 2 * KDIM]
+        t = split3(jnp.concatenate([sides(t_re, t_im), sides(-t_im, t_re)], axis=0))
+        hi, mid, lo = t[0:16], t[16:32], t[32:48]
+        lefts.append(jnp.concatenate([hi, hi, hi, mid, mid, lo], axis=0))
+    copies = []
+    for z in range(GROUP):
+        for x in range(NX):
+            lanes = slice(x * wide, (x + 1) * wide)
+            pieces = basis[z, :, lanes]
+            right = jnp.concatenate([pieces, pieces[0:32], pieces[0:16]], axis=0)
+            rest = flat[x, z] - dot_tn(lefts[z], right)[0 : 2 * SHARE]
+            result[0, z, :, lanes] = rest[0:SHARE]
+            result[1, z, :, lanes] = rest[SHARE:]
+        for r in range(2):
+            copies.append(
+                pltpu.make_async_copy(result.at[r, z], o_hbm.at[r, z], sems.at[r, z])
+            )
+            copies[-1].start()
+    for copy in copies:
+        copy.wait()
 
 
 def finish(flat, own, far, at):
     return pl.pallas_call(
         final_kernel,
-        grid=(GROUP,),
         out_shape=jax.ShapeDtypeStruct((2, GROUP, SHARE, INPUTS), F32),
         in_specs=[in_vmem] * 3 + [pl.BlockSpec(memory_space=pltpu.SMEM)],
-        out_specs=pl.BlockSpec((2, 1, SHARE, INPUTS), lambda z: (0, z, 0, 0)),
-        scratch_shapes=[pltpu.VMEM((6 * KDIM, INPUTS), BF16)],
+        out_specs=pl.BlockSpec(memory_space=pltpu.HBM),
+        scratch_shapes=[
+            pltpu.VMEM((GROUP, 6 * KDIM, INPUTS), BF16),
+            pltpu.VMEM((2, GROUP, SHARE, INPUTS), F32),
+            pltpu.SemaphoreType.DMA((2, GROUP)),
+        ],
         compiler_params=params(16),
         cost_estimate=cost(6),
     )(flat, own, far, at)

time: 116 us -> 108 us (0.931)
  Pallas kernels: 31.5 us -> 26.3 us
  blocking collectives: 16.1 us -> 14.5 us
    pallas_call x1, Pallas kernels: 8.95 us -> 4.93 us  [finish(): pl.pallas_call(final_kernel, out_shape=jax.ShapeDtypeStruct((2, GROUP, SH...]
    all_to_all x1, waiting for transfers between devices: 0.01 us -> 3.18 us  [body(): blocks = lax.all_to_all(turned, ('x', 'z'), 0, 0, tiled=True)]
    ppermute x9, waiting for transfers between devices: 6.86 us -> 4.66 us  [sums_over(): return [s] + [lax.ppermute(s, 'y', turned_by(NY, d)) for d in range(1, NY)]]
    unnamed x2 -> x8, local copies, waits for them, and re-layouts: 0.01 us -> 2.19 us
    ppermute x1, starting transfers between devices: 1.28 us -> 3.45 us  [body(): lax.ppermute(blocks[:, 1], 'core', turned_by(NC, 1))]
    all_to_all x1, blocking collectives: 16.1 us -> 14.5 us  [body(): own = lax.all_to_all(many, ('y', 'z'), 0, 0, tiled=True)]
    all_to_all x1, starting transfers between devices: 5.11 us -> 3.7 us  [body(): blocks = lax.all_to_all(turned, ('x', 'z'), 0, 0, tiled=True)]
    pallas_call x1, Pallas kernels: 11.8 us -> 10.4 us  [channelize(): pl.pallas_call(channelize_kernel, out_shape=jax.ShapeDtypeStruct((NX * NZ...]
  transfers between devices with their start and end apart: 19 -> 19, of which waited for: 11 -> 11; matrix products, arithmetic and copies ran while one was open for 5% -> 4% of each run, Pallas kernels for 8% -> 9%
where the time goes in v5:
time: 108 us
  starting transfers between devices  40.9 us (38%)
  Pallas kernels  26.3 us (24%)
  waiting for transfers between devices  19.7 us (18%)
  blocking collectives  14.5 us (13%)
  local copies, waits for them, and re-layouts  5.39 us (5%)
    all_to_all x1, blocking collectives, body(): own = lax.all_to_all(many, ('y', 'z'), 0, 0, tiled=True)  14.5 us
    ppermute x9, starting transfers between devices, sums_over(): return [s] + [lax.ppermute(s, 'y', turned_by(NY, d)) for d in range(1, NY)]  11 us
    pallas_call x1, Pallas kernels, channelize(): pl.pallas_call(channelize_kernel, out_shape=jax.ShapeDtypeStruct((NX * NZ...  10.4 us
    all_to_all x1, starting transfers between devices, body(): v = lax.all_to_all(parcels, ('x', 'z'), 0, 0, tiled=True)  8.44 us
    all_to_all x1, waiting for transfers between devices, body(): v = lax.all_to_all(parcels, ('x', 'z'), 0, 0, tiled=True)  7.65 us
    ppermute x3, starting transfers between devices, core_sum(): return s + lax.ppermute(s, 'core', turned_by(NC, 1))  7.14 us
    ppermute x3, starting transfers between devices, body(): lax.ppermute(parts[d], 'y', turned_by(NY, d))  4.99 us
    pallas_call x1, Pallas kernels, finish(): pl.pallas_call(final_kernel, out_shape=jax.ShapeDtypeStruct((2, GROUP, SH...  4.93 us
  transfers between devices with their start and end apart: 19, of which 11 were waited for; matrix products, arithmetic and copies ran while one was open for 4% of the time, Pallas kernels for 9%

profile of v5, /device:TPU:1, one launch (start us, length us, event | category | flops | bytes accessed | tf_op | source)
XLA Modules:
  0.0 107.8 jit_solution(16913908842013238558)
XLA Ops:
  0.0 10.4 %shard_map.37.v_ref = bf16[16,2,32,768]{3,2,1,0:T(8,128)(2,1)} custom-call(s32[12]{0:T(128)} %ids_ref.1, bf16[32,98688]{1,0:T(8,128)(2,1)} %x_hbm.1), custom_call_target="tpu_custom_call" | custom-call | flops 7200000000 | bytes 24000000 | tf_op jit(solution)/shard_map/pallas_call | solution.py:150
  10.4 8.4 %all-to-all-start = ((bf16[16,2,32,768]{3,2,1,0:T(8,128)(2,1)}), bf16[16,2,32,768]{3,2,1,0:T(8,128)(2,1)S(1)}, u32[]{:S(2)}, u32[]{:S(2)}) async-start(bf16[16,2,32,768]{3,2,1,0:T(8,128)(2,1)} %shard_map.37.v_ref), calls=%async_computation | async-start | bytes 3145728 | tf_op jit(solution)/shard_map/all_to_all | solution.py:483
  18.9 0.1 pad_add_fusion.y_ref.at_ref.core_ref
  18.9 1.4 %copy-done = bf16[16,2,32,768]{3,2,1,0:T(8,128)(2,1)S(1)} copy-done((bf16[16,2,32,768]{3,2,1,0:T(8,128)(2,1)S(1)}, bf16[16,2,32,768]{3,2,1,0:T(8,128)(2,1)}, u32[]{:S(2)}) %copy-start) | copy-done | bytes 1572888
  20.3 2.6 %shard_map.41 = (bf16[2,24,32,128]{3,2,1,0:T(8,128)(2,1)S(1)}, bf16[2,24,32,128]{3,2,1,0:T(8,128)(2,1)}, bf16[2,24,32,128]{3,2,1,0:T(8,128)(2,1)S(1)}, bf16[2,24,32,128]{3,2,1,0:T(8,128)(2,1)S(1)}) custom-call(s32[2]{0:T(128)S(1)} %pad_add_fusion.y_ref.at_ref.core_ref, bf16[16,2,32,768]{3,2,1,0:T(8,128)(2,1)S(1)} %copy-done), custom_call_target="tpu_custom_call" | custom-call | flops 3600000000 | bytes 12000000 | tf_op jit(solution)/shard_map/pallas_call | solution.py:189
  22.9 0.8 copy-done.1
  23.7 1.3 %collective-permute-start.9 = (bf16[2,24,32,128]{3,2,1,0:T(8,128)(2,1)}, bf16[2,24,32,128]{3,2,1,0:T(8,128)(2,1)S(1)}, u32[]{:S(2)}, u32[]{:S(2)}) collective-permute-start(bf16[2,24,32,128]{3,2,1,0:T(8,128)(2,1)} %get-tuple-element.23), channel_id=1, source_target_pairs={{0,8},{8,16},{16,24},{24,0},{1,9},{9,17},{17,25},{25,1},{2,10},{10... | collective-permute-start | bytes 1179656 | tf_op jit(solution)/shard_map/ppermute | solution.py:485
  25.0 2.6 %collective-permute-start.10 = (bf16[2,24,32,128]{3,2,1,0:T(8,128)(2,1)S(1)}, bf16[2,24,32,128]{3,2,1,0:T(8,128)(2,1)S(1)}, u32[]{:S(2)}, u32[]{:S(2)}) collective-permute-start(bf16[2,24,32,128]{3,2,1,0:T(8,128)(2,1)S(1)} %get-tuple-element.24), channel_id=1, source_target_pairs={{0,16},{8,24},{16,0},{24,8},{1,17},{9,25},{17,1},{25,9},{2,18},{10... | collective-permute-start | bytes 1179656 | tf_op jit(solution)/shard_map/ppermute | solution.py:485
  27.6 1.1 collective-permute-start.11
  28.7 1.9 %reshape.9 = f32[16,4,4,4,2,32]{5,4,3,2,1,0:T(2,128)} reshape(f32[2,8,4096]{2,1,0:T(8,128)S(1)} %copy-done.3) | data formatting | bytes 524288 | tf_op jit(solution)/shard_map/reshape | solution.py:487
  30.6 1.1 %constant_dynamic-slice_fusion = f32[16,4,1,4,1,32]{5,4,3,2,1,0:T(1,128)S(1)} fusion(f32[16,4,4,4,2,32]{5,4,3,2,1,0:T(2,128)} %reshape.9, s32[]{:T(128)S(6)} %select_n.51, s32[]{:T(128)S(6)} %select_n.53), kind=kLoop, calls=%fused_computation.52 | loop fusion | bytes 65544 | tf_op jit(solution)/shard_map/jit(dynamic_index_in_dim)/dynamic_slice | solution.py:489
  31.7 0.1 reshape.10.q_ref.z_ref
  31.8 7.7 %all-to-all-done.v_ref = bf16[16,2,32,768]{3,2,1,0:T(8,128)(2,1)S(1)} async-done(((bf16[16,2,32,768]{3,2,1,0:T(8,128)(2,1)}), bf16[16,2,32,768]{3,2,1,0:T(8,128)(2,1)S(1)}, u32[]{:S(2)}, u32[]{:S(2)}) %all-to-all-start) | async-done | bytes 1572896 | tf_op jit(solution)/shard_map/all_to_all | solution.py:483
  39.5 0.3 shard_map.38
  39.8 4.1 %collective-permute-start = (f32[16,768]{1,0:T(8,128)S(1)}, f32[16,768]{1,0:T(8,128)S(1)}, u32[]{:S(2)}, u32[]{:S(2)}) collective-permute-start(f32[16,768]{1,0:T(8,128)S(1)} %shard_map.38), channel_id=1, source_target_pairs={{0,1},{1,0},{2,3},{3,2},{4,5},{5,4},{6,7},{7,6},{8,9},{9,8},{10,11... | collective-permute-start | bytes 147464 | tf_op jit(solution)/shard_map/ppermute | solution.py:476
  44.0 0.9 collective-permute-done
  44.8 1.3 %collective-permute-start.1 = (f32[16,768]{1,0:T(8,128)S(1)}, f32[16,768]{1,0:T(8,128)S(1)}, u32[]{:S(2)}, u32[]{:S(2)}) collective-permute-start(f32[16,768]{1,0:T(8,128)S(1)} %add.69.s0), channel_id=1, source_target_pairs={{0,8},{8,16},{16,24},{24,0},{1,9},{9,17},{17,25},{25,1},{2,10},{10... | collective-permute-start | bytes 147464 | tf_op jit(solution)/shard_map/ppermute | solution.py:472
  46.1 2.6 %collective-permute-start.2 = (f32[16,768]{1,0:T(8,128)S(1)}, f32[16,768]{1,0:T(8,128)S(1)}, u32[]{:S(2)}, u32[]{:S(2)}) collective-permute-start(f32[16,768]{1,0:T(8,128)S(1)} %add.69.s0), channel_id=1, source_target_pairs={{0,16},{8,24},{16,0},{24,8},{1,17},{9,25},{17,1},{25,9},{2,18},{10... | collective-permute-start | bytes 147464 | tf_op jit(solution)/shard_map/ppermute | solution.py:472
  48.8 1.1 collective-permute-start.3
  49.9 2.7 %shard_map.42 = bf16[16,2,144,128]{3,2,1,0:T(8,128)(2,1)} custom-call(s32[2]{0:T(128)S(1)} %pad_add_fusion.y_ref.at_ref.core_ref, bf16[2,24,32,128]{3,2,1,0:T(8,128)(2,1)S(1)} %copy-done.2, bf16[2,24,32,128]{3,2,1,0:T(8,128)(2,1)S(1)} %collective-permute-done.9.refs_1_, bf16[2,24,32,128]{3,2,1,0:T(8,128)(2,1)S(1)} %collective-permute-done.10.refs_2_, ...), custom_call_target="tpu_custom_call" | custom-call | flops 2700000000 | bytes 9000000 | tf_op jit(solution)/shard_map/pallas_call | solution.py:226
  52.5 3.7 %all-to-all-start.1 = ((bf16[16,2,144,128]{3,2,1,0:T(8,128)(2,1)}), bf16[16,2,144,128]{3,2,1,0:T(8,128)(2,1)S(1)}, u32[]{:S(2)}, u32[]{:S(2)}) async-start(bf16[16,2,144,128]{3,2,1,0:T(8,128)(2,1)} %shard_map.42), calls=%async_computation.1 | async-start | bytes 2359296 | tf_op jit(solution)/shard_map/all_to_all | solution.py:493
  56.3 1.1 shard_map.39
  57.3 1.4 %collective-permute-start.4 = (f32[16,896]{1,0:T(8,128)S(1)}, f32[16,896]{1,0:T(8,128)S(1)}, u32[]{:S(2)}, u32[]{:S(2)}) collective-permute-start(f32[16,896]{1,0:T(8,128)S(1)} %get-tuple-element.19), channel_id=1, source_target_pairs={{0,1},{1,0},{2,3},{3,2},{4,5},{5,4},{6,7},{7,6},{8,9},{9,8},{10,11... | collective-permute-start | bytes 172040 | tf_op jit(solution)/shard_map/ppermute | solution.py:476
  58.8 0.9 collective-permute-done.4
  59.7 0.4 collective-permute-start.5
  60.1 0.7 collective-permute-start.6
  60.8 1.9 %collective-permute-start.7 = (f32[16,896]{1,0:T(8,128)S(1)}, f32[16,896]{1,0:T(8,128)S(1)}, u32[]{:S(2)}, u32[]{:S(2)}) collective-permute-start(f32[16,896]{1,0:T(8,128)S(1)} %add.70.s0), channel_id=1, source_target_pairs={{0,24},{8,0},{16,8},{24,16},{1,25},{9,1},{17,9},{25,17},{2,26},{10... | collective-permute-start | bytes 172040 | tf_op jit(solution)/shard_map/ppermute | solution.py:472
  62.8 1.5 %collective-permute-done.5.s1 = f32[16,896]{1,0:T(8,128)S(1)} collective-permute-done((f32[16,896]{1,0:T(8,128)S(1)}, f32[16,896]{1,0:T(8,128)S(1)}, u32[]{:S(2)}, u32[]{:S(2)}) %collective-permute-start.5) | collective-permute-done | bytes 57376 | tf_op jit(solution)/shard_map/ppermute | solution.py:472
  64.2 0.7 collective-permute-done.6.s2
  64.9 0.6 collective-permute-done.7.s3
  65.5 1.7 %shard_map.40 = (f32[16,512]{1,0:T(8,128)S(1)}, f32[16,896]{1,0:T(8,128)S(1)}) custom-call(bf16[16,2,32,768]{3,2,1,0:T(8,128)(2,1)S(1)} %all-to-all-done.v_ref, f32[16,512]{1,0:T(8,128)S(1)} %get-tuple-element.18.z_ref, f32[16,896]{1,0:T(8,128)S(1)} %add.70.s0, f32[16,896]{1,0:T(8,128)S(1)} %collective-permute-done.5.s1, ...), custom_call_target="tpu_custom_call" | custom-call | flops 4499999744 | bytes 15000000 | tf_op jit(solution)/shard_map/pallas_call | solution.py:329
  67.2 1.6 %collective-permute-start.8 = (f32[16,896]{1,0:T(8,128)S(1)}, f32[16,896]{1,0:T(8,128)S(1)}, u32[]{:S(2)}, u32[]{:S(2)}) collective-permute-start(f32[16,896]{1,0:T(8,128)S(1)} %get-tuple-element.21), channel_id=1, source_target_pairs={{0,1},{1,0},{2,3},{3,2},{4,5},{5,4},{6,7},{7,6},{8,9},{9,8},{10,11... | collective-permute-start | bytes 172040 | tf_op jit(solution)/shard_map/ppermute | solution.py:476
  68.8 0.9 collective-permute-done.8
  69.7 3.2 %all-to-all-done.1 = bf16[16,2,144,128]{3,2,1,0:T(8,128)(2,1)S(1)} async-done(((bf16[16,2,144,128]{3,2,1,0:T(8,128)(2,1)}), bf16[16,2,144,128]{3,2,1,0:T(8,128)(2,1)S(1)}, u32[]{:S(2)}, u32[]{:S(2)}) %all-to-all-start.1) | async-done | bytes 1179680 | tf_op jit(solution)/shard_map/all_to_all | solution.py:493
  72.8 0.1 slice_bitcast_fusion
  72.9 3.5 %collective-permute-start.12 = (bf16[16,144,128]{2,1,0:T(8,128)(2,1)S(1)}, bf16[16,144,128]{2,1,0:T(8,128)(2,1)S(1)}, u32[]{:S(2)}, u32[]{:S(2)}) collective-permute-start(bf16[16,144,128]{2,1,0:T(8,128)(2,1)S(1)} %get-tuple-element.31), channel_id=1, source_target_pairs={{0,1},{1,0},{2,3},{3,2},{4,5},{5,4},{6,7},{7,6},{8,9},{9,8},{10,11... | collective-permute-start | bytes 1769480 | tf_op jit(solution)/shard_map/ppermute | solution.py:499
  76.4 0.6 select_convert_fusion.place_ref
  77.0 0.5 collective-permute-start.13
  77.5 1.7 %collective-permute-start.14 = (f32[16,896]{1,0:T(8,128)S(1)}, f32[16,896]{1,0:T(8,128)S(1)}, u32[]{:S(2)}, u32[]{:S(2)}) collective-permute-start(f32[16,896]{1,0:T(8,128)S(1)} %add.71.s0), channel_id=1, source_target_pairs={{0,16},{8,24},{16,0},{24,8},{1,17},{9,25},{17,1},{25,9},{2,18},{10... | collective-permute-start | bytes 172040 | tf_op jit(solution)/shard_map/ppermute | solution.py:472
  79.1 0.8 collective-permute-start.15
  80.0 1.4 %shard_map.43.flat = f32[4,3,48,1024]{3,2,1,0:T(8,128)S(1)} custom-call(bf16[16,144,128]{2,1,0:T(8,128)(2,1)S(1)} %get-tuple-element.32.mine_ref, bf16[16,144,128]{2,1,0:T(8,128)(2,1)S(1)} %collective-permute-done.12.theirs_ref, bf16[1024,1024]{1,0:T(8,128)(2,1)S(1)} %select_convert_fusion.place_ref), custom_call_target="tpu_custom_call" | custom-call | flops 3600000000 | bytes 12000000 | tf_op jit(solution)/shard_map/pallas_call | solution.py:360
  81.4 1.1 collective-permute-done.13.s1
  82.4 0.9 collective-permute-done.15.s3
  83.3 1.3 %shard_map.44 = f32[16,16,512]{2,1,0:T(8,128)S(1)} custom-call(bf16[16,2,32,768]{3,2,1,0:T(8,128)(2,1)S(1)} %all-to-all-done.v_ref, f32[16,512]{1,0:T(8,128)S(1)} %get-tuple-element.29.z_ref, f32[16,896]{1,0:T(8,128)S(1)} %add.71.s0, f32[16,896]{1,0:T(8,128)S(1)} %collective-permute-done.13.s1, f32[16,896]{1,0:T(8,128)S(1)} %collective-permute-done.14.s2, ...), custom_call_target="tpu_custom_call" | custom-call | flops 4499999744 | bytes 15000000 | tf_op jit(solution)/shard_map/pallas_call | solution.py:329
  84.6 14.5 %all_to_all.15.own_ref = f32[16,16,512]{2,1,0:T(8,128)S(1)} all-to-all(f32[16,16,512]{2,1,0:T(8,128)S(1)} %shard_map.44), channel_id=1, replica_groups=mesh['x'=4,'y'=4,'z'=4,'core'=2] {'y','z'}, dimensions={0} | all-to-all | bytes 1048576 | tf_op jit(solution)/shard_map/all_to_all | solution.py:503
  99.0 2.1 %collective-permute-start.16 = (f32[16,16,512]{2,1,0:T(8,128)S(1)}, f32[16,16,512]{2,1,0:T(8,128)S(1)}, u32[]{:S(2)}, u32[]{:S(2)}) collective-permute-start(f32[16,16,512]{2,1,0:T(8,128)S(1)} %all_to_all.15.own_ref), channel_id=1, source_target_pairs={{0,1},{1,0},{2,3},{3,2},{4,5},{5,4},{6,7},{7,6},{8,9},{9,8},{10,11... | collective-permute-start | bytes 1572872 | tf_op jit(solution)/shard_map/ppermute | solution.py:504
  101.2 1.5 %collective-permute-done.16.far_ref = f32[16,16,512]{2,1,0:T(8,128)S(1)} collective-permute-done((f32[16,16,512]{2,1,0:T(8,128)S(1)}, f32[16,16,512]{2,1,0:T(8,128)S(1)}, u32[]{:S(2)}, u32[]{:S(2)}) %collective-permute-start.16) | collective-permute-done | bytes 524320 | tf_op jit(solution)/shard_map/ppermute | solution.py:504
  102.7 4.9 %shard_map.45 = f32[2,3,24,4096]{3,2,1,0:T(8,128)} custom-call(f32[4,3,48,1024]{3,2,1,0:T(8,128)S(1)} %shard_map.43.flat, f32[16,16,512]{2,1,0:T(8,128)S(1)} %all_to_all.15.own_ref, f32[16,16,512]{2,1,0:T(8,128)S(1)} %collective-permute-done.16.far_ref, s32[2]{0:T(128)S(1)} %pad_add_fusion.y_ref.at_ref.core_ref), custom_call_target="tpu_custom_call" | custom-call | flops 5400000000 | bytes 18000000 | tf_op jit(solution)/shard_map/pallas_call | solution.py:452
  (23 shorter events, 0.1 us)
Async XLA Ops:
  10.4 29.1 %all-to-all-start = ((bf16[16,2,32,768]{3,2,1,0:T(8,128)(2,1)}), bf16[16,2,32,768]{3,2,1,0:T(8,128)(2,1)S(1)}, u32[]{:S(2)}, u32[]{:S(2)}) async-start(bf16[16,2,32,768]{3,2,1,0:T(8,128)(2,1)} %shard_map.37.v_ref), calls=%async_computation | async-start | bytes 3145728 | tf_op jit(solution)/shard_map/all_to_all | solution.py:483
  18.9 1.4 %copy-start = (bf16[16,2,32,768]{3,2,1,0:T(8,128)(2,1)S(1)}, bf16[16,2,32,768]{3,2,1,0:T(8,128)(2,1)}, u32[]{:S(2)}) copy-start(bf16[16,2,32,768]{3,2,1,0:T(8,128)(2,1)} %shard_map.37.v_ref) | copy-start | bytes 4718596
  20.3 8.3 %copy-start.3 = (f32[2,8,4096]{2,1,0:T(8,128)S(1)}, f32[2,8,4096]{2,1,0:T(8,128)}, u32[]{:S(2)}) copy-start(f32[2,8,4096]{2,1,0:T(8,128)} %param.5) | copy-start | bytes 786436
  22.9 0.8 copy-start.1
  23.7 25.1 %collective-permute-start.9 = (bf16[2,24,32,128]{3,2,1,0:T(8,128)(2,1)}, bf16[2,24,32,128]{3,2,1,0:T(8,128)(2,1)S(1)}, u32[]{:S(2)}, u32[]{:S(2)}) collective-permute-start(bf16[2,24,32,128]{3,2,1,0:T(8,128)(2,1)} %get-tuple-element.23), channel_id=1, source_target_pairs={{0,8},{8,16},{16,24},{24,0},{1,9},{9,17},{17,25},{25,1},{2,10},{10... | collective-permute-start | bytes 1179656 | tf_op jit(solution)/shard_map/ppermute | solution.py:485
  25.0 24.9 %collective-permute-start.10 = (bf16[2,24,32,128]{3,2,1,0:T(8,128)(2,1)S(1)}, bf16[2,24,32,128]{3,2,1,0:T(8,128)(2,1)S(1)}, u32[]{:S(2)}, u32[]{:S(2)}) collective-permute-start(bf16[2,24,32,128]{3,2,1,0:T(8,128)(2,1)S(1)} %get-tuple-element.24), channel_id=1, source_target_pairs={{0,16},{8,24},{16,0},{24,8},{1,17},{9,25},{17,1},{25,9},{2,18},{10... | collective-permute-start | bytes 1179656 | tf_op jit(solution)/shard_map/ppermute | solution.py:485
  27.6 22.2 %collective-permute-start.11 = (bf16[2,24,32,128]{3,2,1,0:T(8,128)(2,1)S(1)}, bf16[2,24,32,128]{3,2,1,0:T(8,128)(2,1)}, u32[]{:S(2)}, u32[]{:S(2)}) collective-permute-start(bf16[2,24,32,128]{3,2,1,0:T(8,128)(2,1)S(1)} %get-tuple-element.25), channel_id=1, source_target_pairs={{0,24},{8,0},{16,8},{24,16},{1,25},{9,1},{17,9},{25,17},{2,26},{10... | collective-permute-start | bytes 1179656 | tf_op jit(solution)/shard_map/ppermute | solution.py:485
  39.5 10.4 %copy-start.2 = (bf16[2,24,32,128]{3,2,1,0:T(8,128)(2,1)S(1)}, bf16[2,24,32,128]{3,2,1,0:T(8,128)(2,1)}, u32[]{:S(2)}) copy-start(bf16[2,24,32,128]{3,2,1,0:T(8,128)(2,1)} %copy-done.1) | copy-start | bytes 1179652
  39.8 5.0 %collective-permute-start = (f32[16,768]{1,0:T(8,128)S(1)}, f32[16,768]{1,0:T(8,128)S(1)}, u32[]{:S(2)}, u32[]{:S(2)}) collective-permute-start(f32[16,768]{1,0:T(8,128)S(1)} %shard_map.38), channel_id=1, source_target_pairs={{0,1},{1,0},{2,3},{3,2},{4,5},{5,4},{6,7},{7,6},{8,9},{9,8},{10,11... | collective-permute-start | bytes 147464 | tf_op jit(solution)/shard_map/ppermute | solution.py:476
  44.8 11.4 %collective-permute-start.1 = (f32[16,768]{1,0:T(8,128)S(1)}, f32[16,768]{1,0:T(8,128)S(1)}, u32[]{:S(2)}, u32[]{:S(2)}) collective-permute-start(f32[16,768]{1,0:T(8,128)S(1)} %add.69.s0), channel_id=1, source_target_pairs={{0,8},{8,16},{16,24},{24,0},{1,9},{9,17},{17,25},{25,1},{2,10},{10... | collective-permute-start | bytes 147464 | tf_op jit(solution)/shard_map/ppermute | solution.py:472
  46.1 10.1 %collective-permute-start.2 = (f32[16,768]{1,0:T(8,128)S(1)}, f32[16,768]{1,0:T(8,128)S(1)}, u32[]{:S(2)}, u32[]{:S(2)}) collective-permute-start(f32[16,768]{1,0:T(8,128)S(1)} %add.69.s0), channel_id=1, source_target_pairs={{0,16},{8,24},{16,0},{24,8},{1,17},{9,25},{17,1},{25,9},{2,18},{10... | collective-permute-start | bytes 147464 | tf_op jit(solution)/shard_map/ppermute | solution.py:472
  48.8 7.5 %collective-permute-start.3 = (f32[16,768]{1,0:T(8,128)S(1)}, f32[16,768]{1,0:T(8,128)S(1)}, u32[]{:S(2)}, u32[]{:S(2)}) collective-permute-start(f32[16,768]{1,0:T(8,128)S(1)} %add.69.s0), channel_id=1, source_target_pairs={{0,24},{8,0},{16,8},{24,16},{1,25},{9,1},{17,9},{25,17},{2,26},{10... | collective-permute-start | bytes 147464 | tf_op jit(solution)/shard_map/ppermute | solution.py:472
  52.5 20.3 %all-to-all-start.1 = ((bf16[16,2,144,128]{3,2,1,0:T(8,128)(2,1)}), bf16[16,2,144,128]{3,2,1,0:T(8,128)(2,1)S(1)}, u32[]{:S(2)}, u32[]{:S(2)}) async-start(bf16[16,2,144,128]{3,2,1,0:T(8,128)(2,1)} %shard_map.42), calls=%async_computation.1 | async-start | bytes 2359296 | tf_op jit(solution)/shard_map/all_to_all | solution.py:493
  57.3 2.3 %collective-permute-start.4 = (f32[16,896]{1,0:T(8,128)S(1)}, f32[16,896]{1,0:T(8,128)S(1)}, u32[]{:S(2)}, u32[]{:S(2)}) collective-permute-start(f32[16,896]{1,0:T(8,128)S(1)} %get-tuple-element.19), channel_id=1, source_target_pairs={{0,1},{1,0},{2,3},{3,2},{4,5},{5,4},{6,7},{7,6},{8,9},{9,8},{10,11... | collective-permute-start | bytes 172040 | tf_op jit(solution)/shard_map/ppermute | solution.py:476
  59.7 4.6 %collective-permute-start.5 = (f32[16,896]{1,0:T(8,128)S(1)}, f32[16,896]{1,0:T(8,128)S(1)}, u32[]{:S(2)}, u32[]{:S(2)}) collective-permute-start(f32[16,896]{1,0:T(8,128)S(1)} %add.70.s0), channel_id=1, source_target_pairs={{0,8},{8,16},{16,24},{24,0},{1,9},{9,17},{17,25},{25,1},{2,10},{10... | collective-permute-start | bytes 172040 | tf_op jit(solution)/shard_map/ppermute | solution.py:472
  60.1 4.8 %collective-permute-start.6 = (f32[16,896]{1,0:T(8,128)S(1)}, f32[16,896]{1,0:T(8,128)S(1)}, u32[]{:S(2)}, u32[]{:S(2)}) collective-permute-start(f32[16,896]{1,0:T(8,128)S(1)} %add.70.s0), channel_id=1, source_target_pairs={{0,16},{8,24},{16,0},{24,8},{1,17},{9,25},{17,1},{25,9},{2,18},{10... | collective-permute-start | bytes 172040 | tf_op jit(solution)/shard_map/ppermute | solution.py:472
  60.8 4.7 %collective-permute-start.7 = (f32[16,896]{1,0:T(8,128)S(1)}, f32[16,896]{1,0:T(8,128)S(1)}, u32[]{:S(2)}, u32[]{:S(2)}) collective-permute-start(f32[16,896]{1,0:T(8,128)S(1)} %add.70.s0), channel_id=1, source_target_pairs={{0,24},{8,0},{16,8},{24,16},{1,25},{9,1},{17,9},{25,17},{2,26},{10... | collective-permute-start | bytes 172040 | tf_op jit(solution)/shard_map/ppermute | solution.py:472
  67.2 2.5 %collective-permute-start.8 = (f32[16,896]{1,0:T(8,128)S(1)}, f32[16,896]{1,0:T(8,128)S(1)}, u32[]{:S(2)}, u32[]{:S(2)}) collective-permute-start(f32[16,896]{1,0:T(8,128)S(1)} %get-tuple-element.21), channel_id=1, source_target_pairs={{0,1},{1,0},{2,3},{3,2},{4,5},{5,4},{6,7},{7,6},{8,9},{9,8},{10,11... | collective-permute-start | bytes 172040 | tf_op jit(solution)/shard_map/ppermute | solution.py:476
  72.9 7.1 %collective-permute-start.12 = (bf16[16,144,128]{2,1,0:T(8,128)(2,1)S(1)}, bf16[16,144,128]{2,1,0:T(8,128)(2,1)S(1)}, u32[]{:S(2)}, u32[]{:S(2)}) collective-permute-start(bf16[16,144,128]{2,1,0:T(8,128)(2,1)S(1)} %get-tuple-element.31), channel_id=1, source_target_pairs={{0,1},{1,0},{2,3},{3,2},{4,5},{5,4},{6,7},{7,6},{8,9},{9,8},{10,11... | collective-permute-start | bytes 1769480 | tf_op jit(solution)/shard_map/ppermute | solution.py:499
  77.0 5.4 %collective-permute-start.13 = (f32[16,896]{1,0:T(8,128)S(1)}, f32[16,896]{1,0:T(8,128)S(1)}, u32[]{:S(2)}, u32[]{:S(2)}) collective-permute-start(f32[16,896]{1,0:T(8,128)S(1)} %add.71.s0), channel_id=1, source_target_pairs={{0,8},{8,16},{16,24},{24,0},{1,9},{9,17},{17,25},{25,1},{2,10},{10... | collective-permute-start | bytes 172040 | tf_op jit(solution)/shard_map/ppermute | solution.py:472
  77.5 4.9 %collective-permute-start.14 = (f32[16,896]{1,0:T(8,128)S(1)}, f32[16,896]{1,0:T(8,128)S(1)}, u32[]{:S(2)}, u32[]{:S(2)}) collective-permute-start(f32[16,896]{1,0:T(8,128)S(1)} %add.71.s0), channel_id=1, source_target_pairs={{0,16},{8,24},{16,0},{24,8},{1,17},{9,25},{17,1},{25,9},{2,18},{10... | collective-permute-start | bytes 172040 | tf_op jit(solution)/shard_map/ppermute | solution.py:472
  79.1 4.1 %collective-permute-start.15 = (f32[16,896]{1,0:T(8,128)S(1)}, f32[16,896]{1,0:T(8,128)S(1)}, u32[]{:S(2)}, u32[]{:S(2)}) collective-permute-start(f32[16,896]{1,0:T(8,128)S(1)} %add.71.s0), channel_id=1, source_target_pairs={{0,24},{8,0},{16,8},{24,16},{1,25},{9,1},{17,9},{25,17},{2,26},{10... | collective-permute-start | bytes 172040 | tf_op jit(solution)/shard_map/ppermute | solution.py:472
  99.0 3.7 %collective-permute-start.16 = (f32[16,16,512]{2,1,0:T(8,128)S(1)}, f32[16,16,512]{2,1,0:T(8,128)S(1)}, u32[]{:S(2)}, u32[]{:S(2)}) collective-permute-start(f32[16,16,512]{2,1,0:T(8,128)S(1)} %all_to_all.15.own_ref), channel_id=1, source_target_pairs={{0,1},{1,0},{2,3},{3,2},{4,5},{5,4},{6,7},{7,6},{8,9},{9,8},{10,11... | collective-permute-start | bytes 1572872 | tf_op jit(solution)/shard_map/ppermute | solution.py:504

commit v6 on v5

--- a/solution.py
+++ b/solution.py
@@ -494,13 +494,12 @@
     place = placing(y, core)
     z, s = step(0, v, z, sums)
     z, s = step(1, v, z, sums_over(core_sum(s)))
-    s, blocks = lax.optimization_barrier((core_sum(s), blocks))
-    sums = sums_over(s)
+    sums = sums_over(core_sum(s))
+    tail, blocks = lax.optimization_barrier((sums[3], blocks))
+    (many,) = step(2, v, z, sums[:3] + [tail])
+    own = lax.all_to_all(many, ("y", "z"), 0, 0, tiled=True)
     mine, theirs = blocks[:, 0], lax.ppermute(blocks[:, 1], "core", turned_by(NC, 1))
     flat = arrange(mine, theirs, place)
-    z, flat = lax.optimization_barrier((z, flat))
-    (many,) = step(2, v, z, sums)
-    own = lax.all_to_all(many, ("y", "z"), 0, 0, tiled=True)
     far = lax.ppermute(own, "core", turned_by(NC, 1))
     return finish(flat, own, far, at)
 

time: 108 us -> 105 us (0.972)
  blocking collectives: 14.5 us -> 0 us
  starting transfers between devices: 40.9 us -> 46.2 us
  waiting for transfers between devices: 19.7 us -> 24.7 us
    all_to_all x1 -> x0, blocking collectives: 14.5 us -> none  [body(): own = lax.all_to_all(many, ('y', 'z'), 0, 0, tiled=True)]
    all_to_all x0 -> x1, waiting for transfers between devices: none -> 6.66 us  [body(): own = lax.all_to_all(many, ('y', 'z'), 0, 0, tiled=True)]
    all_to_all x0 -> x1, starting transfers between devices: none -> 5.95 us  [body(): own = lax.all_to_all(many, ('y', 'z'), 0, 0, tiled=True)]
    all_to_all x1, waiting for transfers between devices: 3.18 us -> 0.01 us  [body(): blocks = lax.all_to_all(turned, ('x', 'z'), 0, 0, tiled=True)]
    ppermute x9, waiting for transfers between devices: 4.66 us -> 7.68 us  [sums_over(): return [s] + [lax.ppermute(s, 'y', turned_by(NY, d)) for d in range(1, NY)]]
    ppermute x1, waiting for transfers between devices: 1.54 us -> 0.01 us  [body(): far = lax.ppermute(own, 'core', turned_by(NC, 1))]
    ppermute x1, starting transfers between devices: 2.14 us -> 3.25 us  [body(): far = lax.ppermute(own, 'core', turned_by(NC, 1))]
  transfers between devices with their start and end apart: 19 -> 20, of which waited for: 11 -> 10; matrix products, arithmetic and copies ran while one was open for 4% -> 4% of each run, Pallas kernels for 9% -> 9%
where the time goes in v6:
time: 105 us; the launch traced here: 104 us
  starting transfers between devices  46.2 us (44%)
  Pallas kernels  27.1 us (26%)
  waiting for transfers between devices  24.7 us (24%)
  local copies, waits for them, and re-layouts  5.39 us (5%)
    ppermute x9, starting transfers between devices, sums_over(): return [s] + [lax.ppermute(s, 'y', turned_by(NY, d)) for d in range(1, NY)]  10.6 us
    pallas_call x1, Pallas kernels, channelize(): pl.pallas_call(channelize_kernel, out_shape=jax.ShapeDtypeStruct((NX * NZ...  10.4 us
    all_to_all x1, starting transfers between devices, body(): v = lax.all_to_all(parcels, ('x', 'z'), 0, 0, tiled=True)  8.44 us
    all_to_all x1, waiting for transfers between devices, body(): v = lax.all_to_all(parcels, ('x', 'z'), 0, 0, tiled=True)  7.69 us
    ppermute x9, waiting for transfers between devices, sums_over(): return [s] + [lax.ppermute(s, 'y', turned_by(NY, d)) for d in range(1, NY)]  7.68 us
    ppermute x3, starting transfers between devices, core_sum(): return s + lax.ppermute(s, 'core', turned_by(NC, 1))  6.79 us
    all_to_all x1, waiting for transfers between devices, body(): own = lax.all_to_all(many, ('y', 'z'), 0, 0, tiled=True)  6.66 us
    all_to_all x1, starting transfers between devices, body(): own = lax.all_to_all(many, ('y', 'z'), 0, 0, tiled=True)  5.95 us
  transfers between devices with their start and end apart: 20, of which 10 were waited for; matrix products, arithmetic and copies ran while one was open for 4% of the time, Pallas kernels for 9%

profile of v6, /device:TPU:1, one launch (start us, length us, event | category | flops | bytes accessed | tf_op | source)
XLA Modules:
  0.0 104.5 jit_solution(4191520281166606640)
XLA Ops:
  0.0 10.4 %shard_map.37.v_ref = bf16[16,2,32,768]{3,2,1,0:T(8,128)(2,1)} custom-call(s32[12]{0:T(128)} %ids_ref.1, bf16[32,98688]{1,0:T(8,128)(2,1)} %x_hbm.1), custom_call_target="tpu_custom_call" | custom-call | flops 7200000000 | bytes 24000000 | tf_op jit(solution)/shard_map/pallas_call | solution.py:150
  10.4 8.4 %all-to-all-start = ((bf16[16,2,32,768]{3,2,1,0:T(8,128)(2,1)}), bf16[16,2,32,768]{3,2,1,0:T(8,128)(2,1)S(1)}, u32[]{:S(2)}, u32[]{:S(2)}) async-start(bf16[16,2,32,768]{3,2,1,0:T(8,128)(2,1)} %shard_map.37.v_ref), calls=%async_computation | async-start | bytes 3145728 | tf_op jit(solution)/shard_map/all_to_all | solution.py:483
  18.9 0.1 pad_add_fusion.y_ref.at_ref.core_ref
  18.9 1.4 %copy-done = bf16[16,2,32,768]{3,2,1,0:T(8,128)(2,1)S(1)} copy-done((bf16[16,2,32,768]{3,2,1,0:T(8,128)(2,1)S(1)}, bf16[16,2,32,768]{3,2,1,0:T(8,128)(2,1)}, u32[]{:S(2)}) %copy-start) | copy-done | bytes 1572888
  20.3 2.6 %shard_map.41 = (bf16[2,24,32,128]{3,2,1,0:T(8,128)(2,1)S(1)}, bf16[2,24,32,128]{3,2,1,0:T(8,128)(2,1)}, bf16[2,24,32,128]{3,2,1,0:T(8,128)(2,1)S(1)}, bf16[2,24,32,128]{3,2,1,0:T(8,128)(2,1)S(1)}) custom-call(s32[2]{0:T(128)S(1)} %pad_add_fusion.y_ref.at_ref.core_ref, bf16[16,2,32,768]{3,2,1,0:T(8,128)(2,1)S(1)} %copy-done), custom_call_target="tpu_custom_call" | custom-call | flops 3600000000 | bytes 12000000 | tf_op jit(solution)/shard_map/pallas_call | solution.py:189
  22.9 0.8 copy-done.1
  23.7 1.3 %collective-permute-start.10 = (bf16[2,24,32,128]{3,2,1,0:T(8,128)(2,1)}, bf16[2,24,32,128]{3,2,1,0:T(8,128)(2,1)S(1)}, u32[]{:S(2)}, u32[]{:S(2)}) collective-permute-start(bf16[2,24,32,128]{3,2,1,0:T(8,128)(2,1)} %get-tuple-element.20), channel_id=1, source_target_pairs={{0,8},{8,16},{16,24},{24,0},{1,9},{9,17},{17,25},{25,1},{2,10},{10... | collective-permute-start | bytes 1179656 | tf_op jit(solution)/shard_map/ppermute | solution.py:485
  25.0 2.6 %collective-permute-start.11 = (bf16[2,24,32,128]{3,2,1,0:T(8,128)(2,1)S(1)}, bf16[2,24,32,128]{3,2,1,0:T(8,128)(2,1)S(1)}, u32[]{:S(2)}, u32[]{:S(2)}) collective-permute-start(bf16[2,24,32,128]{3,2,1,0:T(8,128)(2,1)S(1)} %get-tuple-element.21), channel_id=1, source_target_pairs={{0,16},{8,24},{16,0},{24,8},{1,17},{9,25},{17,1},{25,9},{2,18},{10... | collective-permute-start | bytes 1179656 | tf_op jit(solution)/shard_map/ppermute | solution.py:485
  27.6 1.1 %collective-permute-start.12 = (bf16[2,24,32,128]{3,2,1,0:T(8,128)(2,1)S(1)}, bf16[2,24,32,128]{3,2,1,0:T(8,128)(2,1)}, u32[]{:S(2)}, u32[]{:S(2)}) collective-permute-start(bf16[2,24,32,128]{3,2,1,0:T(8,128)(2,1)S(1)} %get-tuple-element.22), channel_id=1, source_target_pairs={{0,24},{8,0},{16,8},{24,16},{1,25},{9,1},{17,9},{25,17},{2,26},{10... | collective-permute-start | bytes 1179656 | tf_op jit(solution)/shard_map/ppermute | solution.py:485
  28.7 1.9 %reshape.9 = f32[16,4,4,4,2,32]{5,4,3,2,1,0:T(2,128)} reshape(f32[2,8,4096]{2,1,0:T(8,128)S(1)} %copy-done.3) | data formatting | bytes 524288 | tf_op jit(solution)/shard_map/reshape | solution.py:487
  30.6 1.1 %constant_dynamic-slice_fusion = f32[16,4,1,4,1,32]{5,4,3,2,1,0:T(1,128)S(1)} fusion(f32[16,4,4,4,2,32]{5,4,3,2,1,0:T(2,128)} %reshape.9, s32[]{:T(128)S(6)} %select_n.51, s32[]{:T(128)S(6)} %select_n.53), kind=kLoop, calls=%fused_computation.52 | loop fusion | bytes 65544 | tf_op jit(solution)/shard_map/jit(dynamic_index_in_dim)/dynamic_slice | solution.py:489
  31.7 0.1 reshape.10.q_ref.z_ref
  31.8 7.7 %all-to-all-done.v_ref = bf16[16,2,32,768]{3,2,1,0:T(8,128)(2,1)S(1)} async-done(((bf16[16,2,32,768]{3,2,1,0:T(8,128)(2,1)}), bf16[16,2,32,768]{3,2,1,0:T(8,128)(2,1)S(1)}, u32[]{:S(2)}, u32[]{:S(2)}) %all-to-all-start) | async-done | bytes 1572896 | tf_op jit(solution)/shard_map/all_to_all | solution.py:483
  39.5 0.3 shard_map.38
  39.8 4.2 %collective-permute-start = (f32[16,768]{1,0:T(8,128)S(1)}, f32[16,768]{1,0:T(8,128)S(1)}, u32[]{:S(2)}, u32[]{:S(2)}) collective-permute-start(f32[16,768]{1,0:T(8,128)S(1)} %shard_map.38), channel_id=1, source_target_pairs={{0,1},{1,0},{2,3},{3,2},{4,5},{5,4},{6,7},{7,6},{8,9},{9,8},{10,11... | collective-permute-start | bytes 147464 | tf_op jit(solution)/shard_map/ppermute | solution.py:476
  44.0 0.9 collective-permute-done
  44.8 2.7 %collective-permute-start.3 = (f32[16,768]{1,0:T(8,128)S(1)}, f32[16,768]{1,0:T(8,128)S(1)}, u32[]{:S(2)}, u32[]{:S(2)}) collective-permute-start(f32[16,768]{1,0:T(8,128)S(1)} %add.69.s0), channel_id=1, source_target_pairs={{0,24},{8,0},{16,8},{24,16},{1,25},{9,1},{17,9},{25,17},{2,26},{10... | collective-permute-start | bytes 147464 | tf_op jit(solution)/shard_map/ppermute | solution.py:472
  47.6 0.4 collective-permute-start.2
  47.9 0.7 collective-permute-start.1
  48.6 0.0 collective-permute-done.11.refs_2_
  48.6 0.0 collective-permute-done.12.refs_3_
  48.6 2.7 %shard_map.42 = bf16[16,2,144,128]{3,2,1,0:T(8,128)(2,1)} custom-call(s32[2]{0:T(128)S(1)} %pad_add_fusion.y_ref.at_ref.core_ref, bf16[2,24,32,128]{3,2,1,0:T(8,128)(2,1)S(1)} %copy-done.2, bf16[2,24,32,128]{3,2,1,0:T(8,128)(2,1)S(1)} %collective-permute-done.10.refs_1_, bf16[2,24,32,128]{3,2,1,0:T(8,128)(2,1)S(1)} %collective-permute-done.11.refs_2_, ...), custom_call_target="tpu_custom_call" | custom-call | flops 2700000000 | bytes 9000000 | tf_op jit(solution)/shard_map/pallas_call | solution.py:226
  51.3 3.7 %all-to-all-start.1 = ((bf16[16,2,144,128]{3,2,1,0:T(8,128)(2,1)}), bf16[16,2,144,128]{3,2,1,0:T(8,128)(2,1)S(1)}, u32[]{:S(2)}, u32[]{:S(2)}) async-start(bf16[16,2,144,128]{3,2,1,0:T(8,128)(2,1)} %shard_map.42), calls=%async_computation.1 | async-start | bytes 2359296 | tf_op jit(solution)/shard_map/all_to_all | solution.py:493
  55.0 0.0 collective-permute-done.2.s2
  55.1 1.1 %shard_map.39 = (f32[16,512]{1,0:T(8,128)S(1)}, f32[16,896]{1,0:T(8,128)S(1)}) custom-call(bf16[16,2,32,768]{3,2,1,0:T(8,128)(2,1)S(1)} %all-to-all-done.v_ref, f32[16,512]{1,0:T(8,128)S(1)} %reshape.10.q_ref.z_ref, f32[16,768]{1,0:T(8,128)S(1)} %add.69.s0, f32[16,768]{1,0:T(8,128)S(1)} %collective-permute-done.1.s1, ...), custom_call_target="tpu_custom_call" | custom-call | flops 4499999744 | bytes 15000000 | tf_op jit(solution)/shard_map/pallas_call | solution.py:329
  56.1 1.4 %collective-permute-start.4 = (f32[16,896]{1,0:T(8,128)S(1)}, f32[16,896]{1,0:T(8,128)S(1)}, u32[]{:S(2)}, u32[]{:S(2)}) collective-permute-start(f32[16,896]{1,0:T(8,128)S(1)} %get-tuple-element.17), channel_id=1, source_target_pairs={{0,1},{1,0},{2,3},{3,2},{4,5},{5,4},{6,7},{7,6},{8,9},{9,8},{10,11... | collective-permute-start | bytes 172040 | tf_op jit(solution)/shard_map/ppermute | solution.py:476
  57.6 0.9 collective-permute-done.4
  58.4 2.0 %collective-permute-start.7 = (f32[16,896]{1,0:T(8,128)S(1)}, f32[16,896]{1,0:T(8,128)S(1)}, u32[]{:S(2)}, u32[]{:S(2)}) collective-permute-start(f32[16,896]{1,0:T(8,128)S(1)} %add.70.s0), channel_id=1, source_target_pairs={{0,24},{8,0},{16,8},{24,16},{1,25},{9,1},{17,9},{25,17},{2,26},{10... | collective-permute-start | bytes 172040 | tf_op jit(solution)/shard_map/ppermute | solution.py:472
  60.5 1.4 %collective-permute-start.6 = (f32[16,896]{1,0:T(8,128)S(1)}, f32[16,896]{1,0:T(8,128)S(1)}, u32[]{:S(2)}, u32[]{:S(2)}) collective-permute-start(f32[16,896]{1,0:T(8,128)S(1)} %add.70.s0), channel_id=1, source_target_pairs={{0,16},{8,24},{16,0},{24,8},{1,17},{9,25},{17,1},{25,9},{2,18},{10... | collective-permute-start | bytes 172040 | tf_op jit(solution)/shard_map/ppermute | solution.py:472
  61.9 0.1 collective-permute-done.7.s3
  61.9 3.4 %collective-permute-done.6.s2 = f32[16,896]{1,0:T(8,128)S(1)} collective-permute-done((f32[16,896]{1,0:T(8,128)S(1)}, f32[16,896]{1,0:T(8,128)S(1)}, u32[]{:S(2)}, u32[]{:S(2)}) %collective-permute-start.6) | collective-permute-done | bytes 57376 | tf_op jit(solution)/shard_map/ppermute | solution.py:472
  65.3 1.7 %collective-permute-done.5.s1 = f32[16,896]{1,0:T(8,128)S(1)} collective-permute-done((f32[16,896]{1,0:T(8,128)S(1)}, f32[16,896]{1,0:T(8,128)S(1)}, u32[]{:S(2)}, u32[]{:S(2)}) %collective-permute-start.5) | collective-permute-done | bytes 57376 | tf_op jit(solution)/shard_map/ppermute | solution.py:472
  67.0 1.7 %shard_map.40 = (f32[16,512]{1,0:T(8,128)S(1)}, f32[16,896]{1,0:T(8,128)S(1)}) custom-call(bf16[16,2,32,768]{3,2,1,0:T(8,128)(2,1)S(1)} %all-to-all-done.v_ref, f32[16,512]{1,0:T(8,128)S(1)} %get-tuple-element.16.z_ref, f32[16,896]{1,0:T(8,128)S(1)} %add.70.s0, f32[16,896]{1,0:T(8,128)S(1)} %collective-permute-done.5.s1, ...), custom_call_target="tpu_custom_call" | custom-call | flops 4499999744 | bytes 15000000 | tf_op jit(solution)/shard_map/pallas_call | solution.py:329
  68.7 1.2 %collective-permute-start.8 = (f32[16,896]{1,0:T(8,128)S(1)}, f32[16,896]{1,0:T(8,128)S(1)}, u32[]{:S(2)}, u32[]{:S(2)}) collective-permute-start(f32[16,896]{1,0:T(8,128)S(1)} %get-tuple-element.18), channel_id=1, source_target_pairs={{0,1},{1,0},{2,3},{3,2},{4,5},{5,4},{6,7},{7,6},{8,9},{9,8},{10,11... | collective-permute-start | bytes 172040 | tf_op jit(solution)/shard_map/ppermute | solution.py:476
  69.9 0.9 collective-permute-done.8
  70.8 0.8 collective-permute-start.15
  71.6 2.7 %collective-permute-start.9 = (f32[16,896]{1,0:T(8,128)S(1)}, f32[16,896]{1,0:T(8,128)S(1)}, u32[]{:S(2)}, u32[]{:S(2)}) collective-permute-start(f32[16,896]{1,0:T(8,128)S(1)} %add.71.s0), channel_id=1, source_target_pairs={{0,24},{8,0},{16,8},{24,16},{1,25},{9,1},{17,9},{25,17},{2,26},{10... | collective-permute-start | bytes 172040 | tf_op jit(solution)/shard_map/ppermute | solution.py:472
  74.3 1.2 %collective-permute-done.9.s3 = f32[16,896]{1,0:T(8,128)S(1)} collective-permute-done((f32[16,896]{1,0:T(8,128)S(1)}, f32[16,896]{1,0:T(8,128)S(1)}, u32[]{:S(2)}, u32[]{:S(2)}) %collective-permute-start.9) | collective-permute-done | bytes 57376 | tf_op jit(solution)/shard_map/ppermute | solution.py:472
  75.5 1.3 %collective-permute-done.14.s1 = f32[16,896]{1,0:T(8,128)S(1)} collective-permute-done((f32[16,896]{1,0:T(8,128)S(1)}, f32[16,896]{1,0:T(8,128)S(1)}, u32[]{:S(2)}, u32[]{:S(2)}) %collective-permute-start.14) | collective-permute-done | bytes 57376 | tf_op jit(solution)/shard_map/ppermute | solution.py:472
  76.8 2.1 %shard_map.44 = f32[16,16,512]{2,1,0:T(8,128)} custom-call(bf16[16,2,32,768]{3,2,1,0:T(8,128)(2,1)S(1)} %all-to-all-done.v_ref, f32[16,512]{1,0:T(8,128)S(1)} %get-tuple-element.25.z_ref, f32[16,896]{1,0:T(8,128)S(1)} %add.71.s0, f32[16,896]{1,0:T(8,128)S(1)} %collective-permute-done.14.s1, f32[16,896]{1,0:T(8,128)S(1)} %collective-permute-done.15.s2, ...), custom_call_target="tpu_custom_call" | custom-call | flops 4499999744 | bytes 15000000 | tf_op jit(solution)/shard_map/pallas_call | solution.py:329
  78.9 5.9 %all-to-all-start.2 = ((f32[16,16,512]{2,1,0:T(8,128)}), f32[16,16,512]{2,1,0:T(8,128)S(1)}, u32[]{:S(2)}, u32[]{:S(2)}) async-start(f32[16,16,512]{2,1,0:T(8,128)} %shard_map.44), calls=%async_computation.2 | async-start | bytes 1048576 | tf_op jit(solution)/shard_map/all_to_all | solution.py:500
  84.8 0.1 slice_bitcast_fusion
  84.9 2.5 %collective-permute-start.13 = (bf16[16,144,128]{2,1,0:T(8,128)(2,1)S(1)}, bf16[16,144,128]{2,1,0:T(8,128)(2,1)S(1)}, u32[]{:S(2)}, u32[]{:S(2)}) collective-permute-start(bf16[16,144,128]{2,1,0:T(8,128)(2,1)S(1)} %get-tuple-element.27), channel_id=1, source_target_pairs={{0,1},{1,0},{2,3},{3,2},{4,5},{5,4},{6,7},{7,6},{8,9},{9,8},{10,11... | collective-permute-start | bytes 1769480 | tf_op jit(solution)/shard_map/ppermute | solution.py:501
  87.4 6.7 %all-to-all-done.2.own_ref = f32[16,16,512]{2,1,0:T(8,128)S(1)} async-done(((f32[16,16,512]{2,1,0:T(8,128)}), f32[16,16,512]{2,1,0:T(8,128)S(1)}, u32[]{:S(2)}, u32[]{:S(2)}) %all-to-all-start.2) | async-done | bytes 524320 | tf_op jit(solution)/shard_map/all_to_all | solution.py:500
  94.1 3.2 %collective-permute-start.16 = (f32[16,16,512]{2,1,0:T(8,128)S(1)}, f32[16,16,512]{2,1,0:T(8,128)S(1)}, u32[]{:S(2)}, u32[]{:S(2)}) collective-permute-start(f32[16,16,512]{2,1,0:T(8,128)S(1)} %all-to-all-done.2.own_ref), channel_id=1, source_target_pairs={{0,1},{1,0},{2,3},{3,2},{4,5},{5,4},{6,7},{7,6},{8,9},{9,8},{10,11... | collective-permute-start | bytes 1572872 | tf_op jit(solution)/shard_map/ppermute | solution.py:503
  97.3 0.6 select_convert_fusion.place_ref
  98.0 1.4 %shard_map.43.flat = f32[4,3,48,1024]{3,2,1,0:T(8,128)S(1)} custom-call(bf16[16,144,128]{2,1,0:T(8,128)(2,1)S(1)} %get-tuple-element.28.mine_ref, bf16[16,144,128]{2,1,0:T(8,128)(2,1)S(1)} %collective-permute-done.13.theirs_ref, bf16[1024,1024]{1,0:T(8,128)(2,1)S(1)} %select_convert_fusion.place_ref), custom_call_target="tpu_custom_call" | custom-call | flops 3600000000 | bytes 12000000 | tf_op jit(solution)/shard_map/pallas_call | solution.py:360
  99.4 4.9 %shard_map.45 = f32[2,3,24,4096]{3,2,1,0:T(8,128)} custom-call(f32[4,3,48,1024]{3,2,1,0:T(8,128)S(1)} %shard_map.43.flat, f32[16,16,512]{2,1,0:T(8,128)S(1)} %all-to-all-done.2.own_ref, f32[16,16,512]{2,1,0:T(8,128)S(1)} %collective-permute-done.16.far_ref, s32[2]{0:T(128)S(1)} %pad_add_fusion.y_ref.at_ref.core_ref), custom_call_target="tpu_custom_call" | custom-call | flops 5400000000 | bytes 18000000 | tf_op jit(solution)/shard_map/pallas_call | solution.py:452
  (24 shorter events, 0.1 us)
Async XLA Ops:
  10.4 29.1 %all-to-all-start = ((bf16[16,2,32,768]{3,2,1,0:T(8,128)(2,1)}), bf16[16,2,32,768]{3,2,1,0:T(8,128)(2,1)S(1)}, u32[]{:S(2)}, u32[]{:S(2)}) async-start(bf16[16,2,32,768]{3,2,1,0:T(8,128)(2,1)} %shard_map.37.v_ref), calls=%async_computation | async-start | bytes 3145728 | tf_op jit(solution)/shard_map/all_to_all | solution.py:483
  18.9 1.4 %copy-start = (bf16[16,2,32,768]{3,2,1,0:T(8,128)(2,1)S(1)}, bf16[16,2,32,768]{3,2,1,0:T(8,128)(2,1)}, u32[]{:S(2)}) copy-start(bf16[16,2,32,768]{3,2,1,0:T(8,128)(2,1)} %shard_map.37.v_ref) | copy-start | bytes 4718596
  20.3 8.3 %copy-start.3 = (f32[2,8,4096]{2,1,0:T(8,128)S(1)}, f32[2,8,4096]{2,1,0:T(8,128)}, u32[]{:S(2)}) copy-start(f32[2,8,4096]{2,1,0:T(8,128)} %param.5) | copy-start | bytes 786436
  22.9 0.8 copy-start.1
  23.7 24.3 %collective-permute-start.10 = (bf16[2,24,32,128]{3,2,1,0:T(8,128)(2,1)}, bf16[2,24,32,128]{3,2,1,0:T(8,128)(2,1)S(1)}, u32[]{:S(2)}, u32[]{:S(2)}) collective-permute-start(bf16[2,24,32,128]{3,2,1,0:T(8,128)(2,1)} %get-tuple-element.20), channel_id=1, source_target_pairs={{0,8},{8,16},{16,24},{24,0},{1,9},{9,17},{17,25},{25,1},{2,10},{10... | collective-permute-start | bytes 1179656 | tf_op jit(solution)/shard_map/ppermute | solution.py:485
  25.0 23.6 %collective-permute-start.11 = (bf16[2,24,32,128]{3,2,1,0:T(8,128)(2,1)S(1)}, bf16[2,24,32,128]{3,2,1,0:T(8,128)(2,1)S(1)}, u32[]{:S(2)}, u32[]{:S(2)}) collective-permute-start(bf16[2,24,32,128]{3,2,1,0:T(8,128)(2,1)S(1)} %get-tuple-element.21), channel_id=1, source_target_pairs={{0,16},{8,24},{16,0},{24,8},{1,17},{9,25},{17,1},{25,9},{2,18},{10... | collective-permute-start | bytes 1179656 | tf_op jit(solution)/shard_map/ppermute | solution.py:485
  27.6 21.0 %collective-permute-start.12 = (bf16[2,24,32,128]{3,2,1,0:T(8,128)(2,1)S(1)}, bf16[2,24,32,128]{3,2,1,0:T(8,128)(2,1)}, u32[]{:S(2)}, u32[]{:S(2)}) collective-permute-start(bf16[2,24,32,128]{3,2,1,0:T(8,128)(2,1)S(1)} %get-tuple-element.22), channel_id=1, source_target_pairs={{0,24},{8,0},{16,8},{24,16},{1,25},{9,1},{17,9},{25,17},{2,26},{10... | collective-permute-start | bytes 1179656 | tf_op jit(solution)/shard_map/ppermute | solution.py:485
  39.5 9.2 %copy-start.2 = (bf16[2,24,32,128]{3,2,1,0:T(8,128)(2,1)S(1)}, bf16[2,24,32,128]{3,2,1,0:T(8,128)(2,1)}, u32[]{:S(2)}) copy-start(bf16[2,24,32,128]{3,2,1,0:T(8,128)(2,1)} %copy-done.1) | copy-start | bytes 1179652
  39.8 5.0 %collective-permute-start = (f32[16,768]{1,0:T(8,128)S(1)}, f32[16,768]{1,0:T(8,128)S(1)}, u32[]{:S(2)}, u32[]{:S(2)}) collective-permute-start(f32[16,768]{1,0:T(8,128)S(1)} %shard_map.38), channel_id=1, source_target_pairs={{0,1},{1,0},{2,3},{3,2},{4,5},{5,4},{6,7},{7,6},{8,9},{9,8},{10,11... | collective-permute-start | bytes 147464 | tf_op jit(solution)/shard_map/ppermute | solution.py:476
  44.8 10.2 %collective-permute-start.3 = (f32[16,768]{1,0:T(8,128)S(1)}, f32[16,768]{1,0:T(8,128)S(1)}, u32[]{:S(2)}, u32[]{:S(2)}) collective-permute-start(f32[16,768]{1,0:T(8,128)S(1)} %add.69.s0), channel_id=1, source_target_pairs={{0,24},{8,0},{16,8},{24,16},{1,25},{9,1},{17,9},{25,17},{2,26},{10... | collective-permute-start | bytes 147464 | tf_op jit(solution)/shard_map/ppermute | solution.py:472
  47.6 7.5 %collective-permute-start.2 = (f32[16,768]{1,0:T(8,128)S(1)}, f32[16,768]{1,0:T(8,128)S(1)}, u32[]{:S(2)}, u32[]{:S(2)}) collective-permute-start(f32[16,768]{1,0:T(8,128)S(1)} %add.69.s0), channel_id=1, source_target_pairs={{0,16},{8,24},{16,0},{24,8},{1,17},{9,25},{17,1},{25,9},{2,18},{10... | collective-permute-start | bytes 147464 | tf_op jit(solution)/shard_map/ppermute | solution.py:472
  47.9 7.1 %collective-permute-start.1 = (f32[16,768]{1,0:T(8,128)S(1)}, f32[16,768]{1,0:T(8,128)S(1)}, u32[]{:S(2)}, u32[]{:S(2)}) collective-permute-start(f32[16,768]{1,0:T(8,128)S(1)} %add.69.s0), channel_id=1, source_target_pairs={{0,8},{8,16},{16,24},{24,0},{1,9},{9,17},{17,25},{25,1},{2,10},{10... | collective-permute-start | bytes 147464 | tf_op jit(solution)/shard_map/ppermute | solution.py:472
  51.3 24.2 %all-to-all-start.1 = ((bf16[16,2,144,128]{3,2,1,0:T(8,128)(2,1)}), bf16[16,2,144,128]{3,2,1,0:T(8,128)(2,1)S(1)}, u32[]{:S(2)}, u32[]{:S(2)}) async-start(bf16[16,2,144,128]{3,2,1,0:T(8,128)(2,1)} %shard_map.42), calls=%async_computation.1 | async-start | bytes 2359296 | tf_op jit(solution)/shard_map/all_to_all | solution.py:493
  56.1 2.3 %collective-permute-start.4 = (f32[16,896]{1,0:T(8,128)S(1)}, f32[16,896]{1,0:T(8,128)S(1)}, u32[]{:S(2)}, u32[]{:S(2)}) collective-permute-start(f32[16,896]{1,0:T(8,128)S(1)} %get-tuple-element.17), channel_id=1, source_target_pairs={{0,1},{1,0},{2,3},{3,2},{4,5},{5,4},{6,7},{7,6},{8,9},{9,8},{10,11... | collective-permute-start | bytes 172040 | tf_op jit(solution)/shard_map/ppermute | solution.py:476
  58.4 3.5 %collective-permute-start.7 = (f32[16,896]{1,0:T(8,128)S(1)}, f32[16,896]{1,0:T(8,128)S(1)}, u32[]{:S(2)}, u32[]{:S(2)}) collective-permute-start(f32[16,896]{1,0:T(8,128)S(1)} %add.70.s0), channel_id=1, source_target_pairs={{0,24},{8,0},{16,8},{24,16},{1,25},{9,1},{17,9},{25,17},{2,26},{10... | collective-permute-start | bytes 172040 | tf_op jit(solution)/shard_map/ppermute | solution.py:472
  60.5 4.8 %collective-permute-start.6 = (f32[16,896]{1,0:T(8,128)S(1)}, f32[16,896]{1,0:T(8,128)S(1)}, u32[]{:S(2)}, u32[]{:S(2)}) collective-permute-start(f32[16,896]{1,0:T(8,128)S(1)} %add.70.s0), channel_id=1, source_target_pairs={{0,16},{8,24},{16,0},{24,8},{1,17},{9,25},{17,1},{25,9},{2,18},{10... | collective-permute-start | bytes 172040 | tf_op jit(solution)/shard_map/ppermute | solution.py:472
  61.9 5.1 %collective-permute-start.5 = (f32[16,896]{1,0:T(8,128)S(1)}, f32[16,896]{1,0:T(8,128)S(1)}, u32[]{:S(2)}, u32[]{:S(2)}) collective-permute-start(f32[16,896]{1,0:T(8,128)S(1)} %add.70.s0), channel_id=1, source_target_pairs={{0,8},{8,16},{16,24},{24,0},{1,9},{9,17},{17,25},{25,1},{2,10},{10... | collective-permute-start | bytes 172040 | tf_op jit(solution)/shard_map/ppermute | solution.py:472
  68.7 2.1 %collective-permute-start.8 = (f32[16,896]{1,0:T(8,128)S(1)}, f32[16,896]{1,0:T(8,128)S(1)}, u32[]{:S(2)}, u32[]{:S(2)}) collective-permute-start(f32[16,896]{1,0:T(8,128)S(1)} %get-tuple-element.18), channel_id=1, source_target_pairs={{0,1},{1,0},{2,3},{3,2},{4,5},{5,4},{6,7},{7,6},{8,9},{9,8},{10,11... | collective-permute-start | bytes 172040 | tf_op jit(solution)/shard_map/ppermute | solution.py:476
  70.8 4.7 %collective-permute-start.15 = (f32[16,896]{1,0:T(8,128)S(1)}, f32[16,896]{1,0:T(8,128)S(1)}, u32[]{:S(2)}, u32[]{:S(2)}) collective-permute-start(f32[16,896]{1,0:T(8,128)S(1)} %add.71.s0), channel_id=1, source_target_pairs={{0,16},{8,24},{16,0},{24,8},{1,17},{9,25},{17,1},{25,9},{2,18},{10... | collective-permute-start | bytes 172040 | tf_op jit(solution)/shard_map/ppermute | solution.py:472
  71.6 5.2 %collective-permute-start.14 = (f32[16,896]{1,0:T(8,128)S(1)}, f32[16,896]{1,0:T(8,128)S(1)}, u32[]{:S(2)}, u32[]{:S(2)}) collective-permute-start(f32[16,896]{1,0:T(8,128)S(1)} %add.71.s0), channel_id=1, source_target_pairs={{0,8},{8,16},{16,24},{24,0},{1,9},{9,17},{17,25},{25,1},{2,10},{10... | collective-permute-start | bytes 172040 | tf_op jit(solution)/shard_map/ppermute | solution.py:472
  71.6 3.9 %collective-permute-start.9 = (f32[16,896]{1,0:T(8,128)S(1)}, f32[16,896]{1,0:T(8,128)S(1)}, u32[]{:S(2)}, u32[]{:S(2)}) collective-permute-start(f32[16,896]{1,0:T(8,128)S(1)} %add.71.s0), channel_id=1, source_target_pairs={{0,24},{8,0},{16,8},{24,16},{1,25},{9,1},{17,9},{25,17},{2,26},{10... | collective-permute-start | bytes 172040 | tf_op jit(solution)/shard_map/ppermute | solution.py:472
  78.9 15.2 %all-to-all-start.2 = ((f32[16,16,512]{2,1,0:T(8,128)}), f32[16,16,512]{2,1,0:T(8,128)S(1)}, u32[]{:S(2)}, u32[]{:S(2)}) async-start(f32[16,16,512]{2,1,0:T(8,128)} %shard_map.44), calls=%async_computation.2 | async-start | bytes 1048576 | tf_op jit(solution)/shard_map/all_to_all | solution.py:500
  84.9 13.0 %collective-permute-start.13 = (bf16[16,144,128]{2,1,0:T(8,128)(2,1)S(1)}, bf16[16,144,128]{2,1,0:T(8,128)(2,1)S(1)}, u32[]{:S(2)}, u32[]{:S(2)}) collective-permute-start(bf16[16,144,128]{2,1,0:T(8,128)(2,1)S(1)} %get-tuple-element.27), channel_id=1, source_target_pairs={{0,1},{1,0},{2,3},{3,2},{4,5},{5,4},{6,7},{7,6},{8,9},{9,8},{10,11... | collective-permute-start | bytes 1769480 | tf_op jit(solution)/shard_map/ppermute | solution.py:501
  94.1 5.3 %collective-permute-start.16 = (f32[16,16,512]{2,1,0:T(8,128)S(1)}, f32[16,16,512]{2,1,0:T(8,128)S(1)}, u32[]{:S(2)}, u32[]{:S(2)}) collective-permute-start(f32[16,16,512]{2,1,0:T(8,128)S(1)} %all-to-all-done.2.own_ref), channel_id=1, source_target_pairs={{0,1},{1,0},{2,3},{3,2},{4,5},{5,4},{6,7},{7,6},{8,9},{9,8},{10,11... | collective-permute-start | bytes 1572872 | tf_op jit(solution)/shard_map/ppermute | solution.py:503

commit v7 on v6

--- a/solution.py
+++ b/solution.py
@@ -67,8 +67,8 @@
     return x[:n] + (x[n : 2 * n] + x[2 * n :])
 
 
-STEP_ROWS = 16
-CHUNKS = 4
+STEP_ROWS = 32
+CHUNKS = 2
 
 
 def fill_table(ids_ref, turned):
@@ -96,7 +96,7 @@
             turned[q * RC : (q + 1) * RC, (q + m) * P_SIZE : (q + m + 1) * P_SIZE] = taps
 
 
-def channelize_kernel(ids_ref, x_hbm, o_ref, x_ref, turned, table, wide, tall, sems):
+def channelize_kernel(ids_ref, x_hbm, o_hbm, x_ref, o_ref, turned, table, wide, tall, sems, out_sems):
     step = ROWS // CHUNKS * PHASES * P_SIZE
     halo = (TAPS - 1) * P_SIZE
     copies = []
@@ -137,6 +137,7 @@
         for q in range(PHASES):
             tall[:, n, q * 128 : (q + 1) * 128] = turned_n[q * RC : (q + 1) * RC]
 
+    copies = []
     for x in range(NX):
         for z in range(NZ):
             for r in range(2):
@@ -144,6 +145,11 @@
                     o_ref[x * NZ + z, r] = tall[r * CHANNELS + x * GROUP + z].astype(BF16)
                 else:
                     o_ref[x * NZ + z, r] = jnp.zeros((LOCAL, SPECTRA), BF16)
+        part = pl.ds(x * NZ, NZ)
+        copies.append(pltpu.make_async_copy(o_ref.at[part], o_hbm.at[part], out_sems.at[x]))
+        copies[-1].start()
+    for copy in copies:
+        copy.wait()
 
 
 def channelize(ids, x):
@@ -151,14 +157,16 @@
         channelize_kernel,
         out_shape=jax.ShapeDtypeStruct((NX * NZ, 2, LOCAL, SPECTRA), BF16),
         in_specs=[pl.BlockSpec(memory_space=pltpu.SMEM), pl.BlockSpec(memory_space=pltpu.HBM)],
-        out_specs=in_vmem,
+        out_specs=pl.BlockSpec(memory_space=pltpu.HBM),
         scratch_shapes=[
             pltpu.VMEM(x.shape, BF16),
+            pltpu.VMEM((NX * NZ, 2, LOCAL, SPECTRA), BF16),
             pltpu.VMEM((256, SPAN), F32),
             pltpu.VMEM((SPAN, 256), BF16),
             pltpu.VMEM((ROWS, LOCAL, 256), F32),
             pltpu.VMEM((RC, LOCAL, SPECTRA), F32),
             pltpu.SemaphoreType.DMA((CHUNKS,)),
+            pltpu.SemaphoreType.DMA((NX,)),
         ],
         compiler_params=params(58),
         cost_estimate=cost(8),
@@ -345,7 +353,8 @@
     return jnp.where(row == source, 1.0, 0.0).astype(BF16)
 
 
-def arrange_kernel(mine_ref, theirs_ref, place_ref, flat):
+def arrange_kernel(mine_ref, theirs_ref, place_ref, flat, done):
+    done[...] = jnp.zeros((8, 128), F32)
     rows = []
     for x in range(NX):
         parts = []
@@ -353,21 +362,24 @@
             parts += [mine_ref[x * NZ + z], theirs_ref[x * NZ + z]]
         rows.append(jnp.concatenate(parts, axis=1))
     got = dot_nn(jnp.concatenate(rows, axis=0), place_ref[...])
-    flat[...] = got.reshape(NX, GROUP, 2 * SHARE, NY * 256)
+    flat[...] = got.astype(BF16).reshape(NX, GROUP, 2 * SHARE, NY * 256)
 
 
 def arrange(mine, theirs, place):
     return pl.pallas_call(
         arrange_kernel,
-        out_shape=jax.ShapeDtypeStruct((NX, GROUP, 2 * SHARE, NY * 256), F32),
+        out_shape=[
+            jax.ShapeDtypeStruct((NX, GROUP, 2 * SHARE, NY * 256), BF16),
+            jax.ShapeDtypeStruct((8, 128), F32),
+        ],
         in_specs=[in_vmem] * 3,
-        out_specs=in_vmem,
+        out_specs=[in_vmem] * 2,
         compiler_params=params(16),
         cost_estimate=cost(4),
     )(mine, theirs, place)
 
 
-def final_kernel(flat, own_ref, far_ref, core_ref, o_hbm, basis, result, sems):
+def final_kernel(flat, own_ref, far_ref, core_ref, done_ref, o_hbm, basis, result, sems):
     lane = lax.broadcasted_iota(jnp.int32, (2 * KDIM, 128), 1) // 32
     is_zero = core_ref[1] == 0
     wide = NY * 256
@@ -393,7 +405,7 @@
                 for k, part in enumerate((left, right)):
                     basis[z, :, at + k * 128 : at + (k + 1) * 128] = split3(part)
             pieces = basis[z, :, x * wide : (x + 1) * wide]
-            block = flat[x, z].astype(BF16)
+            block = flat[x, z]
             right = jnp.concatenate([pieces, block, jnp.zeros((32, wide), BF16)], axis=0)
             products = products + dot_nt(pieces, right)
         g_re, g_im = gram_from(products)
@@ -436,7 +448,7 @@
             lanes = slice(x * wide, (x + 1) * wide)
             pieces = basis[z, :, lanes]
             right = jnp.concatenate([pieces, pieces[0:32], pieces[0:16]], axis=0)
-            rest = flat[x, z] - dot_tn(lefts[z], right)[0 : 2 * SHARE]
+            rest = flat[x, z].astype(F32) - dot_tn(lefts[z], right)[0 : 2 * SHARE]
             result[0, z, :, lanes] = rest[0:SHARE]
             result[1, z, :, lanes] = rest[SHARE:]
         for r in range(2):
@@ -448,11 +460,11 @@
         copy.wait()
 
 
-def finish(flat, own, far, at):
+def finish(flat, own, far, at, done):
     return pl.pallas_call(
         final_kernel,
         out_shape=jax.ShapeDtypeStruct((2, GROUP, SHARE, INPUTS), F32),
-        in_specs=[in_vmem] * 3 + [pl.BlockSpec(memory_space=pltpu.SMEM)],
+        in_specs=[in_vmem] * 3 + [pl.BlockSpec(memory_space=pltpu.SMEM), in_vmem],
         out_specs=pl.BlockSpec(memory_space=pltpu.HBM),
         scratch_shapes=[
             pltpu.VMEM((GROUP, 6 * KDIM, INPUTS), BF16),
@@ -461,7 +473,7 @@
         ],
         compiler_params=params(16),
         cost_estimate=cost(6),
-    )(flat, own, far, at)
+    )(flat, own, far, at, done)
 
 
 def turned_by(count, distance):
@@ -499,9 +511,10 @@
     (many,) = step(2, v, z, sums[:3] + [tail])
     own = lax.all_to_all(many, ("y", "z"), 0, 0, tiled=True)
     mine, theirs = blocks[:, 0], lax.ppermute(blocks[:, 1], "core", turned_by(NC, 1))
-    flat = arrange(mine, theirs, place)
+    flat, done = arrange(mine, theirs, place)
+    own, done = lax.optimization_barrier((own, done))
     far = lax.ppermute(own, "core", turned_by(NC, 1))
-    return finish(flat, own, far, at)
+    return finish(flat, own, far, at, done)
 
 
 def solution(mesh):

time: 105 us -> 105 us (level)
  starting transfers between devices: 46.2 us -> 48 us
  waiting for transfers between devices: 24.7 us -> 23.2 us
    all_to_all x1, waiting for transfers between devices: 6.66 us -> 3.66 us  [body(): own = lax.all_to_all(many, ('y', 'z'), 0, 0, tiled=True)]
    ppermute x1, waiting for transfers between devices: 0.01 us -> 1.54 us  [body(): far = lax.ppermute(own, 'core', turned_by(NC, 1))]
    ppermute x9, starting transfers between devices: 10.6 us -> 11.8 us  [sums_over(): return [s] + [lax.ppermute(s, 'y', turned_by(NY, d)) for d in range(1, NY)]]
  transfers between devices with their start and end apart: 20 -> 20, of which waited for: 10 -> 11; matrix products, arithmetic and copies ran while one was open for 4% -> 4% of each run, Pallas kernels for 9% -> 9%
where the time goes in v7:
time: 105 us; the launch traced here: 104 us
  starting transfers between devices  48 us (46%)
  Pallas kernels  26.9 us (26%)
  waiting for transfers between devices  23.2 us (22%)
  local copies, waits for them, and re-layouts  5.38 us (5%)
    ppermute x9, starting transfers between devices, sums_over(): return [s] + [lax.ppermute(s, 'y', turned_by(NY, d)) for d in range(1, NY)]  11.8 us
    pallas_call x1, Pallas kernels, channelize(): pl.pallas_call(channelize_kernel, out_shape=jax.ShapeDtypeStruct((NX * NZ...  10.2 us
    all_to_all x1, starting transfers between devices, body(): v = lax.all_to_all(parcels, ('x', 'z'), 0, 0, tiled=True)  8.44 us
    all_to_all x1, waiting for transfers between devices, body(): v = lax.all_to_all(parcels, ('x', 'z'), 0, 0, tiled=True)  7.68 us
    ppermute x3, starting transfers between devices, core_sum(): return s + lax.ppermute(s, 'core', turned_by(NC, 1))  7.17 us
    ppermute x9, waiting for transfers between devices, sums_over(): return [s] + [lax.ppermute(s, 'y', turned_by(NY, d)) for d in range(1, NY)]  6.67 us
    all_to_all x1, starting transfers between devices, body(): own = lax.all_to_all(many, ('y', 'z'), 0, 0, tiled=True)  6.23 us
    ppermute x3, starting transfers between devices, body(): lax.ppermute(parts[d], 'y', turned_by(NY, d))  4.99 us
  transfers between devices with their start and end apart: 20, of which 11 were waited for; matrix products, arithmetic and copies ran while one was open for 4% of the time, Pallas kernels for 9%

profile of v7, /device:TPU:1, one launch (start us, length us, event | category | flops | bytes accessed | tf_op | source)
XLA Modules:
  0.0 104.5 jit_solution(9464606460237293256)
XLA Ops:
  0.0 10.2 %shard_map.37.v_ref = bf16[16,2,32,768]{3,2,1,0:T(8,128)(2,1)} custom-call(s32[12]{0:T(128)} %ids_ref.1, bf16[32,98688]{1,0:T(8,128)(2,1)} %x_hbm.1), custom_call_target="tpu_custom_call" | custom-call | flops 7200000000 | bytes 24000000 | tf_op jit(solution)/shard_map/pallas_call | solution.py:156
  10.2 8.4 %all-to-all-start = ((bf16[16,2,32,768]{3,2,1,0:T(8,128)(2,1)}), bf16[16,2,32,768]{3,2,1,0:T(8,128)(2,1)S(1)}, u32[]{:S(2)}, u32[]{:S(2)}) async-start(bf16[16,2,32,768]{3,2,1,0:T(8,128)(2,1)} %shard_map.37.v_ref), calls=%async_computation | async-start | bytes 3145728 | tf_op jit(solution)/shard_map/all_to_all | solution.py:495
  18.6 0.1 pad_add_fusion.y_ref.at_ref.core_ref
  18.7 1.4 %copy-done = bf16[16,2,32,768]{3,2,1,0:T(8,128)(2,1)S(1)} copy-done((bf16[16,2,32,768]{3,2,1,0:T(8,128)(2,1)S(1)}, bf16[16,2,32,768]{3,2,1,0:T(8,128)(2,1)}, u32[]{:S(2)}) %copy-start) | copy-done | bytes 1572888
  20.1 2.6 %shard_map.41 = (bf16[2,24,32,128]{3,2,1,0:T(8,128)(2,1)S(1)}, bf16[2,24,32,128]{3,2,1,0:T(8,128)(2,1)}, bf16[2,24,32,128]{3,2,1,0:T(8,128)(2,1)S(1)}, bf16[2,24,32,128]{3,2,1,0:T(8,128)(2,1)S(1)}) custom-call(s32[2]{0:T(128)S(1)} %pad_add_fusion.y_ref.at_ref.core_ref, bf16[16,2,32,768]{3,2,1,0:T(8,128)(2,1)S(1)} %copy-done), custom_call_target="tpu_custom_call" | custom-call | flops 3600000000 | bytes 12000000 | tf_op jit(solution)/shard_map/pallas_call | solution.py:197
  22.7 0.8 copy-done.1
  23.5 1.3 %collective-permute-start.10 = (bf16[2,24,32,128]{3,2,1,0:T(8,128)(2,1)}, bf16[2,24,32,128]{3,2,1,0:T(8,128)(2,1)S(1)}, u32[]{:S(2)}, u32[]{:S(2)}) collective-permute-start(bf16[2,24,32,128]{3,2,1,0:T(8,128)(2,1)} %get-tuple-element.24), channel_id=1, source_target_pairs={{0,8},{8,16},{16,24},{24,0},{1,9},{9,17},{17,25},{25,1},{2,10},{10... | collective-permute-start | bytes 1179656 | tf_op jit(solution)/shard_map/ppermute | solution.py:497
  24.8 2.6 %collective-permute-start.11 = (bf16[2,24,32,128]{3,2,1,0:T(8,128)(2,1)S(1)}, bf16[2,24,32,128]{3,2,1,0:T(8,128)(2,1)S(1)}, u32[]{:S(2)}, u32[]{:S(2)}) collective-permute-start(bf16[2,24,32,128]{3,2,1,0:T(8,128)(2,1)S(1)} %get-tuple-element.25), channel_id=1, source_target_pairs={{0,16},{8,24},{16,0},{24,8},{1,17},{9,25},{17,1},{25,9},{2,18},{10... | collective-permute-start | bytes 1179656 | tf_op jit(solution)/shard_map/ppermute | solution.py:497
  27.4 1.1 %collective-permute-start.12 = (bf16[2,24,32,128]{3,2,1,0:T(8,128)(2,1)S(1)}, bf16[2,24,32,128]{3,2,1,0:T(8,128)(2,1)}, u32[]{:S(2)}, u32[]{:S(2)}) collective-permute-start(bf16[2,24,32,128]{3,2,1,0:T(8,128)(2,1)S(1)} %get-tuple-element.26), channel_id=1, source_target_pairs={{0,24},{8,0},{16,8},{24,16},{1,25},{9,1},{17,9},{25,17},{2,26},{10... | collective-permute-start | bytes 1179656 | tf_op jit(solution)/shard_map/ppermute | solution.py:497
  28.4 1.9 %reshape.9 = f32[16,4,4,4,2,32]{5,4,3,2,1,0:T(2,128)} reshape(f32[2,8,4096]{2,1,0:T(8,128)S(1)} %copy-done.3) | data formatting | bytes 524288 | tf_op jit(solution)/shard_map/reshape | solution.py:499
  30.3 1.1 %constant_dynamic-slice_fusion = f32[16,4,1,4,1,32]{5,4,3,2,1,0:T(1,128)S(1)} fusion(f32[16,4,4,4,2,32]{5,4,3,2,1,0:T(2,128)} %reshape.9, s32[]{:T(128)S(6)} %select_n.51, s32[]{:T(128)S(6)} %select_n.53), kind=kLoop, calls=%fused_computation.52 | loop fusion | bytes 65544 | tf_op jit(solution)/shard_map/jit(dynamic_index_in_dim)/dynamic_slice | solution.py:501
  31.4 0.1 reshape.10.q_ref.z_ref
  31.6 7.7 %all-to-all-done.v_ref = bf16[16,2,32,768]{3,2,1,0:T(8,128)(2,1)S(1)} async-done(((bf16[16,2,32,768]{3,2,1,0:T(8,128)(2,1)}), bf16[16,2,32,768]{3,2,1,0:T(8,128)(2,1)S(1)}, u32[]{:S(2)}, u32[]{:S(2)}) %all-to-all-start) | async-done | bytes 1572896 | tf_op jit(solution)/shard_map/all_to_all | solution.py:495
  39.2 0.3 shard_map.38
  39.6 4.2 %collective-permute-start = (f32[16,768]{1,0:T(8,128)S(1)}, f32[16,768]{1,0:T(8,128)S(1)}, u32[]{:S(2)}, u32[]{:S(2)}) collective-permute-start(f32[16,768]{1,0:T(8,128)S(1)} %shard_map.38), channel_id=1, source_target_pairs={{0,1},{1,0},{2,3},{3,2},{4,5},{5,4},{6,7},{7,6},{8,9},{9,8},{10,11... | collective-permute-start | bytes 147464 | tf_op jit(solution)/shard_map/ppermute | solution.py:488
  43.7 0.9 collective-permute-done
  44.6 1.3 %collective-permute-start.1 = (f32[16,768]{1,0:T(8,128)S(1)}, f32[16,768]{1,0:T(8,128)S(1)}, u32[]{:S(2)}, u32[]{:S(2)}) collective-permute-start(f32[16,768]{1,0:T(8,128)S(1)} %add.69.s0), channel_id=1, source_target_pairs={{0,8},{8,16},{16,24},{24,0},{1,9},{9,17},{17,25},{25,1},{2,10},{10... | collective-permute-start | bytes 147464 | tf_op jit(solution)/shard_map/ppermute | solution.py:484
  45.9 2.6 %collective-permute-start.2 = (f32[16,768]{1,0:T(8,128)S(1)}, f32[16,768]{1,0:T(8,128)S(1)}, u32[]{:S(2)}, u32[]{:S(2)}) collective-permute-start(f32[16,768]{1,0:T(8,128)S(1)} %add.69.s0), channel_id=1, source_target_pairs={{0,16},{8,24},{16,0},{24,8},{1,17},{9,25},{17,1},{25,9},{2,18},{10... | collective-permute-start | bytes 147464 | tf_op jit(solution)/shard_map/ppermute | solution.py:484
  48.5 0.0 collective-permute-done.10.refs_1_
  48.5 1.1 %collective-permute-start.3 = (f32[16,768]{1,0:T(8,128)S(1)}, f32[16,768]{1,0:T(8,128)S(1)}, u32[]{:S(2)}, u32[]{:S(2)}) collective-permute-start(f32[16,768]{1,0:T(8,128)S(1)} %add.69.s0), channel_id=1, source_target_pairs={{0,24},{8,0},{16,8},{24,16},{1,25},{9,1},{17,9},{25,17},{2,26},{10... | collective-permute-start | bytes 147464 | tf_op jit(solution)/shard_map/ppermute | solution.py:484
  49.6 2.7 %shard_map.42 = bf16[16,2,144,128]{3,2,1,0:T(8,128)(2,1)} custom-call(s32[2]{0:T(128)S(1)} %pad_add_fusion.y_ref.at_ref.core_ref, bf16[2,24,32,128]{3,2,1,0:T(8,128)(2,1)S(1)} %copy-done.2, bf16[2,24,32,128]{3,2,1,0:T(8,128)(2,1)S(1)} %collective-permute-done.10.refs_1_, bf16[2,24,32,128]{3,2,1,0:T(8,128)(2,1)S(1)} %collective-permute-done.11.refs_2_, ...), custom_call_target="tpu_custom_call" | custom-call | flops 2700000000 | bytes 9000000 | tf_op jit(solution)/shard_map/pallas_call | solution.py:234
  52.3 3.7 %all-to-all-start.1 = ((bf16[16,2,144,128]{3,2,1,0:T(8,128)(2,1)}), bf16[16,2,144,128]{3,2,1,0:T(8,128)(2,1)S(1)}, u32[]{:S(2)}, u32[]{:S(2)}) async-start(bf16[16,2,144,128]{3,2,1,0:T(8,128)(2,1)} %shard_map.42), calls=%async_computation.1 | async-start | bytes 2359296 | tf_op jit(solution)/shard_map/all_to_all | solution.py:505
  56.0 1.1 %shard_map.39 = (f32[16,512]{1,0:T(8,128)S(1)}, f32[16,896]{1,0:T(8,128)S(1)}) custom-call(bf16[16,2,32,768]{3,2,1,0:T(8,128)(2,1)S(1)} %all-to-all-done.v_ref, f32[16,512]{1,0:T(8,128)S(1)} %reshape.10.q_ref.z_ref, f32[16,768]{1,0:T(8,128)S(1)} %add.69.s0, f32[16,768]{1,0:T(8,128)S(1)} %collective-permute-done.1.s1, ...), custom_call_target="tpu_custom_call" | custom-call | flops 4499999744 | bytes 15000000 | tf_op jit(solution)/shard_map/pallas_call | solution.py:337
  57.1 1.4 %collective-permute-start.4 = (f32[16,896]{1,0:T(8,128)S(1)}, f32[16,896]{1,0:T(8,128)S(1)}, u32[]{:S(2)}, u32[]{:S(2)}) collective-permute-start(f32[16,896]{1,0:T(8,128)S(1)} %get-tuple-element.21), channel_id=1, source_target_pairs={{0,1},{1,0},{2,3},{3,2},{4,5},{5,4},{6,7},{7,6},{8,9},{9,8},{10,11... | collective-permute-start | bytes 172040 | tf_op jit(solution)/shard_map/ppermute | solution.py:488
  58.5 0.9 collective-permute-done.4
  59.4 0.4 collective-permute-start.5
  59.9 0.7 collective-permute-start.6
  60.6 1.9 %collective-permute-start.7 = (f32[16,896]{1,0:T(8,128)S(1)}, f32[16,896]{1,0:T(8,128)S(1)}, u32[]{:S(2)}, u32[]{:S(2)}) collective-permute-start(f32[16,896]{1,0:T(8,128)S(1)} %add.70.s0), channel_id=1, source_target_pairs={{0,24},{8,0},{16,8},{24,16},{1,25},{9,1},{17,9},{25,17},{2,26},{10... | collective-permute-start | bytes 172040 | tf_op jit(solution)/shard_map/ppermute | solution.py:484
  62.5 1.5 %collective-permute-done.5.s1 = f32[16,896]{1,0:T(8,128)S(1)} collective-permute-done((f32[16,896]{1,0:T(8,128)S(1)}, f32[16,896]{1,0:T(8,128)S(1)}, u32[]{:S(2)}, u32[]{:S(2)}) %collective-permute-start.5) | collective-permute-done | bytes 57376 | tf_op jit(solution)/shard_map/ppermute | solution.py:484
  64.0 0.7 collective-permute-done.6.s2
  64.7 0.6 collective-permute-done.7.s3
  65.3 1.7 %shard_map.40 = (f32[16,512]{1,0:T(8,128)S(1)}, f32[16,896]{1,0:T(8,128)S(1)}) custom-call(bf16[16,2,32,768]{3,2,1,0:T(8,128)(2,1)S(1)} %all-to-all-done.v_ref, f32[16,512]{1,0:T(8,128)S(1)} %get-tuple-element.20.z_ref, f32[16,896]{1,0:T(8,128)S(1)} %add.70.s0, f32[16,896]{1,0:T(8,128)S(1)} %collective-permute-done.5.s1, ...), custom_call_target="tpu_custom_call" | custom-call | flops 4499999744 | bytes 15000000 | tf_op jit(solution)/shard_map/pallas_call | solution.py:337
  67.0 1.6 %collective-permute-start.8 = (f32[16,896]{1,0:T(8,128)S(1)}, f32[16,896]{1,0:T(8,128)S(1)}, u32[]{:S(2)}, u32[]{:S(2)}) collective-permute-start(f32[16,896]{1,0:T(8,128)S(1)} %get-tuple-element.22), channel_id=1, source_target_pairs={{0,1},{1,0},{2,3},{3,2},{4,5},{5,4},{6,7},{7,6},{8,9},{9,8},{10,11... | collective-permute-start | bytes 172040 | tf_op jit(solution)/shard_map/ppermute | solution.py:488
  68.5 0.9 collective-permute-done.8
  69.4 2.4 %collective-permute-start.9 = (f32[16,896]{1,0:T(8,128)S(1)}, f32[16,896]{1,0:T(8,128)S(1)}, u32[]{:S(2)}, u32[]{:S(2)}) collective-permute-start(f32[16,896]{1,0:T(8,128)S(1)} %add.71.s0), channel_id=1, source_target_pairs={{0,24},{8,0},{16,8},{24,16},{1,25},{9,1},{17,9},{25,17},{2,26},{10... | collective-permute-start | bytes 172040 | tf_op jit(solution)/shard_map/ppermute | solution.py:484
  71.8 1.3 %collective-permute-start.15 = (f32[16,896]{1,0:T(8,128)S(1)}, f32[16,896]{1,0:T(8,128)S(1)}, u32[]{:S(2)}, u32[]{:S(2)}) collective-permute-start(f32[16,896]{1,0:T(8,128)S(1)} %add.71.s0), channel_id=1, source_target_pairs={{0,16},{8,24},{16,0},{24,8},{1,17},{9,25},{17,1},{25,9},{2,18},{10... | collective-permute-start | bytes 172040 | tf_op jit(solution)/shard_map/ppermute | solution.py:484
  73.1 3.9 %collective-permute-done.14.s1 = f32[16,896]{1,0:T(8,128)S(1)} collective-permute-done((f32[16,896]{1,0:T(8,128)S(1)}, f32[16,896]{1,0:T(8,128)S(1)}, u32[]{:S(2)}, u32[]{:S(2)}) %collective-permute-start.14) | collective-permute-done | bytes 57376 | tf_op jit(solution)/shard_map/ppermute | solution.py:484
  77.1 2.1 %shard_map.44 = f32[16,16,512]{2,1,0:T(8,128)} custom-call(bf16[16,2,32,768]{3,2,1,0:T(8,128)(2,1)S(1)} %all-to-all-done.v_ref, f32[16,512]{1,0:T(8,128)S(1)} %get-tuple-element.30.z_ref, f32[16,896]{1,0:T(8,128)S(1)} %add.71.s0, f32[16,896]{1,0:T(8,128)S(1)} %collective-permute-done.14.s1, f32[16,896]{1,0:T(8,128)S(1)} %collective-permute-done.15.s2, ...), custom_call_target="tpu_custom_call" | custom-call | flops 4499999744 | bytes 15000000 | tf_op jit(solution)/shard_map/pallas_call | solution.py:337
  79.1 6.2 %all-to-all-start.2 = ((f32[16,16,512]{2,1,0:T(8,128)}), f32[16,16,512]{2,1,0:T(8,128)S(1)}, u32[]{:S(2)}, u32[]{:S(2)}) async-start(f32[16,16,512]{2,1,0:T(8,128)} %shard_map.44), calls=%async_computation.2 | async-start | bytes 1048576 | tf_op jit(solution)/shard_map/all_to_all | solution.py:512
  85.4 0.1 slice_bitcast_fusion
  85.5 2.5 %collective-permute-start.13 = (bf16[16,144,128]{2,1,0:T(8,128)(2,1)S(1)}, bf16[16,144,128]{2,1,0:T(8,128)(2,1)S(1)}, u32[]{:S(2)}, u32[]{:S(2)}) collective-permute-start(bf16[16,144,128]{2,1,0:T(8,128)(2,1)S(1)} %get-tuple-element.35), channel_id=1, source_target_pairs={{0,1},{1,0},{2,3},{3,2},{4,5},{5,4},{6,7},{7,6},{8,9},{9,8},{10,11... | collective-permute-start | bytes 1769480 | tf_op jit(solution)/shard_map/ppermute | solution.py:513
  87.9 0.6 select_convert_fusion.place_ref
  88.6 1.0 collective-permute-done.13.theirs_ref
  89.5 1.4 %shard_map.43 = (bf16[4,3,48,1024]{3,2,1,0:T(8,128)(2,1)S(1)}, f32[8,128]{1,0:T(8,128)S(1)}) custom-call(bf16[16,144,128]{2,1,0:T(8,128)(2,1)S(1)} %get-tuple-element.36.mine_ref, bf16[16,144,128]{2,1,0:T(8,128)(2,1)S(1)} %collective-permute-done.13.theirs_ref, bf16[1024,1024]{1,0:T(8,128)(2,1)S(1)} %select_convert_fusion.place_ref), custom_call_target="tpu_custom_call" | custom-call | flops 3600000000 | bytes 12000000 | tf_op jit(solution)/shard_map/pallas_call | solution.py:369
  90.9 3.7 %all-to-all-done.2.own_ref = f32[16,16,512]{2,1,0:T(8,128)S(1)} async-done(((f32[16,16,512]{2,1,0:T(8,128)}), f32[16,16,512]{2,1,0:T(8,128)S(1)}, u32[]{:S(2)}, u32[]{:S(2)}) %all-to-all-start.2) | async-done | bytes 524320 | tf_op jit(solution)/shard_map/all_to_all | solution.py:512
  94.6 3.2 %collective-permute-start.16 = (f32[16,16,512]{2,1,0:T(8,128)S(1)}, f32[16,16,512]{2,1,0:T(8,128)S(1)}, u32[]{:S(2)}, u32[]{:S(2)}) collective-permute-start(f32[16,16,512]{2,1,0:T(8,128)S(1)} %all-to-all-done.2.own_ref), channel_id=1, source_target_pairs={{0,1},{1,0},{2,3},{3,2},{4,5},{5,4},{6,7},{7,6},{8,9},{9,8},{10,11... | collective-permute-start | bytes 1572872 | tf_op jit(solution)/shard_map/ppermute | solution.py:516
  97.8 1.5 %collective-permute-done.16.far_ref = f32[16,16,512]{2,1,0:T(8,128)S(1)} collective-permute-done((f32[16,16,512]{2,1,0:T(8,128)S(1)}, f32[16,16,512]{2,1,0:T(8,128)S(1)}, u32[]{:S(2)}, u32[]{:S(2)}) %collective-permute-start.16) | collective-permute-done | bytes 524320 | tf_op jit(solution)/shard_map/ppermute | solution.py:516
  99.4 4.9 %shard_map.45 = f32[2,3,24,4096]{3,2,1,0:T(8,128)} custom-call(bf16[4,3,48,1024]{3,2,1,0:T(8,128)(2,1)S(1)} %get-tuple-element.29.flat, f32[16,16,512]{2,1,0:T(8,128)S(1)} %all-to-all-done.2.own_ref, f32[16,16,512]{2,1,0:T(8,128)S(1)} %collective-permute-done.16.far_ref, s32[2]{0:T(128)S(1)} %pad_add_fusion.y_ref.at_ref.core_ref, ...), custom_call_target="tpu_custom_call" | custom-call | flops 5400000000 | bytes 18000000 | tf_op jit(solution)/shard_map/pallas_call | solution.py:464
  (24 shorter events, 0.1 us)
Async XLA Ops:
  10.2 29.1 %all-to-all-start = ((bf16[16,2,32,768]{3,2,1,0:T(8,128)(2,1)}), bf16[16,2,32,768]{3,2,1,0:T(8,128)(2,1)S(1)}, u32[]{:S(2)}, u32[]{:S(2)}) async-start(bf16[16,2,32,768]{3,2,1,0:T(8,128)(2,1)} %shard_map.37.v_ref), calls=%async_computation | async-start | bytes 3145728 | tf_op jit(solution)/shard_map/all_to_all | solution.py:495
  18.7 1.4 %copy-start = (bf16[16,2,32,768]{3,2,1,0:T(8,128)(2,1)S(1)}, bf16[16,2,32,768]{3,2,1,0:T(8,128)(2,1)}, u32[]{:S(2)}) copy-start(bf16[16,2,32,768]{3,2,1,0:T(8,128)(2,1)} %shard_map.37.v_ref) | copy-start | bytes 4718596
  20.1 8.3 %copy-start.3 = (f32[2,8,4096]{2,1,0:T(8,128)S(1)}, f32[2,8,4096]{2,1,0:T(8,128)}, u32[]{:S(2)}) copy-start(f32[2,8,4096]{2,1,0:T(8,128)} %param.5) | copy-start | bytes 786436
  22.7 0.8 copy-start.1
  23.5 25.1 %collective-permute-start.10 = (bf16[2,24,32,128]{3,2,1,0:T(8,128)(2,1)}, bf16[2,24,32,128]{3,2,1,0:T(8,128)(2,1)S(1)}, u32[]{:S(2)}, u32[]{:S(2)}) collective-permute-start(bf16[2,24,32,128]{3,2,1,0:T(8,128)(2,1)} %get-tuple-element.24), channel_id=1, source_target_pairs={{0,8},{8,16},{16,24},{24,0},{1,9},{9,17},{17,25},{25,1},{2,10},{10... | collective-permute-start | bytes 1179656 | tf_op jit(solution)/shard_map/ppermute | solution.py:497
  24.8 24.9 %collective-permute-start.11 = (bf16[2,24,32,128]{3,2,1,0:T(8,128)(2,1)S(1)}, bf16[2,24,32,128]{3,2,1,0:T(8,128)(2,1)S(1)}, u32[]{:S(2)}, u32[]{:S(2)}) collective-permute-start(bf16[2,24,32,128]{3,2,1,0:T(8,128)(2,1)S(1)} %get-tuple-element.25), channel_id=1, source_target_pairs={{0,16},{8,24},{16,0},{24,8},{1,17},{9,25},{17,1},{25,9},{2,18},{10... | collective-permute-start | bytes 1179656 | tf_op jit(solution)/shard_map/ppermute | solution.py:497
  27.4 22.2 %collective-permute-start.12 = (bf16[2,24,32,128]{3,2,1,0:T(8,128)(2,1)S(1)}, bf16[2,24,32,128]{3,2,1,0:T(8,128)(2,1)}, u32[]{:S(2)}, u32[]{:S(2)}) collective-permute-start(bf16[2,24,32,128]{3,2,1,0:T(8,128)(2,1)S(1)} %get-tuple-element.26), channel_id=1, source_target_pairs={{0,24},{8,0},{16,8},{24,16},{1,25},{9,1},{17,9},{25,17},{2,26},{10... | collective-permute-start | bytes 1179656 | tf_op jit(solution)/shard_map/ppermute | solution.py:497
  39.2 10.4 %copy-start.2 = (bf16[2,24,32,128]{3,2,1,0:T(8,128)(2,1)S(1)}, bf16[2,24,32,128]{3,2,1,0:T(8,128)(2,1)}, u32[]{:S(2)}) copy-start(bf16[2,24,32,128]{3,2,1,0:T(8,128)(2,1)} %copy-done.1) | copy-start | bytes 1179652
  39.6 5.0 %collective-permute-start = (f32[16,768]{1,0:T(8,128)S(1)}, f32[16,768]{1,0:T(8,128)S(1)}, u32[]{:S(2)}, u32[]{:S(2)}) collective-permute-start(f32[16,768]{1,0:T(8,128)S(1)} %shard_map.38), channel_id=1, source_target_pairs={{0,1},{1,0},{2,3},{3,2},{4,5},{5,4},{6,7},{7,6},{8,9},{9,8},{10,11... | collective-permute-start | bytes 147464 | tf_op jit(solution)/shard_map/ppermute | solution.py:488
  44.6 11.4 %collective-permute-start.1 = (f32[16,768]{1,0:T(8,128)S(1)}, f32[16,768]{1,0:T(8,128)S(1)}, u32[]{:S(2)}, u32[]{:S(2)}) collective-permute-start(f32[16,768]{1,0:T(8,128)S(1)} %add.69.s0), channel_id=1, source_target_pairs={{0,8},{8,16},{16,24},{24,0},{1,9},{9,17},{17,25},{25,1},{2,10},{10... | collective-permute-start | bytes 147464 | tf_op jit(solution)/shard_map/ppermute | solution.py:484
  45.9 10.1 %collective-permute-start.2 = (f32[16,768]{1,0:T(8,128)S(1)}, f32[16,768]{1,0:T(8,128)S(1)}, u32[]{:S(2)}, u32[]{:S(2)}) collective-permute-start(f32[16,768]{1,0:T(8,128)S(1)} %add.69.s0), channel_id=1, source_target_pairs={{0,16},{8,24},{16,0},{24,8},{1,17},{9,25},{17,1},{25,9},{2,18},{10... | collective-permute-start | bytes 147464 | tf_op jit(solution)/shard_map/ppermute | solution.py:484
  48.5 7.5 %collective-permute-start.3 = (f32[16,768]{1,0:T(8,128)S(1)}, f32[16,768]{1,0:T(8,128)S(1)}, u32[]{:S(2)}, u32[]{:S(2)}) collective-permute-start(f32[16,768]{1,0:T(8,128)S(1)} %add.69.s0), channel_id=1, source_target_pairs={{0,24},{8,0},{16,8},{24,16},{1,25},{9,1},{17,9},{25,17},{2,26},{10... | collective-permute-start | bytes 147464 | tf_op jit(solution)/shard_map/ppermute | solution.py:484
  52.3 20.8 %all-to-all-start.1 = ((bf16[16,2,144,128]{3,2,1,0:T(8,128)(2,1)}), bf16[16,2,144,128]{3,2,1,0:T(8,128)(2,1)S(1)}, u32[]{:S(2)}, u32[]{:S(2)}) async-start(bf16[16,2,144,128]{3,2,1,0:T(8,128)(2,1)} %shard_map.42), calls=%async_computation.1 | async-start | bytes 2359296 | tf_op jit(solution)/shard_map/all_to_all | solution.py:505
  57.1 2.3 %collective-permute-start.4 = (f32[16,896]{1,0:T(8,128)S(1)}, f32[16,896]{1,0:T(8,128)S(1)}, u32[]{:S(2)}, u32[]{:S(2)}) collective-permute-start(f32[16,896]{1,0:T(8,128)S(1)} %get-tuple-element.21), channel_id=1, source_target_pairs={{0,1},{1,0},{2,3},{3,2},{4,5},{5,4},{6,7},{7,6},{8,9},{9,8},{10,11... | collective-permute-start | bytes 172040 | tf_op jit(solution)/shard_map/ppermute | solution.py:488
  59.4 4.6 %collective-permute-start.5 = (f32[16,896]{1,0:T(8,128)S(1)}, f32[16,896]{1,0:T(8,128)S(1)}, u32[]{:S(2)}, u32[]{:S(2)}) collective-permute-start(f32[16,896]{1,0:T(8,128)S(1)} %add.70.s0), channel_id=1, source_target_pairs={{0,8},{8,16},{16,24},{24,0},{1,9},{9,17},{17,25},{25,1},{2,10},{10... | collective-permute-start | bytes 172040 | tf_op jit(solution)/shard_map/ppermute | solution.py:484
  59.9 4.8 %collective-permute-start.6 = (f32[16,896]{1,0:T(8,128)S(1)}, f32[16,896]{1,0:T(8,128)S(1)}, u32[]{:S(2)}, u32[]{:S(2)}) collective-permute-start(f32[16,896]{1,0:T(8,128)S(1)} %add.70.s0), channel_id=1, source_target_pairs={{0,16},{8,24},{16,0},{24,8},{1,17},{9,25},{17,1},{25,9},{2,18},{10... | collective-permute-start | bytes 172040 | tf_op jit(solution)/shard_map/ppermute | solution.py:484
  60.6 4.7 %collective-permute-start.7 = (f32[16,896]{1,0:T(8,128)S(1)}, f32[16,896]{1,0:T(8,128)S(1)}, u32[]{:S(2)}, u32[]{:S(2)}) collective-permute-start(f32[16,896]{1,0:T(8,128)S(1)} %add.70.s0), channel_id=1, source_target_pairs={{0,24},{8,0},{16,8},{24,16},{1,25},{9,1},{17,9},{25,17},{2,26},{10... | collective-permute-start | bytes 172040 | tf_op jit(solution)/shard_map/ppermute | solution.py:484
  67.0 2.5 %collective-permute-start.8 = (f32[16,896]{1,0:T(8,128)S(1)}, f32[16,896]{1,0:T(8,128)S(1)}, u32[]{:S(2)}, u32[]{:S(2)}) collective-permute-start(f32[16,896]{1,0:T(8,128)S(1)} %get-tuple-element.22), channel_id=1, source_target_pairs={{0,1},{1,0},{2,3},{3,2},{4,5},{5,4},{6,7},{7,6},{8,9},{9,8},{10,11... | collective-permute-start | bytes 172040 | tf_op jit(solution)/shard_map/ppermute | solution.py:488
  69.4 3.7 %collective-permute-start.9 = (f32[16,896]{1,0:T(8,128)S(1)}, f32[16,896]{1,0:T(8,128)S(1)}, u32[]{:S(2)}, u32[]{:S(2)}) collective-permute-start(f32[16,896]{1,0:T(8,128)S(1)} %add.71.s0), channel_id=1, source_target_pairs={{0,24},{8,0},{16,8},{24,16},{1,25},{9,1},{17,9},{25,17},{2,26},{10... | collective-permute-start | bytes 172040 | tf_op jit(solution)/shard_map/ppermute | solution.py:484
  71.8 5.2 %collective-permute-start.14 = (f32[16,896]{1,0:T(8,128)S(1)}, f32[16,896]{1,0:T(8,128)S(1)}, u32[]{:S(2)}, u32[]{:S(2)}) collective-permute-start(f32[16,896]{1,0:T(8,128)S(1)} %add.71.s0), channel_id=1, source_target_pairs={{0,8},{8,16},{16,24},{24,0},{1,9},{9,17},{17,25},{25,1},{2,10},{10... | collective-permute-start | bytes 172040 | tf_op jit(solution)/shard_map/ppermute | solution.py:484
  71.8 5.2 %collective-permute-start.15 = (f32[16,896]{1,0:T(8,128)S(1)}, f32[16,896]{1,0:T(8,128)S(1)}, u32[]{:S(2)}, u32[]{:S(2)}) collective-permute-start(f32[16,896]{1,0:T(8,128)S(1)} %add.71.s0), channel_id=1, source_target_pairs={{0,16},{8,24},{16,0},{24,8},{1,17},{9,25},{17,1},{25,9},{2,18},{10... | collective-permute-start | bytes 172040 | tf_op jit(solution)/shard_map/ppermute | solution.py:484
  79.1 15.5 %all-to-all-start.2 = ((f32[16,16,512]{2,1,0:T(8,128)}), f32[16,16,512]{2,1,0:T(8,128)S(1)}, u32[]{:S(2)}, u32[]{:S(2)}) async-start(f32[16,16,512]{2,1,0:T(8,128)} %shard_map.44), calls=%async_computation.2 | async-start | bytes 1048576 | tf_op jit(solution)/shard_map/all_to_all | solution.py:512
  85.5 4.1 %collective-permute-start.13 = (bf16[16,144,128]{2,1,0:T(8,128)(2,1)S(1)}, bf16[16,144,128]{2,1,0:T(8,128)(2,1)S(1)}, u32[]{:S(2)}, u32[]{:S(2)}) collective-permute-start(bf16[16,144,128]{2,1,0:T(8,128)(2,1)S(1)} %get-tuple-element.35), channel_id=1, source_target_pairs={{0,1},{1,0},{2,3},{3,2},{4,5},{5,4},{6,7},{7,6},{8,9},{9,8},{10,11... | collective-permute-start | bytes 1769480 | tf_op jit(solution)/shard_map/ppermute | solution.py:513
  94.6 4.8 %collective-permute-start.16 = (f32[16,16,512]{2,1,0:T(8,128)S(1)}, f32[16,16,512]{2,1,0:T(8,128)S(1)}, u32[]{:S(2)}, u32[]{:S(2)}) collective-permute-start(f32[16,16,512]{2,1,0:T(8,128)S(1)} %all-to-all-done.2.own_ref), channel_id=1, source_target_pairs={{0,1},{1,0},{2,3},{3,2},{4,5},{5,4},{6,7},{7,6},{8,9},{9,8},{10,11... | collective-permute-start | bytes 1572872 | tf_op jit(solution)/shard_map/ppermute | solution.py:516

commit v8 on v7

--- a/solution.py
+++ b/solution.py
@@ -298,13 +298,10 @@
     z_re = i_re * (1.0 / SPECTRA) + LOADING * q[0]
     z_im = i_im * (1.0 / SPECTRA) + LOADING * q[1]
     z = jnp.concatenate([z_re, z_im], axis=0)
+    outs[0][...] = z
     if step == 2:
-        (many_ref,) = outs
-        for d in range(NY * NZ):
-            many_ref[d] = z
         return
-    new_z, new_s = outs
-    new_z[...] = z
+    new_s = outs[1]
     pieces = split3(z)
     u_re, u_im = project(v, pieces)
     padded = jnp.concatenate([pieces, jnp.zeros((80, HELD), BF16)], axis=0)
@@ -327,13 +324,9 @@
 
 
 def step(at, v, z, sums):
-    if at == 2:
-        shapes = [jax.ShapeDtypeStruct((NY * NZ, 2 * KDIM, HELD), F32)]
-    else:
-        shapes = [
-            jax.ShapeDtypeStruct((2 * KDIM, HELD), F32),
-            jax.ShapeDtypeStruct((2 * KDIM, SPECTRA + 128), F32),
-        ]
+    shapes = [jax.ShapeDtypeStruct((2 * KDIM, HELD), F32)]
+    if at < 2:
+        shapes.append(jax.ShapeDtypeStruct((2 * KDIM, SPECTRA + 128), F32))
     return pl.pallas_call(
         functools.partial(step_kernel, at),
         out_shape=shapes,
@@ -379,17 +372,19 @@
     )(mine, theirs, place)
 
 
-def final_kernel(flat, own_ref, far_ref, core_ref, done_ref, o_hbm, basis, result, sems):
+def final_kernel(flat, *refs):
+    own_refs, far_refs = refs[0:NY], refs[NY : 2 * NY]
+    at_ref, _, o_hbm, basis, result, sems = refs[2 * NY :]
     lane = lax.broadcasted_iota(jnp.int32, (2 * KDIM, 128), 1) // 32
-    is_zero = core_ref[1] == 0
+    is_zero = at_ref[1] == 0
     wide = NY * 256
-    solved = []
-    for z in range(GROUP):
-        products = jnp.zeros((48, 128), F32)
-        for x in range(NX):
-            lanes = slice(x * 128, (x + 1) * 128)
-            for y in range(NY):
-                own, far = own_ref[y * NZ + z, :, lanes], far_ref[y * NZ + z, :, lanes]
+    for d in range(NY):
+        y = (at_ref[0] + NY - d) % NY
+        for z in range(GROUP):
+            from_z = (at_ref[2] + NZ - z) % NZ
+            for x in range(NX):
+                lanes = slice(x * 128, (x + 1) * 128)
+                own, far = own_refs[d][from_z, :, lanes], far_refs[d][from_z, :, lanes]
                 a, b = jnp.where(is_zero, own, far), jnp.where(is_zero, far, own)
                 left = jnp.where(
                     lane < 2,
@@ -401,9 +396,13 @@
                     jnp.where(lane == 0, pltpu.roll(a, 64, 1), pltpu.roll(b, 96, 1)),
                     jnp.where(lane == 2, pltpu.roll(a, 96, 1), b),
                 )
-                at = (x * NY + y) * 256
                 for k, part in enumerate((left, right)):
-                    basis[z, :, at + k * 128 : at + (k + 1) * 128] = split3(part)
+                    start = pl.multiple_of(x * wide + y * 256 + k * 128, 128)
+                    basis[z, :, pl.ds(start, 128)] = split3(part)
+    solved = []
+    for z in range(GROUP):
+        products = jnp.zeros((48, 128), F32)
+        for x in range(NX):
             pieces = basis[z, :, x * wide : (x + 1) * wide]
             block = flat[x, z]
             right = jnp.concatenate([pieces, block, jnp.zeros((32, wide), BF16)], axis=0)
@@ -464,7 +463,7 @@
     return pl.pallas_call(
         final_kernel,
         out_shape=jax.ShapeDtypeStruct((2, GROUP, SHARE, INPUTS), F32),
-        in_specs=[in_vmem] * 3 + [pl.BlockSpec(memory_space=pltpu.SMEM), in_vmem],
+        in_specs=[in_vmem] * (1 + 2 * NY) + [pl.BlockSpec(memory_space=pltpu.SMEM), in_vmem],
         out_specs=pl.BlockSpec(memory_space=pltpu.HBM),
         scratch_shapes=[
             pltpu.VMEM((GROUP, 6 * KDIM, INPUTS), BF16),
@@ -473,7 +472,7 @@
         ],
         compiler_params=params(16),
         cost_estimate=cost(6),
-    )(flat, own, far, at, done)
+    )(flat, *own, *far, at, done)
 
 
 def turned_by(count, distance):
@@ -490,30 +489,34 @@
 
 def body(voltages, channel_ids, start_basis):
     y, core = lax.axis_index("y"), lax.axis_index("core")
-    at = jnp.stack([y, core]).astype(jnp.int32)
+    at = jnp.stack([y, core, lax.axis_index("z")]).astype(jnp.int32)
     parcels = channelize(channel_ids, voltages)
     v = lax.all_to_all(parcels, ("x", "z"), 0, 0, tiled=True)
     parts = spread(at, parcels)
     parts = [parts[0]] + [lax.ppermute(parts[d], "y", turned_by(NY, d)) for d in range(1, NY)]
-    turned = turn(at, parts)
     split = start_basis.reshape(2 * KDIM, NX, NY, NZ, NC, LOCAL)
     split = lax.dynamic_index_in_dim(split, y, 2, keepdims=False)
     z = lax.dynamic_index_in_dim(split, core, 3, keepdims=False).reshape(2 * KDIM, HELD)
+    place = placing(y, core)
     s = core_sum(first(v, z))
+    sums = sums_over(s)
+    *parts, tail = lax.optimization_barrier((*parts, sums[3]))
+    z, s = step(0, v, z, sums[:3] + [tail])
+    turned = turn(at, parts)
+    s = core_sum(s)
     sums = sums_over(s)
     turned = lax.optimization_barrier((turned, s))[0]
     blocks = lax.all_to_all(turned, ("x", "z"), 0, 0, tiled=True)
-    place = placing(y, core)
-    z, s = step(0, v, z, sums)
-    z, s = step(1, v, z, sums_over(core_sum(s)))
-    sums = sums_over(core_sum(s))
-    tail, blocks = lax.optimization_barrier((sums[3], blocks))
-    (many,) = step(2, v, z, sums[:3] + [tail])
-    own = lax.all_to_all(many, ("y", "z"), 0, 0, tiled=True)
+    z, s = step(1, v, z, sums)
+    (z,) = step(2, v, z, sums_over(core_sum(s)))
     mine, theirs = blocks[:, 0], lax.ppermute(blocks[:, 1], "core", turned_by(NC, 1))
     flat, done = arrange(mine, theirs, place)
-    own, done = lax.optimization_barrier((own, done))
-    far = lax.ppermute(own, "core", turned_by(NC, 1))
+    along_z = [z] + [lax.ppermute(z, "z", turned_by(NZ, d)) for d in range(1, NZ)]
+    column = jnp.stack(along_z)
+    own = [column] + [lax.ppermute(column, "y", turned_by(NY, d)) for d in range(1, NY)]
+    *late, done = lax.optimization_barrier((*own[1:], done))
+    own = own[:1] + late
+    far = [lax.ppermute(part, "core", turned_by(NC, 1)) for part in own]
     return finish(flat, own, far, at, done)
 
 

time: 105 us -> 106 us (level)
  starting transfers between devices: 48 us -> 51 us
  waiting for transfers between devices: 23.2 us -> 20.5 us
  local copies, waits for them, and re-layouts: 5.38 us -> 6.6 us
    ppermute x1 -> x10, starting transfers between devices: 3.25 us -> 11.2 us  [the longest x3 5.05 us: body(): lax.ppermute(z, 'z', turned_by(NZ, d))]
    all_to_all x1 -> x0, starting transfers between devices: 6.23 us -> none  [body(): own = lax.all_to_all(many, ('y', 'z'), 0, 0, tiled=True)]
    all_to_all x1 -> x0, waiting for transfers between devices: 3.66 us -> none  [body(): own = lax.all_to_all(many, ('y', 'z'), 0, 0, tiled=True)]
    ppermute x1 -> x10, waiting for transfers between devices: 1.54 us -> 4.7 us  [the longest x3 3.67 us: body(): lax.ppermute(column, 'y', turned_by(NY, d))]
    squeeze x1, local copies, waits for them, and re-layouts: 0.08 us -> 1.32 us  [body(): blocks[:, 1]]
  transfers between devices with their start and end apart: 20 -> 28, of which waited for: 11 -> 14; matrix products, arithmetic and copies ran while one was open for 4% -> 5% of each run, Pallas kernels for 9% -> 9%
where the time goes in v8:
time: 106 us; the launch traced here: 105 us
  starting transfers between devices  51 us (48%)
  Pallas kernels  26.3 us (25%)
  waiting for transfers between devices  20.5 us (19%)
  local copies, waits for them, and re-layouts  6.6 us (6%)
    ppermute x9, starting transfers between devices, sums_over(): return [s] + [lax.ppermute(s, 'y', turned_by(NY, d)) for d in range(1, NY)]  11.8 us
    pallas_call x1, Pallas kernels, channelize(): pl.pallas_call(channelize_kernel, out_shape=jax.ShapeDtypeStruct((NX * NZ...  10.2 us
    all_to_all x1, starting transfers between devices, body(): v = lax.all_to_all(parcels, ('x', 'z'), 0, 0, tiled=True)  8.44 us
    all_to_all x1, waiting for transfers between devices, body(): v = lax.all_to_all(parcels, ('x', 'z'), 0, 0, tiled=True)  7.59 us
    ppermute x3, starting transfers between devices, core_sum(): return s + lax.ppermute(s, 'core', turned_by(NC, 1))  6.69 us
    ppermute x9, waiting for transfers between devices, sums_over(): return [s] + [lax.ppermute(s, 'y', turned_by(NY, d)) for d in range(1, NY)]  6.02 us
    pallas_call x1, Pallas kernels, finish(): pl.pallas_call(final_kernel, out_shape=jax.ShapeDtypeStruct((2, GROUP, SH...  5.56 us
    ppermute x3, starting transfers between devices, body(): lax.ppermute(z, 'z', turned_by(NZ, d))  5.05 us
  transfers between devices with their start and end apart: 28, of which 14 were waited for; matrix products, arithmetic and copies ran while one was open for 5% of the time, Pallas kernels for 9%

profile of v8, /device:TPU:1, one launch (start us, length us, event | category | flops | bytes accessed | tf_op | source)
XLA Modules:
  0.0 105.4 jit_solution(8050340456526729041)
XLA Ops:
  0.0 10.2 %shard_map.37.v_ref = bf16[16,2,32,768]{3,2,1,0:T(8,128)(2,1)} custom-call(s32[12]{0:T(128)} %ids_ref.1, bf16[32,98688]{1,0:T(8,128)(2,1)} %x_hbm.1), custom_call_target="tpu_custom_call" | custom-call | flops 7200000000 | bytes 24000000 | tf_op jit(solution)/shard_map/pallas_call | solution.py:156
  10.2 8.4 %all-to-all-start = ((bf16[16,2,32,768]{3,2,1,0:T(8,128)(2,1)}), bf16[16,2,32,768]{3,2,1,0:T(8,128)(2,1)S(1)}, u32[]{:S(2)}, u32[]{:S(2)}) async-start(bf16[16,2,32,768]{3,2,1,0:T(8,128)(2,1)} %shard_map.37.v_ref), calls=%async_computation | async-start | bytes 3145728 | tf_op jit(solution)/shard_map/all_to_all | solution.py:494
  18.7 1.4 %copy-done = bf16[16,2,32,768]{3,2,1,0:T(8,128)(2,1)S(1)} copy-done((bf16[16,2,32,768]{3,2,1,0:T(8,128)(2,1)S(1)}, bf16[16,2,32,768]{3,2,1,0:T(8,128)(2,1)}, u32[]{:S(2)}) %copy-start) | copy-done | bytes 1572888
  20.1 2.7 %shard_map.38 = (bf16[2,24,32,128]{3,2,1,0:T(8,128)(2,1)S(1)}, bf16[2,24,32,128]{3,2,1,0:T(8,128)(2,1)}, bf16[2,24,32,128]{3,2,1,0:T(8,128)(2,1)}, bf16[2,24,32,128]{3,2,1,0:T(8,128)(2,1)S(1)}) custom-call(s32[3]{0:T(128)S(1)} %pad_add_fusion.y_ref.at_ref.refs_8_, bf16[16,2,32,768]{3,2,1,0:T(8,128)(2,1)S(1)} %copy-done), custom_call_target="tpu_custom_call" | custom-call | flops 3600000000 | bytes 12000000 | tf_op jit(solution)/shard_map/pallas_call | solution.py:197
  22.8 0.7 copy-done.1
  23.5 1.3 %collective-permute-start = (bf16[2,24,32,128]{3,2,1,0:T(8,128)(2,1)}, bf16[2,24,32,128]{3,2,1,0:T(8,128)(2,1)S(1)}, u32[]{:S(2)}, u32[]{:S(2)}) collective-permute-start(bf16[2,24,32,128]{3,2,1,0:T(8,128)(2,1)} %get-tuple-element.26), channel_id=1, source_target_pairs={{0,8},{8,16},{16,24},{24,0},{1,9},{9,17},{17,25},{25,1},{2,10},{10... | collective-permute-start | bytes 1179656 | tf_op jit(solution)/shard_map/ppermute | solution.py:496
  24.8 2.6 %collective-permute-start.1 = (bf16[2,24,32,128]{3,2,1,0:T(8,128)(2,1)}, bf16[2,24,32,128]{3,2,1,0:T(8,128)(2,1)S(1)}, u32[]{:S(2)}, u32[]{:S(2)}) collective-permute-start(bf16[2,24,32,128]{3,2,1,0:T(8,128)(2,1)} %get-tuple-element.27), channel_id=1, source_target_pairs={{0,16},{8,24},{16,0},{24,8},{1,17},{9,25},{17,1},{25,9},{2,18},{10... | collective-permute-start | bytes 1179656 | tf_op jit(solution)/shard_map/ppermute | solution.py:496
  27.5 1.1 %collective-permute-start.2 = (bf16[2,24,32,128]{3,2,1,0:T(8,128)(2,1)S(1)}, bf16[2,24,32,128]{3,2,1,0:T(8,128)(2,1)S(1)}, u32[]{:S(2)}, u32[]{:S(2)}) collective-permute-start(bf16[2,24,32,128]{3,2,1,0:T(8,128)(2,1)S(1)} %get-tuple-element.28), channel_id=1, source_target_pairs={{0,24},{8,0},{16,8},{24,16},{1,25},{9,1},{17,9},{25,17},{2,26},{10... | collective-permute-start | bytes 1179656 | tf_op jit(solution)/shard_map/ppermute | solution.py:496
  28.5 1.9 %reshape.9 = f32[16,4,4,4,2,32]{5,4,3,2,1,0:T(2,128)} reshape(f32[2,8,4096]{2,1,0:T(8,128)S(1)} %copy-done.3) | data formatting | bytes 524288 | tf_op jit(solution)/shard_map/reshape | solution.py:497
  30.4 1.1 %constant_dynamic-slice_fusion = f32[16,4,1,4,1,32]{5,4,3,2,1,0:T(1,128)S(1)} fusion(f32[16,4,4,4,2,32]{5,4,3,2,1,0:T(2,128)} %reshape.9, s32[]{:T(128)S(6)} %select_n.51, s32[]{:T(128)S(6)} %select_n.53), kind=kLoop, calls=%fused_computation.53 | loop fusion | bytes 65544 | tf_op jit(solution)/shard_map/jit(dynamic_index_in_dim)/dynamic_slice | solution.py:499
  31.7 7.6 %all-to-all-done.v_ref = bf16[16,2,32,768]{3,2,1,0:T(8,128)(2,1)S(1)} async-done(((bf16[16,2,32,768]{3,2,1,0:T(8,128)(2,1)}), bf16[16,2,32,768]{3,2,1,0:T(8,128)(2,1)S(1)}, u32[]{:S(2)}, u32[]{:S(2)}) %all-to-all-start) | async-done | bytes 1572896 | tf_op jit(solution)/shard_map/all_to_all | solution.py:494
  39.6 4.2 %collective-permute-start.3 = (f32[16,768]{1,0:T(8,128)S(1)}, f32[16,768]{1,0:T(8,128)S(1)}, u32[]{:S(2)}, u32[]{:S(2)}) collective-permute-start(f32[16,768]{1,0:T(8,128)S(1)} %shard_map.39), channel_id=1, source_target_pairs={{0,1},{1,0},{2,3},{3,2},{4,5},{5,4},{6,7},{7,6},{8,9},{9,8},{10,11... | collective-permute-start | bytes 147464 | tf_op jit(solution)/shard_map/ppermute | solution.py:487
  43.7 0.9 collective-permute-done.3
  44.6 2.7 %collective-permute-start.4 = (f32[16,768]{1,0:T(8,128)S(1)}, f32[16,768]{1,0:T(8,128)S(1)}, u32[]{:S(2)}, u32[]{:S(2)}) collective-permute-start(f32[16,768]{1,0:T(8,128)S(1)} %add.69.s0), channel_id=1, source_target_pairs={{0,24},{8,0},{16,8},{24,16},{1,25},{9,1},{17,9},{25,17},{2,26},{10... | collective-permute-start | bytes 147464 | tf_op jit(solution)/shard_map/ppermute | solution.py:483
  47.4 1.6 %collective-permute-start.6 = (f32[16,768]{1,0:T(8,128)S(1)}, f32[16,768]{1,0:T(8,128)S(1)}, u32[]{:S(2)}, u32[]{:S(2)}) collective-permute-start(f32[16,768]{1,0:T(8,128)S(1)} %add.69.s0), channel_id=1, source_target_pairs={{0,16},{8,24},{16,0},{24,8},{1,17},{9,25},{17,1},{25,9},{2,18},{10... | collective-permute-start | bytes 147464 | tf_op jit(solution)/shard_map/ppermute | solution.py:483
  49.0 2.7 %collective-permute-done.5.s1 = f32[16,768]{1,0:T(8,128)S(1)} collective-permute-done((f32[16,768]{1,0:T(8,128)S(1)}, f32[16,768]{1,0:T(8,128)S(1)}, u32[]{:S(2)}, u32[]{:S(2)}) %collective-permute-start.5) | collective-permute-done | bytes 49184 | tf_op jit(solution)/shard_map/ppermute | solution.py:483
  52.2 1.1 %shard_map.41 = (f32[16,512]{1,0:T(8,128)S(1)}, f32[16,896]{1,0:T(8,128)S(1)}) custom-call(bf16[16,2,32,768]{3,2,1,0:T(8,128)(2,1)S(1)} %all-to-all-done.v_ref, f32[16,512]{1,0:T(8,128)S(1)} %reshape.10.q_ref.z_ref, f32[16,768]{1,0:T(8,128)S(1)} %add.69.s0, f32[16,768]{1,0:T(8,128)S(1)} %collective-permute-done.5.s1, ...), custom_call_target="tpu_custom_call" | custom-call | flops 4499999744 | bytes 15000000 | tf_op jit(solution)/shard_map/pallas_call | solution.py:330
  53.2 1.8 %collective-permute-start.7 = (f32[16,896]{1,0:T(8,128)S(1)}, f32[16,896]{1,0:T(8,128)S(1)}, u32[]{:S(2)}, u32[]{:S(2)}) collective-permute-start(f32[16,896]{1,0:T(8,128)S(1)} %get-tuple-element.34), channel_id=1, source_target_pairs={{0,1},{1,0},{2,3},{3,2},{4,5},{5,4},{6,7},{7,6},{8,9},{9,8},{10,11... | collective-permute-start | bytes 172040 | tf_op jit(solution)/shard_map/ppermute | solution.py:487
  55.0 2.2 %shard_map.40 = bf16[16,2,144,128]{3,2,1,0:T(8,128)(2,1)} custom-call(s32[3]{0:T(128)S(1)} %pad_add_fusion.y_ref.at_ref.refs_8_, bf16[2,24,32,128]{3,2,1,0:T(8,128)(2,1)S(1)} %copy-done.2, bf16[2,24,32,128]{3,2,1,0:T(8,128)(2,1)S(1)} %collective-permute-done.refs_1_, bf16[2,24,32,128]{3,2,1,0:T(8,128)(2,1)S(1)} %collective-permute-done.1.refs_2_, ...), custom_call_target="tpu_custom_call" | custom-call | flops 2700000000 | bytes 9000000 | tf_op jit(solution)/shard_map/pallas_call | solution.py:234
  57.2 1.7 %collective-permute-start.10 = (f32[16,896]{1,0:T(8,128)S(1)}, f32[16,896]{1,0:T(8,128)S(1)}, u32[]{:S(2)}, u32[]{:S(2)}) collective-permute-start(f32[16,896]{1,0:T(8,128)S(1)} %add.70.s0), channel_id=1, source_target_pairs={{0,16},{8,24},{16,0},{24,8},{1,17},{9,25},{17,1},{25,9},{2,18},{10... | collective-permute-start | bytes 172040 | tf_op jit(solution)/shard_map/ppermute | solution.py:483
  59.0 1.1 %collective-permute-start.11 = (f32[16,896]{1,0:T(8,128)S(1)}, f32[16,896]{1,0:T(8,128)S(1)}, u32[]{:S(2)}, u32[]{:S(2)}) collective-permute-start(f32[16,896]{1,0:T(8,128)S(1)} %add.70.s0), channel_id=1, source_target_pairs={{0,24},{8,0},{16,8},{24,16},{1,25},{9,1},{17,9},{25,17},{2,26},{10... | collective-permute-start | bytes 172040 | tf_op jit(solution)/shard_map/ppermute | solution.py:483
  60.1 0.5 collective-permute-start.9
  60.6 4.4 %all-to-all-start.1 = ((bf16[16,2,144,128]{3,2,1,0:T(8,128)(2,1)}), bf16[16,2,144,128]{3,2,1,0:T(8,128)(2,1)}, u32[]{:S(2)}, u32[]{:S(2)}) async-start(bf16[16,2,144,128]{3,2,1,0:T(8,128)(2,1)} %shard_map.40), calls=%async_computation.1 | async-start | bytes 2359296 | tf_op jit(solution)/shard_map/all_to_all | solution.py:509
  65.0 1.7 %shard_map.43 = (f32[16,512]{1,0:T(8,128)S(1)}, f32[16,896]{1,0:T(8,128)S(1)}) custom-call(bf16[16,2,32,768]{3,2,1,0:T(8,128)(2,1)S(1)} %all-to-all-done.v_ref, f32[16,512]{1,0:T(8,128)S(1)} %get-tuple-element.37.z_ref, f32[16,896]{1,0:T(8,128)S(1)} %add.70.s0, f32[16,896]{1,0:T(8,128)S(1)} %collective-permute-done.9.s1, ...), custom_call_target="tpu_custom_call" | custom-call | flops 4499999744 | bytes 15000000 | tf_op jit(solution)/shard_map/pallas_call | solution.py:330
  66.7 0.8 collective-permute-start.12
  67.5 0.9 collective-permute-done.12
  68.4 1.6 %collective-permute-start.13 = (f32[16,896]{1,0:T(8,128)S(1)}, f32[16,896]{1,0:T(8,128)S(1)}, u32[]{:S(2)}, u32[]{:S(2)}) collective-permute-start(f32[16,896]{1,0:T(8,128)S(1)} %add.81.s0), channel_id=1, source_target_pairs={{0,8},{8,16},{16,24},{24,0},{1,9},{9,17},{17,25},{25,1},{2,10},{10... | collective-permute-start | bytes 172040 | tf_op jit(solution)/shard_map/ppermute | solution.py:483
  70.0 1.6 %collective-permute-start.14 = (f32[16,896]{1,0:T(8,128)S(1)}, f32[16,896]{1,0:T(8,128)S(1)}, u32[]{:S(2)}, u32[]{:S(2)}) collective-permute-start(f32[16,896]{1,0:T(8,128)S(1)} %add.81.s0), channel_id=1, source_target_pairs={{0,16},{8,24},{16,0},{24,8},{1,17},{9,25},{17,1},{25,9},{2,18},{10... | collective-permute-start | bytes 172040 | tf_op jit(solution)/shard_map/ppermute | solution.py:483
  71.6 0.9 collective-permute-start.15
  72.4 0.6 collective-permute-done.13.s1
  73.0 2.0 %collective-permute-done.14.s2 = f32[16,896]{1,0:T(8,128)S(1)} collective-permute-done((f32[16,896]{1,0:T(8,128)S(1)}, f32[16,896]{1,0:T(8,128)S(1)}, u32[]{:S(2)}, u32[]{:S(2)}) %collective-permute-start.14) | collective-permute-done | bytes 57376 | tf_op jit(solution)/shard_map/ppermute | solution.py:483
  75.3 1.2 %shard_map.44 = f32[16,512]{1,0:T(8,128)S(1)} custom-call(bf16[16,2,32,768]{3,2,1,0:T(8,128)(2,1)S(1)} %all-to-all-done.v_ref, f32[16,512]{1,0:T(8,128)S(1)} %get-tuple-element.38.z_ref, f32[16,896]{1,0:T(8,128)S(1)} %add.81.s0, f32[16,896]{1,0:T(8,128)S(1)} %collective-permute-done.13.s1, f32[16,896]{1,0:T(8,128)S(1)} %collective-permute-done.14.s2, ...), custom_call_target="tpu_custom_call" | custom-call | flops 4499999744 | bytes 15000000 | tf_op jit(solution)/shard_map/pallas_call | solution.py:330
  76.5 1.5 %collective-permute-start.16 = (f32[16,512]{1,0:T(8,128)S(1)}, f32[16,512]{1,0:T(8,128)S(1)}, u32[]{:S(2)}, u32[]{:S(2)}) collective-permute-start(f32[16,512]{1,0:T(8,128)S(1)} %shard_map.44), channel_id=1, source_target_pairs={{0,2},{2,4},{4,6},{6,0},{1,3},{3,5},{5,7},{7,1},{8,10},{10,12},{12... | collective-permute-start | bytes 98312 | tf_op jit(solution)/shard_map/ppermute | solution.py:514
  78.0 2.4 %collective-permute-start.17 = (f32[16,512]{1,0:T(8,128)S(1)}, f32[16,512]{1,0:T(8,128)S(1)}, u32[]{:S(2)}, u32[]{:S(2)}) collective-permute-start(f32[16,512]{1,0:T(8,128)S(1)} %shard_map.44), channel_id=1, source_target_pairs={{0,4},{2,6},{4,0},{6,2},{1,5},{3,7},{5,1},{7,3},{8,12},{10,14},{12... | collective-permute-start | bytes 98312 | tf_op jit(solution)/shard_map/ppermute | solution.py:514
  80.4 1.2 %collective-permute-start.18 = (f32[16,512]{1,0:T(8,128)S(1)}, f32[16,512]{1,0:T(8,128)S(1)}, u32[]{:S(2)}, u32[]{:S(2)}) collective-permute-start(f32[16,512]{1,0:T(8,128)S(1)} %shard_map.44), channel_id=1, source_target_pairs={{0,6},{2,0},{4,2},{6,4},{1,7},{3,1},{5,3},{7,5},{8,14},{10,8},{12,... | collective-permute-start | bytes 98312 | tf_op jit(solution)/shard_map/ppermute | solution.py:514
  82.0 1.3 %slice_bitcast_fusion = (bf16[16,144,128]{2,1,0:T(8,128)(2,1)S(1)}, bf16[16,144,128]{2,1,0:T(8,128)(2,1)S(1)}) fusion(bf16[16,2,144,128]{3,2,1,0:T(8,128)(2,1)} %all-to-all-done.1), kind=kLoop, calls=%fused_computation.29 | loop fusion | bytes 2359296 | tf_op jit(solution)/shard_map/squeeze | solution.py:512
  83.3 3.4 %collective-permute-start.8 = (bf16[16,144,128]{2,1,0:T(8,128)(2,1)S(1)}, bf16[16,144,128]{2,1,0:T(8,128)(2,1)S(1)}, u32[]{:S(2)}, u32[]{:S(2)}) collective-permute-start(bf16[16,144,128]{2,1,0:T(8,128)(2,1)S(1)} %get-tuple-element.45), channel_id=1, source_target_pairs={{0,1},{1,0},{2,3},{3,2},{4,5},{5,4},{6,7},{7,6},{8,9},{9,8},{10,11... | collective-permute-start | bytes 1769480 | tf_op jit(solution)/shard_map/ppermute | solution.py:512
  86.7 0.6 select_convert_fusion.place_ref
  87.4 1.5 %collective-permute-start.19 = (f32[4,16,512]{2,1,0:T(8,128)S(1)}, f32[4,16,512]{2,1,0:T(8,128)S(1)}, u32[]{:S(2)}, u32[]{:S(2)}) collective-permute-start(f32[4,16,512]{2,1,0:T(8,128)S(1)} %pad_maximum_fusion.refs_0_), channel_id=1, source_target_pairs={{0,8},{8,16},{16,24},{24,0},{1,9},{9,17},{17,25},{25,1},{2,10},{10... | collective-permute-start | bytes 393224 | tf_op jit(solution)/shard_map/ppermute | solution.py:516
  89.0 1.9 %collective-permute-start.20 = (f32[4,16,512]{2,1,0:T(8,128)S(1)}, f32[4,16,512]{2,1,0:T(8,128)S(1)}, u32[]{:S(2)}, u32[]{:S(2)}) collective-permute-start(f32[4,16,512]{2,1,0:T(8,128)S(1)} %pad_maximum_fusion.refs_0_), channel_id=1, source_target_pairs={{0,16},{8,24},{16,0},{24,8},{1,17},{9,25},{17,1},{25,9},{2,18},{10... | collective-permute-start | bytes 393224 | tf_op jit(solution)/shard_map/ppermute | solution.py:516
  90.9 0.6 collective-permute-start.21
  91.4 0.8 collective-permute-start.22
  92.2 1.4 %shard_map.42 = (bf16[4,3,48,1024]{3,2,1,0:T(8,128)(2,1)S(1)}, f32[8,128]{1,0:T(8,128)S(1)}) custom-call(bf16[16,144,128]{2,1,0:T(8,128)(2,1)S(1)} %get-tuple-element.46.mine_ref, bf16[16,144,128]{2,1,0:T(8,128)(2,1)S(1)} %collective-permute-done.8.theirs_ref, bf16[1024,1024]{1,0:T(8,128)(2,1)S(1)} %select_convert_fusion.place_ref), custom_call_target="tpu_custom_call" | custom-call | flops 3600000000 | bytes 12000000 | tf_op jit(solution)/shard_map/pallas_call | solution.py:362
  93.8 3.5 %collective-permute-done.20.refs_2_ = f32[4,16,512]{2,1,0:T(8,128)S(1)} collective-permute-done((f32[4,16,512]{2,1,0:T(8,128)S(1)}, f32[4,16,512]{2,1,0:T(8,128)S(1)}, u32[]{:S(2)}, u32[]{:S(2)}) %collective-permute-start.20) | collective-permute-done | bytes 131104 | tf_op jit(solution)/shard_map/ppermute | solution.py:516
  97.3 0.8 collective-permute-start.23
  98.1 0.5 collective-permute-start.25
  98.6 0.5 collective-permute-done.23.refs_5_
  99.7 5.6 %shard_map.45 = f32[2,3,24,4096]{3,2,1,0:T(8,128)} custom-call(bf16[4,3,48,1024]{3,2,1,0:T(8,128)(2,1)S(1)} %get-tuple-element.36.flat, f32[4,16,512]{2,1,0:T(8,128)S(1)} %pad_maximum_fusion.refs_0_, f32[4,16,512]{2,1,0:T(8,128)S(1)} %collective-permute-done.19.refs_1_, f32[4,16,512]{2,1,0:T(8,128)S(1)} %collective-permute-done.20.refs_2_, ...), custom_call_target="tpu_custom_call" | custom-call | flops 5400000000 | bytes 18000000 | tf_op jit(solution)/shard_map/pallas_call | solution.py:463
  (41 shorter events, 2.5 us)
Async XLA Ops:
  10.2 29.1 %all-to-all-start = ((bf16[16,2,32,768]{3,2,1,0:T(8,128)(2,1)}), bf16[16,2,32,768]{3,2,1,0:T(8,128)(2,1)S(1)}, u32[]{:S(2)}, u32[]{:S(2)}) async-start(bf16[16,2,32,768]{3,2,1,0:T(8,128)(2,1)} %shard_map.37.v_ref), calls=%async_computation | async-start | bytes 3145728 | tf_op jit(solution)/shard_map/all_to_all | solution.py:494
  18.7 1.4 %copy-start = (bf16[16,2,32,768]{3,2,1,0:T(8,128)(2,1)S(1)}, bf16[16,2,32,768]{3,2,1,0:T(8,128)(2,1)}, u32[]{:S(2)}) copy-start(bf16[16,2,32,768]{3,2,1,0:T(8,128)(2,1)} %shard_map.37.v_ref) | copy-start | bytes 4718596
  20.1 8.4 %copy-start.3 = (f32[2,8,4096]{2,1,0:T(8,128)S(1)}, f32[2,8,4096]{2,1,0:T(8,128)}, u32[]{:S(2)}) copy-start(f32[2,8,4096]{2,1,0:T(8,128)} %param.5) | copy-start | bytes 786436
  22.8 0.7 copy-start.1
  23.5 23.8 %collective-permute-start = (bf16[2,24,32,128]{3,2,1,0:T(8,128)(2,1)}, bf16[2,24,32,128]{3,2,1,0:T(8,128)(2,1)S(1)}, u32[]{:S(2)}, u32[]{:S(2)}) collective-permute-start(bf16[2,24,32,128]{3,2,1,0:T(8,128)(2,1)} %get-tuple-element.26), channel_id=1, source_target_pairs={{0,8},{8,16},{16,24},{24,0},{1,9},{9,17},{17,25},{25,1},{2,10},{10... | collective-permute-start | bytes 1179656 | tf_op jit(solution)/shard_map/ppermute | solution.py:496
  24.8 24.2 %collective-permute-start.1 = (bf16[2,24,32,128]{3,2,1,0:T(8,128)(2,1)}, bf16[2,24,32,128]{3,2,1,0:T(8,128)(2,1)S(1)}, u32[]{:S(2)}, u32[]{:S(2)}) collective-permute-start(bf16[2,24,32,128]{3,2,1,0:T(8,128)(2,1)} %get-tuple-element.27), channel_id=1, source_target_pairs={{0,16},{8,24},{16,0},{24,8},{1,17},{9,25},{17,1},{25,9},{2,18},{10... | collective-permute-start | bytes 1179656 | tf_op jit(solution)/shard_map/ppermute | solution.py:496
  27.5 21.6 %collective-permute-start.2 = (bf16[2,24,32,128]{3,2,1,0:T(8,128)(2,1)S(1)}, bf16[2,24,32,128]{3,2,1,0:T(8,128)(2,1)S(1)}, u32[]{:S(2)}, u32[]{:S(2)}) collective-permute-start(bf16[2,24,32,128]{3,2,1,0:T(8,128)(2,1)S(1)} %get-tuple-element.28), channel_id=1, source_target_pairs={{0,24},{8,0},{16,8},{24,16},{1,25},{9,1},{17,9},{25,17},{2,26},{10... | collective-permute-start | bytes 1179656 | tf_op jit(solution)/shard_map/ppermute | solution.py:496
  39.6 5.1 %collective-permute-start.3 = (f32[16,768]{1,0:T(8,128)S(1)}, f32[16,768]{1,0:T(8,128)S(1)}, u32[]{:S(2)}, u32[]{:S(2)}) collective-permute-start(f32[16,768]{1,0:T(8,128)S(1)} %shard_map.39), channel_id=1, source_target_pairs={{0,1},{1,0},{2,3},{3,2},{4,5},{5,4},{6,7},{7,6},{8,9},{9,8},{10,11... | collective-permute-start | bytes 147464 | tf_op jit(solution)/shard_map/ppermute | solution.py:487
  44.6 4.4 %collective-permute-start.4 = (f32[16,768]{1,0:T(8,128)S(1)}, f32[16,768]{1,0:T(8,128)S(1)}, u32[]{:S(2)}, u32[]{:S(2)}) collective-permute-start(f32[16,768]{1,0:T(8,128)S(1)} %add.69.s0), channel_id=1, source_target_pairs={{0,24},{8,0},{16,8},{24,16},{1,25},{9,1},{17,9},{25,17},{2,26},{10... | collective-permute-start | bytes 147464 | tf_op jit(solution)/shard_map/ppermute | solution.py:483
  47.4 4.4 %collective-permute-start.5 = (f32[16,768]{1,0:T(8,128)S(1)}, f32[16,768]{1,0:T(8,128)S(1)}, u32[]{:S(2)}, u32[]{:S(2)}) collective-permute-start(f32[16,768]{1,0:T(8,128)S(1)} %add.69.s0), channel_id=1, source_target_pairs={{0,8},{8,16},{16,24},{24,0},{1,9},{9,17},{17,25},{25,1},{2,10},{10... | collective-permute-start | bytes 147464 | tf_op jit(solution)/shard_map/ppermute | solution.py:483
  47.4 4.8 %collective-permute-start.6 = (f32[16,768]{1,0:T(8,128)S(1)}, f32[16,768]{1,0:T(8,128)S(1)}, u32[]{:S(2)}, u32[]{:S(2)}) collective-permute-start(f32[16,768]{1,0:T(8,128)S(1)} %add.69.s0), channel_id=1, source_target_pairs={{0,16},{8,24},{16,0},{24,8},{1,17},{9,25},{17,1},{25,9},{2,18},{10... | collective-permute-start | bytes 147464 | tf_op jit(solution)/shard_map/ppermute | solution.py:483
  49.0 6.0 %copy-start.2 = (bf16[2,24,32,128]{3,2,1,0:T(8,128)(2,1)S(1)}, bf16[2,24,32,128]{3,2,1,0:T(8,128)(2,1)}, u32[]{:S(2)}) copy-start(bf16[2,24,32,128]{3,2,1,0:T(8,128)(2,1)} %copy-done.1) | copy-start | bytes 1179652
  53.2 4.0 %collective-permute-start.7 = (f32[16,896]{1,0:T(8,128)S(1)}, f32[16,896]{1,0:T(8,128)S(1)}, u32[]{:S(2)}, u32[]{:S(2)}) collective-permute-start(f32[16,896]{1,0:T(8,128)S(1)} %get-tuple-element.34), channel_id=1, source_target_pairs={{0,1},{1,0},{2,3},{3,2},{4,5},{5,4},{6,7},{7,6},{8,9},{9,8},{10,11... | collective-permute-start | bytes 172040 | tf_op jit(solution)/shard_map/ppermute | solution.py:487
  57.2 7.8 %collective-permute-start.10 = (f32[16,896]{1,0:T(8,128)S(1)}, f32[16,896]{1,0:T(8,128)S(1)}, u32[]{:S(2)}, u32[]{:S(2)}) collective-permute-start(f32[16,896]{1,0:T(8,128)S(1)} %add.70.s0), channel_id=1, source_target_pairs={{0,16},{8,24},{16,0},{24,8},{1,17},{9,25},{17,1},{25,9},{2,18},{10... | collective-permute-start | bytes 172040 | tf_op jit(solution)/shard_map/ppermute | solution.py:483
  59.0 6.0 %collective-permute-start.11 = (f32[16,896]{1,0:T(8,128)S(1)}, f32[16,896]{1,0:T(8,128)S(1)}, u32[]{:S(2)}, u32[]{:S(2)}) collective-permute-start(f32[16,896]{1,0:T(8,128)S(1)} %add.70.s0), channel_id=1, source_target_pairs={{0,24},{8,0},{16,8},{24,16},{1,25},{9,1},{17,9},{25,17},{2,26},{10... | collective-permute-start | bytes 172040 | tf_op jit(solution)/shard_map/ppermute | solution.py:483
  60.1 4.9 %collective-permute-start.9 = (f32[16,896]{1,0:T(8,128)S(1)}, f32[16,896]{1,0:T(8,128)S(1)}, u32[]{:S(2)}, u32[]{:S(2)}) collective-permute-start(f32[16,896]{1,0:T(8,128)S(1)} %add.70.s0), channel_id=1, source_target_pairs={{0,8},{8,16},{16,24},{24,0},{1,9},{9,17},{17,25},{25,1},{2,10},{10... | collective-permute-start | bytes 172040 | tf_op jit(solution)/shard_map/ppermute | solution.py:483
  60.6 21.4 %all-to-all-start.1 = ((bf16[16,2,144,128]{3,2,1,0:T(8,128)(2,1)}), bf16[16,2,144,128]{3,2,1,0:T(8,128)(2,1)}, u32[]{:S(2)}, u32[]{:S(2)}) async-start(bf16[16,2,144,128]{3,2,1,0:T(8,128)(2,1)} %shard_map.40), calls=%async_computation.1 | async-start | bytes 2359296 | tf_op jit(solution)/shard_map/all_to_all | solution.py:509
  66.7 1.6 %collective-permute-start.12 = (f32[16,896]{1,0:T(8,128)S(1)}, f32[16,896]{1,0:T(8,128)S(1)}, u32[]{:S(2)}, u32[]{:S(2)}) collective-permute-start(f32[16,896]{1,0:T(8,128)S(1)} %get-tuple-element.39), channel_id=1, source_target_pairs={{0,1},{1,0},{2,3},{3,2},{4,5},{5,4},{6,7},{7,6},{8,9},{9,8},{10,11... | collective-permute-start | bytes 172040 | tf_op jit(solution)/shard_map/ppermute | solution.py:487
  68.4 4.7 %collective-permute-start.13 = (f32[16,896]{1,0:T(8,128)S(1)}, f32[16,896]{1,0:T(8,128)S(1)}, u32[]{:S(2)}, u32[]{:S(2)}) collective-permute-start(f32[16,896]{1,0:T(8,128)S(1)} %add.81.s0), channel_id=1, source_target_pairs={{0,8},{8,16},{16,24},{24,0},{1,9},{9,17},{17,25},{25,1},{2,10},{10... | collective-permute-start | bytes 172040 | tf_op jit(solution)/shard_map/ppermute | solution.py:483
  70.0 5.0 %collective-permute-start.14 = (f32[16,896]{1,0:T(8,128)S(1)}, f32[16,896]{1,0:T(8,128)S(1)}, u32[]{:S(2)}, u32[]{:S(2)}) collective-permute-start(f32[16,896]{1,0:T(8,128)S(1)} %add.81.s0), channel_id=1, source_target_pairs={{0,16},{8,24},{16,0},{24,8},{1,17},{9,25},{17,1},{25,9},{2,18},{10... | collective-permute-start | bytes 172040 | tf_op jit(solution)/shard_map/ppermute | solution.py:483
  71.6 3.8 %collective-permute-start.15 = (f32[16,896]{1,0:T(8,128)S(1)}, f32[16,896]{1,0:T(8,128)S(1)}, u32[]{:S(2)}, u32[]{:S(2)}) collective-permute-start(f32[16,896]{1,0:T(8,128)S(1)} %add.81.s0), channel_id=1, source_target_pairs={{0,24},{8,0},{16,8},{24,16},{1,25},{9,1},{17,9},{25,17},{2,26},{10... | collective-permute-start | bytes 172040 | tf_op jit(solution)/shard_map/ppermute | solution.py:483
  76.5 10.8 %collective-permute-start.16 = (f32[16,512]{1,0:T(8,128)S(1)}, f32[16,512]{1,0:T(8,128)S(1)}, u32[]{:S(2)}, u32[]{:S(2)}) collective-permute-start(f32[16,512]{1,0:T(8,128)S(1)} %shard_map.44), channel_id=1, source_target_pairs={{0,2},{2,4},{4,6},{6,0},{1,3},{3,5},{5,7},{7,1},{8,10},{10,12},{12... | collective-permute-start | bytes 98312 | tf_op jit(solution)/shard_map/ppermute | solution.py:514
  78.0 9.4 %collective-permute-start.17 = (f32[16,512]{1,0:T(8,128)S(1)}, f32[16,512]{1,0:T(8,128)S(1)}, u32[]{:S(2)}, u32[]{:S(2)}) collective-permute-start(f32[16,512]{1,0:T(8,128)S(1)} %shard_map.44), channel_id=1, source_target_pairs={{0,4},{2,6},{4,0},{6,2},{1,5},{3,7},{5,1},{7,3},{8,12},{10,14},{12... | collective-permute-start | bytes 98312 | tf_op jit(solution)/shard_map/ppermute | solution.py:514
  80.4 7.0 %collective-permute-start.18 = (f32[16,512]{1,0:T(8,128)S(1)}, f32[16,512]{1,0:T(8,128)S(1)}, u32[]{:S(2)}, u32[]{:S(2)}) collective-permute-start(f32[16,512]{1,0:T(8,128)S(1)} %shard_map.44), channel_id=1, source_target_pairs={{0,6},{2,0},{4,2},{6,4},{1,7},{3,1},{5,3},{7,5},{8,14},{10,8},{12,... | collective-permute-start | bytes 98312 | tf_op jit(solution)/shard_map/ppermute | solution.py:514
  83.3 9.0 %collective-permute-start.8 = (bf16[16,144,128]{2,1,0:T(8,128)(2,1)S(1)}, bf16[16,144,128]{2,1,0:T(8,128)(2,1)S(1)}, u32[]{:S(2)}, u32[]{:S(2)}) collective-permute-start(bf16[16,144,128]{2,1,0:T(8,128)(2,1)S(1)} %get-tuple-element.45), channel_id=1, source_target_pairs={{0,1},{1,0},{2,3},{3,2},{4,5},{5,4},{6,7},{7,6},{8,9},{9,8},{10,11... | collective-permute-start | bytes 1769480 | tf_op jit(solution)/shard_map/ppermute | solution.py:512
  87.4 6.4 %collective-permute-start.19 = (f32[4,16,512]{2,1,0:T(8,128)S(1)}, f32[4,16,512]{2,1,0:T(8,128)S(1)}, u32[]{:S(2)}, u32[]{:S(2)}) collective-permute-start(f32[4,16,512]{2,1,0:T(8,128)S(1)} %pad_maximum_fusion.refs_0_), channel_id=1, source_target_pairs={{0,8},{8,16},{16,24},{24,0},{1,9},{9,17},{17,25},{25,1},{2,10},{10... | collective-permute-start | bytes 393224 | tf_op jit(solution)/shard_map/ppermute | solution.py:516
  89.0 8.3 %collective-permute-start.20 = (f32[4,16,512]{2,1,0:T(8,128)S(1)}, f32[4,16,512]{2,1,0:T(8,128)S(1)}, u32[]{:S(2)}, u32[]{:S(2)}) collective-permute-start(f32[4,16,512]{2,1,0:T(8,128)S(1)} %pad_maximum_fusion.refs_0_), channel_id=1, source_target_pairs={{0,16},{8,24},{16,0},{24,8},{1,17},{9,25},{17,1},{25,9},{2,18},{10... | collective-permute-start | bytes 393224 | tf_op jit(solution)/shard_map/ppermute | solution.py:516
  90.9 6.4 %collective-permute-start.21 = (f32[4,16,512]{2,1,0:T(8,128)S(1)}, f32[4,16,512]{2,1,0:T(8,128)S(1)}, u32[]{:S(2)}, u32[]{:S(2)}) collective-permute-start(f32[4,16,512]{2,1,0:T(8,128)S(1)} %pad_maximum_fusion.refs_0_), channel_id=1, source_target_pairs={{0,24},{8,0},{16,8},{24,16},{1,25},{9,1},{17,9},{25,17},{2,26},{10... | collective-permute-start | bytes 393224 | tf_op jit(solution)/shard_map/ppermute | solution.py:516
  91.4 7.2 %collective-permute-start.22 = (f32[4,16,512]{2,1,0:T(8,128)S(1)}, f32[4,16,512]{2,1,0:T(8,128)S(1)}, u32[]{:S(2)}, u32[]{:S(2)}) collective-permute-start(f32[4,16,512]{2,1,0:T(8,128)S(1)} %pad_maximum_fusion.refs_0_), channel_id=1, source_target_pairs={{0,1},{1,0},{2,3},{3,2},{4,5},{5,4},{6,7},{7,6},{8,9},{9,8},{10,11... | collective-permute-start | bytes 393224 | tf_op jit(solution)/shard_map/ppermute | solution.py:519
  97.3 1.8 %collective-permute-start.23 = (f32[4,16,512]{2,1,0:T(8,128)S(1)}, f32[4,16,512]{2,1,0:T(8,128)S(1)}, u32[]{:S(2)}, u32[]{:S(2)}) collective-permute-start(f32[4,16,512]{2,1,0:T(8,128)S(1)} %collective-permute-done.19.refs_1_), channel_id=1, source_target_pairs={{0,1},{1,0},{2,3},{3,2},{4,5},{5,4},{6,7},{7,6},{8,9},{9,8},{10,11... | collective-permute-start | bytes 393224 | tf_op jit(solution)/shard_map/ppermute | solution.py:519
  98.1 1.3 %collective-permute-start.24 = (f32[4,16,512]{2,1,0:T(8,128)S(1)}, f32[4,16,512]{2,1,0:T(8,128)S(1)}, u32[]{:S(2)}, u32[]{:S(2)}) collective-permute-start(f32[4,16,512]{2,1,0:T(8,128)S(1)} %collective-permute-done.20.refs_2_), channel_id=1, source_target_pairs={{0,1},{1,0},{2,3},{3,2},{4,5},{5,4},{6,7},{7,6},{8,9},{9,8},{10,11... | collective-permute-start | bytes 393224 | tf_op jit(solution)/shard_map/ppermute | solution.py:519
  98.1 1.5 %collective-permute-start.25 = (f32[4,16,512]{2,1,0:T(8,128)S(1)}, f32[4,16,512]{2,1,0:T(8,128)S(1)}, u32[]{:S(2)}, u32[]{:S(2)}) collective-permute-start(f32[4,16,512]{2,1,0:T(8,128)S(1)} %collective-permute-done.21.refs_3_), channel_id=1, source_target_pairs={{0,1},{1,0},{2,3},{3,2},{4,5},{5,4},{6,7},{7,6},{8,9},{9,8},{10,11... | collective-permute-start | bytes 393224 | tf_op jit(solution)/shard_map/ppermute | solution.py:519

commit v9 on v8

--- a/solution.py
+++ b/solution.py
@@ -352,7 +352,7 @@
     for x in range(NX):
         parts = []
         for z in range(NZ):
-            parts += [mine_ref[x * NZ + z], theirs_ref[x * NZ + z]]
+            parts += [mine_ref[x * NZ + z, 0], theirs_ref[x * NZ + z]]
         rows.append(jnp.concatenate(parts, axis=1))
     got = dot_nn(jnp.concatenate(rows, axis=0), place_ref[...])
     flat[...] = got.astype(BF16).reshape(NX, GROUP, 2 * SHARE, NY * 256)
@@ -509,8 +509,8 @@
     blocks = lax.all_to_all(turned, ("x", "z"), 0, 0, tiled=True)
     z, s = step(1, v, z, sums)
     (z,) = step(2, v, z, sums_over(core_sum(s)))
-    mine, theirs = blocks[:, 0], lax.ppermute(blocks[:, 1], "core", turned_by(NC, 1))
-    flat, done = arrange(mine, theirs, place)
+    theirs = lax.ppermute(blocks[:, 1], "core", turned_by(NC, 1))
+    flat, done = arrange(blocks, theirs, place)
     along_z = [z] + [lax.ppermute(z, "z", turned_by(NZ, d)) for d in range(1, NZ)]
     column = jnp.stack(along_z)
     own = [column] + [lax.ppermute(column, "y", turned_by(NY, d)) for d in range(1, NY)]

time: 106 us -> 104 us (0.981)
  waiting for transfers between devices: 20.5 us -> 19.2 us
  Pallas kernels: 26.3 us -> 25.2 us
    squeeze x1, local copies, waits for them, and re-layouts: 1.32 us -> 0.04 us  [body(): theirs = lax.ppermute(blocks[:, 1], 'core', turned_by(NC, 1))]
    unnamed x8 -> x10, local copies, waits for them, and re-layouts: 2.16 us -> 3.17 us
  transfers between devices with their start and end apart: 28 -> 28, of which waited for: 14 -> 13; matrix products, arithmetic and copies ran while one was open for 5% -> 4% of each run, Pallas kernels for 9% -> 8%
where the time goes in v9:
time: 104 us; the launch traced here: 103 us
  starting transfers between devices  51.5 us (50%)
  Pallas kernels  25.2 us (24%)
  waiting for transfers between devices  19.2 us (18%)
  local copies, waits for them, and re-layouts  6.33 us (6%)
    ppermute x9, starting transfers between devices, sums_over(): return [s] + [lax.ppermute(s, 'y', turned_by(NY, d)) for d in range(1, NY)]  11.3 us
    pallas_call x1, Pallas kernels, channelize(): pl.pallas_call(channelize_kernel, out_shape=jax.ShapeDtypeStruct((NX * NZ...  10.2 us
    all_to_all x1, starting transfers between devices, body(): v = lax.all_to_all(parcels, ('x', 'z'), 0, 0, tiled=True)  8.44 us
    all_to_all x1, waiting for transfers between devices, body(): v = lax.all_to_all(parcels, ('x', 'z'), 0, 0, tiled=True)  7.59 us
    ppermute x3, starting transfers between devices, core_sum(): return s + lax.ppermute(s, 'core', turned_by(NC, 1))  7.37 us
    ppermute x9, waiting for transfers between devices, sums_over(): return [s] + [lax.ppermute(s, 'y', turned_by(NY, d)) for d in range(1, NY)]  5.95 us
    pallas_call x1, Pallas kernels, finish(): pl.pallas_call(final_kernel, out_shape=jax.ShapeDtypeStruct((2, GROUP, SH...  5.56 us
    ppermute x3, starting transfers between devices, body(): lax.ppermute(z, 'z', turned_by(NZ, d))  5.18 us
  transfers between devices with their start and end apart: 28, of which 13 were waited for; matrix products, arithmetic and copies ran while one was open for 4% of the time, Pallas kernels for 8%

profile of v9, /device:TPU:1, one launch (start us, length us, event | category | flops | bytes accessed | tf_op | source)
XLA Modules:
  0.0 103.4 jit_solution(17881205121787657394)
XLA Ops:
  0.0 10.2 %shard_map.37.v_ref = bf16[16,2,32,768]{3,2,1,0:T(8,128)(2,1)} custom-call(s32[12]{0:T(128)} %ids_ref.1, bf16[32,98688]{1,0:T(8,128)(2,1)} %x_hbm.1), custom_call_target="tpu_custom_call" | custom-call | flops 7200000000 | bytes 24000000 | tf_op jit(solution)/shard_map/pallas_call | solution.py:156
  10.2 8.4 %all-to-all-start = ((bf16[16,2,32,768]{3,2,1,0:T(8,128)(2,1)}), bf16[16,2,32,768]{3,2,1,0:T(8,128)(2,1)S(1)}, u32[]{:S(2)}, u32[]{:S(2)}) async-start(bf16[16,2,32,768]{3,2,1,0:T(8,128)(2,1)} %shard_map.37.v_ref), calls=%async_computation | async-start | bytes 3145728 | tf_op jit(solution)/shard_map/all_to_all | solution.py:494
  18.7 1.4 %copy-done = bf16[16,2,32,768]{3,2,1,0:T(8,128)(2,1)S(1)} copy-done((bf16[16,2,32,768]{3,2,1,0:T(8,128)(2,1)S(1)}, bf16[16,2,32,768]{3,2,1,0:T(8,128)(2,1)}, u32[]{:S(2)}) %copy-start) | copy-done | bytes 1572888
  20.1 2.7 %shard_map.38 = (bf16[2,24,32,128]{3,2,1,0:T(8,128)(2,1)S(1)}, bf16[2,24,32,128]{3,2,1,0:T(8,128)(2,1)}, bf16[2,24,32,128]{3,2,1,0:T(8,128)(2,1)}, bf16[2,24,32,128]{3,2,1,0:T(8,128)(2,1)S(1)}) custom-call(s32[3]{0:T(128)S(1)} %pad_add_fusion.y_ref.at_ref.refs_8_, bf16[16,2,32,768]{3,2,1,0:T(8,128)(2,1)S(1)} %copy-done), custom_call_target="tpu_custom_call" | custom-call | flops 3600000000 | bytes 12000000 | tf_op jit(solution)/shard_map/pallas_call | solution.py:197
  22.8 0.7 copy-done.2
  23.5 1.3 %collective-permute-start = (bf16[2,24,32,128]{3,2,1,0:T(8,128)(2,1)}, bf16[2,24,32,128]{3,2,1,0:T(8,128)(2,1)S(1)}, u32[]{:S(2)}, u32[]{:S(2)}) collective-permute-start(bf16[2,24,32,128]{3,2,1,0:T(8,128)(2,1)} %get-tuple-element.26), channel_id=1, source_target_pairs={{0,8},{8,16},{16,24},{24,0},{1,9},{9,17},{17,25},{25,1},{2,10},{10... | collective-permute-start | bytes 1179656 | tf_op jit(solution)/shard_map/ppermute | solution.py:496
  24.8 2.6 %collective-permute-start.1 = (bf16[2,24,32,128]{3,2,1,0:T(8,128)(2,1)}, bf16[2,24,32,128]{3,2,1,0:T(8,128)(2,1)S(1)}, u32[]{:S(2)}, u32[]{:S(2)}) collective-permute-start(bf16[2,24,32,128]{3,2,1,0:T(8,128)(2,1)} %get-tuple-element.27), channel_id=1, source_target_pairs={{0,16},{8,24},{16,0},{24,8},{1,17},{9,25},{17,1},{25,9},{2,18},{10... | collective-permute-start | bytes 1179656 | tf_op jit(solution)/shard_map/ppermute | solution.py:496
  27.5 1.1 %collective-permute-start.2 = (bf16[2,24,32,128]{3,2,1,0:T(8,128)(2,1)S(1)}, bf16[2,24,32,128]{3,2,1,0:T(8,128)(2,1)S(1)}, u32[]{:S(2)}, u32[]{:S(2)}) collective-permute-start(bf16[2,24,32,128]{3,2,1,0:T(8,128)(2,1)S(1)} %get-tuple-element.28), channel_id=1, source_target_pairs={{0,24},{8,0},{16,8},{24,16},{1,25},{9,1},{17,9},{25,17},{2,26},{10... | collective-permute-start | bytes 1179656 | tf_op jit(solution)/shard_map/ppermute | solution.py:496
  28.5 1.9 %reshape.9 = f32[16,4,4,4,2,32]{5,4,3,2,1,0:T(2,128)} reshape(f32[2,8,4096]{2,1,0:T(8,128)S(1)} %copy-done.4) | data formatting | bytes 524288 | tf_op jit(solution)/shard_map/reshape | solution.py:497
  30.4 1.1 %constant_dynamic-slice_fusion = f32[16,4,1,4,1,32]{5,4,3,2,1,0:T(1,128)S(1)} fusion(f32[16,4,4,4,2,32]{5,4,3,2,1,0:T(2,128)} %reshape.9, s32[]{:T(128)S(6)} %select_n.51, s32[]{:T(128)S(6)} %select_n.53), kind=kLoop, calls=%fused_computation.52 | loop fusion | bytes 65544 | tf_op jit(solution)/shard_map/jit(dynamic_index_in_dim)/dynamic_slice | solution.py:499
  31.7 7.6 %all-to-all-done.v_ref = bf16[16,2,32,768]{3,2,1,0:T(8,128)(2,1)S(1)} async-done(((bf16[16,2,32,768]{3,2,1,0:T(8,128)(2,1)}), bf16[16,2,32,768]{3,2,1,0:T(8,128)(2,1)S(1)}, u32[]{:S(2)}, u32[]{:S(2)}) %all-to-all-start) | async-done | bytes 1572896 | tf_op jit(solution)/shard_map/all_to_all | solution.py:494
  39.6 4.2 %collective-permute-start.3 = (f32[16,768]{1,0:T(8,128)S(1)}, f32[16,768]{1,0:T(8,128)S(1)}, u32[]{:S(2)}, u32[]{:S(2)}) collective-permute-start(f32[16,768]{1,0:T(8,128)S(1)} %shard_map.39), channel_id=1, source_target_pairs={{0,1},{1,0},{2,3},{3,2},{4,5},{5,4},{6,7},{7,6},{8,9},{9,8},{10,11... | collective-permute-start | bytes 147464 | tf_op jit(solution)/shard_map/ppermute | solution.py:487
  43.7 0.9 collective-permute-done.3
  44.6 2.7 %collective-permute-start.4 = (f32[16,768]{1,0:T(8,128)S(1)}, f32[16,768]{1,0:T(8,128)S(1)}, u32[]{:S(2)}, u32[]{:S(2)}) collective-permute-start(f32[16,768]{1,0:T(8,128)S(1)} %add.69.s0), channel_id=1, source_target_pairs={{0,24},{8,0},{16,8},{24,16},{1,25},{9,1},{17,9},{25,17},{2,26},{10... | collective-permute-start | bytes 147464 | tf_op jit(solution)/shard_map/ppermute | solution.py:483
  47.4 1.6 %collective-permute-start.6 = (f32[16,768]{1,0:T(8,128)S(1)}, f32[16,768]{1,0:T(8,128)S(1)}, u32[]{:S(2)}, u32[]{:S(2)}) collective-permute-start(f32[16,768]{1,0:T(8,128)S(1)} %add.69.s0), channel_id=1, source_target_pairs={{0,16},{8,24},{16,0},{24,8},{1,17},{9,25},{17,1},{25,9},{2,18},{10... | collective-permute-start | bytes 147464 | tf_op jit(solution)/shard_map/ppermute | solution.py:483
  49.0 2.7 %collective-permute-done.5.s1 = f32[16,768]{1,0:T(8,128)S(1)} collective-permute-done((f32[16,768]{1,0:T(8,128)S(1)}, f32[16,768]{1,0:T(8,128)S(1)}, u32[]{:S(2)}, u32[]{:S(2)}) %collective-permute-start.5) | collective-permute-done | bytes 49184 | tf_op jit(solution)/shard_map/ppermute | solution.py:483
  52.2 1.1 %shard_map.41 = (f32[16,512]{1,0:T(8,128)S(1)}, f32[16,896]{1,0:T(8,128)S(1)}) custom-call(bf16[16,2,32,768]{3,2,1,0:T(8,128)(2,1)S(1)} %all-to-all-done.v_ref, f32[16,512]{1,0:T(8,128)S(1)} %reshape.10.q_ref.z_ref, f32[16,768]{1,0:T(8,128)S(1)} %add.69.s0, f32[16,768]{1,0:T(8,128)S(1)} %collective-permute-done.5.s1, ...), custom_call_target="tpu_custom_call" | custom-call | flops 4499999744 | bytes 15000000 | tf_op jit(solution)/shard_map/pallas_call | solution.py:330
  53.2 1.8 %collective-permute-start.7 = (f32[16,896]{1,0:T(8,128)S(1)}, f32[16,896]{1,0:T(8,128)S(1)}, u32[]{:S(2)}, u32[]{:S(2)}) collective-permute-start(f32[16,896]{1,0:T(8,128)S(1)} %get-tuple-element.34), channel_id=1, source_target_pairs={{0,1},{1,0},{2,3},{3,2},{4,5},{5,4},{6,7},{7,6},{8,9},{9,8},{10,11... | collective-permute-start | bytes 172040 | tf_op jit(solution)/shard_map/ppermute | solution.py:487
  55.0 1.2 %shard_map.40 = bf16[16,2,144,128]{3,2,1,0:T(8,128)(2,1)S(1)} custom-call(s32[3]{0:T(128)S(1)} %pad_add_fusion.y_ref.at_ref.refs_8_, bf16[2,24,32,128]{3,2,1,0:T(8,128)(2,1)S(1)} %copy-done.3, bf16[2,24,32,128]{3,2,1,0:T(8,128)(2,1)S(1)} %collective-permute-done.refs_1_, bf16[2,24,32,128]{3,2,1,0:T(8,128)(2,1)S(1)} %collective-permute-done.1.refs_2_, ...), custom_call_target="tpu_custom_call" | custom-call | flops 2700000000 | bytes 9000000 | tf_op jit(solution)/shard_map/pallas_call | solution.py:234
  56.2 1.0 copy-done.1
  57.2 1.7 %collective-permute-start.10 = (f32[16,896]{1,0:T(8,128)S(1)}, f32[16,896]{1,0:T(8,128)S(1)}, u32[]{:S(2)}, u32[]{:S(2)}) collective-permute-start(f32[16,896]{1,0:T(8,128)S(1)} %add.70.s0), channel_id=1, source_target_pairs={{0,16},{8,24},{16,0},{24,8},{1,17},{9,25},{17,1},{25,9},{2,18},{10... | collective-permute-start | bytes 172040 | tf_op jit(solution)/shard_map/ppermute | solution.py:483
  59.0 1.1 %collective-permute-start.11 = (f32[16,896]{1,0:T(8,128)S(1)}, f32[16,896]{1,0:T(8,128)S(1)}, u32[]{:S(2)}, u32[]{:S(2)}) collective-permute-start(f32[16,896]{1,0:T(8,128)S(1)} %add.70.s0), channel_id=1, source_target_pairs={{0,24},{8,0},{16,8},{24,16},{1,25},{9,1},{17,9},{25,17},{2,26},{10... | collective-permute-start | bytes 172040 | tf_op jit(solution)/shard_map/ppermute | solution.py:483
  60.1 0.5 collective-permute-start.9
  60.6 3.7 %all-to-all-start.1 = ((bf16[16,2,144,128]{3,2,1,0:T(8,128)(2,1)}), bf16[16,2,144,128]{3,2,1,0:T(8,128)(2,1)S(1)}, u32[]{:S(2)}, u32[]{:S(2)}) async-start(bf16[16,2,144,128]{3,2,1,0:T(8,128)(2,1)} %copy-done.1), calls=%async_computation.1 | async-start | bytes 2359296 | tf_op jit(solution)/shard_map/all_to_all | solution.py:509
  64.3 1.7 %shard_map.43 = (f32[16,512]{1,0:T(8,128)S(1)}, f32[16,896]{1,0:T(8,128)S(1)}) custom-call(bf16[16,2,32,768]{3,2,1,0:T(8,128)(2,1)S(1)} %all-to-all-done.v_ref, f32[16,512]{1,0:T(8,128)S(1)} %get-tuple-element.37.z_ref, f32[16,896]{1,0:T(8,128)S(1)} %add.70.s0, f32[16,896]{1,0:T(8,128)S(1)} %collective-permute-done.9.s1, ...), custom_call_target="tpu_custom_call" | custom-call | flops 4499999744 | bytes 15000000 | tf_op jit(solution)/shard_map/pallas_call | solution.py:330
  66.0 1.4 %collective-permute-start.12 = (f32[16,896]{1,0:T(8,128)S(1)}, f32[16,896]{1,0:T(8,128)S(1)}, u32[]{:S(2)}, u32[]{:S(2)}) collective-permute-start(f32[16,896]{1,0:T(8,128)S(1)} %get-tuple-element.39), channel_id=1, source_target_pairs={{0,1},{1,0},{2,3},{3,2},{4,5},{5,4},{6,7},{7,6},{8,9},{9,8},{10,11... | collective-permute-start | bytes 172040 | tf_op jit(solution)/shard_map/ppermute | solution.py:487
  67.5 0.9 collective-permute-done.12
  68.4 1.1 %collective-permute-start.13 = (f32[16,896]{1,0:T(8,128)S(1)}, f32[16,896]{1,0:T(8,128)S(1)}, u32[]{:S(2)}, u32[]{:S(2)}) collective-permute-start(f32[16,896]{1,0:T(8,128)S(1)} %add.81.s0), channel_id=1, source_target_pairs={{0,8},{8,16},{16,24},{24,0},{1,9},{9,17},{17,25},{25,1},{2,10},{10... | collective-permute-start | bytes 172040 | tf_op jit(solution)/shard_map/ppermute | solution.py:483
  69.4 1.6 %collective-permute-start.14 = (f32[16,896]{1,0:T(8,128)S(1)}, f32[16,896]{1,0:T(8,128)S(1)}, u32[]{:S(2)}, u32[]{:S(2)}) collective-permute-start(f32[16,896]{1,0:T(8,128)S(1)} %add.81.s0), channel_id=1, source_target_pairs={{0,16},{8,24},{16,0},{24,8},{1,17},{9,25},{17,1},{25,9},{2,18},{10... | collective-permute-start | bytes 172040 | tf_op jit(solution)/shard_map/ppermute | solution.py:483
  71.1 0.9 collective-permute-start.15
  71.9 1.0 collective-permute-done.13.s1
  72.9 1.5 %collective-permute-done.14.s2 = f32[16,896]{1,0:T(8,128)S(1)} collective-permute-done((f32[16,896]{1,0:T(8,128)S(1)}, f32[16,896]{1,0:T(8,128)S(1)}, u32[]{:S(2)}, u32[]{:S(2)}) %collective-permute-start.14) | collective-permute-done | bytes 57376 | tf_op jit(solution)/shard_map/ppermute | solution.py:483
  74.8 1.2 %shard_map.44 = f32[16,512]{1,0:T(8,128)S(1)} custom-call(bf16[16,2,32,768]{3,2,1,0:T(8,128)(2,1)S(1)} %all-to-all-done.v_ref, f32[16,512]{1,0:T(8,128)S(1)} %get-tuple-element.38.z_ref, f32[16,896]{1,0:T(8,128)S(1)} %add.81.s0, f32[16,896]{1,0:T(8,128)S(1)} %collective-permute-done.13.s1, f32[16,896]{1,0:T(8,128)S(1)} %collective-permute-done.14.s2, ...), custom_call_target="tpu_custom_call" | custom-call | flops 4499999744 | bytes 15000000 | tf_op jit(solution)/shard_map/pallas_call | solution.py:330
  76.0 1.6 %collective-permute-start.16 = (f32[16,512]{1,0:T(8,128)S(1)}, f32[16,512]{1,0:T(8,128)S(1)}, u32[]{:S(2)}, u32[]{:S(2)}) collective-permute-start(f32[16,512]{1,0:T(8,128)S(1)} %shard_map.44), channel_id=1, source_target_pairs={{0,2},{2,4},{4,6},{6,0},{1,3},{3,5},{5,7},{7,1},{8,10},{10,12},{12... | collective-permute-start | bytes 98312 | tf_op jit(solution)/shard_map/ppermute | solution.py:514
  77.6 2.4 %collective-permute-start.17 = (f32[16,512]{1,0:T(8,128)S(1)}, f32[16,512]{1,0:T(8,128)S(1)}, u32[]{:S(2)}, u32[]{:S(2)}) collective-permute-start(f32[16,512]{1,0:T(8,128)S(1)} %shard_map.44), channel_id=1, source_target_pairs={{0,4},{2,6},{4,0},{6,2},{1,5},{3,7},{5,1},{7,3},{8,12},{10,14},{12... | collective-permute-start | bytes 98312 | tf_op jit(solution)/shard_map/ppermute | solution.py:514
  80.0 1.2 %collective-permute-start.18 = (f32[16,512]{1,0:T(8,128)S(1)}, f32[16,512]{1,0:T(8,128)S(1)}, u32[]{:S(2)}, u32[]{:S(2)}) collective-permute-start(f32[16,512]{1,0:T(8,128)S(1)} %shard_map.44), channel_id=1, source_target_pairs={{0,6},{2,0},{4,2},{6,4},{1,7},{3,1},{5,3},{7,5},{8,14},{10,8},{12,... | collective-permute-start | bytes 98312 | tf_op jit(solution)/shard_map/ppermute | solution.py:514
  81.3 3.4 %collective-permute-start.8 = (bf16[16,144,128]{2,1,0:T(8,128)(2,1)S(1)}, bf16[16,144,128]{2,1,0:T(8,128)(2,1)S(1)}, u32[]{:S(2)}, u32[]{:S(2)}) collective-permute-start(bf16[16,144,128]{2,1,0:T(8,128)(2,1)S(1)} %slice_bitcast_fusion), channel_id=1, source_target_pairs={{0,1},{1,0},{2,3},{3,2},{4,5},{5,4},{6,7},{7,6},{8,9},{9,8},{10,11... | collective-permute-start | bytes 1769480 | tf_op jit(solution)/shard_map/ppermute | solution.py:512
  84.7 0.6 select_convert_fusion.place_ref
  85.4 1.5 %collective-permute-start.19 = (f32[4,16,512]{2,1,0:T(8,128)S(1)}, f32[4,16,512]{2,1,0:T(8,128)S(1)}, u32[]{:S(2)}, u32[]{:S(2)}) collective-permute-start(f32[4,16,512]{2,1,0:T(8,128)S(1)} %pad_maximum_fusion.refs_0_), channel_id=1, source_target_pairs={{0,8},{8,16},{16,24},{24,0},{1,9},{9,17},{17,25},{25,1},{2,10},{10... | collective-permute-start | bytes 393224 | tf_op jit(solution)/shard_map/ppermute | solution.py:516
  86.9 2.0 %collective-permute-start.20 = (f32[4,16,512]{2,1,0:T(8,128)S(1)}, f32[4,16,512]{2,1,0:T(8,128)S(1)}, u32[]{:S(2)}, u32[]{:S(2)}) collective-permute-start(f32[4,16,512]{2,1,0:T(8,128)S(1)} %pad_maximum_fusion.refs_0_), channel_id=1, source_target_pairs={{0,16},{8,24},{16,0},{24,8},{1,17},{9,25},{17,1},{25,9},{2,18},{10... | collective-permute-start | bytes 393224 | tf_op jit(solution)/shard_map/ppermute | solution.py:516
  88.8 0.5 collective-permute-start.21
  89.4 1.3 %collective-permute-start.22 = (f32[4,16,512]{2,1,0:T(8,128)S(1)}, f32[4,16,512]{2,1,0:T(8,128)S(1)}, u32[]{:S(2)}, u32[]{:S(2)}) collective-permute-start(f32[4,16,512]{2,1,0:T(8,128)S(1)} %pad_maximum_fusion.refs_0_), channel_id=1, source_target_pairs={{0,1},{1,0},{2,3},{3,2},{4,5},{5,4},{6,7},{7,6},{8,9},{9,8},{10,11... | collective-permute-start | bytes 393224 | tf_op jit(solution)/shard_map/ppermute | solution.py:519
  90.7 1.4 %shard_map.42 = (bf16[4,3,48,1024]{3,2,1,0:T(8,128)(2,1)S(1)}, f32[8,128]{1,0:T(8,128)S(1)}) custom-call(bf16[16,2,144,128]{3,2,1,0:T(8,128)(2,1)S(1)} %all-to-all-done.1.mine_ref, bf16[16,144,128]{2,1,0:T(8,128)(2,1)S(1)} %collective-permute-done.8.theirs_ref, bf16[1024,1024]{1,0:T(8,128)(2,1)S(1)} %select_convert_fusion.place_ref), custom_call_target="tpu_custom_call" | custom-call | flops 3600000000 | bytes 12000000 | tf_op jit(solution)/shard_map/pallas_call | solution.py:362
  92.1 2.7 %collective-permute-done.20.refs_2_ = f32[4,16,512]{2,1,0:T(8,128)S(1)} collective-permute-done((f32[4,16,512]{2,1,0:T(8,128)S(1)}, f32[4,16,512]{2,1,0:T(8,128)S(1)}, u32[]{:S(2)}, u32[]{:S(2)}) %collective-permute-start.20) | collective-permute-done | bytes 131104 | tf_op jit(solution)/shard_map/ppermute | solution.py:516
  94.8 1.3 %collective-permute-start.23 = (f32[4,16,512]{2,1,0:T(8,128)S(1)}, f32[4,16,512]{2,1,0:T(8,128)S(1)}, u32[]{:S(2)}, u32[]{:S(2)}) collective-permute-start(f32[4,16,512]{2,1,0:T(8,128)S(1)} %collective-permute-done.19.refs_1_), channel_id=1, source_target_pairs={{0,1},{1,0},{2,3},{3,2},{4,5},{5,4},{6,7},{7,6},{8,9},{9,8},{10,11... | collective-permute-start | bytes 393224 | tf_op jit(solution)/shard_map/ppermute | solution.py:519
  96.1 0.5 collective-permute-start.25
  96.6 0.5 collective-permute-done.23.refs_5_
  97.6 5.6 %shard_map.45 = f32[2,3,24,4096]{3,2,1,0:T(8,128)} custom-call(bf16[4,3,48,1024]{3,2,1,0:T(8,128)(2,1)S(1)} %get-tuple-element.36.flat, f32[4,16,512]{2,1,0:T(8,128)S(1)} %pad_maximum_fusion.refs_0_, f32[4,16,512]{2,1,0:T(8,128)S(1)} %collective-permute-done.19.refs_1_, f32[4,16,512]{2,1,0:T(8,128)S(1)} %collective-permute-done.20.refs_2_, ...), custom_call_target="tpu_custom_call" | custom-call | flops 5400000000 | bytes 18000000 | tf_op jit(solution)/shard_map/pallas_call | solution.py:463
  (43 shorter events, 2.2 us)
Async XLA Ops:
  10.2 29.1 %all-to-all-start = ((bf16[16,2,32,768]{3,2,1,0:T(8,128)(2,1)}), bf16[16,2,32,768]{3,2,1,0:T(8,128)(2,1)S(1)}, u32[]{:S(2)}, u32[]{:S(2)}) async-start(bf16[16,2,32,768]{3,2,1,0:T(8,128)(2,1)} %shard_map.37.v_ref), calls=%async_computation | async-start | bytes 3145728 | tf_op jit(solution)/shard_map/all_to_all | solution.py:494
  18.7 1.4 %copy-start = (bf16[16,2,32,768]{3,2,1,0:T(8,128)(2,1)S(1)}, bf16[16,2,32,768]{3,2,1,0:T(8,128)(2,1)}, u32[]{:S(2)}) copy-start(bf16[16,2,32,768]{3,2,1,0:T(8,128)(2,1)} %shard_map.37.v_ref) | copy-start | bytes 4718596
  20.1 8.4 %copy-start.4 = (f32[2,8,4096]{2,1,0:T(8,128)S(1)}, f32[2,8,4096]{2,1,0:T(8,128)}, u32[]{:S(2)}) copy-start(f32[2,8,4096]{2,1,0:T(8,128)} %param.5) | copy-start | bytes 786436
  22.8 0.7 copy-start.2
  23.5 23.8 %collective-permute-start = (bf16[2,24,32,128]{3,2,1,0:T(8,128)(2,1)}, bf16[2,24,32,128]{3,2,1,0:T(8,128)(2,1)S(1)}, u32[]{:S(2)}, u32[]{:S(2)}) collective-permute-start(bf16[2,24,32,128]{3,2,1,0:T(8,128)(2,1)} %get-tuple-element.26), channel_id=1, source_target_pairs={{0,8},{8,16},{16,24},{24,0},{1,9},{9,17},{17,25},{25,1},{2,10},{10... | collective-permute-start | bytes 1179656 | tf_op jit(solution)/shard_map/ppermute | solution.py:496
  24.8 24.2 %collective-permute-start.1 = (bf16[2,24,32,128]{3,2,1,0:T(8,128)(2,1)}, bf16[2,24,32,128]{3,2,1,0:T(8,128)(2,1)S(1)}, u32[]{:S(2)}, u32[]{:S(2)}) collective-permute-start(bf16[2,24,32,128]{3,2,1,0:T(8,128)(2,1)} %get-tuple-element.27), channel_id=1, source_target_pairs={{0,16},{8,24},{16,0},{24,8},{1,17},{9,25},{17,1},{25,9},{2,18},{10... | collective-permute-start | bytes 1179656 | tf_op jit(solution)/shard_map/ppermute | solution.py:496
  27.5 21.6 %collective-permute-start.2 = (bf16[2,24,32,128]{3,2,1,0:T(8,128)(2,1)S(1)}, bf16[2,24,32,128]{3,2,1,0:T(8,128)(2,1)S(1)}, u32[]{:S(2)}, u32[]{:S(2)}) collective-permute-start(bf16[2,24,32,128]{3,2,1,0:T(8,128)(2,1)S(1)} %get-tuple-element.28), channel_id=1, source_target_pairs={{0,24},{8,0},{16,8},{24,16},{1,25},{9,1},{17,9},{25,17},{2,26},{10... | collective-permute-start | bytes 1179656 | tf_op jit(solution)/shard_map/ppermute | solution.py:496
  39.6 5.1 %collective-permute-start.3 = (f32[16,768]{1,0:T(8,128)S(1)}, f32[16,768]{1,0:T(8,128)S(1)}, u32[]{:S(2)}, u32[]{:S(2)}) collective-permute-start(f32[16,768]{1,0:T(8,128)S(1)} %shard_map.39), channel_id=1, source_target_pairs={{0,1},{1,0},{2,3},{3,2},{4,5},{5,4},{6,7},{7,6},{8,9},{9,8},{10,11... | collective-permute-start | bytes 147464 | tf_op jit(solution)/shard_map/ppermute | solution.py:487
  44.6 4.4 %collective-permute-start.4 = (f32[16,768]{1,0:T(8,128)S(1)}, f32[16,768]{1,0:T(8,128)S(1)}, u32[]{:S(2)}, u32[]{:S(2)}) collective-permute-start(f32[16,768]{1,0:T(8,128)S(1)} %add.69.s0), channel_id=1, source_target_pairs={{0,24},{8,0},{16,8},{24,16},{1,25},{9,1},{17,9},{25,17},{2,26},{10... | collective-permute-start | bytes 147464 | tf_op jit(solution)/shard_map/ppermute | solution.py:483
  47.4 4.4 %collective-permute-start.5 = (f32[16,768]{1,0:T(8,128)S(1)}, f32[16,768]{1,0:T(8,128)S(1)}, u32[]{:S(2)}, u32[]{:S(2)}) collective-permute-start(f32[16,768]{1,0:T(8,128)S(1)} %add.69.s0), channel_id=1, source_target_pairs={{0,8},{8,16},{16,24},{24,0},{1,9},{9,17},{17,25},{25,1},{2,10},{10... | collective-permute-start | bytes 147464 | tf_op jit(solution)/shard_map/ppermute | solution.py:483
  47.4 4.8 %collective-permute-start.6 = (f32[16,768]{1,0:T(8,128)S(1)}, f32[16,768]{1,0:T(8,128)S(1)}, u32[]{:S(2)}, u32[]{:S(2)}) collective-permute-start(f32[16,768]{1,0:T(8,128)S(1)} %add.69.s0), channel_id=1, source_target_pairs={{0,16},{8,24},{16,0},{24,8},{1,17},{9,25},{17,1},{25,9},{2,18},{10... | collective-permute-start | bytes 147464 | tf_op jit(solution)/shard_map/ppermute | solution.py:483
  49.0 6.0 %copy-start.3 = (bf16[2,24,32,128]{3,2,1,0:T(8,128)(2,1)S(1)}, bf16[2,24,32,128]{3,2,1,0:T(8,128)(2,1)}, u32[]{:S(2)}) copy-start(bf16[2,24,32,128]{3,2,1,0:T(8,128)(2,1)} %copy-done.2) | copy-start | bytes 1179652
  53.2 4.0 %collective-permute-start.7 = (f32[16,896]{1,0:T(8,128)S(1)}, f32[16,896]{1,0:T(8,128)S(1)}, u32[]{:S(2)}, u32[]{:S(2)}) collective-permute-start(f32[16,896]{1,0:T(8,128)S(1)} %get-tuple-element.34), channel_id=1, source_target_pairs={{0,1},{1,0},{2,3},{3,2},{4,5},{5,4},{6,7},{7,6},{8,9},{9,8},{10,11... | collective-permute-start | bytes 172040 | tf_op jit(solution)/shard_map/ppermute | solution.py:487
  56.2 1.0 copy-start.1
  57.2 7.1 %collective-permute-start.10 = (f32[16,896]{1,0:T(8,128)S(1)}, f32[16,896]{1,0:T(8,128)S(1)}, u32[]{:S(2)}, u32[]{:S(2)}) collective-permute-start(f32[16,896]{1,0:T(8,128)S(1)} %add.70.s0), channel_id=1, source_target_pairs={{0,16},{8,24},{16,0},{24,8},{1,17},{9,25},{17,1},{25,9},{2,18},{10... | collective-permute-start | bytes 172040 | tf_op jit(solution)/shard_map/ppermute | solution.py:483
  59.0 5.3 %collective-permute-start.11 = (f32[16,896]{1,0:T(8,128)S(1)}, f32[16,896]{1,0:T(8,128)S(1)}, u32[]{:S(2)}, u32[]{:S(2)}) collective-permute-start(f32[16,896]{1,0:T(8,128)S(1)} %add.70.s0), channel_id=1, source_target_pairs={{0,24},{8,0},{16,8},{24,16},{1,25},{9,1},{17,9},{25,17},{2,26},{10... | collective-permute-start | bytes 172040 | tf_op jit(solution)/shard_map/ppermute | solution.py:483
  60.1 4.2 %collective-permute-start.9 = (f32[16,896]{1,0:T(8,128)S(1)}, f32[16,896]{1,0:T(8,128)S(1)}, u32[]{:S(2)}, u32[]{:S(2)}) collective-permute-start(f32[16,896]{1,0:T(8,128)S(1)} %add.70.s0), channel_id=1, source_target_pairs={{0,8},{8,16},{16,24},{24,0},{1,9},{9,17},{17,25},{25,1},{2,10},{10... | collective-permute-start | bytes 172040 | tf_op jit(solution)/shard_map/ppermute | solution.py:483
  60.6 20.7 %all-to-all-start.1 = ((bf16[16,2,144,128]{3,2,1,0:T(8,128)(2,1)}), bf16[16,2,144,128]{3,2,1,0:T(8,128)(2,1)S(1)}, u32[]{:S(2)}, u32[]{:S(2)}) async-start(bf16[16,2,144,128]{3,2,1,0:T(8,128)(2,1)} %copy-done.1), calls=%async_computation.1 | async-start | bytes 2359296 | tf_op jit(solution)/shard_map/all_to_all | solution.py:509
  66.0 2.3 %collective-permute-start.12 = (f32[16,896]{1,0:T(8,128)S(1)}, f32[16,896]{1,0:T(8,128)S(1)}, u32[]{:S(2)}, u32[]{:S(2)}) collective-permute-start(f32[16,896]{1,0:T(8,128)S(1)} %get-tuple-element.39), channel_id=1, source_target_pairs={{0,1},{1,0},{2,3},{3,2},{4,5},{5,4},{6,7},{7,6},{8,9},{9,8},{10,11... | collective-permute-start | bytes 172040 | tf_op jit(solution)/shard_map/ppermute | solution.py:487
  68.4 4.6 %collective-permute-start.13 = (f32[16,896]{1,0:T(8,128)S(1)}, f32[16,896]{1,0:T(8,128)S(1)}, u32[]{:S(2)}, u32[]{:S(2)}) collective-permute-start(f32[16,896]{1,0:T(8,128)S(1)} %add.81.s0), channel_id=1, source_target_pairs={{0,8},{8,16},{16,24},{24,0},{1,9},{9,17},{17,25},{25,1},{2,10},{10... | collective-permute-start | bytes 172040 | tf_op jit(solution)/shard_map/ppermute | solution.py:483
  69.4 4.9 %collective-permute-start.14 = (f32[16,896]{1,0:T(8,128)S(1)}, f32[16,896]{1,0:T(8,128)S(1)}, u32[]{:S(2)}, u32[]{:S(2)}) collective-permute-start(f32[16,896]{1,0:T(8,128)S(1)} %add.81.s0), channel_id=1, source_target_pairs={{0,16},{8,24},{16,0},{24,8},{1,17},{9,25},{17,1},{25,9},{2,18},{10... | collective-permute-start | bytes 172040 | tf_op jit(solution)/shard_map/ppermute | solution.py:483
  71.1 3.7 %collective-permute-start.15 = (f32[16,896]{1,0:T(8,128)S(1)}, f32[16,896]{1,0:T(8,128)S(1)}, u32[]{:S(2)}, u32[]{:S(2)}) collective-permute-start(f32[16,896]{1,0:T(8,128)S(1)} %add.81.s0), channel_id=1, source_target_pairs={{0,24},{8,0},{16,8},{24,16},{1,25},{9,1},{17,9},{25,17},{2,26},{10... | collective-permute-start | bytes 172040 | tf_op jit(solution)/shard_map/ppermute | solution.py:483
  76.0 9.4 %collective-permute-start.16 = (f32[16,512]{1,0:T(8,128)S(1)}, f32[16,512]{1,0:T(8,128)S(1)}, u32[]{:S(2)}, u32[]{:S(2)}) collective-permute-start(f32[16,512]{1,0:T(8,128)S(1)} %shard_map.44), channel_id=1, source_target_pairs={{0,2},{2,4},{4,6},{6,0},{1,3},{3,5},{5,7},{7,1},{8,10},{10,12},{12... | collective-permute-start | bytes 98312 | tf_op jit(solution)/shard_map/ppermute | solution.py:514
  77.6 7.8 %collective-permute-start.17 = (f32[16,512]{1,0:T(8,128)S(1)}, f32[16,512]{1,0:T(8,128)S(1)}, u32[]{:S(2)}, u32[]{:S(2)}) collective-permute-start(f32[16,512]{1,0:T(8,128)S(1)} %shard_map.44), channel_id=1, source_target_pairs={{0,4},{2,6},{4,0},{6,2},{1,5},{3,7},{5,1},{7,3},{8,12},{10,14},{12... | collective-permute-start | bytes 98312 | tf_op jit(solution)/shard_map/ppermute | solution.py:514
  80.0 5.4 %collective-permute-start.18 = (f32[16,512]{1,0:T(8,128)S(1)}, f32[16,512]{1,0:T(8,128)S(1)}, u32[]{:S(2)}, u32[]{:S(2)}) collective-permute-start(f32[16,512]{1,0:T(8,128)S(1)} %shard_map.44), channel_id=1, source_target_pairs={{0,6},{2,0},{4,2},{6,4},{1,7},{3,1},{5,3},{7,5},{8,14},{10,8},{12,... | collective-permute-start | bytes 98312 | tf_op jit(solution)/shard_map/ppermute | solution.py:514
  81.3 9.4 %collective-permute-start.8 = (bf16[16,144,128]{2,1,0:T(8,128)(2,1)S(1)}, bf16[16,144,128]{2,1,0:T(8,128)(2,1)S(1)}, u32[]{:S(2)}, u32[]{:S(2)}) collective-permute-start(bf16[16,144,128]{2,1,0:T(8,128)(2,1)S(1)} %slice_bitcast_fusion), channel_id=1, source_target_pairs={{0,1},{1,0},{2,3},{3,2},{4,5},{5,4},{6,7},{7,6},{8,9},{9,8},{10,11... | collective-permute-start | bytes 1769480 | tf_op jit(solution)/shard_map/ppermute | solution.py:512
  85.4 6.7 %collective-permute-start.19 = (f32[4,16,512]{2,1,0:T(8,128)S(1)}, f32[4,16,512]{2,1,0:T(8,128)S(1)}, u32[]{:S(2)}, u32[]{:S(2)}) collective-permute-start(f32[4,16,512]{2,1,0:T(8,128)S(1)} %pad_maximum_fusion.refs_0_), channel_id=1, source_target_pairs={{0,8},{8,16},{16,24},{24,0},{1,9},{9,17},{17,25},{25,1},{2,10},{10... | collective-permute-start | bytes 393224 | tf_op jit(solution)/shard_map/ppermute | solution.py:516
  86.9 7.9 %collective-permute-start.20 = (f32[4,16,512]{2,1,0:T(8,128)S(1)}, f32[4,16,512]{2,1,0:T(8,128)S(1)}, u32[]{:S(2)}, u32[]{:S(2)}) collective-permute-start(f32[4,16,512]{2,1,0:T(8,128)S(1)} %pad_maximum_fusion.refs_0_), channel_id=1, source_target_pairs={{0,16},{8,24},{16,0},{24,8},{1,17},{9,25},{17,1},{25,9},{2,18},{10... | collective-permute-start | bytes 393224 | tf_op jit(solution)/shard_map/ppermute | solution.py:516
  88.8 5.9 %collective-permute-start.21 = (f32[4,16,512]{2,1,0:T(8,128)S(1)}, f32[4,16,512]{2,1,0:T(8,128)S(1)}, u32[]{:S(2)}, u32[]{:S(2)}) collective-permute-start(f32[4,16,512]{2,1,0:T(8,128)S(1)} %pad_maximum_fusion.refs_0_), channel_id=1, source_target_pairs={{0,24},{8,0},{16,8},{24,16},{1,25},{9,1},{17,9},{25,17},{2,26},{10... | collective-permute-start | bytes 393224 | tf_op jit(solution)/shard_map/ppermute | solution.py:516
  89.4 7.3 %collective-permute-start.22 = (f32[4,16,512]{2,1,0:T(8,128)S(1)}, f32[4,16,512]{2,1,0:T(8,128)S(1)}, u32[]{:S(2)}, u32[]{:S(2)}) collective-permute-start(f32[4,16,512]{2,1,0:T(8,128)S(1)} %pad_maximum_fusion.refs_0_), channel_id=1, source_target_pairs={{0,1},{1,0},{2,3},{3,2},{4,5},{5,4},{6,7},{7,6},{8,9},{9,8},{10,11... | collective-permute-start | bytes 393224 | tf_op jit(solution)/shard_map/ppermute | solution.py:519
  94.8 2.3 %collective-permute-start.23 = (f32[4,16,512]{2,1,0:T(8,128)S(1)}, f32[4,16,512]{2,1,0:T(8,128)S(1)}, u32[]{:S(2)}, u32[]{:S(2)}) collective-permute-start(f32[4,16,512]{2,1,0:T(8,128)S(1)} %collective-permute-done.19.refs_1_), channel_id=1, source_target_pairs={{0,1},{1,0},{2,3},{3,2},{4,5},{5,4},{6,7},{7,6},{8,9},{9,8},{10,11... | collective-permute-start | bytes 393224 | tf_op jit(solution)/shard_map/ppermute | solution.py:519
  96.1 1.3 %collective-permute-start.24 = (f32[4,16,512]{2,1,0:T(8,128)S(1)}, f32[4,16,512]{2,1,0:T(8,128)S(1)}, u32[]{:S(2)}, u32[]{:S(2)}) collective-permute-start(f32[4,16,512]{2,1,0:T(8,128)S(1)} %collective-permute-done.20.refs_2_), channel_id=1, source_target_pairs={{0,1},{1,0},{2,3},{3,2},{4,5},{5,4},{6,7},{7,6},{8,9},{9,8},{10,11... | collective-permute-start | bytes 393224 | tf_op jit(solution)/shard_map/ppermute | solution.py:519
  96.1 1.5 %collective-permute-start.25 = (f32[4,16,512]{2,1,0:T(8,128)S(1)}, f32[4,16,512]{2,1,0:T(8,128)S(1)}, u32[]{:S(2)}, u32[]{:S(2)}) collective-permute-start(f32[4,16,512]{2,1,0:T(8,128)S(1)} %collective-permute-done.21.refs_3_), channel_id=1, source_target_pairs={{0,1},{1,0},{2,3},{3,2},{4,5},{5,4},{6,7},{7,6},{8,9},{9,8},{10,11... | collective-permute-start | bytes 393224 | tf_op jit(solution)/shard_map/ppermute | solution.py:519
